TPU v7x, 32 devices: a whole 2x2x4 slice. The times are simulated.
32 devices in a mesh: section: 2 (over core), fsdp: 8 (over z, x), tp: 2 (over y).
Axes of the slice: x: 2, y: 2, z: 4, core: 2. Of those that a mesh axis runs over, the one named last changes fastest.
Arguments:
- inputs: bfloat16 [8, 2, 512, 2048], P('fsdp', None, 'tp'), may hold values from -6 to 6
- cotangent: bfloat16 [8, 2, 512, 2048], P('fsdp', None, 'tp'), may hold values from -6 to 6
- norm_gain: bfloat16 [2, 2048], P('section', 'fsdp'), may hold values from 0.5 to 1.5
- w_zx: bfloat16 [2, 2048, 2, 4096], P('section', 'fsdp', None, 'tp'), may hold values from -1 to 1
- w_bc: bfloat16 [2, 2048, 256], P('section', 'fsdp'), may hold values from -0.125 to 0.125
- w_dt: bfloat16 [2, 2048, 64], P('section', 'fsdp', 'tp'), may hold values from -0.125 to 0.125
- conv_x: float32 [2, 4, 4096], P('section', None, 'tp'), may hold values from -3 to 3
- conv_xb: float32 [2, 4096], P('section', 'tp'), may hold values from -0.5 to 0.5
- conv_bc: float32 [2, 4, 256], P('section'), may hold values from -3 to 3
- conv_bcb: float32 [2, 256], P('section'), may hold values from -0.5 to 0.5
- dt_bias: float32 [2, 64], P('section', 'tp'), may hold values from -5 to -1
- a_log: float32 [2, 64], P('section', 'tp'), may hold values from 0 to 2.77
- d_skip: float32 [2, 64], P('section', 'tp'), may hold values from 0.5 to 2
- gate_gain: float32 [2, 4096], P('section', 'tp'), may hold values from 0.5 to 1.5
- w_out: bfloat16 [2, 2048, 4096], P('section', 'fsdp', 'tp'), may hold values from -0.09375 to 0.09375
Outputs:
- outputs: float32 [8, 2, 512, 2048], P('fsdp', 'section', 'tp')
- grad_inputs: float32 [8, 2, 512, 2048], P('fsdp', 'section', 'tp')
- grad_norm_gain: float32 [2, 2048], P('section', 'fsdp')
- grad_w_zx: float32 [2, 2048, 2, 4096], P('section', 'fsdp', None, 'tp')
- grad_w_bc: float32 [2, 2048, 256], P('section', 'fsdp')
- grad_w_dt: float32 [2, 2048, 64], P('section', 'fsdp', 'tp')
- grad_conv_x: float32 [2, 4, 4096], P('section', None, 'tp')
- grad_conv_xb: float32 [2, 4096], P('section', 'tp')
- grad_conv_bc: float32 [2, 4, 256], P('section')
- grad_conv_bcb: float32 [2, 256], P('section')
- grad_dt_bias: float32 [2, 64], P('section', 'tp')
- grad_a_log: float32 [2, 64], P('section', 'tp')
- grad_d_skip: float32 [2, 64], P('section', 'tp')
- grad_gate_gain: float32 [2, 4096], P('section', 'tp')
- grad_w_out: float32 [2, 2048, 4096], P('section', 'fsdp', 'tp')
All inputs are finite; a program needn't handle non-finite values.
Results may differ from a plain program's by a relative error of at most 0.015.
Values may be sent and summed in bfloat16 or wider, within the bound.
A program may use at most 320 MiB of HBM per device.

v0:
```python
import jax
import jax.numpy as jnp
from jax import lax
from jax.sharding import PartitionSpec as P

CONV = 4
BLOCK = 256
DI = 4096


NORM_EPSILON = 1e-05
HIGHEST_PRECISION = lax.Precision.HIGHEST


def passed_along(block, axis, distance):
    devices = range(lax.axis_size(axis))
    route = [((i - distance) % len(devices), i) for i in devices]
    return lax.ppermute(block, axis, route)


def causal_conv(pre_rows, carried_rows, kernel, offset):
    kernel_width = kernel.shape[0]
    length = pre_rows.shape[0]
    padded = jnp.concatenate([carried_rows, pre_rows], axis=0)
    result = offset[None, :] + kernel[kernel_width - 1][None, :] * padded[kernel_width - 1 :]
    for offset_step in range(kernel_width - 1):
        result = result + kernel[offset_step][None, :] * padded[offset_step : offset_step + length]
    return (result, padded[length:])


def scan_heads(head_inputs, step_sizes, decay_rates, in_map, out_map, carried, block_len):
    length = head_inputs.shape[0]
    log_decay = step_sizes * decay_rates[None, :]
    positions = jnp.arange(block_len)
    causal = positions[:, None] >= positions[None, :]
    pieces = []
    for number in range(length // block_len):
        first_row = number * block_len
        scaled_inputs = (
            head_inputs[first_row : first_row + block_len]
            * step_sizes[first_row : first_row + block_len][:, :, None]
        )
        block_in = in_map[first_row : first_row + block_len]
        block_out = out_map[first_row : first_row + block_len]
        cumulative = jnp.cumsum(log_decay[first_row : first_row + block_len], axis=0)
        by_head = cumulative.T
        log_gaps = by_head[:, :, None] - by_head[:, None, :]
        weights = jnp.exp(jnp.where(causal[None], log_gaps, -10000.0))
        scores = jnp.dot(block_out, block_in.T, precision=HIGHEST_PRECISION)
        within = jnp.einsum(
            "hij,jhp->ihp", weights * scores[None], scaled_inputs, precision=HIGHEST_PRECISION
        )
        entering = (
            jnp.einsum("in,hpn->ihp", block_out, carried, precision=HIGHEST_PRECISION)
            * jnp.exp(cumulative)[:, :, None]
        )
        pieces.append(within + entering)
        remaining = jnp.exp(cumulative[-1:] - cumulative)
        carried = carried * jnp.exp(cumulative[-1])[:, None, None] + jnp.einsum(
            "jhp,jn->hpn",
            scaled_inputs * remaining[:, :, None],
            block_in,
            precision=HIGHEST_PRECISION,
        )
    return (jnp.concatenate(pieces, axis=0), carried)


def mix_tokens(pre_zx, pre_bc, pre_dt, head_params, carried, tail_x, tail_bc):
    conv_x, conv_xb, conv_bc, conv_bcb, dt_bias, a_log, d_skip = head_params
    head_count = pre_dt.shape[1]
    state_size = pre_bc.shape[1] // 2
    length = pre_zx.shape[0]
    conv_rows_x, tail_x = causal_conv(pre_zx[:, 1], tail_x, conv_x, conv_xb)
    conv_rows_bc, tail_bc = causal_conv(pre_bc, tail_bc, conv_bc, conv_bcb)
    head_inputs = jax.nn.silu(conv_rows_x).reshape(length, head_count, -1)
    shared = jax.nn.silu(conv_rows_bc)
    step_sizes = jax.nn.softplus(pre_dt + dt_bias[None, :])
    decay_rates = -jnp.exp(a_log)
    outputs, carried = scan_heads(
        head_inputs,
        step_sizes,
        decay_rates,
        shared[:, :state_size],
        shared[:, state_size:],
        carried,
        BLOCK,
    )
    outputs = outputs + d_skip[None, :, None] * head_inputs
    gated_rows = outputs.reshape(length, -1) * jax.nn.silu(pre_zx[:, 0])
    return (gated_rows, jnp.sum(gated_rows * gated_rows, axis=1), carried, tail_x, tail_bc)


def norm_rows(residual, gain_row):
    scale_rows = lax.rsqrt(jnp.mean(residual * residual, axis=1, keepdims=True) + NORM_EPSILON)
    return residual * scale_rows * gain_row[None, :]


def gate_norm(gated_rows, squares, gain_row):
    return gated_rows * lax.rsqrt(squares[:, None] / DI + NORM_EPSILON) * gain_row[None, :]


def put_row(buffer_rows, slot_index, value_rows, is_live):
    previous = lax.dynamic_index_in_dim(buffer_rows, slot_index, 0, keepdims=False)
    return lax.dynamic_update_index_in_dim(
        buffer_rows, jnp.where(is_live, value_rows, previous), slot_index, 0
    )


def take_row(buffer_rows, slot_index):
    return lax.dynamic_index_in_dim(buffer_rows, slot_index, 0, keepdims=False)


def weight_terms(normed_rows, grad_zx, grad_bc, grad_dt, grad_branch, mixed_rows):
    return (
        jnp.einsum("td,tkc->dkc", normed_rows, grad_zx, preferred_element_type=jnp.float32)[None],
        jnp.einsum("td,tj->dj", normed_rows, grad_bc, preferred_element_type=jnp.float32)[None],
        jnp.einsum("td,tj->dj", normed_rows, grad_dt, preferred_element_type=jnp.float32)[None],
        jnp.einsum("td,tc->dc", grad_branch, mixed_rows, preferred_element_type=jnp.float32)[None],
    )


def local(
    inputs,
    cotangent,
    norm_gain,
    w_zx,
    w_bc,
    w_dt,
    conv_x,
    conv_xb,
    conv_bc,
    conv_bcb,
    dt_bias,
    a_log,
    d_skip,
    gate_gain,
    w_out,
):
    section_count = lax.axis_size("section")
    section_index = lax.axis_index("section")
    tp_first = (lax.axis_index("tp") == 0).astype(jnp.float32)
    micro_count = inputs.shape[1]
    tick_count = micro_count + section_count - 1
    local_rows = inputs.shape[2]
    width_model = inputs.shape[3]
    gathered_weights = (
        lax.all_gather(norm_gain, "fsdp", axis=1, tiled=True),
        lax.all_gather(w_zx, "fsdp", axis=1, tiled=True),
        lax.all_gather(w_bc, "fsdp", axis=1, tiled=True),
        lax.all_gather(w_dt, "fsdp", axis=1, tiled=True),
        lax.all_gather(w_out, "fsdp", axis=1, tiled=True),
    )
    gain_in, proj_zx, proj_bc, proj_dt, proj_out = [tensor[0] for tensor in gathered_weights]
    gain_float = gain_in.astype(jnp.float32)
    small_params = (conv_x[0], conv_xb[0], conv_bc[0], conv_bcb[0], dt_bias[0], a_log[0], d_skip[0])
    gate_row = gate_gain[0]
    head_count = dt_bias.shape[1]
    channels = conv_x.shape[2]
    pair_width = conv_bc.shape[2]
    block_rows = local_rows * lax.axis_size("tp")
    state_shape = (head_count, channels // head_count, pair_width // 2)
    input_rows = inputs[0]
    upstream_rows_all = cotangent[0]

    def forward_tick(tick_number, state):
        (
            incoming,
            wrapped_rows,
            result,
            carried,
            tail_x,
            tail_bc,
            saved_resid,
            saved_normed,
            saved_zx,
            saved_bc,
            saved_dt,
            saved_state,
            saved_tail_x,
            saved_tail_bc,
            saved_squares,
            saved_mixed,
        ) = state
        micro_index = tick_number - section_index
        is_live = (micro_index >= 0) & (micro_index < micro_count)
        slot_index = jnp.clip(micro_index, 0, micro_count - 1)
        fresh_rows = take_row(input_rows, slot_index).astype(jnp.float32)
        residual = jnp.where(section_index == 0, fresh_rows, incoming)
        normed = norm_rows(residual, gain_float).astype(jnp.bfloat16)
        normed_all = lax.all_gather(normed, "tp", axis=0, tiled=True)
        pre_zx = jnp.einsum("td,dkc->tkc", normed_all, proj_zx, preferred_element_type=jnp.float32)
        pre_bc = jnp.dot(normed_all, proj_bc, preferred_element_type=jnp.float32)
        pre_dt = jnp.dot(normed_all, proj_dt, preferred_element_type=jnp.float32)
        gated_rows, squares_part, next_state, next_tail_x, next_tail_bc = mix_tokens(
            pre_zx, pre_bc, pre_dt, small_params, carried, tail_x, tail_bc
        )
        squares = lax.psum(squares_part, "tp")
        mixed_rows = gate_norm(gated_rows, squares, gate_row).astype(jnp.bfloat16)
        partial_rows = jnp.einsum(
            "tc,dc->td", mixed_rows, proj_out, preferred_element_type=jnp.float32
        )
        branch = lax.psum_scatter(partial_rows, "tp", scatter_dimension=0, tiled=True)
        result = residual + branch
        saved_resid = put_row(saved_resid, slot_index, residual, is_live)
        saved_normed = put_row(saved_normed, slot_index, normed_all, is_live)
        saved_zx = put_row(saved_zx, slot_index, pre_zx, is_live)
        saved_bc = put_row(saved_bc, slot_index, pre_bc, is_live)
        saved_dt = put_row(saved_dt, slot_index, pre_dt, is_live)
        saved_state = put_row(saved_state, slot_index, carried, is_live)
        saved_tail_x = put_row(saved_tail_x, slot_index, tail_x, is_live)
        saved_tail_bc = put_row(saved_tail_bc, slot_index, tail_bc, is_live)
        saved_squares = put_row(saved_squares, slot_index, squares, is_live)
        saved_mixed = put_row(saved_mixed, slot_index, mixed_rows, is_live)
        carried = jnp.where(is_live, next_state, carried)
        tail_x = jnp.where(is_live, next_tail_x, tail_x)
        tail_bc = jnp.where(is_live, next_tail_bc, tail_bc)
        incoming = passed_along(result, "section", 1)
        wrapped_rows = jnp.where(tick_number == section_count - 1, incoming, wrapped_rows)
        return (
            incoming,
            wrapped_rows,
            result,
            carried,
            tail_x,
            tail_bc,
            saved_resid,
            saved_normed,
            saved_zx,
            saved_bc,
            saved_dt,
            saved_state,
            saved_tail_x,
            saved_tail_bc,
            saved_squares,
            saved_mixed,
        )

    zero_rows = jnp.zeros((local_rows, width_model), jnp.float32)
    forward_start = (
        zero_rows,
        zero_rows,
        zero_rows,
        jnp.zeros(state_shape, jnp.float32),
        jnp.zeros((CONV - 1, channels), jnp.float32),
        jnp.zeros((CONV - 1, pair_width), jnp.float32),
        jnp.zeros((micro_count, local_rows, width_model), jnp.float32),
        jnp.zeros((micro_count, block_rows, width_model), jnp.bfloat16),
        jnp.zeros((micro_count, block_rows, 2, channels), jnp.float32),
        jnp.zeros((micro_count, block_rows, pair_width), jnp.float32),
        jnp.zeros((micro_count, block_rows, head_count), jnp.float32),
        jnp.zeros((micro_count,) + state_shape, jnp.float32),
        jnp.zeros((micro_count, CONV - 1, channels), jnp.float32),
        jnp.zeros((micro_count, CONV - 1, pair_width), jnp.float32),
        jnp.zeros((micro_count, block_rows), jnp.float32),
        jnp.zeros((micro_count, block_rows, channels), jnp.bfloat16),
    )
    (
        unused_incoming,
        wrapped_rows,
        result,
        unused_carried,
        unused_tail_x,
        unused_tail_bc,
        saved_resid,
        saved_normed,
        saved_zx,
        saved_bc,
        saved_dt,
        saved_state,
        saved_tail_x,
        saved_tail_bc,
        saved_squares,
        saved_mixed,
    ) = lax.fori_loop(0, tick_count, forward_tick, forward_start)
    output_rows = jnp.where(section_index == 0, wrapped_rows, result)

    def backward_tick(tick_number, state):
        (
            grad_in,
            wrapped_grad,
            grad_start,
            grad_state,
            grad_tail_x,
            grad_tail_bc,
            head_totals,
            gate_total,
            norm_total,
            store_zx,
            store_bc,
            store_dt,
            store_branch,
            running,
        ) = state
        micro_index = micro_count - 1 - tick_number + section_count - 1 - section_index
        is_live = (micro_index >= 0) & (micro_index < micro_count)
        slot_index = jnp.clip(micro_index, 0, micro_count - 1)
        upstream = take_row(upstream_rows_all, slot_index).astype(jnp.float32)
        grad_result = jnp.where(section_index == section_count - 1, upstream, grad_in)
        grad_branch = lax.all_gather(grad_result.astype(jnp.bfloat16), "tp", axis=0, tiled=True)
        grad_mixed = jnp.dot(grad_branch, proj_out, preferred_element_type=jnp.float32)
        mixer_out, mixer_pull = jax.vjp(
            mix_tokens,
            take_row(saved_zx, slot_index),
            take_row(saved_bc, slot_index),
            take_row(saved_dt, slot_index),
            small_params,
            take_row(saved_state, slot_index),
            take_row(saved_tail_x, slot_index),
            take_row(saved_tail_bc, slot_index),
        )
        gate_out, gate_pull = jax.vjp(
            gate_norm, mixer_out[0], take_row(saved_squares, slot_index), gate_row
        )
        grad_gated, grad_squares_part, grad_gate_row = gate_pull(grad_mixed)
        grad_squares = lax.psum(grad_squares_part, "tp")
        (
            grad_zx,
            grad_bc_part,
            grad_dt,
            grad_head,
            grad_state_in,
            grad_tail_x_in,
            grad_tail_bc_in,
        ) = mixer_pull((grad_gated, grad_squares, grad_state, grad_tail_x, grad_tail_bc))
        grad_bc = lax.psum(grad_bc_part, "tp")
        zx_low = grad_zx.astype(jnp.bfloat16)
        bc_low = grad_bc.astype(jnp.bfloat16)
        dt_low = grad_dt.astype(jnp.bfloat16)
        grad_normed_part = jnp.einsum(
            "tkc,dkc->td", zx_low, proj_zx, preferred_element_type=jnp.float32
        )
        grad_normed_part = grad_normed_part + jnp.einsum(
            "tj,dj->td", dt_low, proj_dt, preferred_element_type=jnp.float32
        )
        grad_normed_part = grad_normed_part + tp_first * jnp.einsum(
            "tj,dj->td", bc_low, proj_bc, preferred_element_type=jnp.float32
        )
        grad_normed = lax.psum_scatter(grad_normed_part, "tp", scatter_dimension=0, tiled=True)
        unused_norm, norm_pull = jax.vjp(norm_rows, take_row(saved_resid, slot_index), gain_float)
        grad_residual, grad_gain = norm_pull(grad_normed)
        grad_start = grad_result + grad_residual
        head_totals = tuple(
            (
                total_part + jnp.where(is_live, tick_part, 0.0)
                for total_part, tick_part in zip(head_totals, grad_head)
            )
        )
        gate_total = gate_total + jnp.where(is_live, grad_gate_row, 0.0)
        grad_state = jnp.where(is_live, grad_state_in, grad_state)
        grad_tail_x = jnp.where(is_live, grad_tail_x_in, grad_tail_x)
        grad_tail_bc = jnp.where(is_live, grad_tail_bc_in, grad_tail_bc)
        norm_total = norm_total + jnp.where(is_live, grad_gain, 0.0)
        store_zx = put_row(store_zx, slot_index, zx_low, is_live)
        store_bc = put_row(store_bc, slot_index, bc_low, is_live)
        store_dt = put_row(store_dt, slot_index, dt_low, is_live)
        store_branch = put_row(store_branch, slot_index, grad_branch, is_live)
        grad_in = passed_along(grad_start.astype(jnp.bfloat16), "section", -1).astype(
            grad_start.dtype
        )
        wrapped_grad = jnp.where(tick_number == section_count - 1, grad_in, wrapped_grad)
        return (
            grad_in,
            wrapped_grad,
            grad_start,
            grad_state,
            grad_tail_x,
            grad_tail_bc,
            head_totals,
            gate_total,
            norm_total,
            store_zx,
            store_bc,
            store_dt,
            store_branch,
            running,
        )

    backward_start = (
        zero_rows,
        zero_rows,
        zero_rows,
        jnp.zeros(state_shape, jnp.float32),
        jnp.zeros((CONV - 1, channels), jnp.float32),
        jnp.zeros((CONV - 1, pair_width), jnp.float32),
        tuple((jnp.zeros_like(tensor) for tensor in small_params)),
        jnp.zeros_like(gate_row),
        jnp.zeros((width_model,), jnp.float32),
        jnp.zeros((micro_count, block_rows, 2, channels), jnp.bfloat16),
        jnp.zeros((micro_count, block_rows, pair_width), jnp.bfloat16),
        jnp.zeros((micro_count, block_rows, head_count), jnp.bfloat16),
        jnp.zeros((micro_count, block_rows, width_model), jnp.bfloat16),
        (
            jnp.zeros(norm_gain.shape, jnp.float32),
            jnp.zeros(w_zx.shape, jnp.float32),
            jnp.zeros(w_bc.shape, jnp.float32),
            jnp.zeros(w_dt.shape, jnp.float32),
            jnp.zeros(w_out.shape, jnp.float32),
        ),
    )
    (
        unused_grad_in,
        wrapped_grad,
        grad_start,
        unused_grad_state,
        unused_grad_tail_x,
        unused_grad_tail_bc,
        head_totals,
        gate_total,
        norm_total,
        store_zx,
        store_bc,
        store_dt,
        store_branch,
        running,
    ) = lax.fori_loop(0, tick_count, backward_tick, backward_start)
    input_grads = jnp.where(section_index == 0, grad_start, wrapped_grad)
    rows_all = micro_count * block_rows
    all_terms = weight_terms(
        saved_normed.reshape(rows_all, width_model),
        store_zx.reshape(rows_all, 2, channels),
        store_bc.reshape(rows_all, pair_width),
        store_dt.reshape(rows_all, head_count),
        store_branch.reshape(rows_all, width_model),
        saved_mixed.reshape(rows_all, channels),
    )
    summed = (
        lax.psum_scatter(norm_total[None], "fsdp", scatter_dimension=1, tiled=True),
        lax.psum_scatter(all_terms[0], "fsdp", scatter_dimension=1, tiled=True),
        lax.psum_scatter(all_terms[1], "fsdp", scatter_dimension=1, tiled=True),
        lax.psum_scatter(all_terms[2], "fsdp", scatter_dimension=1, tiled=True),
        lax.psum_scatter(all_terms[3], "fsdp", scatter_dimension=1, tiled=True),
    )
    head_sums = (
        lax.psum(head_totals[0].astype(jnp.bfloat16), "fsdp").astype(jnp.float32),
        lax.psum(head_totals[1].astype(jnp.bfloat16), "fsdp").astype(jnp.float32),
        lax.psum(head_totals[2].astype(jnp.bfloat16), "fsdp").astype(jnp.float32),
        lax.psum(head_totals[3].astype(jnp.bfloat16), "fsdp").astype(jnp.float32),
        lax.psum(head_totals[4].astype(jnp.bfloat16), "fsdp").astype(jnp.float32),
        lax.psum(head_totals[5].astype(jnp.bfloat16), "fsdp").astype(jnp.float32),
        lax.psum(head_totals[6].astype(jnp.bfloat16), "fsdp").astype(jnp.float32),
        lax.psum(gate_total.astype(jnp.bfloat16), "fsdp").astype(jnp.float32),
    )
    shared_sums = lax.psum((summed[0], head_sums[2], head_sums[3]), "tp")
    return (
        output_rows[None, None],
        input_grads[None, None],
        shared_sums[0],
        summed[1],
        summed[2],
        summed[3],
        head_sums[0][None],
        head_sums[1][None],
        shared_sums[1][None],
        shared_sums[2][None],
        head_sums[4][None],
        head_sums[5][None],
        head_sums[6][None],
        head_sums[7][None],
        summed[4],
    )


def solution(mesh):
    placed = (
        P("fsdp", None, "tp", None),
        P("fsdp", None, "tp", None),
        P("section", "fsdp"),
        P("section", "fsdp", None, "tp"),
        P("section", "fsdp", None),
        P("section", "fsdp", "tp"),
        P("section", None, "tp"),
        P("section", "tp"),
        P("section", None, None),
        P("section", None),
        P("section", "tp"),
        P("section", "tp"),
        P("section", "tp"),
        P("section", "tp"),
        P("section", "fsdp", "tp"),
    )
    return jax.shard_map(
        local,
        mesh=mesh,
        in_specs=placed,
        out_specs=(
            P("fsdp", "section", "tp", None),
            P("fsdp", "section", "tp", None),
            P("section", "fsdp"),
            P("section", "fsdp", None, "tp"),
            P("section", "fsdp", None),
            P("section", "fsdp", "tp"),
            P("section", None, "tp"),
            P("section", "tp"),
            P("section", None, None),
            P("section", None),
            P("section", "tp"),
            P("section", "tp"),
            P("section", "tp"),
            P("section", "tp"),
            P("section", "fsdp", "tp"),
        ),
        check_vma=False,
    )
```

profile of v0, /device:TPU:9, one launch (start us, length us, event | category | flops | bytes accessed | tf_op | source)
XLA Modules:
  0.0 3396.3 jit_solution(16009288080780572898)
XLA Ops:
  12.8 14.6 all_gather.37
  27.5 28.9 all_gather.39
  56.9 120.8 %all-gather.10.cloned.1.call-done = bf16[1,2048,2048]{2,1,0:T(8,128)(2,1)} async-done(((bf16[1,256,2048]{2,1,0:T(8,128)(2,1)}), bf16[1,2048,2048]{2,1,0:T(8,128)(2,1)}) %all-gather.10.cloned.1.call-update) | async-done | bytes 8388624 | tf_op jit(solution)/shard_map/all_gather | solution.py:151
  177.7 228.6 %all-gather.6.cloned.1.call-done = bf16[1,2048,2,2048]{3,1,2,0:T(8,128)(2,1)} async-done(((bf16[1,256,2,2048]{3,1,2,0:T(8,128)(2,1)}), bf16[1,2048,2,2048]{3,1,2,0:T(8,128)(2,1)}) %all-gather.6.cloned.1.call-update) | async-done | bytes 16777232 | tf_op jit(solution)/shard_map/all_gather | solution.py:148
  426.8 711.2 %while.100 = (s32[]{:T(128)}, f32[256,2048]{1,0:T(8,128)S(1)}, f32[256,2048]{1,0:T(8,128)}, f32[256,2048]{1,0:T(8,128)}, f32[32,64,128]{2,1,0:T(8,128)S(1)}, /*i...) while((s32[]{:T(128)}, f32[256,2048]{1,0:T(8,128)S(1)}, ...), condition=%wide.region_9.10_spmd.clone, body=%wide.region_0.9_spmd.clone.sunk | while | flops 20203182080 | bytes 421568192 | solution.py:274
  468.4 17.3 all-gather.12.cloned.1.call-done
  498.1 19.3 bitcast_dynamic-update-slice_fusion.24
  614.5 46.6 %reduce-scatter.20.cloned.1.call-done = f32[256,2048]{1,0:T(8,128)} async-done(((f32[512,2048]{1,0:T(8,128)}), f32[256,2048]{1,0:T(8,128)}) %reduce-scatter.20.cloned.1.call-update) | async-done | bytes 2097168 | tf_op jit(solution)/shard_map/while/body/eval_jaxpr/reduce_scatter | solution.py:202
  699.1 16.3 all-gather.12.cloned.1.call-done
  727.8 19.3 bitcast_dynamic-update-slice_fusion.24
  844.1 46.6 %reduce-scatter.20.cloned.1.call-done = f32[256,2048]{1,0:T(8,128)} async-done(((f32[512,2048]{1,0:T(8,128)}), f32[256,2048]{1,0:T(8,128)}) %reduce-scatter.20.cloned.1.call-update) | async-done | bytes 2097168 | tf_op jit(solution)/shard_map/while/body/eval_jaxpr/reduce_scatter | solution.py:202
  928.8 16.3 all-gather.12.cloned.1.call-done
  957.5 19.3 bitcast_dynamic-update-slice_fusion.24
  1074.0 46.6 %reduce-scatter.20.cloned.1.call-done = f32[256,2048]{1,0:T(8,128)} async-done(((f32[512,2048]{1,0:T(8,128)}), f32[256,2048]{1,0:T(8,128)}) %reduce-scatter.20.cloned.1.call-update) | async-done | bytes 2097168 | tf_op jit(solution)/shard_map/while/body/eval_jaxpr/reduce_scatter | solution.py:202
  1147.9 1207.4 %while.101 = (s32[]{:T(128)}, f32[256,2048]{1,0:T(8,128)S(1)}, f32[256,2048]{1,0:T(8,128)}, f32[256,2048]{1,0:T(8,128)}, f32[32,64,128]{2,1,0:T(8,128)S(1)}, /*i...) while((s32[]{:T(128)}, f32[256,2048]{1,0:T(8,128)S(1)}, ...), condition=%wide.region_57.58_spmd.clone, body=%wide.region_10.57_spmd.clone.sunk | while | flops 32835846144 | bytes 921765376 | solution.py:415
  1216.1 12.4 bitcast_add_fusion.18
  1231.5 12.0 bitcast_add_fusion.19
  1259.9 14.2 multiply_reduce_fusion.41
  1334.3 15.5 fusion.541
  1402.5 14.7 all-reduce.39
  1429.1 12.4 fusion.551
  1463.7 18.1 fusion.552
  1513.7 25.3 reduce-scatter.22.cloned.1.call-done
  1612.5 12.4 bitcast_add_fusion.18
  1627.9 12.0 bitcast_add_fusion.19
  1657.0 14.2 multiply_reduce_fusion.41
  1731.4 15.5 fusion.541
  1770.7 11.4 multiply_reduce_fusion.47
  1799.6 14.7 all-reduce.39
  1826.2 12.4 fusion.551
  1860.8 18.1 fusion.552
  1911.6 24.6 reduce-scatter.22.cloned.1.call-done
  2009.8 12.4 bitcast_add_fusion.18
  2025.1 12.0 bitcast_add_fusion.19
  2054.2 14.2 multiply_reduce_fusion.41
  2128.6 15.5 fusion.541
  2167.9 11.4 multiply_reduce_fusion.47
  2196.8 14.7 all-reduce.39
  2223.4 12.4 fusion.551
  2258.0 18.1 fusion.552
  2308.8 24.7 reduce-scatter.22.cloned.1.call-done
  2357.4 25.3 convolution_bitcast_fusion.1
  2392.3 15.3 convolution_bitcast_fusion.2
  2408.5 28.7 all-reduce.37
  2451.6 516.0 %reduce-scatter.10.cloned.1.call-done = f32[1,256,2,2048]{3,1,2,0:T(8,128)} async-done(((f32[1,2048,2,2048]{3,1,2,0:T(8,128)}), f32[1,256,2,2048]{3,1,2,0:T(8,128)}) %reduce-scatter.10.cloned.1.call-update) | async-done | bytes 4194320 | tf_op jit(solution)/shard_map/reduce_scatter | solution.py:428
  2975.0 56.2 %reduce-scatter.14.cloned.1.call-done = f32[1,256,32]{1,2,0:T(8,128)} async-done(((f32[1,2048,32]{1,2,0:T(8,128)}), f32[1,256,32]{1,2,0:T(8,128)}) %reduce-scatter.14.cloned.1.call-update) | async-done | bytes 32784 | tf_op jit(solution)/shard_map/reduce_scatter | solution.py:430
  3031.3 71.1 %reduce-scatter.12.cloned.1.call-done = f32[1,256,256]{2,1,0:T(8,128)} async-done(((f32[1,2048,256]{2,1,0:T(8,128)}), f32[1,256,256]{2,1,0:T(8,128)}) %reduce-scatter.12.cloned.1.call-update) | async-done | bytes 262160 | tf_op jit(solution)/shard_map/reduce_scatter | solution.py:429
  3102.4 286.8 %reduce-scatter.16.cloned.1.call-done = f32[1,256,2048]{2,1,0:T(8,128)} async-done(((f32[1,2048,2048]{2,1,0:T(8,128)}), f32[1,256,2048]{2,1,0:T(8,128)}) %reduce-scatter.16.cloned.1.call-update) | async-done | bytes 2097168 | tf_op jit(solution)/shard_map/reduce_scatter | solution.py:431
  (1797 shorter events, 1302.0 us)
Async XLA Ops:
  7.2 49.2 %copy-start.184 = (f32[1,32]{1,0:T(1,128)S(1)}, f32[1,32]{1,0:T(1,128)}, u32[]{:S(2)}) copy-start(f32[1,32]{1,0:T(1,128)} %param.30) | copy-start | bytes 388
  7.2 49.7 %all-gather.8.cloned.1.call-start = ((), (), s32[]{:S(2)}) async-start(), calls=%async_computation.8 | async-start | bytes 1179648 | tf_op jit(solution)/shard_map/all_gather | solution.py:149
  7.9 169.8 %all-gather.10.cloned.1.call-start = ((), (), s32[]{:S(2)}) async-start(), calls=%async_computation.9 | async-start | bytes 9437184 | tf_op jit(solution)/shard_map/all_gather | solution.py:151
  8.7 397.6 %all-gather.6.cloned.1.call-start = ((), (), s32[]{:S(2)}) async-start(), calls=%async_computation.7 | async-start | bytes 18874368 | tf_op jit(solution)/shard_map/all_gather | solution.py:148
  447.8 37.9 %copy-start.163 = (f32[1,32]{1,0:T(1,128)}, f32[1,32]{1,0:T(1,128)S(1)}, u32[]{:S(2)}) copy-start(f32[1,32]{1,0:T(1,128)S(1)} %get-tuple-element.3555) | copy-start | bytes 388 | tf_op jit(solution)/shard_map/while
  447.8 37.9 %all-gather.12.cloned.1.call-start = ((), (), s32[]{:S(2)}) async-start(), calls=%async_computation.15 | async-start | bytes 3145728 | tf_op jit(solution)/shard_map/while/body/eval_jaxpr/all_gather | solution.py:190
  452.0 209.0 %reduce-scatter.20.cloned.1.call-start = ((), (), s32[]{:S(2)}) async-start(), calls=%async_computation.16 | async-start | bytes 6291456 | tf_op jit(solution)/shard_map/while/body/eval_jaxpr/reduce_scatter | solution.py:202
  614.4 52.2 %copy-start.172 = (f32[32]{0:T(128)S(1)}, f32[32]{0:T(128)}, u32[]{:S(2)}) copy-start(f32[32]{0:T(128)} %copy-done.171) | copy-start | bytes 388 | tf_op jit(solution)/shard_map/while
  614.4 52.2 %copy-start.156 = (f32[2,512]{1,0:T(2,128)S(1)}, f32[2,512]{1,0:T(2,128)}, u32[]{:S(2)}) copy-start(f32[2,512]{1,0:T(2,128)} %get-tuple-element.3507) | copy-start | bytes 12292 | tf_op jit(solution)/shard_map/while
  614.4 52.3 %copy-start.88 = (f32[256,32]{0,1:T(8,128)S(1)}, f32[256,32]{0,1:T(8,128)}, u32[]{:S(2)}) copy-start(f32[256,32]{0,1:T(8,128)} %get-tuple-element.3304) | copy-start | bytes 98308 | tf_op jit(solution)/shard_map/while
  664.7 11.7 collective-permute-start
  678.4 37.0 %copy-start.163 = (f32[1,32]{1,0:T(1,128)}, f32[1,32]{1,0:T(1,128)S(1)}, u32[]{:S(2)}) copy-start(f32[1,32]{1,0:T(1,128)S(1)} %get-tuple-element.3555) | copy-start | bytes 388 | tf_op jit(solution)/shard_map/while
  678.4 37.0 %all-gather.12.cloned.1.call-start = ((), (), s32[]{:S(2)}) async-start(), calls=%async_computation.15 | async-start | bytes 3145728 | tf_op jit(solution)/shard_map/while/body/eval_jaxpr/all_gather | solution.py:190
  682.6 208.2 %reduce-scatter.20.cloned.1.call-start = ((), (), s32[]{:S(2)}) async-start(), calls=%async_computation.16 | async-start | bytes 6291456 | tf_op jit(solution)/shard_map/while/body/eval_jaxpr/reduce_scatter | solution.py:202
  844.1 52.3 %copy-start.172 = (f32[32]{0:T(128)S(1)}, f32[32]{0:T(128)}, u32[]{:S(2)}) copy-start(f32[32]{0:T(128)} %copy-done.171) | copy-start | bytes 388 | tf_op jit(solution)/shard_map/while
  844.1 52.3 %copy-start.156 = (f32[2,512]{1,0:T(2,128)S(1)}, f32[2,512]{1,0:T(2,128)}, u32[]{:S(2)}) copy-start(f32[2,512]{1,0:T(2,128)} %get-tuple-element.3507) | copy-start | bytes 12292 | tf_op jit(solution)/shard_map/while
  844.1 52.4 %copy-start.88 = (f32[256,32]{0,1:T(8,128)S(1)}, f32[256,32]{0,1:T(8,128)}, u32[]{:S(2)}) copy-start(f32[256,32]{0,1:T(8,128)} %get-tuple-element.3304) | copy-start | bytes 98308 | tf_op jit(solution)/shard_map/while
  894.4 11.7 collective-permute-start
  908.2 37.0 %copy-start.163 = (f32[1,32]{1,0:T(1,128)}, f32[1,32]{1,0:T(1,128)S(1)}, u32[]{:S(2)}) copy-start(f32[1,32]{1,0:T(1,128)S(1)} %get-tuple-element.3555) | copy-start | bytes 388 | tf_op jit(solution)/shard_map/while
  908.2 37.0 %all-gather.12.cloned.1.call-start = ((), (), s32[]{:S(2)}) async-start(), calls=%async_computation.15 | async-start | bytes 3145728 | tf_op jit(solution)/shard_map/while/body/eval_jaxpr/all_gather | solution.py:190
  912.4 208.2 %reduce-scatter.20.cloned.1.call-start = ((), (), s32[]{:S(2)}) async-start(), calls=%async_computation.16 | async-start | bytes 6291456 | tf_op jit(solution)/shard_map/while/body/eval_jaxpr/reduce_scatter | solution.py:202
  1074.0 52.2 %copy-start.172 = (f32[32]{0:T(128)S(1)}, f32[32]{0:T(128)}, u32[]{:S(2)}) copy-start(f32[32]{0:T(128)} %copy-done.171) | copy-start | bytes 388 | tf_op jit(solution)/shard_map/while
  1074.0 52.2 %copy-start.156 = (f32[2,512]{1,0:T(2,128)S(1)}, f32[2,512]{1,0:T(2,128)}, u32[]{:S(2)}) copy-start(f32[2,512]{1,0:T(2,128)} %get-tuple-element.3507) | copy-start | bytes 12292 | tf_op jit(solution)/shard_map/while
  1074.0 52.3 %copy-start.88 = (f32[256,32]{0,1:T(8,128)S(1)}, f32[256,32]{0,1:T(8,128)}, u32[]{:S(2)}) copy-start(f32[256,32]{0,1:T(8,128)} %get-tuple-element.3304) | copy-start | bytes 98308 | tf_op jit(solution)/shard_map/while
  1124.2 11.7 collective-permute-start
  1156.5 103.4 %all-gather.14.cloned.1.call-start = ((), (), s32[]{:S(2)}) async-start(), calls=%async_computation.17 | async-start | bytes 3145728 | tf_op jit(solution)/shard_map/while/body/eval_jaxpr/all_gather | solution.py:299
  1159.9 379.2 %reduce-scatter.22.cloned.1.call-start = ((), (), s32[]{:S(2)}) async-start(), calls=%async_computation.18 | async-start | bytes 6291456 | tf_op jit(solution)/shard_map/while/body/eval_jaxpr/reduce_scatter | solution.py:338
  1160.7 36.2 %copy-start.63 = (f32[512,32]{0,1:T(8,128)}, f32[512,32]{0,1:T(8,128)S(1)}, u32[]{:S(2)}) copy-start(f32[512,32]{0,1:T(8,128)S(1)} %get-tuple-element.3371) | copy-start | bytes 196612 | tf_op jit(solution)/shard_map/while
  1196.8 111.1 %copy-start.12 = (f32[256,2048]{0,1:T(8,128)}, f32[256,2048]{0,1:T(8,128)S(1)}, u32[]{:S(2)}) copy-start(f32[256,2048]{0,1:T(8,128)S(1)} %copy.418) | copy-start | bytes 6291460 | tf_op jit(solution)/shard_map/while
  1323.9 30.4 copy-start.10
  1546.2 4.3 collective-permute-start.1
  1552.9 104.1 %all-gather.14.cloned.1.call-start = ((), (), s32[]{:S(2)}) async-start(), calls=%async_computation.17 | async-start | bytes 3145728 | tf_op jit(solution)/shard_map/while/body/eval_jaxpr/all_gather | solution.py:299
  1556.3 380.0 %reduce-scatter.22.cloned.1.call-start = ((), (), s32[]{:S(2)}) async-start(), calls=%async_computation.18 | async-start | bytes 6291456 | tf_op jit(solution)/shard_map/while/body/eval_jaxpr/reduce_scatter | solution.py:338
  1557.1 36.2 %copy-start.63 = (f32[512,32]{0,1:T(8,128)}, f32[512,32]{0,1:T(8,128)S(1)}, u32[]{:S(2)}) copy-start(f32[512,32]{0,1:T(8,128)S(1)} %get-tuple-element.3371) | copy-start | bytes 196612 | tf_op jit(solution)/shard_map/while
  1593.2 111.8 %copy-start.12 = (f32[256,2048]{0,1:T(8,128)}, f32[256,2048]{0,1:T(8,128)S(1)}, u32[]{:S(2)}) copy-start(f32[256,2048]{0,1:T(8,128)S(1)} %copy.418) | copy-start | bytes 6291460 | tf_op jit(solution)/shard_map/while
  1721.0 30.4 copy-start.10
  1943.4 4.3 collective-permute-start.1
  1950.1 104.1 %all-gather.14.cloned.1.call-start = ((), (), s32[]{:S(2)}) async-start(), calls=%async_computation.17 | async-start | bytes 3145728 | tf_op jit(solution)/shard_map/while/body/eval_jaxpr/all_gather | solution.py:299
  1953.5 380.1 %reduce-scatter.22.cloned.1.call-start = ((), (), s32[]{:S(2)}) async-start(), calls=%async_computation.18 | async-start | bytes 6291456 | tf_op jit(solution)/shard_map/while/body/eval_jaxpr/reduce_scatter | solution.py:338
  1954.3 36.2 %copy-start.63 = (f32[512,32]{0,1:T(8,128)}, f32[512,32]{0,1:T(8,128)S(1)}, u32[]{:S(2)}) copy-start(f32[512,32]{0,1:T(8,128)S(1)} %get-tuple-element.3371) | copy-start | bytes 196612 | tf_op jit(solution)/shard_map/while
  1990.4 111.8 %copy-start.12 = (f32[256,2048]{0,1:T(8,128)}, f32[256,2048]{0,1:T(8,128)S(1)}, u32[]{:S(2)}) copy-start(f32[256,2048]{0,1:T(8,128)S(1)} %copy.418) | copy-start | bytes 6291460 | tf_op jit(solution)/shard_map/while
  2340.7 4.3 collective-permute-start.1
  2355.3 90.5 %reduce-scatter.18.cloned.1.call-start = ((), (), s32[]{:S(2)}) async-start(), calls=%async_computation.14 | async-start | bytes 1179648
  2357.4 610.2 %reduce-scatter.10.cloned.1.call-start = ((), (), s32[]{:S(2)}) async-start(), calls=%async_computation.10 | async-start | bytes 37748736 | tf_op jit(solution)/shard_map/reduce_scatter | solution.py:428
  2382.8 648.5 %reduce-scatter.14.cloned.1.call-start = ((), (), s32[]{:S(2)}) async-start(), calls=%async_computation.12 | async-start | bytes 294912 | tf_op jit(solution)/shard_map/reduce_scatter | solution.py:430
  2387.4 715.0 %reduce-scatter.12.cloned.1.call-start = ((), (), s32[]{:S(2)}) async-start(), calls=%async_computation.11 | async-start | bytes 2359296 | tf_op jit(solution)/shard_map/reduce_scatter | solution.py:429
  2392.3 996.9 %reduce-scatter.16.cloned.1.call-start = ((), (), s32[]{:S(2)}) async-start(), calls=%async_computation.13 | async-start | bytes 18874368 | tf_op jit(solution)/shard_map/reduce_scatter | solution.py:431
  2407.8 32.9 copy-start.52
  (495 other events, 3360.5 us)
Sparse Core Ops, SparseCore 0:
  10.2 43.7 all-gather.7
  56.1 121.5 all-gather.9
  180.5 225.7 all-gather.5
  452.1 33.5 all-gather.11
  605.5 55.4 reduce-scatter.19
  682.7 32.6 all-gather.11
  835.2 55.5 reduce-scatter.19
  912.5 32.6 all-gather.11
  1065.1 55.4 reduce-scatter.19
  1160.0 32.7 all-gather.13
  1482.0 56.9 reduce-scatter.21
  1556.4 33.0 all-gather.13
  1879.1 57.1 reduce-scatter.21
  1953.6 33.1 all-gather.13
  2276.3 57.1 reduce-scatter.21
  2359.2 61.2 reduce-scatter.17
  2424.5 543.0 reduce-scatter.9
  2971.7 59.5 reduce-scatter.13
  3035.8 66.5 reduce-scatter.11
  3107.1 282.0 reduce-scatter.15
where the time goes:
time: 3410 us; the launch traced here: 3400 us
  waiting for transfers between devices  1550 us (45%)
  matrix products  741 us (22%)
  other arithmetic  471 us (14%)
  local copies, waits for them, and re-layouts  429 us (13%)
  blocking collectives  146 us (4%)
  loops' own time  44.1 us (1%)
    reduce_scatter x1, waiting for transfers between devices, local(): lax.psum_scatter(all_terms[0], 'fsdp', scatter_dimension=1, tiled=True)  516 us
    reduce_scatter x1, waiting for transfers between devices, local(): lax.psum_scatter(all_terms[3], 'fsdp', scatter_dimension=1, tiled=True)  287 us
    dot_general x24, matrix products, scan_heads(): jnp.einsum('hij,jhp->ihp', weights * scores[None], scaled_inputs, precisi...  272 us
    all_gather x1, waiting for transfers between devices, local(): lax.all_gather(w_zx, 'fsdp', axis=1, tiled=True)  229 us
    reduce_scatter x3, waiting for transfers between devices, forward_tick(): lax.psum_scatter(partial_rows, 'tp', scatter_dimension=0, tiled=True)  140 us
    all_gather x1, waiting for transfers between devices, local(): lax.all_gather(w_out, 'fsdp', axis=1, tiled=True)  121 us
    dot_general x24, matrix products, scan_heads(): jnp.einsum('in,hpn->ihp', block_out, carried, precision=HIGHEST_PRECISION)  97.4 us
    dynamic_slice x36, local copies, waits for them, and re-layouts, put_row(): lax.dynamic_index_in_dim(buffer_rows, slot_index, 0, keepdims=False)  83.6 us
  transfers between devices with their start and end apart: 26, of which 15 were waited for; matrix products, arithmetic and copies ran while one was open for 17% of the time, Pallas kernels for 0%

commit v1 on v0

v1 whole, which is shorter than its diff:
```python
import jax
import jax.numpy as jnp
from jax import lax
from jax.experimental import pallas as pl
from jax.experimental.pallas import tpu as pltpu
from jax.sharding import PartitionSpec as P

CONV = 4
DI = 4096
EPS = 1e-05
CHUNK = 128
LANES = 128
HALO = 8
NEG = -10000.0
HIGHEST = lax.Precision.HIGHEST
F32 = jnp.float32
BF16 = jnp.bfloat16
VMEM_LIMIT = 56 * 1024 * 1024


def sigmoid(v):
    return 0.5 * jnp.tanh(0.5 * v) + 0.5


def dot_nn(a, b):
    return lax.dot_general(a, b, (((1,), (0,)), ((), ())), preferred_element_type=F32)


def dot_nt(a, b):
    return lax.dot_general(a, b, (((1,), (1,)), ((), ())), preferred_element_type=F32)


def dot_exact(a, b):
    return lax.dot_general(
        a, b, (((1,), (0,)), ((), ())), preferred_element_type=F32, precision=HIGHEST
    )


def split(a):
    high = a.astype(BF16)
    return high, (a - high.astype(F32)).astype(BF16)


def dot3(a, b, dot=dot_nn):
    return dot(a[0], b[0]) + (dot(a[1], b[0]) + dot(a[0], b[1]))


def tri(shape, keep):
    rows = lax.broadcasted_iota(jnp.int32, shape, 0)
    cols = lax.broadcasted_iota(jnp.int32, shape, 1)
    return keep(rows, cols)


def expand(columns, spread, heads):
    high = columns.astype(BF16).astype(F32)
    rest = columns - high
    packed = high + pltpu.roll(rest, heads, 1)
    return dot_nn(packed.astype(BF16), spread)


def step_terms(pre_dt, slab, channels, heads, spread):
    lane = lax.broadcasted_iota(jnp.int32, pre_dt.shape, 1)
    live = lane < heads
    arg = pre_dt + slab[5:6, channels : channels + LANES]
    dt = jnp.where(live, jnp.maximum(arg, 0.0) + jnp.log1p(jnp.exp(-jnp.abs(arg))), 0.0)
    decay = slab[6:7, channels : channels + LANES]
    lower = tri((CHUNK, CHUNK), lambda r, c: r >= c).astype(F32)
    cum = dot_exact(lower, dt * decay)
    last = cum[CHUNK - 1 : CHUNK, :]
    grown = jnp.where(live, jnp.exp(cum), 0.0)
    left = jnp.where(live, jnp.exp(last - cum), 0.0)
    wide = expand(jnp.concatenate([dt, grown, left], axis=0), spread, heads)
    return arg, dt, decay, cum, wide[:CHUNK], wide[CHUNK : 2 * CHUNK], wide[2 * CHUNK :]


def conv_rows(buffer, slab):
    out = slab[4:5, :] + slab[CONV - 1 : CONV, :] * buffer[HALO : HALO + CHUNK, :]
    for k in range(CONV - 1):
        first = HALO - (CONV - 1) + k
        out = out + slab[k : k + 1, :] * buffer[first : first + CHUNK, :]
    return out


def forward_kernel(
    pre, tail, start, slab, spread, u, sq, y, entering, leaving, state, buffer, *, channels, heads
):
    step = pl.program_id(0)
    size = channels + 2 * LANES

    @pl.when(step == 0)
    def _():
        state[...] = start[...]
        buffer[0:HALO, :] = tail[...]

    @pl.when(step > 0)
    def _():
        buffer[0:HALO, :] = buffer[CHUNK : CHUNK + HALO, :]

    buffer[HALO:, :] = pre[:, channels : channels + size]
    entering[0] = state[...]
    conv = conv_rows(buffer, slab)
    act = conv * sigmoid(conv)
    xs = act[:, :channels]
    in_map = act[:, channels : channels + LANES]
    out_map = act[:, channels + LANES :]
    arg, dt, decay, cum, dt_w, grown_w, left_w = step_terms(
        pre[:, channels + size :], slab, channels, heads, spread[...]
    )
    cum_t = cum.T
    xt = xs * dt_w
    xt_s = split(xt)
    out_s = split(out_map)
    scores = dot3(out_s, split(in_map), dot_nt)
    held = state[...]
    base = grown_w * dot3(out_s, split(held)) + slab[6:7, :channels] * xs
    state[...] = held * grown_w[CHUNK - 1 : CHUNK, :] + dot3(
        split(in_map.T), split(xt * left_w)
    )
    causal = tri((CHUNK, CHUNK), lambda r, c: r >= c)
    first_half = lax.broadcasted_iota(jnp.int32, (CHUNK, LANES), 1) < LANES // 2
    zero = jnp.zeros((CHUNK, LANES), BF16)
    for pair in range(channels // LANES):
        cols = slice(pair * LANES, (pair + 1) * LANES)
        mats = []
        for h in (2 * pair, 2 * pair + 1):
            gap = cum[:, h : h + 1] - cum_t[h : h + 1, :]
            mats.append(scores * jnp.exp(jnp.where(causal, gap, NEG)))
        stacked = tuple(
            jnp.concatenate(
                [jnp.where(first_half, xp[:, cols], zero), jnp.where(first_half, zero, xp[:, cols])],
                axis=0,
            )
            for xp in xt_s
        )
        y[:, cols] = base[:, cols] + dot3(split(jnp.concatenate(mats, axis=1)), stacked)
    z = pre[:, :channels]
    gated = y[...] * (z * sigmoid(z))
    sq[...] = jnp.sum(gated * gated, axis=1, keepdims=True)
    u[...] = (gated * slab[5:6, :channels]).astype(BF16)

    @pl.when(step == pl.num_programs(0) - 1)
    def _():
        leaving[...] = state[...]


def backward_kernel(
    q,
    kappa,
    pre,
    before,
    tail,
    y,
    entering,
    grad_start,
    e_start,
    slab,
    spread,
    gather,
    gpre,
    grad_leaving,
    e_leaving,
    sums,
    grad,
    buffer,
    e_buffer,
    *,
    channels,
    heads,
):
    step = pl.program_id(0)
    steps = pl.num_programs(0)
    size = channels + 2 * LANES

    @pl.when(step == 0)
    def _():
        grad[...] = grad_start[...]
        e_buffer[CHUNK:, :] = e_start[...]
        sums[...] = jnp.zeros_like(sums)

    @pl.when(step > 0)
    def _():
        e_buffer[CHUNK:, :] = e_buffer[0:HALO, :]

    @pl.when(step == steps - 1)
    def _():
        buffer[0:HALO, :] = tail[...]

    @pl.when(step < steps - 1)
    def _():
        buffer[0:HALO, :] = before[:, channels : channels + size]

    buffer[HALO:, :] = pre[:, channels : channels + size]
    conv = conv_rows(buffer, slab)
    sig = sigmoid(conv)
    act = conv * sig
    d_act = sig * (1.0 + conv * (1.0 - sig))
    xs = act[:, :channels]
    in_map = act[:, channels : channels + LANES]
    out_map = act[:, channels + LANES :]
    arg, dt, decay, cum, dt_w, grown_w, left_w = step_terms(
        pre[:, channels + size :], slab, channels, heads, spread[...]
    )
    cum_t = cum.T

    z = pre[:, :channels]
    sig_z = sigmoid(z)
    silu_z = z * sig_z
    yv = y[...]
    gated = yv * silu_z
    qv = q[...]
    sums[5:6, :channels] += jnp.sum(qv * gated, axis=0, keepdims=True)
    g_gated = qv * slab[5:6, :channels] - gated * kappa[...]
    gpre[:, :channels] = (g_gated * yv * (sig_z * (1.0 + z * (1.0 - sig_z)))).astype(BF16)
    gy = g_gated * silu_z
    gy_b = gy.astype(BF16)
    sums[6:7, :channels] += jnp.sum(gy * xs, axis=0, keepdims=True)

    xt = xs * dt_w
    xt_b = xt.astype(BF16)
    in_b = in_map.astype(BF16)
    out_b = out_map.astype(BF16)
    held = entering[0]
    held_b = held.astype(BF16)
    g_state = grad[...]
    g_state_b = g_state.astype(BF16)
    grown_last = grown_w[CHUNK - 1 : CHUNK, :]

    from_state = grown_w * dot_nn(out_b, held_b)
    ge_b = (grown_w * gy).astype(BF16)
    g_out_map = dot_nt(ge_b, held_b)
    g_xt = left_w * dot_nn(in_b, g_state_b)
    g_in_map = dot_nt((xt * left_w).astype(BF16), g_state_b)
    through = jnp.sum(g_state * held, axis=0, keepdims=True) * grown_last
    grad[...] = g_state * grown_last + dot_nn(out_map.T.astype(BF16), ge_b)
    row_terms = gy * from_state
    col_terms = xt * g_xt

    scores_t = dot3(split(in_map), split(out_map), dot_nt)
    later = tri((CHUNK, CHUNK), lambda r, c: c >= r)
    first_half = lax.broadcasted_iota(jnp.int32, (CHUNK, LANES), 1) < LANES // 2
    lane = lax.broadcasted_iota(jnp.int32, (CHUNK, LANES), 1)
    zero = jnp.zeros((CHUNK, LANES), BF16)
    g_scores_t = jnp.zeros((CHUNK, CHUNK), F32)
    gap_rows = []
    gap_cols = jnp.zeros((CHUNK, LANES), F32)
    g_xt_parts = []
    for pair in range(channels // LANES):
        cols = slice(pair * LANES, (pair + 1) * LANES)
        gp = gy_b[:, cols]
        stacked = jnp.concatenate(
            [jnp.where(first_half, gp, zero), jnp.where(first_half, zero, gp)], axis=0
        )
        g_mats = dot_nt(xt_b[:, cols], stacked)
        mats = []
        for number in range(2):
            h = 2 * pair + number
            gap = cum_t[h : h + 1, :] - cum[:, h : h + 1]
            weight = jnp.exp(jnp.where(later, gap, NEG))
            mats.append((scores_t * weight).astype(BF16))
            g_score = g_mats[:, number * CHUNK : (number + 1) * CHUNK] * weight
            g_scores_t = g_scores_t + g_score
            g_gap = g_score * scores_t
            gap_rows.append(jnp.sum(g_gap, axis=0, keepdims=True))
            gap_cols = jnp.where(lane == h, jnp.sum(g_gap, axis=1, keepdims=True), gap_cols)
        g_xt_parts.append(g_xt[:, cols] + dot_nn(jnp.concatenate(mats, axis=1), stacked))
    g_xt = jnp.concatenate(g_xt_parts, axis=1)
    g_scores_b = g_scores_t.astype(BF16)
    g_in_map = g_in_map + dot_nn(g_scores_b, out_b)
    g_out_map = g_out_map + dot_nn(g_scores_t.T.astype(BF16), in_b)
    g_xs = slab[6:7, :channels] * gy + dt_w * g_xt

    pad = jnp.zeros((CHUNK - heads, CHUNK), F32)
    gap_rows_t = jnp.concatenate(gap_rows + [pad], axis=0).T
    packed = jnp.concatenate(
        [xs * g_xt, row_terms, col_terms, jnp.broadcast_to(through, (HALO, channels))], axis=0
    )
    high, rest = split(packed)
    grouped = dot_nn(high, gather[...]) + dot_nn(rest, gather[...])
    direct = grouped[:CHUNK]
    row_sum = grouped[CHUNK : 2 * CHUNK]
    col_sum = grouped[2 * CHUNK : 3 * CHUNK]
    through_sum = grouped[3 * CHUNK : 3 * CHUNK + 1]
    upper = tri((CHUNK, CHUNK), lambda r, c: c >= r).astype(F32)
    below = tri((CHUNK, CHUNK), lambda r, c: r > c).astype(F32)
    g_log = (
        dot_exact(upper, gap_rows_t - gap_cols + row_sum) + dot_exact(below, col_sum) + through_sum
    )
    g_dt = direct + g_log * decay
    g_dtin = jnp.where(lane < heads, g_dt * sigmoid(arg), 0.0)
    sums[5:6, channels : channels + LANES] += jnp.sum(g_dtin, axis=0, keepdims=True)
    sums[6:7, channels : channels + LANES] += decay * jnp.sum(dt * g_log, axis=0, keepdims=True)

    e = jnp.concatenate([g_xs, g_in_map, g_out_map], axis=1) * d_act
    e_buffer[0:CHUNK, :] = e
    sums[4:5, :] += jnp.sum(e, axis=0, keepdims=True)
    for k in range(CONV):
        first = HALO - (CONV - 1) + k
        sums[k : k + 1, :] += jnp.sum(e * buffer[first : first + CHUNK, :], axis=0, keepdims=True)
    g_pre = slab[CONV - 1 : CONV, :] * e
    for k in range(CONV - 1):
        first = CONV - 1 - k
        g_pre = g_pre + slab[k : k + 1, :] * e_buffer[first : first + CHUNK, :]
    gpre[:, channels : channels + size] = g_pre.astype(BF16)
    gpre[:, channels + size :] = g_dtin.astype(BF16)

    @pl.when(step == steps - 1)
    def _():
        grad_leaving[...] = grad[...]
        e_leaving[...] = e_buffer[0:HALO, :]


def fixed(shape):
    return pl.BlockSpec(shape, lambda i: (0,) * len(shape))


def mixer_forward(pre, tail, start, slab, spread, heads):
    rows, width = pre.shape
    state_size, channels = start.shape
    size = channels + 2 * LANES
    steps = rows // CHUNK
    by_row = lambda cols: pl.BlockSpec((CHUNK, cols), lambda i: (i, 0))
    shape = jax.ShapeDtypeStruct

    def body(*refs):
        forward_kernel(*refs, channels=channels, heads=heads)

    return pl.pallas_call(
        body,
        grid=(steps,),
        in_specs=[
            by_row(width),
            fixed((HALO, size)),
            fixed(start.shape),
            fixed(slab.shape),
            fixed(spread.shape),
        ],
        out_specs=[
            by_row(channels),
            by_row(1),
            by_row(channels),
            pl.BlockSpec((1, state_size, channels), lambda i: (i, 0, 0)),
            fixed(start.shape),
        ],
        out_shape=[
            shape((rows, channels), BF16),
            shape((rows, 1), F32),
            shape((rows, channels), F32),
            shape((steps, state_size, channels), F32),
            shape(start.shape, F32),
        ],
        scratch_shapes=[
            pltpu.VMEM((state_size, channels), F32),
            pltpu.VMEM((CHUNK + HALO, size), F32),
        ],
        compiler_params=pltpu.CompilerParams(
            dimension_semantics=("arbitrary",), vmem_limit_bytes=VMEM_LIMIT
        ),
        cost_estimate=pl.CostEstimate(
            flops=rows * channels * 2 * 600, bytes_accessed=rows * channels * 24, transcendentals=0
        ),
        name="mixer_forward",
    )(pre, tail, start, slab, spread)


def mixer_backward(q, kappa, pre, tail, y, entering, grad, e_rows, slab, spread, gather, heads):
    rows, width = pre.shape
    state_size, channels = grad.shape
    size = channels + 2 * LANES
    steps = rows // CHUNK
    by_row = lambda cols: pl.BlockSpec((CHUNK, cols), lambda i: (steps - 1 - i, 0))
    shape = jax.ShapeDtypeStruct
    groups = CHUNK // HALO

    def body(*refs):
        backward_kernel(*refs, channels=channels, heads=heads)

    return pl.pallas_call(
        body,
        grid=(steps,),
        in_specs=[
            by_row(channels),
            by_row(1),
            by_row(width),
            pl.BlockSpec(
                (HALO, width), lambda i: (jnp.maximum((steps - 1 - i) * groups - 1, 0), 0)
            ),
            fixed((HALO, size)),
            by_row(channels),
            pl.BlockSpec((1, state_size, channels), lambda i: (steps - 1 - i, 0, 0)),
            fixed(grad.shape),
            fixed(e_rows.shape),
            fixed(slab.shape),
            fixed(spread.shape),
            fixed(gather.shape),
        ],
        out_specs=[by_row(width), fixed(grad.shape), fixed(e_rows.shape), fixed(slab.shape)],
        out_shape=[
            shape((rows, width), BF16),
            shape(grad.shape, F32),
            shape(e_rows.shape, F32),
            shape(slab.shape, F32),
        ],
        scratch_shapes=[
            pltpu.VMEM((state_size, channels), F32),
            pltpu.VMEM((CHUNK + HALO, size), F32),
            pltpu.VMEM((CHUNK + HALO, size), F32),
        ],
        compiler_params=pltpu.CompilerParams(
            dimension_semantics=("arbitrary",), vmem_limit_bytes=VMEM_LIMIT
        ),
        cost_estimate=pl.CostEstimate(
            flops=rows * channels * 2 * 1800, bytes_accessed=rows * channels * 32, transcendentals=0
        ),
        name="mixer_backward",
    )(q, kappa, pre, pre, tail, y, entering, grad, e_rows, slab, spread, gather)


SWAP = [(0, 1), (1, 0)]


def swap_core(value):
    return lax.ppermute(value, "section", SWAP)


def swap_tp(value):
    return lax.ppermute(value, "tp", SWAP)


def by_index(index, own, other):
    first = index == 0
    return jnp.stack([jnp.where(first, own, other), jnp.where(first, other, own)])


def pick(pair, index):
    return lax.dynamic_index_in_dim(pair, index, 0, keepdims=False)


def gather_tokens(own, core, half):
    both = by_index(half, own, swap_tp(own))
    whole = by_index(core, both, swap_core(both))
    whole = jnp.moveaxis(whole, 0, 1)
    return whole.reshape((4 * own.shape[0],) + own.shape[1:])


def scatter_tokens(part, core, half):
    rows = part.shape[0] // 4
    split = part.reshape((2, 2, rows) + part.shape[1:])
    mine = lax.dynamic_index_in_dim(split, core, 1, keepdims=False)
    theirs = lax.dynamic_index_in_dim(split, 1 - core, 1, keepdims=False)
    total = mine + swap_core(theirs)
    sent = pick(total, 1 - half)
    if part.ndim > 1:
        sent = sent.astype(BF16)
    return pick(total, half) + swap_tp(sent).astype(F32)


def local(
    inputs,
    cotangent,
    norm_gain,
    w_zx,
    w_bc,
    w_dt,
    conv_x,
    conv_xb,
    conv_bc,
    conv_bcb,
    dt_bias,
    a_log,
    d_skip,
    gate_gain,
    w_out,
):
    cores = lax.axis_size("section")
    core = lax.axis_index("section")
    half = lax.axis_index("tp")
    micros = inputs.shape[1]
    rows = inputs.shape[2] // cores
    channels = w_zx.shape[3] // cores
    heads = w_dt.shape[2] // cores
    width = channels // heads
    shared = w_bc.shape[2]
    depth = w_zx.shape[1]
    in_width = 2 * channels + shared + LANES
    gain_pair = by_index(core, norm_gain[0], swap_core(norm_gain[0]))
    gains = lax.all_gather(gain_pair, "fsdp", axis=1, tiled=True).astype(F32)

    def cut(tensor, index, size):
        return lax.dynamic_slice_in_dim(tensor, index * size, size, tensor.ndim - 1)

    def weight_shard(index):
        zx = cut(w_zx[0], index, channels).reshape(depth, 2 * channels)
        steps = jnp.pad(cut(w_dt[0], index, heads), ((0, 0), (0, LANES - heads)))
        return jnp.concatenate([zx, w_bc[0], steps, cut(w_out[0], index, channels)], axis=1)

    def slab_of(index):
        pad = jnp.zeros((LANES - heads,), F32)
        steps = jnp.concatenate([cut(dt_bias[0], index, heads), pad])
        decay = jnp.concatenate([-jnp.exp(cut(a_log[0], index, heads)), pad])
        skip = jnp.repeat(cut(d_skip[0], index, heads), width)
        rest = jnp.zeros((shared - LANES,), F32)
        taps = jnp.concatenate([cut(conv_x[0], index, channels), conv_bc[0]], axis=1)
        bias = jnp.concatenate([cut(conv_xb[0], index, channels), conv_bcb[0]])
        return jnp.concatenate(
            [
                taps,
                bias[None],
                jnp.concatenate([cut(gate_gain[0], index, channels), steps, rest])[None],
                jnp.concatenate([skip, decay, rest])[None],
                jnp.zeros((1, channels + shared), F32),
            ]
        )

    own_shard = weight_shard(core)
    got_shard = swap_core(weight_shard(1 - core))
    own_slab = slab_of(core)
    got_slab = swap_core(slab_of(1 - core))
    projections, slabs = [], []
    for layer in range(2):
        shard = jnp.where(core == layer, own_shard, got_shard)
        projections.append(
            (
                lax.all_gather(shard[:, :in_width], "fsdp", axis=0, tiled=True),
                lax.all_gather(shard[:, in_width:], "fsdp", axis=0, tiled=True),
            )
        )
        slabs.append(jnp.where(core == layer, own_slab, got_slab))

    lane = jnp.arange(LANES)
    head_of = jnp.arange(channels) // width
    spread = ((lane[:, None] % heads == head_of[None, :]) & (lane[:, None] < 2 * heads)).astype(BF16)
    gather = (head_of[:, None] == lane[None, :]).astype(BF16)

    def own_rows(tensor):
        return [
            lax.dynamic_slice_in_dim(tensor[0, m], core * rows, rows, 0).astype(F32)
            for m in range(micros)
        ]

    hidden = own_rows(inputs)
    size = channels + shared
    saved = []
    for layer in range(2):
        w_in, w_back = projections[layer]
        slab = slabs[layer]
        state = jnp.zeros((shared // 2, channels), F32)
        tail = jnp.zeros((HALO, size), F32)
        kept = []
        next_hidden = []
        for m in range(micros):
            h = hidden[m]
            scale = lax.rsqrt(jnp.mean(h * h, axis=1, keepdims=True) + EPS)
            normed = gather_tokens((h * scale * gains[layer][None]).astype(BF16), core, half)
            pre = dot_nn(normed, w_in)
            u, squares, y, entering, state = mixer_forward(pre, tail, state, slab, spread, heads)
            part = dot_nt(u, w_back)
            total = scatter_tokens(part, core, half)
            squares = scatter_tokens(squares[:, 0], core, half)
            r = lax.rsqrt(squares / DI + EPS)[:, None]
            branch = r * total
            next_hidden.append(h + branch)
            kept.append((h, scale, normed, pre, tail, y, u, entering, r, branch))
            tail = pre[-HALO:, channels : channels + size]
        saved.append(kept)
        hidden = next_hidden

    grads = own_rows(cotangent)
    reduced = [None, None]
    small = [None, None]
    for layer in (1, 0):
        w_in, w_back = projections[layer]
        slab = slabs[layer]
        state = jnp.zeros((shared // 2, channels), F32)
        e_rows = jnp.zeros((HALO, size), F32)
        next_grads = [None] * micros
        gpres = [None] * micros
        backs = [None] * micros
        totals = jnp.zeros(slab.shape, F32)
        gain_total = jnp.zeros((w_out.shape[1] * lax.axis_size("fsdp"),), F32)
        for m in reversed(range(micros)):
            h, scale, normed, pre, tail, y, u, entering, r, branch = saved[layer][m]
            g = grads[m]
            kappa = r * r * jnp.sum(g * branch, axis=1, keepdims=True) / DI
            back = gather_tokens((g * r).astype(BF16), core, half)
            kappa = gather_tokens(kappa[:, 0], core, half)[:, None]
            q = dot_nn(back, w_back)
            gpre, state, e_rows, sums = mixer_backward(
                q, kappa, pre, tail, y, entering, state, e_rows, slab, spread, gather, heads
            )
            g_norm = scatter_tokens(dot_nt(gpre, w_in), core, half)
            gain_total = gain_total + jnp.sum(g_norm * (h * scale), axis=0)
            g_norm = g_norm * gains[layer][None]
            mean = jnp.mean(g_norm * h, axis=1, keepdims=True)
            next_grads[m] = g + scale * g_norm - h * (scale * scale * scale) * mean
            gpres[m] = gpre
            backs[m] = back
            totals = totals + sums
        grads = next_grads
        normed_all = jnp.concatenate([saved[layer][m][2] for m in range(micros)])
        u_all = jnp.concatenate([saved[layer][m][6] for m in range(micros)])
        over_tokens = (((0,), (0,)), ((), ()))
        grad_back = lax.dot_general(
            jnp.concatenate(backs), u_all, over_tokens, preferred_element_type=F32
        ).astype(BF16)
        grad_in = lax.dot_general(
            normed_all, jnp.concatenate(gpres), over_tokens, preferred_element_type=F32
        ).astype(BF16)
        reduced[layer] = (
            lax.psum_scatter(grad_in, "fsdp", scatter_dimension=0, tiled=True),
            lax.psum_scatter(grad_back, "fsdp", scatter_dimension=0, tiled=True),
        )
        small[layer] = jnp.concatenate([totals.reshape(-1), gain_total])

    small_sums = jnp.stack(small)
    devices = lax.axis_size("fsdp")
    if devices & (devices - 1) == 0:
        bit = 1
        while bit < devices:
            small_sums = small_sums + lax.ppermute(
                small_sums, "fsdp", [(i, i ^ bit) for i in range(devices)]
            )
            bit *= 2
    else:
        small_sums = lax.psum(small_sums, "fsdp")
    own = pick(small_sums, core)
    got = swap_core(pick(small_sums, 1 - core))
    count = slabs[0].size
    halves = by_index(core, own[:count], got[:count]).reshape((2,) + slabs[0].shape)
    both = own + got
    common = jnp.concatenate(
        [both[:count].reshape(slabs[0].shape)[:5, channels:].reshape(-1), both[count:]]
    )
    common = common + swap_tp(common)
    conv_sum = common[: 5 * shared].reshape(5, shared)
    gain_sum = lax.dynamic_slice_in_dim(
        common[5 * shared :], lax.axis_index("fsdp") * depth, depth, 0
    )
    wide = jnp.concatenate([halves[0, :7, :channels], halves[1, :7, :channels]], axis=1)
    narrow = jnp.concatenate(
        [halves[j, 5:7, channels : channels + heads] for j in range(2)], axis=1
    )
    skip_sum = wide[6].reshape(2 * heads, width).sum(axis=1)

    mine = [jnp.where(core == 0, reduced[0][i], reduced[1][i]) for i in range(2)]
    theirs = [jnp.where(core == 0, reduced[1][i], reduced[0][i]) for i in range(2)]
    got = [swap_core(v) for v in theirs]
    in_pair = by_index(core, mine[0], got[0]).astype(F32)
    back_pair = by_index(core, mine[1], got[1]).astype(F32)
    g_zx = jnp.concatenate(
        [in_pair[j, :, : 2 * channels].reshape(depth, 2, channels) for j in range(2)], axis=2
    )
    g_bc = in_pair[:, :, 2 * channels : 2 * channels + shared].sum(axis=0)
    g_dt = jnp.concatenate(
        [in_pair[j, :, 2 * channels + shared : 2 * channels + shared + heads] for j in range(2)],
        axis=1,
    )
    g_back = jnp.concatenate([back_pair[0], back_pair[1]], axis=1)
    g_bc = g_bc + swap_tp(g_bc)

    def placed_rows(parts):
        own = jnp.where(core == 0, parts[0], parts[1])
        other = jnp.where(core == 0, parts[1], parts[0])
        return by_index(core, own, swap_core(other)).reshape(1, 1, 2 * rows, -1)

    return (
        placed_rows(hidden),
        placed_rows(grads),
        gain_sum[None],
        g_zx[None],
        g_bc[None],
        g_dt[None],
        wide[:4][None],
        wide[4][None],
        conv_sum[:4][None],
        conv_sum[4][None],
        narrow[0][None],
        narrow[1][None],
        skip_sum[None],
        wide[5][None],
        g_back[None],
    )


def solution(mesh):
    placed = (
        P("fsdp", None, "tp", None),
        P("fsdp", None, "tp", None),
        P("section", "fsdp"),
        P("section", "fsdp", None, "tp"),
        P("section", "fsdp", None),
        P("section", "fsdp", "tp"),
        P("section", None, "tp"),
        P("section", "tp"),
        P("section", None, None),
        P("section", None),
        P("section", "tp"),
        P("section", "tp"),
        P("section", "tp"),
        P("section", "tp"),
        P("section", "fsdp", "tp"),
    )
    return jax.shard_map(
        local,
        mesh=mesh,
        in_specs=placed,
        out_specs=(
            P("fsdp", "section", "tp", None),
            P("fsdp", "section", "tp", None),
        )
        + placed[2:],
        check_vma=False,
    )
```

time: 3410 us -> 1220 us (0.36)
  waiting for transfers between devices: 1550 us -> 669 us
  matrix products: 741 us -> 154 us
  other arithmetic: 471 us -> 75.6 us
  local copies, waits for them, and re-layouts: 429 us -> 74.6 us
  blocking collectives: 146 us -> 15.4 us
  Pallas kernels: 0 us -> 129 us
  starting transfers between devices: 4.86 us -> 77.4 us
  loops' own time: 44.1 us -> 0 us
    reduce_scatter x10 -> x4, waiting for transfers between devices: 1140 us -> 269 us  [the longest x2 269 us: local(): lax.psum_scatter(grad_in, 'fsdp', scatter_dimension=0, tiled=True)]
    dot_general x121 -> x20, matrix products: 741 us -> 154 us  [the longest x8 57.3 us: dot_nn(): lax.dot_general(a, b, (((1,), (0,)), ((), ())), preferred_element_type=F32)]
    ppermute x6 -> x61, waiting for transfers between devices: 0.02 us -> 166 us  [the longest x26 138 us: swap_tp(): return lax.ppermute(value, 'tp', SWAP)]
    all_gather x9 -> x4, waiting for transfers between devices: 399 us -> 234 us  [the longest x2 155 us: local(): lax.all_gather(shard[:, :in_width], 'fsdp', axis=0, tiled=True)]
    reduce_sum x42 -> x9, other arithmetic: 140 us -> 6.42 us  [the longest x2 3.31 us: local(): gain_total = gain_total + jnp.sum(g_norm * (h * scale), axis=0)]
    pallas_call x0 -> x8, Pallas kernels: none -> 129 us  [the longest x4 82.8 us: mixer_backward(): pl.pallas_call(body, grid=(steps,), in_specs=[by_row(channels), by_row(1)...]
    psum x11 -> x0, blocking collectives: 102 us -> none  [the longest x3 44 us: backward_tick(): grad_bc = lax.psum(grad_bc_part, 'tp')]
    mul x30 -> x4, other arithmetic: 93.1 us -> 1.29 us  [local(): next_grads[m] = g + scale * g_norm - h * (scale * scale * scale) * mean]
  transfers between devices with their start and end apart: 26 -> 69, of which waited for: 15 -> 32; matrix products, arithmetic and copies ran while one was open for 17% -> 21% of each run, Pallas kernels for 0% -> 11%
where the time goes in v1:
time: 1220 us; the launch traced here: 1210 us
  waiting for transfers between devices  669 us (55%)
  matrix products  154 us (13%)
  Pallas kernels  129 us (11%)
  starting transfers between devices  77.4 us (6%)
  other arithmetic  75.6 us (6%)
  local copies, waits for them, and re-layouts  74.6 us (6%)
  between operations  16.6 us (1%)
  blocking collectives  15.4 us (1%)
    reduce_scatter x2, waiting for transfers between devices, local(): lax.psum_scatter(grad_in, 'fsdp', scatter_dimension=0, tiled=True)  269 us
    all_gather x2, waiting for transfers between devices, local(): lax.all_gather(shard[:, :in_width], 'fsdp', axis=0, tiled=True)  155 us
    ppermute x26, waiting for transfers between devices, swap_tp(): return lax.ppermute(value, 'tp', SWAP)  138 us
    pallas_call x4, Pallas kernels, mixer_backward(): pl.pallas_call(body, grid=(steps,), in_specs=[by_row(channels), by_row(1)...  82.8 us
    all_gather x2, waiting for transfers between devices, local(): lax.all_gather(shard[:, in_width:], 'fsdp', axis=0, tiled=True)  78.6 us
    dot_general x8, matrix products, dot_nn(): lax.dot_general(a, b, (((1,), (0,)), ((), ())), preferred_element_type=F32)  57.3 us
    dot_general x8, matrix products, dot_nt(): lax.dot_general(a, b, (((1,), (1,)), ((), ())), preferred_element_type=F32)  51.7 us
    ppermute x32, starting transfers between devices, swap_core(): return lax.ppermute(value, 'section', SWAP)  48.5 us
  transfers between devices with their start and end apart: 69, of which 32 were waited for; matrix products, arithmetic and copies ran while one was open for 21% of the time, Pallas kernels for 11%

profile of v1, /device:TPU:9, one launch (start us, length us, event | category | flops | bytes accessed | tf_op | source)
XLA Modules:
  0.0 1212.7 jit_solution(6226013870658238744)
XLA Ops:
  28.7 15.4 %all_gather.15 = bf16[2,2048]{1,0:T(2,128)(2,1)S(1)} all-gather(bf16[2,256]{1,0:T(2,128)(2,1)S(1)} %pad_maximum_fusion.22), channel_id=1, replica_groups=mesh['section'=2,'fsdp'=8,'tp'=2] {'fsdp'}, dimensions={1}, use_global_device_ids=true | all-gather | bytes 9216 | tf_op jit(solution)/shard_map/all_gather | solution.py:486
  46.9 7.8 collective-permute-done.15
  54.9 8.0 collective-permute-start.16
  74.5 90.0 %all-gather.5.cloned.1.call-done = bf16[2048,2432]{1,0:T(8,128)(2,1)} async-done(((bf16[256,2432]{1,0:T(8,128)(2,1)}), bf16[2048,2432]{1,0:T(8,128)(2,1)}) %all-gather.5.cloned.1.call-update) | async-done | bytes 9961488 | tf_op jit(solution)/shard_map/all_gather | solution.py:523
  164.5 9.2 fusion.139.refs_0_.refs_2_.refs_3_
  176.3 11.5 mixer_forward.4
  187.9 11.4 fusion.143.refs_0_.refs_2_.refs_3_
  199.3 11.7 mixer_forward.6
  211.0 27.9 %all-gather.7.cloned.1.call-done = bf16[2048,1024]{1,0:T(8,128)(2,1)} async-done(((bf16[256,1024]{1,0:T(8,128)(2,1)}), bf16[2048,1024]{1,0:T(8,128)(2,1)}) %all-gather.7.cloned.1.call-update) | async-done | bytes 4194320 | tf_op jit(solution)/shard_map/all_gather | solution.py:524
  268.5 8.4 collective-permute-done.20
  277.3 11.0 collective-permute-done.8
  290.5 10.0 collective-permute-done.9
  300.8 5.4 collective-permute-start.10
  306.2 5.7 collective-permute-done.21
  317.7 65.4 %all-gather.9.cloned.1.call-done = bf16[2048,2432]{1,0:T(8,128)(2,1)} async-done(((bf16[256,2432]{1,0:T(8,128)(2,1)}), bf16[2048,2432]{1,0:T(8,128)(2,1)}) %all-gather.9.cloned.1.call-update) | async-done | bytes 9961488 | tf_op jit(solution)/shard_map/all_gather | solution.py:523
  383.1 9.6 fusion.141.refs_0_.refs_2_.refs_3_
  395.1 11.5 mixer_forward.5
  406.6 50.7 %all-gather.11.cloned.1.call-done = bf16[2048,1024]{1,0:T(8,128)(2,1)} async-done(((bf16[256,1024]{1,0:T(8,128)(2,1)}), bf16[2048,1024]{1,0:T(8,128)(2,1)}) %all-gather.11.cloned.1.call-update) | async-done | bytes 4194320 | tf_op jit(solution)/shard_map/all_gather | solution.py:524
  468.6 7.3 fusion.145.refs_0_.refs_2_.refs_3_
  475.9 11.8 mixer_forward.7
  508.0 19.6 %collective-permute-done.24 = f32[128]{0:T(128)S(1)} collective-permute-done((f32[128]{0:T(128)S(1)}, f32[128]{0:T(128)S(1)}, u32[]{:S(2)}, u32[]{:S(2)}) %collective-permute-start.24) | collective-permute-done | bytes 544 | tf_op jit(solution)/shard_map/ppermute | solution.py:426
  533.4 9.1 collective-permute-done.34
  547.2 6.6 collective-permute-done.30
  571.6 20.6 %mixer_backward.4 = (bf16[512,2432]{1,0:T(8,128)(2,1)}, f32[128,1024]{1,0:T(8,128)}, f32[8,1280]{1,0:T(8,128)}, f32[8,1280]{1,0:T(8,128)}) custom-call(f32[512,1024]{1,0:T(8,128)} %fusion.148.refs_0_, f32[512,1]{1,0:T(8,128)} %copy.65.refs_1_, f32[512,2432]{1,0:T(8,128)} %fusion.145.refs_0_.refs_2_.refs_3_, f32[512,2432]{1,0:T(8,128)} %fusion.145.refs_0_.refs_2_.refs_3_, ...), custom_call_target="tpu_custom_call" | custom-call | flops 1887436800 | bytes 16777216 | tf_op jit(solution)/shard_map/mixer_backward/pallas_call | solution.py:377
  592.2 9.1 fusion.151
  610.2 20.6 %mixer_backward.5 = (bf16[512,2432]{1,0:T(8,128)(2,1)}, f32[128,1024]{1,0:T(8,128)}, f32[8,1280]{1,0:T(8,128)}, f32[8,1280]{1,0:T(8,128)}) custom-call(f32[512,1024]{1,0:T(8,128)} %fusion.147.refs_0_, f32[512,1]{1,0:T(8,128)} %copy.66.refs_1_, f32[512,2432]{1,0:T(8,128)} %copy-done.1, f32[512,2432]{1,0:T(8,128)} %copy-done.1, ...), custom_call_target="tpu_custom_call" | custom-call | flops 1887436800 | bytes 16777216 | tf_op jit(solution)/shard_map/mixer_backward/pallas_call | solution.py:377
  630.8 9.0 fusion.149
  644.2 6.2 fusion.20
  657.9 8.9 collective-permute-done.43
  667.2 10.9 collective-permute-done.37
  682.3 9.1 collective-permute-done.44
  695.6 7.0 collective-permute-done.38
  710.0 6.2 fusion.23
  716.5 17.1 %convolution_convert_fusion = bf16[2048,2432]{1,0:T(8,128)(2,1)} fusion(bf16[512,2432]{1,0:T(8,128)(2,1)} %get-tuple-element.64, bf16[512,2432]{1,0:T(8,128)(2,1)} %get-tuple-element.61, bf16[512,2048]{1,0:T(8,128)(2,1)} %bitcast.495, bf16[512,2048]{1,0:T(8,128)(2,1)} %bitcast.493), kind=kOutput, calls=%fused_computation | convolution fusion | flops 10223878144 | bytes 19136512 | tf_op jit(solution)/shard_map/dot_general | solution.py:605
  741.2 6.5 fusion.152.refs_0_
  747.7 21.0 %mixer_backward.6 = (bf16[512,2432]{1,0:T(8,128)(2,1)}, f32[128,1024]{1,0:T(8,128)}, f32[8,1280]{1,0:T(8,128)}, f32[8,1280]{1,0:T(8,128)}) custom-call(f32[512,1024]{1,0:T(8,128)} %fusion.152.refs_0_, f32[512,1]{1,0:T(8,128)} %copy.71.refs_1_, f32[512,2432]{1,0:T(8,128)} %fusion.143.refs_0_.refs_2_.refs_3_, f32[512,2432]{1,0:T(8,128)} %fusion.143.refs_0_.refs_2_.refs_3_, ...), custom_call_target="tpu_custom_call" | custom-call | flops 1887436800 | bytes 16777216 | tf_op jit(solution)/shard_map/mixer_backward/pallas_call | solution.py:377
  768.8 5.9 fusion.150.refs_0_
  774.7 20.6 %mixer_backward.7 = (bf16[512,2432]{1,0:T(8,128)(2,1)}, f32[128,1024]{1,0:T(8,128)}, f32[8,1280]{1,0:T(8,128)}, f32[8,1280]{1,0:T(8,128)}) custom-call(f32[512,1024]{1,0:T(8,128)} %fusion.150.refs_0_, f32[512,1]{1,0:T(8,128)} %copy.72.refs_1_, f32[512,2432]{1,0:T(8,128)} %copy-done, f32[512,2432]{1,0:T(8,128)} %copy-done, ...), custom_call_target="tpu_custom_call" | custom-call | flops 1887436800 | bytes 16777216 | tf_op jit(solution)/shard_map/mixer_backward/pallas_call | solution.py:377
  795.2 16.0 %convolution_convert_fusion.1 = bf16[2048,2432]{1,0:T(8,128)(2,1)} fusion(bf16[512,2432]{1,0:T(8,128)(2,1)} %get-tuple-element.70, bf16[512,2432]{1,0:T(8,128)(2,1)} %get-tuple-element.69, bf16[512,2048]{1,0:T(8,128)(2,1)S(1)} %bitcast.489, bf16[512,2048]{1,0:T(8,128)(2,1)S(1)} %bitcast.491), kind=kOutput, calls=%fused_computation.1 | convolution fusion | flops 10223878144 | bytes 19136512 | tf_op jit(solution)/shard_map/dot_general | solution.py:605
  811.2 9.1 fusion.154
  823.9 8.6 fusion.153
  846.1 6.7 collective-permute-done.51
  852.8 11.2 collective-permute-done.49
  871.9 9.6 collective-permute-done.54
  886.3 10.4 collective-permute-done.55
  910.1 95.8 %reduce-scatter.7.cloned.1.call-done = bf16[256,2432]{1,0:T(8,128)(2,1)} async-done(((bf16[2048,2432]{1,0:T(8,128)(2,1)}), bf16[256,2432]{1,0:T(8,128)(2,1)}) %reduce-scatter.7.cloned.1.call-update) | async-done | bytes 1245200 | tf_op jit(solution)/shard_map/reduce_scatter | solution.py:609
  1005.9 173.6 %reduce-scatter.5.cloned.1.call-done = bf16[256,2432]{1,0:T(8,128)(2,1)} async-done(((bf16[2048,2432]{1,0:T(8,128)(2,1)}), bf16[256,2432]{1,0:T(8,128)(2,1)}) %reduce-scatter.5.cloned.1.call-update) | async-done | bytes 1245200 | tf_op jit(solution)/shard_map/reduce_scatter | solution.py:609
  1198.6 5.9 maximum_bitcast_fusion
  (563 shorter events, 245.5 us)
Async XLA Ops:
  7.2 157.3 %all-gather.5.cloned.1.call-start = ((), (), s32[]{:S(2)}) async-start(), calls=%async_computation.4 | async-start | bytes 11206656 | tf_op jit(solution)/shard_map/all_gather | solution.py:523
  21.3 217.6 %all-gather.7.cloned.1.call-start = ((), (), s32[]{:S(2)}) async-start(), calls=%async_computation.5 | async-start | bytes 4718592 | tf_op jit(solution)/shard_map/all_gather | solution.py:524
  22.3 360.8 %all-gather.9.cloned.1.call-start = ((), (), s32[]{:S(2)}) async-start(), calls=%async_computation.6 | async-start | bytes 11206656 | tf_op jit(solution)/shard_map/all_gather | solution.py:523
  23.5 433.8 %all-gather.11.cloned.1.call-start = ((), (), s32[]{:S(2)}) async-start(), calls=%async_computation.7 | async-start | bytes 4718592 | tf_op jit(solution)/shard_map/all_gather | solution.py:524
  24.7 45.7 %collective-permute-start.4 = (f32[8,1280]{1,0:T(8,128)S(1)}, f32[8,1280]{1,0:T(8,128)S(1)}, u32[]{:S(2)}, u32[]{:S(2)}) collective-permute-start(f32[8,1280]{1,0:T(8,128)S(1)} %concatenate.96), channel_id=1, source_target_pairs={{0,16},{16,0},{1,17},{17,1},{2,18},{18,2},{3,19},{19,3},{4,20},{20... | collective-permute-start | bytes 122888 | tf_op jit(solution)/shard_map/ppermute | solution.py:422
  44.5 10.2 collective-permute-start.15
  46.5 19.5 %collective-permute-start.1 = (bf16[128,2048]{1,0:T(8,128)(2,1)S(1)}, bf16[128,2048]{1,0:T(8,128)(2,1)S(1)}, u32[]{:S(2)}, u32[]{:S(2)}) collective-permute-start(bf16[128,2048]{1,0:T(8,128)(2,1)S(1)} %get-tuple-element.206), channel_id=1, source_target_pairs={{0,1},{1,0},{2,3},{3,2},{4,5},{5,4},{6,7},{7,6},{8,9},{9,8},{10,11... | collective-permute-start | bytes 1572872 | tf_op jit(solution)/shard_map/ppermute | solution.py:426
  54.9 16.1 %collective-permute-start.16 = (bf16[2,128,2048]{2,1,0:T(8,128)(2,1)S(1)}, bf16[2,128,2048]{2,1,0:T(8,128)(2,1)S(1)}, u32[]{:S(2)}, u32[]{:S(2)}) collective-permute-start(bf16[2,128,2048]{2,1,0:T(8,128)(2,1)S(1)} %pad_maximum_fusion.7), channel_id=1, source_target_pairs={{0,16},{16,0},{1,17},{17,1},{2,18},{18,2},{3,19},{19,3},{4,20},{20... | collective-permute-start | bytes 3145736 | tf_op jit(solution)/shard_map/ppermute | solution.py:422
  247.0 14.7 %collective-permute-start.19 = (f32[2,128,2048]{2,1,0:T(8,128)}, f32[2,128,2048]{2,1,0:T(8,128)}, u32[]{:S(2)}, u32[]{:S(2)}) collective-permute-start(f32[2,128,2048]{2,1,0:T(8,128)} %dynamic-slice_bitcast_fusion.5), channel_id=1, source_target_pairs={{0,16},{16,0},{1,17},{17,1},{2,18},{18,2},{3,19},{19,3},{4,20},{20... | collective-permute-start | bytes 6291464 | tf_op jit(solution)/shard_map/ppermute | solution.py:422
  253.7 12.1 collective-permute-start.7
  257.0 650.7 %reduce-scatter.11.cloned.1.call-start = ((), (), s32[]{:S(2)}) async-start(), calls=%async_computation.11 | async-start | bytes 4718592 | tf_op jit(solution)/shard_map/reduce_scatter | solution.py:610
  260.1 8.3 collective-permute-start.18
  264.5 12.4 %collective-permute-start.20 = (bf16[128,2048]{1,0:T(8,128)(2,1)S(1)}, bf16[128,2048]{1,0:T(8,128)(2,1)S(1)}, u32[]{:S(2)}, u32[]{:S(2)}) collective-permute-start(bf16[128,2048]{1,0:T(8,128)(2,1)S(1)} %fusion.69), channel_id=1, source_target_pairs={{0,1},{1,0},{2,3},{3,2},{4,5},{5,4},{6,7},{7,6},{8,9},{9,8},{10,11... | collective-permute-start | bytes 1572872 | tf_op jit(solution)/shard_map/ppermute | solution.py:426
  267.7 20.5 %collective-permute-start.8 = (bf16[128,2048]{1,0:T(8,128)(2,1)S(1)}, bf16[128,2048]{1,0:T(8,128)(2,1)S(1)}, u32[]{:S(2)}, u32[]{:S(2)}) collective-permute-start(bf16[128,2048]{1,0:T(8,128)(2,1)S(1)} %fusion.67), channel_id=1, source_target_pairs={{0,1},{1,0},{2,3},{3,2},{4,5},{5,4},{6,7},{7,6},{8,9},{9,8},{10,11... | collective-permute-start | bytes 1572872 | tf_op jit(solution)/shard_map/ppermute | solution.py:426
  289.0 11.5 collective-permute-start.9
  290.2 21.7 %collective-permute-start.21 = (bf16[128,2048]{1,0:T(8,128)(2,1)S(1)}, bf16[128,2048]{1,0:T(8,128)(2,1)S(1)}, u32[]{:S(2)}, u32[]{:S(2)}) collective-permute-start(bf16[128,2048]{1,0:T(8,128)(2,1)S(1)} %get-tuple-element.203), channel_id=1, source_target_pairs={{0,1},{1,0},{2,3},{3,2},{4,5},{5,4},{6,7},{7,6},{8,9},{9,8},{10,11... | collective-permute-start | bytes 1572872 | tf_op jit(solution)/shard_map/ppermute | solution.py:426
  300.8 15.1 %collective-permute-start.10 = (bf16[2,128,2048]{2,1,0:T(8,128)(2,1)S(1)}, bf16[2,128,2048]{2,1,0:T(8,128)(2,1)S(1)}, u32[]{:S(2)}, u32[]{:S(2)}) collective-permute-start(bf16[2,128,2048]{2,1,0:T(8,128)(2,1)S(1)} %pad_maximum_fusion.6), channel_id=1, source_target_pairs={{0,16},{16,0},{1,17},{17,1},{2,18},{18,2},{3,19},{19,3},{4,20},{20... | collective-permute-start | bytes 3145736 | tf_op jit(solution)/shard_map/ppermute | solution.py:422
  313.1 153.6 %collective-permute-start.22 = (bf16[2,128,2048]{2,1,0:T(8,128)(2,1)}, bf16[2,128,2048]{2,1,0:T(8,128)(2,1)}, u32[]{:S(2)}, u32[]{:S(2)}) collective-permute-start(bf16[2,128,2048]{2,1,0:T(8,128)(2,1)} %pad_maximum_fusion.8), channel_id=1, source_target_pairs={{0,16},{16,0},{1,17},{17,1},{2,18},{18,2},{3,19},{19,3},{4,20},{20... | collective-permute-start | bytes 3145736 | tf_op jit(solution)/shard_map/ppermute | solution.py:422
  465.0 35.6 %collective-permute-start.13 = (f32[2,128,2048]{2,1,0:T(8,128)}, f32[2,128,2048]{2,1,0:T(8,128)}, u32[]{:S(2)}, u32[]{:S(2)}) collective-permute-start(f32[2,128,2048]{2,1,0:T(8,128)} %dynamic-slice_bitcast_fusion.6), channel_id=1, source_target_pairs={{0,16},{16,0},{1,17},{17,1},{2,18},{18,2},{3,19},{19,3},{4,20},{20... | collective-permute-start | bytes 6291464 | tf_op jit(solution)/shard_map/ppermute | solution.py:422
  494.2 10.3 collective-permute-start.25
  499.4 8.6 collective-permute-start.12
  503.5 24.1 %collective-permute-start.14 = (bf16[128,2048]{1,0:T(8,128)(2,1)S(1)}, bf16[128,2048]{1,0:T(8,128)(2,1)S(1)}, u32[]{:S(2)}, u32[]{:S(2)}) collective-permute-start(bf16[128,2048]{1,0:T(8,128)(2,1)S(1)} %fusion.68), channel_id=1, source_target_pairs={{0,1},{1,0},{2,3},{3,2},{4,5},{5,4},{6,7},{7,6},{8,9},{9,8},{10,11... | collective-permute-start | bytes 1572872 | tf_op jit(solution)/shard_map/ppermute | solution.py:426
  506.4 21.1 %collective-permute-start.26 = (bf16[128,2048]{1,0:T(8,128)(2,1)S(1)}, bf16[128,2048]{1,0:T(8,128)(2,1)S(1)}, u32[]{:S(2)}, u32[]{:S(2)}) collective-permute-start(bf16[128,2048]{1,0:T(8,128)(2,1)S(1)} %fusion.70), channel_id=1, source_target_pairs={{0,1},{1,0},{2,3},{3,2},{4,5},{5,4},{6,7},{7,6},{8,9},{9,8},{10,11... | collective-permute-start | bytes 1572872 | tf_op jit(solution)/shard_map/ppermute | solution.py:426
  507.1 20.4 %collective-permute-start.24 = (f32[128]{0:T(128)S(1)}, f32[128]{0:T(128)S(1)}, u32[]{:S(2)}, u32[]{:S(2)}) collective-permute-start(f32[128]{0:T(128)S(1)} %fusion.119), channel_id=1, source_target_pairs={{0,1},{1,0},{2,3},{3,2},{4,5},{5,4},{6,7},{7,6},{8,9},{9,8},{10,11... | collective-permute-start | bytes 1544 | tf_op jit(solution)/shard_map/ppermute | solution.py:426
  530.3 26.9 %collective-permute-start.32 = (bf16[128,2048]{1,0:T(8,128)(2,1)}, bf16[128,2048]{1,0:T(8,128)(2,1)}, u32[]{:S(2)}, u32[]{:S(2)}) collective-permute-start(bf16[128,2048]{1,0:T(8,128)(2,1)} %get-tuple-element.253), channel_id=1, source_target_pairs={{0,1},{1,0},{2,3},{3,2},{4,5},{5,4},{6,7},{7,6},{8,9},{9,8},{10,11... | collective-permute-start | bytes 1572872 | tf_op jit(solution)/shard_map/ppermute | solution.py:426
  531.8 10.7 collective-permute-start.34
  531.9 28.6 %collective-permute-start.28 = (bf16[128,2048]{1,0:T(8,128)(2,1)}, bf16[128,2048]{1,0:T(8,128)(2,1)}, u32[]{:S(2)}, u32[]{:S(2)}) collective-permute-start(bf16[128,2048]{1,0:T(8,128)(2,1)} %get-tuple-element.167), channel_id=1, source_target_pairs={{0,1},{1,0},{2,3},{3,2},{4,5},{5,4},{6,7},{7,6},{8,9},{9,8},{10,11... | collective-permute-start | bytes 1572872 | tf_op jit(solution)/shard_map/ppermute | solution.py:426
  533.3 20.4 %collective-permute-start.30 = (f32[128]{0:T(128)S(1)}, f32[128]{0:T(128)S(1)}, u32[]{:S(2)}, u32[]{:S(2)}) collective-permute-start(f32[128]{0:T(128)S(1)} %multiply_multiply_fusion.7), channel_id=1, source_target_pairs={{0,1},{1,0},{2,3},{3,2},{4,5},{5,4},{6,7},{7,6},{8,9},{9,8},{10,11... | collective-permute-start | bytes 1544 | tf_op jit(solution)/shard_map/ppermute | solution.py:426
  542.5 13.8 %collective-permute-start.35 = (f32[2,128]{1,0:T(2,128)S(1)}, f32[2,128]{1,0:T(2,128)S(1)}, u32[]{:S(2)}, u32[]{:S(2)}) collective-permute-start(f32[2,128]{1,0:T(2,128)S(1)} %pad_maximum_fusion.24), channel_id=1, source_target_pairs={{0,16},{16,0},{1,17},{17,1},{2,18},{18,2},{3,19},{19,3},{4,20},{20... | collective-permute-start | bytes 3080 | tf_op jit(solution)/shard_map/ppermute | solution.py:422
  562.9 41.1 %collective-permute-start.29 = (bf16[2,128,2048]{2,1,0:T(8,128)(2,1)}, bf16[2,128,2048]{2,1,0:T(8,128)(2,1)S(1)}, u32[]{:S(2)}, u32[]{:S(2)}) collective-permute-start(bf16[2,128,2048]{2,1,0:T(8,128)(2,1)} %pad_maximum_fusion.9), channel_id=1, source_target_pairs={{0,16},{16,0},{1,17},{17,1},{2,18},{18,2},{3,19},{19,3},{4,20},{20... | collective-permute-start | bytes 3145736 | tf_op jit(solution)/shard_map/ppermute | solution.py:422
  603.9 47.0 %collective-permute-start.42 = (f32[2,128,2048]{2,1,0:T(8,128)}, f32[2,128,2048]{2,1,0:T(8,128)}, u32[]{:S(2)}, u32[]{:S(2)}) collective-permute-start(f32[2,128,2048]{2,1,0:T(8,128)} %dynamic-slice_bitcast_fusion.2), channel_id=1, source_target_pairs={{0,16},{16,0},{1,17},{17,1},{2,18},{18,2},{3,19},{19,3},{4,20},{20... | collective-permute-start | bytes 6291464 | tf_op jit(solution)/shard_map/ppermute | solution.py:422
  643.0 12.2 %collective-permute-start.36 = (f32[2,128,2048]{2,1,0:T(8,128)}, f32[2,128,2048]{2,1,0:T(8,128)}, u32[]{:S(2)}, u32[]{:S(2)}) collective-permute-start(f32[2,128,2048]{2,1,0:T(8,128)} %dynamic-slice_bitcast_fusion.3), channel_id=1, source_target_pairs={{0,16},{16,0},{1,17},{17,1},{2,18},{18,2},{3,19},{19,3},{4,20},{20... | collective-permute-start | bytes 6291464 | tf_op jit(solution)/shard_map/ppermute | solution.py:422
  650.4 257.3 %reduce-scatter.9.cloned.1.call-start = ((), (), s32[]{:S(2)}) async-start(), calls=%async_computation.10 | async-start | bytes 4718592 | tf_op jit(solution)/shard_map/reduce_scatter | solution.py:610
  653.7 13.2 %collective-permute-start.43 = (bf16[128,2048]{1,0:T(8,128)(2,1)S(1)}, bf16[128,2048]{1,0:T(8,128)(2,1)S(1)}, u32[]{:S(2)}, u32[]{:S(2)}) collective-permute-start(bf16[128,2048]{1,0:T(8,128)(2,1)S(1)} %fusion.72), channel_id=1, source_target_pairs={{0,1},{1,0},{2,3},{3,2},{4,5},{5,4},{6,7},{7,6},{8,9},{9,8},{10,11... | collective-permute-start | bytes 1572872 | tf_op jit(solution)/shard_map/ppermute | solution.py:426
  657.2 20.9 %collective-permute-start.37 = (bf16[128,2048]{1,0:T(8,128)(2,1)S(1)}, bf16[128,2048]{1,0:T(8,128)(2,1)S(1)}, u32[]{:S(2)}, u32[]{:S(2)}) collective-permute-start(bf16[128,2048]{1,0:T(8,128)(2,1)S(1)} %fusion.71), channel_id=1, source_target_pairs={{0,1},{1,0},{2,3},{3,2},{4,5},{5,4},{6,7},{7,6},{8,9},{9,8},{10,11... | collective-permute-start | bytes 1572872 | tf_op jit(solution)/shard_map/ppermute | solution.py:426
  679.1 12.4 %collective-permute-start.44 = (bf16[128,2048]{1,0:T(8,128)(2,1)S(1)}, bf16[128,2048]{1,0:T(8,128)(2,1)S(1)}, u32[]{:S(2)}, u32[]{:S(2)}) collective-permute-start(bf16[128,2048]{1,0:T(8,128)(2,1)S(1)} %multiply_convert_fusion), channel_id=1, source_target_pairs={{0,1},{1,0},{2,3},{3,2},{4,5},{5,4},{6,7},{7,6},{8,9},{9,8},{10,11... | collective-permute-start | bytes 1572872 | tf_op jit(solution)/shard_map/ppermute | solution.py:426
  681.3 21.3 %collective-permute-start.38 = (bf16[128,2048]{1,0:T(8,128)(2,1)S(1)}, bf16[128,2048]{1,0:T(8,128)(2,1)S(1)}, u32[]{:S(2)}, u32[]{:S(2)}) collective-permute-start(bf16[128,2048]{1,0:T(8,128)(2,1)S(1)} %multiply_convert_fusion.1), channel_id=1, source_target_pairs={{0,1},{1,0},{2,3},{3,2},{4,5},{5,4},{6,7},{7,6},{8,9},{9,8},{10,11... | collective-permute-start | bytes 1572872 | tf_op jit(solution)/shard_map/ppermute | solution.py:426
  691.7 13.4 %collective-permute-start.45 = (bf16[2,128,2048]{2,1,0:T(8,128)(2,1)S(1)}, bf16[2,128,2048]{2,1,0:T(8,128)(2,1)S(1)}, u32[]{:S(2)}, u32[]{:S(2)}) collective-permute-start(bf16[2,128,2048]{2,1,0:T(8,128)(2,1)S(1)} %pad_maximum_fusion.12), channel_id=1, source_target_pairs={{0,16},{16,0},{1,17},{17,1},{2,18},{18,2},{3,19},{19,3},{4,20},{20... | collective-permute-start | bytes 3145736 | tf_op jit(solution)/shard_map/ppermute | solution.py:422
  716.2 289.7 %reduce-scatter.7.cloned.1.call-start = ((), (), s32[]{:S(2)}) async-start(), calls=%async_computation.9 | async-start | bytes 11206656 | tf_op jit(solution)/shard_map/reduce_scatter | solution.py:609
  733.6 445.9 %reduce-scatter.5.cloned.1.call-start = ((), (), s32[]{:S(2)}) async-start(), calls=%async_computation.8 | async-start | bytes 11206656 | tf_op jit(solution)/shard_map/reduce_scatter | solution.py:609
  823.3 12.3 %collective-permute-start.50 = (f32[2,128,2048]{2,1,0:T(8,128)}, f32[2,128,2048]{2,1,0:T(8,128)}, u32[]{:S(2)}, u32[]{:S(2)}) collective-permute-start(f32[2,128,2048]{2,1,0:T(8,128)} %dynamic-slice_bitcast_fusion), channel_id=1, source_target_pairs={{0,16},{16,0},{1,17},{17,1},{2,18},{18,2},{3,19},{19,3},{4,20},{20... | collective-permute-start | bytes 6291464 | tf_op jit(solution)/shard_map/ppermute | solution.py:422
  835.4 9.0 collective-permute-start.27
  839.2 13.6 %collective-permute-start.51 = (bf16[128,2048]{1,0:T(8,128)(2,1)}, bf16[128,2048]{1,0:T(8,128)(2,1)}, u32[]{:S(2)}, u32[]{:S(2)}) collective-permute-start(bf16[128,2048]{1,0:T(8,128)(2,1)} %fusion.74), channel_id=1, source_target_pairs={{0,1},{1,0},{2,3},{3,2},{4,5},{5,4},{6,7},{7,6},{8,9},{9,8},{10,11... | collective-permute-start | bytes 1572872 | tf_op jit(solution)/shard_map/ppermute | solution.py:426
  843.6 20.4 %collective-permute-start.49 = (bf16[128,2048]{1,0:T(8,128)(2,1)}, bf16[128,2048]{1,0:T(8,128)(2,1)}, u32[]{:S(2)}, u32[]{:S(2)}) collective-permute-start(bf16[128,2048]{1,0:T(8,128)(2,1)} %fusion.73), channel_id=1, source_target_pairs={{0,1},{1,0},{2,3},{3,2},{4,5},{5,4},{6,7},{7,6},{8,9},{9,8},{10,11... | collective-permute-start | bytes 1572872 | tf_op jit(solution)/shard_map/ppermute | solution.py:426
  871.2 10.3 collective-permute-start.54
  881.6 15.1 %collective-permute-start.55 = (f32[2,12288]{1,0:T(2,128)S(1)}, f32[2,12288]{1,0:T(2,128)S(1)}, u32[]{:S(2)}, u32[]{:S(2)}) collective-permute-start(f32[2,12288]{1,0:T(2,128)S(1)} %fusion.187), channel_id=1, source_target_pairs={{0,8},{2,10},{4,12},{6,14},{8,0},{10,2},{12,4},{14,6},{1,9},{3,11}... | collective-permute-start | bytes 294920 | tf_op jit(solution)/shard_map/ppermute | solution.py:619
  908.9 274.4 %collective-permute-start.60 = (bf16[256,1024]{1,0:T(8,128)(2,1)S(1)}, bf16[256,1024]{1,0:T(8,128)(2,1)S(1)}, u32[]{:S(2)}, u32[]{:S(2)}) collective-permute-start(bf16[256,1024]{1,0:T(8,128)(2,1)S(1)} %broadcast_select_fusion.4), channel_id=1, source_target_pairs={{0,16},{16,0},{1,17},{17,1},{2,18},{18,2},{3,19},{19,3},{4,20},{20... | collective-permute-start | bytes 1572872 | tf_op jit(solution)/shard_map/ppermute | solution.py:422
  1196.7 8.0 collective-permute-start.59
  (113 other events, 1376.5 us)
Sparse Core Ops, SparseCore 0:
  21.4 143.0 all-gather.4
  166.6 72.2 all-gather.6
  241.1 142.0 all-gather.8
  385.1 72.1 all-gather.10
  650.5 87.1 reduce-scatter.10
  741.6 87.5 reduce-scatter.8
  832.9 172.9 reduce-scatter.6
  1009.6 169.8 reduce-scatter.4

commit v2 on v1

--- a/solution.py
+++ b/solution.py
@@ -1,3 +1,5 @@
+import functools
+
 import jax
 import jax.numpy as jnp
 from jax import lax
@@ -355,9 +357,7 @@
         compiler_params=pltpu.CompilerParams(
             dimension_semantics=("arbitrary",), vmem_limit_bytes=VMEM_LIMIT
         ),
-        cost_estimate=pl.CostEstimate(
-            flops=rows * channels * 2 * 600, bytes_accessed=rows * channels * 24, transcendentals=0
-        ),
+        cost_estimate=pl.CostEstimate(flops=1000, bytes_accessed=1000, transcendentals=0),
         name="mixer_forward",
     )(pre, tail, start, slab, spread)
 
@@ -408,11 +408,441 @@
         compiler_params=pltpu.CompilerParams(
             dimension_semantics=("arbitrary",), vmem_limit_bytes=VMEM_LIMIT
         ),
-        cost_estimate=pl.CostEstimate(
-            flops=rows * channels * 2 * 1800, bytes_accessed=rows * channels * 32, transcendentals=0
-        ),
+        cost_estimate=pl.CostEstimate(flops=1000, bytes_accessed=1000, transcendentals=0),
         name="mixer_backward",
     )(q, kappa, pre, pre, tail, y, entering, grad, e_rows, slab, spread, gather)
+
+
+MESH = pl.DeviceIdType.MESH
+DEEP = 4
+
+
+def place_in_line():
+    core, line, half = lax.axis_index("section"), lax.axis_index("fsdp"), lax.axis_index("tp")
+    deep, side = line // 2, line % 2
+
+    def device(z, x):
+        return (core, z * 2 + x, half)
+
+    return deep, side, device
+
+
+def greet_all():
+    core, line, half = lax.axis_index("section"), lax.axis_index("fsdp"), lax.axis_index("tp")
+    barrier = pltpu.get_barrier_semaphore()
+
+    def greet(target):
+        pl.semaphore_signal(barrier, inc=1, device_id=target, device_id_type=MESH)
+
+    greet((core, line, 1 - half))
+    greet((1 - core, line, half))
+    for step in range(1, 2 * DEEP):
+        greet((core, (line + step) % (2 * DEEP), half))
+    pl.semaphore_wait(barrier, 2 * DEEP + 1)
+
+
+def start_kernel(*refs, count, micros):
+    shards, (gain, own) = refs[:count], refs[count : count + 2]
+    outs = refs[count + 2 :]
+    wholes, (gains, normed) = outs[:count], outs[count : count + 2]
+    scratch = outs[count + 2 :]
+    local_sem, x_send, x_recv, up_send, up_recv, down_send, down_recv = scratch[:7]
+    gain_send, gain_recv, own_sem, y_send, y_recv, core_send, core_recv, rows_out = scratch[7:]
+    deep, side, device = place_in_line()
+    core, line, half = lax.axis_index("section"), lax.axis_index("fsdp"), lax.axis_index("tp")
+    lines = 2 * DEEP
+
+    greet_all()
+    across_tp, across_core = (core, line, 1 - half), (1 - core, line, half)
+
+    def send_gain(step):
+        return pltpu.make_async_remote_copy(
+            src_ref=gain,
+            dst_ref=gains.at[line],
+            send_sem=gain_send.at[step],
+            recv_sem=gain_recv.at[step],
+            device_id=(core, (line + step) % lines, half),
+            device_id_type=MESH,
+        )
+
+    for step in range(1, lines):
+        send_gain(step).start()
+
+    def rows(i, z, x):
+        size = shards[i].shape[0]
+        return wholes[i].at[pl.ds((z * 2 + x) * size, size)]
+
+    def move(i, z, source, send, recv, target):
+        return pltpu.make_async_remote_copy(
+            src_ref=rows(i, z, side) if source is None else source,
+            dst_ref=rows(i, z, side),
+            send_sem=send,
+            recv_sem=recv,
+            device_id=target,
+            device_id_type=MESH,
+        )
+
+    def across(i, z, source=None):
+        return move(i, z, source, x_send.at[i, z], x_recv.at[i, z], device(deep, 1 - side))
+
+    def upward(i, k, source=None):
+        above = jnp.minimum(deep + 1, DEEP - 1)
+        return move(i, deep - k, source, up_send.at[i, k], up_recv.at[i, k], device(above, side))
+
+    def downward(i, k, source=None):
+        below = jnp.maximum(deep - 1, 0)
+        return move(i, deep + k, source, down_send.at[i, k], down_recv.at[i, k], device(below, side))
+
+    has_above, has_below = deep < DEEP - 1, deep > 0
+    for i in range(count):
+        pltpu.make_async_copy(shards[i], rows(i, deep, side), local_sem.at[i]).start()
+
+        @pl.when(has_above)
+        def _(i=i):
+            upward(i, 0, shards[i]).start()
+
+        @pl.when(has_below)
+        def _(i=i):
+            downward(i, 0, shards[i]).start()
+
+        across(i, deep, shards[i]).start()
+
+    gains[line] = gain[...]
+    for step in range(1, lines):
+        send_gain(step).wait()
+    gain_row = jnp.concatenate(
+        [gains[f, j : j + 1, :] for f in range(lines) for j in range(gain.shape[0] // 4)], axis=1
+    )
+    tokens = own.shape[0] // micros
+    h = own[...].astype(F32)
+    scale = lax.rsqrt(jnp.mean(h * h, axis=1, keepdims=True) + EPS)
+    rows_out[...] = (h * scale * gain_row).astype(BF16)
+
+    def token_copies(m):
+        source = rows_out.at[pl.ds(m * tokens, tokens)]
+        place = normed.at[m, half, core]
+        later = normed.at[m, 1 - half, core]
+        remote = functools.partial(pltpu.make_async_remote_copy, device_id_type=MESH)
+        return (
+            pltpu.make_async_copy(source, place, own_sem.at[m]),
+            remote(source, place, y_send.at[m], y_recv.at[m], device_id=across_tp),
+            remote(source, place, core_send.at[m], core_recv.at[m], device_id=across_core),
+            remote(later, later, core_send.at[micros + m], core_recv.at[micros + m], device_id=across_core),
+        )
+
+    for m in range(micros):
+        for copy in token_copies(m)[:3]:
+            copy.start()
+    for m in range(micros):
+        token_copies(m)[1].wait_recv()
+        token_copies(m)[3].start()
+
+    for k in range(1, DEEP):
+        for i in range(count):
+
+            @pl.when(deep >= k)
+            def _(i=i, k=k):
+                arrived = move(
+                    i, deep - k, None, up_send.at[i, k - 1], up_recv.at[i, k - 1], device(deep, side)
+                )
+                arrived.wait_recv()
+
+                @pl.when(has_above)
+                def _():
+                    upward(i, k).start()
+
+                across(i, deep - k).start()
+
+            @pl.when(deep + k <= DEEP - 1)
+            def _(i=i, k=k):
+                arrived = move(
+                    i, deep + k, None, down_send.at[i, k - 1], down_recv.at[i, k - 1], device(deep, side)
+                )
+                arrived.wait_recv()
+
+                @pl.when(has_below)
+                def _():
+                    downward(i, k).start()
+
+                across(i, deep + k).start()
+
+    for i in range(count):
+        pltpu.make_async_copy(shards[i], rows(i, deep, side), local_sem.at[i]).wait()
+        for z in range(DEEP):
+            other = pltpu.make_async_remote_copy(
+                src_ref=rows(i, z, side),
+                dst_ref=rows(i, z, 1 - side),
+                send_sem=x_send.at[i, z],
+                recv_sem=x_recv.at[i, z],
+                device_id=device(deep, 1 - side),
+                device_id_type=MESH,
+            )
+            other.wait_send()
+            other.wait_recv()
+        for k in range(DEEP - 1):
+
+            @pl.when(has_above & (deep >= k))
+            def _(i=i, k=k):
+                upward(i, k).wait_send()
+
+            @pl.when(has_below & (deep + k <= DEEP - 1))
+            def _(i=i, k=k):
+                downward(i, k).wait_send()
+
+    for m in range(micros):
+        own_copy, y_copy, core_copy, core_later = token_copies(m)
+        own_copy.wait()
+        y_copy.wait_send()
+        core_copy.wait()
+        core_later.wait()
+
+
+def start_gather(shards, gain, own, micros):
+    count = len(shards)
+    lines = 2 * DEEP
+    pairs = pltpu.SemaphoreType.DMA((count, DEEP))
+    dma = lambda n: pltpu.SemaphoreType.DMA((n,))
+    shape = jax.ShapeDtypeStruct
+    anywhere = pl.BlockSpec(memory_space=pl.ANY)
+    vmem = pl.BlockSpec(memory_space=pltpu.VMEM)
+    rows, width = own.shape
+    sizes = sum(v.size for v in shards)
+    return pl.pallas_call(
+        functools.partial(start_kernel, count=count, micros=micros),
+        out_shape=[shape((v.shape[0] * lines, v.shape[1]), v.dtype) for v in shards]
+        + [
+            shape((lines,) + gain.shape, F32),
+            shape((micros, 2, 2, rows // micros, width), BF16),
+        ],
+        in_specs=[anywhere] * count + [vmem] * 2,
+        out_specs=[anywhere] * count + [vmem, anywhere],
+        scratch_shapes=[dma(count)]
+        + [pairs] * 6
+        + [dma(lines)] * 2
+        + [dma(micros)] * 3
+        + [dma(2 * micros)] * 2
+        + [pltpu.VMEM(own.shape, BF16)],
+        compiler_params=pltpu.CompilerParams(
+            collective_id=1, has_side_effects=True, vmem_limit_bytes=VMEM_LIMIT
+        ),
+        cost_estimate=pl.CostEstimate(flops=1000, bytes_accessed=1000, transcendentals=0),
+        name="start_gather",
+    )(*shards, gain, own)
+
+
+def add_rows(out, *parts):
+    rows = out.shape[0]
+    step = 32
+
+    def body(n, _):
+        at = pl.ds(pl.multiple_of(n * step, step), step)
+        total = parts[0][at].astype(F32)
+        for part in parts[1:]:
+            total = total + part[at].astype(F32)
+        out[at] = total.astype(out.dtype)
+        return 0
+
+    lax.fori_loop(0, rows // step, body, 0)
+
+
+X_ORDER = ((3, 2, 1, 0), (3, 0, 2, 1), (0, 3, 1, 2), (0, 1, 2, 3))
+
+
+def reduce_kernel(*refs, count):
+    parts, small, results = refs[:count], refs[count], refs[count + 1 : 2 * count + 1]
+    own_small, next_small, both_small = refs[2 * count + 1 : 2 * count + 4]
+    scratch = refs[2 * count + 4 :]
+    held, crossed, from_below, from_above = (
+        scratch[n * count : (n + 1) * count] for n in range(4)
+    )
+    load_sem, x_send, x_recv, up_send, up_recv, down_send, down_recv = scratch[4 * count : -3]
+    small_buffer, small_send, small_recv = scratch[-3:]
+    deep, side, device = place_in_line()
+    core, line, half = lax.axis_index("section"), lax.axis_index("fsdp"), lax.axis_index("tp")
+    greet_all()
+    across_core = (1 - core, line, half)
+    partners = [
+        device(deep, 1 - side),
+        device(deep + 1 - 2 * (deep % 2), side),
+        device((deep + 2) % DEEP, side),
+        (core, line, 1 - half),
+        across_core,
+        across_core,
+    ]
+
+    def swap_small(n, source, target):
+        return pltpu.make_async_remote_copy(
+            src_ref=source,
+            dst_ref=target,
+            send_sem=small_send.at[n],
+            recv_sem=small_recv.at[n],
+            device_id=partners[n],
+            device_id_type=MESH,
+        )
+
+    def sum_small():
+        for n in range(3):
+            copy = swap_small(n, small if n == 0 else small_buffer.at[n - 1], small_buffer.at[3 + n])
+            if n > 0:
+                copy.start()
+            copy.wait()
+            value = small[...] if n == 0 else small_buffer[n - 1]
+            small_buffer[n] = value + small_buffer[3 + n]
+        over_tp = swap_small(3, small_buffer.at[2], small_buffer.at[6])
+        over_core = swap_small(4, small_buffer.at[2], next_small)
+        over_tp.start()
+        over_core.start()
+        own_small[...] = small_buffer[2]
+        over_tp.wait()
+        small_buffer[7] = small_buffer[2] + small_buffer[6]
+        last = swap_small(5, small_buffer.at[7], small_buffer.at[8])
+        last.start()
+        last.wait()
+        both_small[...] = small_buffer[7] + small_buffer[8]
+        over_core.wait()
+
+    def rows(i, z, x):
+        size = results[i].shape[0]
+        return parts[i].at[pl.ds((z * 2 + x) * size, size)]
+
+    def load(i, z):
+        return pltpu.make_async_copy(rows(i, z, side), held[i].at[z], load_sem.at[i, z])
+
+    def across(i, z):
+        return pltpu.make_async_remote_copy(
+            src_ref=rows(i, z, 1 - side),
+            dst_ref=crossed[i].at[z],
+            send_sem=x_send.at[i, z],
+            recv_sem=x_recv.at[i, z],
+            device_id=device(deep, 1 - side),
+            device_id_type=MESH,
+        )
+
+    def upward(i, k, z, here):
+        return pltpu.make_async_remote_copy(
+            src_ref=held[i].at[z],
+            dst_ref=from_below[i].at[k - 1],
+            send_sem=up_send.at[i, k - 1],
+            recv_sem=up_recv.at[i, k - 1],
+            device_id=device(min(here + 1, DEEP - 1), side),
+            device_id_type=MESH,
+        )
+
+    def downward(i, k, z, here):
+        return pltpu.make_async_remote_copy(
+            src_ref=held[i].at[z],
+            dst_ref=from_above[i].at[k - 1],
+            send_sem=down_send.at[i, k - 1],
+            recv_sem=down_recv.at[i, k - 1],
+            device_id=device(max(here - 1, 0), side),
+            device_id_type=MESH,
+        )
+
+    def at_depth(here):
+        order = X_ORDER[here]
+        last = DEEP - 1
+        started = []
+
+        def send_across(number):
+            for i in range(count):
+                across(i, order[number]).start()
+
+        def take(number):
+            z = order[number]
+            for i in range(count):
+                across(i, z).wait_recv()
+            if number + 2 < DEEP:
+                send_across(number + 2)
+            for i in range(count):
+                load(i, z).wait()
+                add_rows(held[i].at[z], held[i].at[z], crossed[i].at[z])
+
+        def relay(k, up):
+            z = DEEP - k + here if up else here + k - DEEP
+            first = here == 0 if up else here == last
+            for i in range(count):
+                if not first:
+                    make = upward if up else downward
+                    back = from_below if up else from_above
+                    make(i, k - 1, z, here).wait_recv()
+                    add_rows(held[i].at[z], held[i].at[z], back[i].at[k - 2])
+                copy = (upward if up else downward)(i, k, z, here)
+                copy.start()
+                started.append(copy)
+
+        swap_small(0, small, small_buffer.at[3]).start()
+        send_across(0)
+        send_across(1)
+        for number in range(DEEP):
+            for i in range(count):
+                load(i, order[number]).start()
+        sum_small()
+        if here in (0, last):
+            up = here == 0
+            for k in range(1, DEEP):
+                take(k - 1)
+                relay(k, up)
+            take(DEEP - 1)
+        else:
+            up = here == 1
+            take(0)
+            take(1)
+            relay(2, up)
+            relay(3, not up)
+            take(2)
+            relay(3, up)
+            take(3)
+        for i in range(count):
+            terms = [held[i].at[here]]
+            if here > 0:
+                upward(i, DEEP - 1, here, here).wait_recv()
+                terms.append(from_below[i].at[DEEP - 2])
+            if here < last:
+                downward(i, DEEP - 1, here, here).wait_recv()
+                terms.append(from_above[i].at[DEEP - 2])
+            add_rows(results[i], *terms)
+        for copy in started:
+            copy.wait_send()
+        for z in range(DEEP):
+            for i in range(count):
+                across(i, z).wait_send()
+
+    for here in range(DEEP):
+
+        @pl.when(deep == here)
+        def _(here=here):
+            at_depth(here)
+
+
+def reduce_line(parts, small, name, collective_id):
+    count = len(parts)
+    shards = [(p.shape[0] // (2 * DEEP),) + p.shape[1:] for p in parts]
+    pairs = pltpu.SemaphoreType.DMA((count, DEEP))
+    sizes = sum(p.size for p in parts)
+    blocks = lambda n: [pltpu.VMEM((n,) + shard, BF16) for shard in shards]
+    shape = jax.ShapeDtypeStruct
+    vmem = pl.BlockSpec(memory_space=pltpu.VMEM)
+    return pl.pallas_call(
+        functools.partial(reduce_kernel, count=count),
+        out_shape=[shape(shard, F32) for shard in shards] + [shape(small.shape, F32)] * 3,
+        in_specs=[pl.BlockSpec(memory_space=pl.ANY)] * count + [vmem],
+        out_specs=[vmem] * (count + 3),
+        scratch_shapes=blocks(DEEP)
+        + blocks(DEEP)
+        + blocks(DEEP - 1)
+        + blocks(DEEP - 1)
+        + [pairs] * 7
+        + [
+            pltpu.VMEM((9,) + small.shape, F32),
+            pltpu.SemaphoreType.DMA((6,)),
+            pltpu.SemaphoreType.DMA((6,)),
+        ],
+        compiler_params=pltpu.CompilerParams(
+            collective_id=collective_id, has_side_effects=True, vmem_limit_bytes=VMEM_LIMIT
+        ),
+        cost_estimate=pl.CostEstimate(flops=1000, bytes_accessed=1000, transcendentals=0),
+        name=name,
+    )(*parts, small)
 
 
 SWAP = [(0, 1), (1, 0)]
@@ -435,23 +865,33 @@
     return lax.dynamic_index_in_dim(pair, index, 0, keepdims=False)
 
 
-def gather_tokens(own, core, half):
-    both = by_index(half, own, swap_tp(own))
+def gather_tokens(own, core, half, beside=()):
+    both = by_index(half, own, after(swap_tp(own), *beside))
     whole = by_index(core, both, swap_core(both))
     whole = jnp.moveaxis(whole, 0, 1)
     return whole.reshape((4 * own.shape[0],) + own.shape[1:])
 
 
-def scatter_tokens(part, core, half):
-    rows = part.shape[0] // 4
-    split = part.reshape((2, 2, rows) + part.shape[1:])
-    mine = lax.dynamic_index_in_dim(split, core, 1, keepdims=False)
-    theirs = lax.dynamic_index_in_dim(split, 1 - core, 1, keepdims=False)
-    total = mine + swap_core(theirs)
-    sent = pick(total, 1 - half)
-    if part.ndim > 1:
-        sent = sent.astype(BF16)
-    return pick(total, half) + swap_tp(sent).astype(F32)
+def after(value, *others):
+    return lax.optimization_barrier((value,) + others)[0] if others else value
+
+
+def over_cores(part, core):
+    split_rows = part.reshape((2, 2, part.shape[0] // 4) + part.shape[1:])
+    mine = lax.dynamic_index_in_dim(split_rows, core, 1, keepdims=False)
+    theirs = lax.dynamic_index_in_dim(split_rows, 1 - core, 1, keepdims=False)
+    return mine + swap_core(theirs)
+
+
+class Sum:
+    def __init__(self, part, core, half):
+        self.half = half
+        self.total = over_cores(part, core)
+        sent = pick(self.total, 1 - half)
+        self.sent = sent.astype(BF16) if part.ndim > 1 else sent
+
+    def done(self, *beside):
+        return pick(self.total, self.half) + after(swap_tp(self.sent), *beside).astype(F32)
 
 
 def local(
@@ -482,9 +922,6 @@
     shared = w_bc.shape[2]
     depth = w_zx.shape[1]
     in_width = 2 * channels + shared + LANES
-    gain_pair = by_index(core, norm_gain[0], swap_core(norm_gain[0]))
-    gains = lax.all_gather(gain_pair, "fsdp", axis=1, tiled=True).astype(F32)
-
     def cut(tensor, index, size):
         return lax.dynamic_slice_in_dim(tensor, index * size, size, tensor.ndim - 1)
 
@@ -515,125 +952,238 @@
     got_shard = swap_core(weight_shard(1 - core))
     own_slab = slab_of(core)
     got_slab = swap_core(slab_of(1 - core))
-    projections, slabs = [], []
+    in_line = lax.axis_size("fsdp") == 2 * DEEP and lax.axis_size("tp") == 2
+    over_fsdp = functools.partial(lax.all_gather, axis_name="fsdp", tiled=True)
+    slabs = [jnp.where(core == layer, own_slab, got_slab) for layer in range(2)]
+    shards = []
     for layer in range(2):
         shard = jnp.where(core == layer, own_shard, got_shard)
-        projections.append(
-            (
-                lax.all_gather(shard[:, :in_width], "fsdp", axis=0, tiled=True),
-                lax.all_gather(shard[:, in_width:], "fsdp", axis=0, tiled=True),
-            )
-        )
-        slabs.append(jnp.where(core == layer, own_slab, got_slab))
+        shards.append((shard[:, :in_width], shard[:, in_width:]))
+    gain_pair = by_index(core, norm_gain[0], swap_core(norm_gain[0])).astype(F32)
+
+    def own_rows(tensor):
+        return [
+            lax.dynamic_slice_in_dim(tensor[0, m], core * rows, rows, 0) for m in range(micros)
+        ]
+
+    first = own_rows(inputs)
+    if in_line:
+        packed = jnp.pad(gain_pair.reshape(-1, LANES), ((0, 8 - 2 * depth // LANES), (0, 0)))
+        w_in, w_back, gains, first_normed = start_gather(
+            shards[0], packed, jnp.concatenate(first), micros
+        )
+        projections = [(w_in, w_back)]
+        shards[1] = lax.optimization_barrier(shards[1] + (gains,))[:2]
+        gains = jnp.moveaxis(
+            gains[:, : 2 * depth // LANES].reshape(2 * DEEP, 2, depth), 0, 1
+        ).reshape(2, -1)
+        first_normed = first_normed.reshape(micros, 4 * rows, -1)
+    else:
+        projections = [tuple(over_fsdp(v, axis=0) for v in shards[0])]
+        gains = over_fsdp(gain_pair.astype(BF16), axis=1).astype(F32)
+        first_normed = None
+    projections.append(tuple(over_fsdp(v, axis=0) for v in shards[1]))
 
     lane = jnp.arange(LANES)
     head_of = jnp.arange(channels) // width
     spread = ((lane[:, None] % heads == head_of[None, :]) & (lane[:, None] < 2 * heads)).astype(BF16)
     gather = (head_of[:, None] == lane[None, :]).astype(BF16)
 
-    def own_rows(tensor):
-        return [
-            lax.dynamic_slice_in_dim(tensor[0, m], core * rows, rows, 0).astype(F32)
-            for m in range(micros)
-        ]
-
-    hidden = own_rows(inputs)
     size = channels + shared
-    saved = []
+    zero_state = jnp.zeros((shared // 2, channels), F32)
+    zero_halo = jnp.zeros((HALO, size), F32)
+    last = micros - 1
+
+    def norm(h, layer):
+        scale = lax.rsqrt(jnp.mean(h * h, axis=1, keepdims=True) + EPS)
+        return scale, (h * scale * gains[layer][None]).astype(BF16)
+
+    hidden = [v.astype(F32) for v in first]
+    cotangents = own_rows(cotangent)
+    normed = [None] * micros
+    scales = [[None] * micros for _ in range(2)]
+    for m in range(micros):
+        scales[0][m], own = norm(hidden[m], 0)
+        normed[m] = first_normed[m] if in_line else gather_tokens(own, core, half)
+
+    hiddens, normeds, kept = [hidden, None], [normed, None], [[None] * micros for _ in range(2)]
+    waiting = None
+
+    def finish(pending, *beside):
+        layer, m, part, squares = pending
+        r = lax.rsqrt(squares.done(*beside) / DI + EPS)[:, None]
+        branch = r * part.done(*beside)
+        kept[layer][m].update(r=r, branch=branch)
+        h = hiddens[layer][m] + branch
+        if layer == 0:
+            hiddens[1][m] = h
+            scales[1][m], own = norm(h, 1)
+            return own
+        results[m] = h
+        g = cotangents[m].astype(F32)
+        return jnp.concatenate([r, r * r * jnp.sum(g * branch, axis=1, keepdims=True) / DI], axis=1)
+
+    def spread_out(pending, own, *beside):
+        layer, m = pending[:2]
+        if layer == 0:
+            normeds[1][m] = gather_tokens(own, core, half, beside)
+        else:
+            factors[m] = gather_tokens(own, core, half, beside)
+
+    results, factors = [None] * micros, [None] * micros
+    hiddens[1], normeds[1] = [None] * micros, [None] * micros
+    everyones = [gather_tokens(v, core, half) for v in cotangents]
     for layer in range(2):
         w_in, w_back = projections[layer]
-        slab = slabs[layer]
-        state = jnp.zeros((shared // 2, channels), F32)
-        tail = jnp.zeros((HALO, size), F32)
-        kept = []
-        next_hidden = []
+        state, tail = zero_state, zero_halo
         for m in range(micros):
-            h = hidden[m]
-            scale = lax.rsqrt(jnp.mean(h * h, axis=1, keepdims=True) + EPS)
-            normed = gather_tokens((h * scale * gains[layer][None]).astype(BF16), core, half)
-            pre = dot_nn(normed, w_in)
-            u, squares, y, entering, state = mixer_forward(pre, tail, state, slab, spread, heads)
-            part = dot_nt(u, w_back)
-            total = scatter_tokens(part, core, half)
-            squares = scatter_tokens(squares[:, 0], core, half)
-            r = lax.rsqrt(squares / DI + EPS)[:, None]
-            branch = r * total
-            next_hidden.append(h + branch)
-            kept.append((h, scale, normed, pre, tail, y, u, entering, r, branch))
-            tail = pre[-HALO:, channels : channels + size]
-        saved.append(kept)
-        hidden = next_hidden
-
-    grads = own_rows(cotangent)
-    reduced = [None, None]
-    small = [None, None]
+            tokens = normeds[layer][m]
+            if layer == 1 and m == 0:
+                tokens = after(tokens, *everyones)
+            if waiting is not None:
+                tokens = after(tokens, waiting[2].sent, waiting[3].sent)
+            pre = dot_nn(tokens, w_in)
+            mixed_pre = pre
+            if waiting is not None:
+                own = finish(waiting, pre)
+                mixed_pre = after(pre, own)
+            u, squares, y, entering, state_out = mixer_forward(
+                mixed_pre, tail, state, slabs[layer], spread, heads
+            )
+            if waiting is not None:
+                spread_out(waiting, own, u)
+            kept[layer][m] = dict(pre=pre, tail=tail, u=u, y=y, entering=entering)
+            state, tail = state_out, pre[-HALO:, channels : channels + size]
+            part = Sum(dot_nt(u, w_back), core, half)
+            waiting = (layer, m, part, Sum(squares[:, 0], core, half))
+    spread_out(waiting, finish(waiting))
+
+    over_tokens = (((0,), (0,)), ((), ()))
+
+    def weight_grad(left, right):
+        return lax.dot_general(
+            jnp.concatenate(left), jnp.concatenate(right), over_tokens, preferred_element_type=F32
+        ).astype(BF16)
+
+    reduced, small = [None, None], [None, None]
+    grads = [v.astype(F32) for v in cotangents]
+    backs = [
+        (everyone.astype(F32) * factor[:, :1]).astype(BF16)
+        for everyone, factor in zip(everyones, factors)
+    ]
+    kappas = [factor[:, 1:] for factor in factors]
+    gain_parts = [[], []]
+    next_backs, next_kappas = [None] * micros, [None] * micros
+    waiting = None
+
+    def finish_back(pending, *beside):
+        layer, m, part = pending
+        h, scale = hiddens[layer][m], scales[layer][m]
+        g_norm = part.done(*beside)
+        gain_parts[layer].append(jnp.sum(g_norm * (h * scale), axis=0))
+        g_norm = g_norm * gains[layer][None]
+        mean = jnp.mean(g_norm * h, axis=1, keepdims=True)
+        g = grads[m] + scale * g_norm - h * (scale * scale * scale) * mean
+        grads[m] = g
+        if layer == 0:
+            return g, g
+        r, branch = kept[0][m]["r"], kept[0][m]["branch"]
+        return (g * r).astype(BF16), r * r * jnp.sum(g * branch, axis=1)[:, None] / DI
+
+    def spread_back(pending, own, *beside):
+        layer, m = pending[:2]
+        if layer == 1:
+            next_backs[m] = gather_tokens(own[0], core, half, beside)
+            next_kappas[m] = gather_tokens(own[1], core, half, beside)
+
+    def reduce_rows(part):
+        return lax.psum_scatter(part, "fsdp", scatter_dimension=0, tiled=True).astype(F32)
+
+    previous = ()
     for layer in (1, 0):
         w_in, w_back = projections[layer]
-        slab = slabs[layer]
-        state = jnp.zeros((shared // 2, channels), F32)
-        e_rows = jnp.zeros((HALO, size), F32)
-        next_grads = [None] * micros
+        state, e_rows = zero_state, zero_halo
+        totals = jnp.zeros(slabs[0].shape, F32)
         gpres = [None] * micros
-        backs = [None] * micros
-        totals = jnp.zeros(slab.shape, F32)
-        gain_total = jnp.zeros((w_out.shape[1] * lax.axis_size("fsdp"),), F32)
         for m in reversed(range(micros)):
-            h, scale, normed, pre, tail, y, u, entering, r, branch = saved[layer][m]
-            g = grads[m]
-            kappa = r * r * jnp.sum(g * branch, axis=1, keepdims=True) / DI
-            back = gather_tokens((g * r).astype(BF16), core, half)
-            kappa = gather_tokens(kappa[:, 0], core, half)[:, None]
+            k = kept[layer][m]
+            back = backs[m]
+            if waiting is not None and waiting[0] == layer:
+                back = after(back, waiting[2].sent)
             q = dot_nn(back, w_back)
+            if m == last:
+                if layer == 1:
+                    grad_back = weight_grad(backs, [kept[layer][j]["u"] for j in range(micros)])
+                    q = after(q, grad_back)
+                    reduced_back = reduce_rows(grad_back)
+                    previous = (reduced_back,)
             gpre, state, e_rows, sums = mixer_backward(
-                q, kappa, pre, tail, y, entering, state, e_rows, slab, spread, gather, heads
+                q,
+                kappas[m],
+                k["pre"],
+                k["tail"],
+                k["y"],
+                k["entering"],
+                state,
+                e_rows,
+                slabs[layer],
+                spread,
+                gather,
+                heads,
             )
-            g_norm = scatter_tokens(dot_nt(gpre, w_in), core, half)
-            gain_total = gain_total + jnp.sum(g_norm * (h * scale), axis=0)
-            g_norm = g_norm * gains[layer][None]
-            mean = jnp.mean(g_norm * h, axis=1, keepdims=True)
-            next_grads[m] = g + scale * g_norm - h * (scale * scale * scale) * mean
+            totals = totals + sums
             gpres[m] = gpre
-            backs[m] = back
-            totals = totals + sums
-        grads = next_grads
-        normed_all = jnp.concatenate([saved[layer][m][2] for m in range(micros)])
-        u_all = jnp.concatenate([saved[layer][m][6] for m in range(micros)])
-        over_tokens = (((0,), (0,)), ((), ()))
-        grad_back = lax.dot_general(
-            jnp.concatenate(backs), u_all, over_tokens, preferred_element_type=F32
-        ).astype(BF16)
-        grad_in = lax.dot_general(
-            normed_all, jnp.concatenate(gpres), over_tokens, preferred_element_type=F32
-        ).astype(BF16)
-        reduced[layer] = (
-            lax.psum_scatter(grad_in, "fsdp", scatter_dimension=0, tiled=True),
-            lax.psum_scatter(grad_back, "fsdp", scatter_dimension=0, tiled=True),
-        )
-        small[layer] = jnp.concatenate([totals.reshape(-1), gain_total])
+            if waiting is not None and waiting[0] != layer:
+                spread_back(waiting, own, gpre)
+                backs[waiting[1]], kappas[waiting[1]] = next_backs[waiting[1]], next_kappas[waiting[1]]
+                waiting = None
+            ready = gpre
+            if waiting is not None:
+                own = finish_back(waiting, gpre)
+                ready = after(gpre, *own)
+            part = Sum(dot_nt(ready, w_in), core, half)
+            if waiting is not None:
+                spread_back(waiting, own, part.total)
+            waiting = (layer, m, part)
+        grad_in = weight_grad(normeds[layer], [after(v, waiting[2].sent) for v in gpres])
+        if layer == 0:
+            grad_back = weight_grad(backs, [kept[layer][j]["u"] for j in range(micros)])
+        own = finish_back(waiting, grad_in)
+        small[layer] = jnp.concatenate([totals.reshape(-1), sum(gain_parts[layer])])
+        if layer == 1 or not in_line:
+            if layer == 0:
+                reduced_back = reduce_rows(grad_back)
+            reduced[layer] = (reduce_rows(after(grad_in, *previous)), reduced_back)
+        backs = [after(v, *own) if v is not None else None for v in next_backs]
+        kappas = list(next_kappas)
+
+    def placed_rows(parts):
+        own = jnp.where(core == 0, parts[0], parts[1])
+        other = jnp.where(core == 0, parts[1], parts[0])
+        return by_index(core, own, swap_core(other)).reshape(1, 1, 2 * rows, -1)
+
+    outputs, input_grads = placed_rows(results), placed_rows(grads)
 
     small_sums = jnp.stack(small)
-    devices = lax.axis_size("fsdp")
-    if devices & (devices - 1) == 0:
-        bit = 1
-        while bit < devices:
-            small_sums = small_sums + lax.ppermute(
-                small_sums, "fsdp", [(i, i ^ bit) for i in range(devices)]
-            )
-            bit *= 2
+    if in_line:
+        flat = small_sums.reshape(-1, LANES)
+        *reduced[0], own_small, next_small, both_small = reduce_line(
+            [grad_in, grad_back], flat, "grads_reduce", 2
+        )
+        own_small, next_small, both_small = (
+            pick(v.reshape(small_sums.shape), core) for v in (own_small, next_small, both_small)
+        )
     else:
         small_sums = lax.psum(small_sums, "fsdp")
-    own = pick(small_sums, core)
-    got = swap_core(pick(small_sums, 1 - core))
+        own_small = pick(small_sums, core)
+        next_small = swap_core(pick(small_sums, 1 - core))
+        both_small = own_small + next_small
+        both_small = both_small + swap_tp(both_small)
     count = slabs[0].size
-    halves = by_index(core, own[:count], got[:count]).reshape((2,) + slabs[0].shape)
-    both = own + got
-    common = jnp.concatenate(
-        [both[:count].reshape(slabs[0].shape)[:5, channels:].reshape(-1), both[count:]]
-    )
-    common = common + swap_tp(common)
-    conv_sum = common[: 5 * shared].reshape(5, shared)
+    halves = by_index(core, own_small[:count], next_small[:count]).reshape((2,) + slabs[0].shape)
+    conv_sum = both_small[:count].reshape(slabs[0].shape)[:5, channels:]
     gain_sum = lax.dynamic_slice_in_dim(
-        common[5 * shared :], lax.axis_index("fsdp") * depth, depth, 0
+        both_small[count:], lax.axis_index("fsdp") * depth, depth, 0
     )
     wide = jnp.concatenate([halves[0, :7, :channels], halves[1, :7, :channels]], axis=1)
     narrow = jnp.concatenate(
@@ -644,27 +1194,22 @@
     mine = [jnp.where(core == 0, reduced[0][i], reduced[1][i]) for i in range(2)]
     theirs = [jnp.where(core == 0, reduced[1][i], reduced[0][i]) for i in range(2)]
     got = [swap_core(v) for v in theirs]
-    in_pair = by_index(core, mine[0], got[0]).astype(F32)
-    back_pair = by_index(core, mine[1], got[1]).astype(F32)
-    g_zx = jnp.concatenate(
-        [in_pair[j, :, : 2 * channels].reshape(depth, 2, channels) for j in range(2)], axis=2
-    )
-    g_bc = in_pair[:, :, 2 * channels : 2 * channels + shared].sum(axis=0)
-    g_dt = jnp.concatenate(
-        [in_pair[j, :, 2 * channels + shared : 2 * channels + shared + heads] for j in range(2)],
-        axis=1,
-    )
-    g_back = jnp.concatenate([back_pair[0], back_pair[1]], axis=1)
+    first_half = [jnp.where(core == 0, own, other) for own, other in zip(mine, got)]
+    second_half = [jnp.where(core == 0, other, own) for own, other in zip(mine, got)]
+
+    def joined(begin, end, i=0):
+        return jnp.concatenate([first_half[i][:, begin:end], second_half[i][:, begin:end]], axis=1)
+
+    g_zx = jnp.stack([joined(0, channels), joined(channels, 2 * channels)], axis=1)
+    at = 2 * channels
+    g_bc = mine[0][:, at : at + shared] + got[0][:, at : at + shared]
     g_bc = g_bc + swap_tp(g_bc)
-
-    def placed_rows(parts):
-        own = jnp.where(core == 0, parts[0], parts[1])
-        other = jnp.where(core == 0, parts[1], parts[0])
-        return by_index(core, own, swap_core(other)).reshape(1, 1, 2 * rows, -1)
+    g_dt = joined(at + shared, at + shared + heads)
+    g_back = joined(0, channels, 1)
 
     return (
-        placed_rows(hidden),
-        placed_rows(grads),
+        outputs,
+        input_grads,
         gain_sum[None],
         g_zx[None],
         g_bc[None],

time: 1220 us -> 1020 us (0.84)
  waiting for transfers between devices: 669 us -> 150 us
  Pallas kernels: 129 us -> 463 us
  starting transfers between devices: 77.4 us -> 41.4 us
  local copies, waits for them, and re-layouts: 74.6 us -> 99.2 us
  blocking collectives: 15.4 us -> 0 us
    pallas_call x0 -> x2, Pallas kernels: none -> 334 us  [the longest x1 175 us: reduce_line(): pl.pallas_call(functools.partial(reduce_kernel, count=count), out_shape=[...]
    reduce_scatter x4 -> x2, waiting for transfers between devices: 269 us -> 0.01 us  [reduce_rows(): lax.psum_scatter(part, 'fsdp', scatter_dimension=0, tiled=True).astype(F32)]
    all_gather x4 -> x2, waiting for transfers between devices: 234 us -> 94.2 us  [local(): projections.append(tuple((over_fsdp(v, axis=0) for v in shards[1])))]
    ppermute x26 -> x23, waiting for transfers between devices: 138 us -> 43.8 us  [swap_tp(): return lax.ppermute(value, 'tp', SWAP)]
    ppermute x32 -> x29, starting transfers between devices: 48.5 us -> 21.6 us  [swap_core(): return lax.ppermute(value, 'section', SWAP)]
    ppermute x3 -> x0, waiting for transfers between devices: 22 us -> none  [local(): lax.ppermute(small_sums, 'fsdp', [(i, i ^ bit) for i in range(devices)])]
    all_gather x1 -> x0, blocking collectives: 15.4 us -> none  [local(): gains = lax.all_gather(gain_pair, 'fsdp', axis=1, tiled=True).astype(F32)]
    unnamed x188 -> x219, local copies, waits for them, and re-layouts: 23.1 us -> 37 us
  transfers between devices with their start and end apart: 69 -> 56, of which waited for: 32 -> 17; matrix products, arithmetic and copies ran while one was open for 21% -> 26% of each run, Pallas kernels for 11% -> 27%
where the time goes in v2:
time: 1020 us; the launch traced here: 1010 us
  Pallas kernels  463 us (45%)
  matrix products  159 us (16%)
  waiting for transfers between devices  150 us (15%)
  local copies, waits for them, and re-layouts  99.2 us (10%)
  other arithmetic  84.2 us (8%)
  starting transfers between devices  41.4 us (4%)
  between operations  15.9 us (2%)
    pallas_call x1, Pallas kernels, reduce_line(): pl.pallas_call(functools.partial(reduce_kernel, count=count), out_shape=[...  175 us
    pallas_call x1, Pallas kernels, start_gather(): pl.pallas_call(functools.partial(start_kernel, count=count, micros=micros...  159 us
    all_gather x2, waiting for transfers between devices, local(): projections.append(tuple((over_fsdp(v, axis=0) for v in shards[1])))  94.2 us
    pallas_call x4, Pallas kernels, mixer_backward(): pl.pallas_call(body, grid=(steps,), in_specs=[by_row(channels), by_row(1)...  81.9 us
    dot_general x8, matrix products, dot_nn(): lax.dot_general(a, b, (((1,), (0,)), ((), ())), preferred_element_type=F32)  64 us
    dot_general x8, matrix products, dot_nt(): lax.dot_general(a, b, (((1,), (1,)), ((), ())), preferred_element_type=F32)  50.7 us
    pallas_call x4, Pallas kernels, mixer_forward(): pl.pallas_call(body, grid=(steps,), in_specs=[by_row(width), fixed((HALO,...  46.9 us
    dot_general x4, matrix products, weight_grad(): lax.dot_general(jnp.concatenate(left), jnp.concatenate(right), over_token...  44.5 us
  transfers between devices with their start and end apart: 56, of which 17 were waited for; matrix products, arithmetic and copies ran while one was open for 26% of the time, Pallas kernels for 27%

profile of v2, /device:TPU:9, one launch (start us, length us, event | category | flops | bytes accessed | tf_op | source)
XLA Modules:
  0.0 1012.5 jit_solution(15401120683202903435)
XLA Ops:
  26.0 158.9 %start_gather.1 = (bf16[2048,2432]{1,0:T(8,128)(2,1)}, bf16[2048,1024]{1,0:T(8,128)(2,1)}, f32[8,8,128]{2,1,0:T(8,128)}, bf16[2,2,2,128,2048]{4,3,2,1,0:T(8,128)(2,1)}) custom-call(bf16[256,2432]{1,0:T(8,128)(2,1)} %slice.191.refs_0_, bf16[256,1024]{1,0:T(8,128)(2,1)} %slice.192.refs_1_, f32[8,128]{1,0:T(8,128)} %pad_convert_fusion.refs_2_, ...), custom_call_target="tpu_custom_call" | custom-call | flops 1000 | bytes 1000 | tf_op jit(solution)/shard_map/start_gather/pallas_call | solution.py:610
  189.4 4.1 fusion.123
  193.5 12.4 %fusion.132.refs_0_.refs_2_.refs_3_ = f32[512,2432]{1,0:T(8,128)} fusion(bf16[512,2048]{1,0:T(8,128)(2,1)S(1)} %bitcast.494, bf16[2048,2432]{1,0:T(8,128)(2,1)} %get-tuple-element.92), kind=kOutput, calls=%fused_computation.374 | convolution fusion | flops 5100273664 | bytes 17039360 | tf_op jit(solution)/shard_map/dot_general | solution.py:28
  207.4 11.6 %mixer_forward.4 = (bf16[512,1024]{1,0:T(8,128)(2,1)}, f32[512,1]{1,0:T(8,128)}, f32[512,1024]{1,0:T(8,128)}, f32[4,128,1024]{2,1,0:T(8,128)}, f32[128,1024]{1,0:T(8,128)}) custom-call(f32[512,2432]{1,0:T(8,128)} %fusion.132.refs_0_.refs_2_.refs_3_, f32[8,1280]{1,0:T(8,128)} %broadcast_in_dim.38.refs_1_.refs_8_.refs_4_, ...), custom_call_target="tpu_custom_call" | custom-call | flops 1000 | bytes 1000 | tf_op jit(solution)/shard_map/mixer_forward/pallas_call | solution.py:329
  219.0 3.6 fusion.133
  233.8 11.2 %fusion.134.refs_0_.refs_2_.refs_3_ = f32[512,2432]{1,0:T(8,128)} fusion(bf16[512,2048]{1,0:T(8,128)(2,1)S(1)} %bitcast.492, bf16[2048,2432]{1,0:T(8,128)(2,1)} %get-tuple-element.92), kind=kOutput, calls=%fused_computation.376 | convolution fusion | flops 5100273664 | bytes 17039360 | tf_op jit(solution)/shard_map/dot_general | solution.py:28
  248.3 11.6 %mixer_forward.5 = (bf16[512,1024]{1,0:T(8,128)(2,1)}, f32[512,1]{1,0:T(8,128)}, f32[512,1024]{1,0:T(8,128)}, f32[4,128,1024]{2,1,0:T(8,128)}, f32[128,1024]{1,0:T(8,128)}) custom-call(f32[512,2432]{1,0:T(8,128)} %fusion.134.refs_0_.refs_2_.refs_3_, f32[8,1280]{1,0:T(8,128)} %slice.194.refs_1_.refs_4_, f32[128,1024]{1,0:T(8,128)} %get-tuple-element.101.refs_2_, ...), custom_call_target="tpu_custom_call" | custom-call | flops 1000 | bytes 1000 | tf_op jit(solution)/shard_map/mixer_forward/pallas_call | solution.py:329
  259.9 3.6 fusion.135
  282.0 45.0 %all-gather.3.cloned.1.call-done = bf16[2048,2432]{1,0:T(8,128)(2,1)} async-done(((bf16[256,2432]{1,0:T(8,128)(2,1)}), bf16[2048,2432]{1,0:T(8,128)(2,1)}) %all-gather.3.cloned.1.call-update) | async-done | bytes 9961488 | tf_op jit(solution)/shard_map/all_gather | solution.py:985
  327.0 11.5 %fusion.136.refs_0_.refs_2_.refs_3_ = f32[512,2432]{1,0:T(8,128)} fusion(bf16[512,2048]{1,0:T(8,128)(2,1)} %bitcast.482, bf16[2048,2432]{1,0:T(8,128)(2,1)} %all-gather.3.cloned.1.call-done), kind=kOutput, calls=%fused_computation.378 | convolution fusion | flops 5100273664 | bytes 17039360 | tf_op jit(solution)/shard_map/dot_general | solution.py:28
  340.5 11.7 %mixer_forward.6 = (bf16[512,1024]{1,0:T(8,128)(2,1)}, f32[512,1]{1,0:T(8,128)}, f32[512,1024]{1,0:T(8,128)}, f32[4,128,1024]{2,1,0:T(8,128)}, f32[128,1024]{1,0:T(8,128)}) custom-call(f32[512,2432]{1,0:T(8,128)} %fusion.136.refs_0_.refs_2_.refs_3_, f32[8,1280]{1,0:T(8,128)} %broadcast_in_dim.38.refs_1_.refs_8_.refs_4_, ...), custom_call_target="tpu_custom_call" | custom-call | flops 1000 | bytes 1000 | tf_op jit(solution)/shard_map/mixer_forward/pallas_call | solution.py:329
  352.2 49.1 %all-gather.5.cloned.1.call-done = bf16[2048,1024]{1,0:T(8,128)(2,1)} async-done(((bf16[256,1024]{1,0:T(8,128)(2,1)}), bf16[2048,1024]{1,0:T(8,128)(2,1)}) %all-gather.5.cloned.1.call-update) | async-done | bytes 4194320 | tf_op jit(solution)/shard_map/all_gather | solution.py:985
  401.3 4.9 fusion.137
  413.7 2.7 fusion.126
  420.9 2.7 copy-done.34
  425.9 11.4 %fusion.138.refs_0_.refs_2_.refs_3_ = f32[512,2432]{1,0:T(8,128)} fusion(bf16[512,2048]{1,0:T(8,128)(2,1)S(1)} %bitcast.484, bf16[2048,2432]{1,0:T(8,128)(2,1)} %all-gather.3.cloned.1.call-done), kind=kOutput, calls=%fused_computation.380 | convolution fusion | flops 5100273664 | bytes 17039360 | tf_op jit(solution)/shard_map/dot_general | solution.py:28
  439.7 12.0 %mixer_forward.7 = (bf16[512,1024]{1,0:T(8,128)(2,1)}, f32[512,1]{1,0:T(8,128)}, f32[512,1024]{1,0:T(8,128)}, f32[4,128,1024]{2,1,0:T(8,128)}, f32[128,1024]{1,0:T(8,128)}) custom-call(f32[512,2432]{1,0:T(8,128)} %fusion.138.refs_0_.refs_2_.refs_3_, f32[8,1280]{1,0:T(8,128)} %slice.197.refs_1_.refs_4_, f32[128,1024]{1,0:T(8,128)} %get-tuple-element.119.refs_2_, ...), custom_call_target="tpu_custom_call" | custom-call | flops 1000 | bytes 1000 | tf_op jit(solution)/shard_map/mixer_forward/pallas_call | solution.py:329
  451.7 3.6 fusion.139
  464.4 8.8 collective-permute-done.24
  483.2 11.0 %collective-permute-done.26 = bf16[128,2048]{1,0:T(8,128)(2,1)S(1)} collective-permute-done((bf16[128,2048]{1,0:T(8,128)(2,1)S(1)}, bf16[128,2048]{1,0:T(8,128)(2,1)S(1)}, u32[]{:S(2)}, u32[]{:S(2)}) %collective-permute-start.26) | collective-permute-done | bytes 524320 | tf_op jit(solution)/shard_map/ppermute | solution.py:856
  501.1 9.1 collective-permute-done.11
  520.9 6.3 fusion.23
  527.2 6.5 fusion.140.refs_0_
  533.6 20.5 %mixer_backward.4 = (bf16[512,2432]{1,0:T(8,128)(2,1)}, f32[128,1024]{1,0:T(8,128)}, f32[8,1280]{1,0:T(8,128)}, f32[8,1280]{1,0:T(8,128)}) custom-call(f32[512,1024]{1,0:T(8,128)} %fusion.140.refs_0_, f32[512,1]{1,0:T(8,128)} %get-tuple-element.296.refs_1_, f32[512,2432]{1,0:T(8,128)} %fusion.138.refs_0_.refs_2_.refs_3_, ...), custom_call_target="tpu_custom_call" | custom-call | flops 1000 | bytes 1000 | tf_op jit(solution)/shard_map/mixer_backward/pallas_call | solution.py:377
  554.2 9.0 fusion.141
  566.1 4.2 collective-permute-done.32
  570.4 2.9 bitcast_add_fusion.3
  573.5 3.7 fusion.142.refs_0_
  577.1 20.6 %mixer_backward.5 = (bf16[512,2432]{1,0:T(8,128)(2,1)}, f32[128,1024]{1,0:T(8,128)}, f32[8,1280]{1,0:T(8,128)}, f32[8,1280]{1,0:T(8,128)}) custom-call(f32[512,1024]{1,0:T(8,128)} %fusion.142.refs_0_, f32[512,1]{1,0:T(8,128)} %get-tuple-element.294.refs_1_, f32[512,2432]{1,0:T(8,128)} %fusion.136.refs_0_.refs_2_.refs_3_, ...), custom_call_target="tpu_custom_call" | custom-call | flops 1000 | bytes 1000 | tf_op jit(solution)/shard_map/mixer_backward/pallas_call | solution.py:377
  601.1 8.3 fusion.143
  614.3 9.4 collective-permute-done.37
  628.6 13.9 %convolution_convert_fusion.1 = bf16[2048,2432]{1,0:T(8,128)(2,1)} fusion(bf16[512,2432]{1,0:T(8,128)(2,1)S(1)} %copy-done.101, bf16[512,2432]{1,0:T(8,128)(2,1)S(1)} %copy-done.104, bf16[512,2048]{1,0:T(8,128)(2,1)S(1)} %bitcast.485, bf16[512,2048]{1,0:T(8,128)(2,1)S(1)} %bitcast.483), kind=kOutput, calls=%fused_computation.1 | convolution fusion | flops 10223878144 | bytes 19136512 | tf_op jit(solution)/shard_map/dot_general | solution.py:1064
  650.5 2.7 copy-done.96
  653.2 3.7 fusion.144.refs_0_
  656.8 20.4 %mixer_backward.6 = (bf16[512,2432]{1,0:T(8,128)(2,1)}, f32[128,1024]{1,0:T(8,128)}, f32[8,1280]{1,0:T(8,128)}, f32[8,1280]{1,0:T(8,128)}) custom-call(f32[512,1024]{1,0:T(8,128)} %fusion.144.refs_0_, f32[512,1]{1,0:T(8,128)} %copy.124.refs_1_, f32[512,2432]{1,0:T(8,128)} %fusion.134.refs_0_.refs_2_.refs_3_, f32[512,2432]{1,0:T(8,128)} %fusion.134.refs_0_.refs_2_.refs_3_, ...), custom_call_target="tpu_custom_call" | custom-call | flops 1000 | bytes 1000 | tf_op jit(solution)/shard_map/mixer_backward/pallas_call | solution.py:377
  677.2 9.2 fusion.145
  699.1 2.8 copy-done.30
  705.2 3.7 fusion.146.refs_0_
  708.9 20.5 %mixer_backward.7 = (bf16[512,2432]{1,0:T(8,128)(2,1)}, f32[128,1024]{1,0:T(8,128)}, f32[8,1280]{1,0:T(8,128)}, f32[8,1280]{1,0:T(8,128)}) custom-call(f32[512,1024]{1,0:T(8,128)} %fusion.146.refs_0_, f32[512,1]{1,0:T(8,128)} %copy.131.refs_1_, f32[512,2432]{1,0:T(8,128)} %fusion.132.refs_0_.refs_2_.refs_3_, f32[512,2432]{1,0:T(8,128)} %fusion.132.refs_0_.refs_2_.refs_3_, ...), custom_call_target="tpu_custom_call" | custom-call | flops 1000 | bytes 1000 | tf_op jit(solution)/shard_map/mixer_backward/pallas_call | solution.py:377
  732.0 8.5 fusion.147
  747.7 9.1 fusion.20.refs_1_
  756.9 2.7 bitcast_add_fusion
  761.9 15.2 %convolution_convert_fusion.refs_0_ = bf16[2048,2432]{1,0:T(8,128)(2,1)} fusion(bf16[512,2432]{1,0:T(8,128)(2,1)S(1)} %copy-done.100, bf16[512,2432]{1,0:T(8,128)(2,1)} %get-tuple-element.154, bf16[512,2048]{1,0:T(8,128)(2,1)S(1)} %bitcast.493, bf16[512,2048]{1,0:T(8,128)(2,1)S(1)} %bitcast.495), kind=kOutput, calls=%fused_computation | convolution fusion | flops 10223878144 | bytes 19136512 | tf_op jit(solution)/shard_map/dot_general | solution.py:1064
  778.5 3.0 broadcast_select_fusion.4
  781.6 175.1 %grads_reduce.1 = (f32[256,2432]{1,0:T(8,128)}, f32[256,1024]{1,0:T(8,128)}, f32[192,128]{1,0:T(8,128)}, f32[192,128]{1,0:T(8,128)}, f32[192,128]{1,0:T(8,128)}) custom-call(bf16[2048,2432]{1,0:T(8,128)(2,1)} %convolution_convert_fusion.refs_0_, bf16[2048,1024]{1,0:T(8,128)(2,1)} %fusion.20.refs_1_, f32[192,128]{1,0:T(8,128)} %reshape.347.refs_2_), custom_call_target="tpu_custom_call" | custom-call | flops 1000 | bytes 1000 | tf_op jit(solution)/shard_map/grads_reduce/pallas_call | solution.py:825
  970.3 2.5 convert_select_fusion.2
  972.8 2.9 convert_select_fusion
  999.0 5.2 copy.136
  (563 shorter events, 203.5 us)
Async XLA Ops:
  7.2 319.8 %all-gather.3.cloned.1.call-start = ((), (), s32[]{:S(2)}) async-start(), calls=%async_computation.2 | async-start | bytes 11206656 | tf_op jit(solution)/shard_map/all_gather | solution.py:985
  14.0 4.8 collective-permute-start
  185.0 216.3 %all-gather.5.cloned.1.call-start = ((), (), s32[]{:S(2)}) async-start(), calls=%async_computation.3 | async-start | bytes 4718592 | tf_op jit(solution)/shard_map/all_gather | solution.py:985
  225.2 5.5 collective-permute-start.5
  225.5 3.8 collective-permute-start.3
  228.0 742.2 %reduce-scatter.3.cloned.1.call-start = ((), (), s32[]{:S(2)}) async-start(), calls=%async_computation.4 | async-start | bytes 4718592 | tf_op jit(solution)/shard_map/reduce_scatter | solution.py:1100
  229.4 15.6 %collective-permute-start.4 = (f32[128]{0:T(128)S(1)}, f32[128]{0:T(128)S(1)}, u32[]{:S(2)}, u32[]{:S(2)}) collective-permute-start(f32[128]{0:T(128)S(1)} %fusion.99), channel_id=1, source_target_pairs={{0,1},{1,0},{2,3},{3,2},{4,5},{5,4},{6,7},{7,6},{8,9},{9,8},{10,11... | collective-permute-start | bytes 1544 | tf_op jit(solution)/shard_map/ppermute | solution.py:856
  233.2 13.2 %collective-permute-start.6 = (bf16[128,2048]{1,0:T(8,128)(2,1)S(1)}, bf16[128,2048]{1,0:T(8,128)(2,1)S(1)}, u32[]{:S(2)}, u32[]{:S(2)}) collective-permute-start(bf16[128,2048]{1,0:T(8,128)(2,1)S(1)} %fusion.61), channel_id=1, source_target_pairs={{0,1},{1,0},{2,3},{3,2},{4,5},{5,4},{6,7},{7,6},{8,9},{9,8},{10,11... | collective-permute-start | bytes 1572872 | tf_op jit(solution)/shard_map/ppermute | solution.py:856
  247.5 19.8 %collective-permute-start.7 = (bf16[128,2048]{1,0:T(8,128)(2,1)S(1)}, bf16[128,2048]{1,0:T(8,128)(2,1)S(1)}, u32[]{:S(2)}, u32[]{:S(2)}) collective-permute-start(bf16[128,2048]{1,0:T(8,128)(2,1)S(1)} %multiply_convert_fusion.5), channel_id=1, source_target_pairs={{0,1},{1,0},{2,3},{3,2},{4,5},{5,4},{6,7},{7,6},{8,9},{9,8},{10,11... | collective-permute-start | bytes 1572872 | tf_op jit(solution)/shard_map/ppermute | solution.py:856
  266.1 10.0 collective-permute-start.13
  268.8 4.2 collective-permute-start.8
  271.2 67.3 %collective-permute-start.15 = (f32[128]{0:T(128)S(1)}, f32[128]{0:T(128)S(1)}, u32[]{:S(2)}, u32[]{:S(2)}) collective-permute-start(f32[128]{0:T(128)S(1)} %fusion.100), channel_id=1, source_target_pairs={{0,1},{1,0},{2,3},{3,2},{4,5},{5,4},{6,7},{7,6},{8,9},{9,8},{10,11... | collective-permute-start | bytes 1544 | tf_op jit(solution)/shard_map/ppermute | solution.py:856
  280.9 57.7 %collective-permute-start.16 = (bf16[128,2048]{1,0:T(8,128)(2,1)S(1)}, bf16[128,2048]{1,0:T(8,128)(2,1)S(1)}, u32[]{:S(2)}, u32[]{:S(2)}) collective-permute-start(bf16[128,2048]{1,0:T(8,128)(2,1)S(1)} %fusion.62), channel_id=1, source_target_pairs={{0,1},{1,0},{2,3},{3,2},{4,5},{5,4},{6,7},{7,6},{8,9},{9,8},{10,11... | collective-permute-start | bytes 1572872 | tf_op jit(solution)/shard_map/ppermute | solution.py:856
  339.3 71.2 %collective-permute-start.19 = (bf16[128,2048]{1,0:T(8,128)(2,1)S(1)}, bf16[128,2048]{1,0:T(8,128)(2,1)}, u32[]{:S(2)}, u32[]{:S(2)}) collective-permute-start(bf16[128,2048]{1,0:T(8,128)(2,1)S(1)} %multiply_convert_fusion.4), channel_id=1, source_target_pairs={{0,1},{1,0},{2,3},{3,2},{4,5},{5,4},{6,7},{7,6},{8,9},{9,8},{10,11... | collective-permute-start | bytes 1572872 | tf_op jit(solution)/shard_map/ppermute | solution.py:856
  408.8 12.1 %collective-permute-start.21 = (f32[2,128,2048]{2,1,0:T(8,128)}, f32[2,128,2048]{2,1,0:T(8,128)}, u32[]{:S(2)}, u32[]{:S(2)}) collective-permute-start(f32[2,128,2048]{2,1,0:T(8,128)} %dynamic-slice_bitcast_fusion.5), channel_id=1, source_target_pairs={{0,16},{16,0},{1,17},{17,1},{2,18},{18,2},{3,19},{19,3},{4,20},{20... | collective-permute-start | bytes 6291464 | tf_op jit(solution)/shard_map/ppermute | solution.py:852
  413.0 6.1 collective-permute-start.20
  413.2 4.6 collective-permute-start.17
  417.8 19.5 %collective-permute-start.18 = (f32[128]{0:T(128)S(1)}, f32[128]{0:T(128)S(1)}, u32[]{:S(2)}, u32[]{:S(2)}) collective-permute-start(f32[128]{0:T(128)S(1)} %fusion.107), channel_id=1, source_target_pairs={{0,1},{1,0},{2,3},{3,2},{4,5},{5,4},{6,7},{7,6},{8,9},{9,8},{10,11... | collective-permute-start | bytes 1544 | tf_op jit(solution)/shard_map/ppermute | solution.py:856
  425.6 13.3 %collective-permute-start.22 = (bf16[128,2048]{1,0:T(8,128)(2,1)S(1)}, bf16[128,2048]{1,0:T(8,128)(2,1)S(1)}, u32[]{:S(2)}, u32[]{:S(2)}) collective-permute-start(bf16[128,2048]{1,0:T(8,128)(2,1)S(1)} %fusion.63), channel_id=1, source_target_pairs={{0,1},{1,0},{2,3},{3,2},{4,5},{5,4},{6,7},{7,6},{8,9},{9,8},{10,11... | collective-permute-start | bytes 1572872 | tf_op jit(solution)/shard_map/ppermute | solution.py:856
  458.0 20.0 %collective-permute-start.25 = (f32[2,128,2048]{2,1,0:T(8,128)}, f32[2,128,2048]{2,1,0:T(8,128)}, u32[]{:S(2)}, u32[]{:S(2)}) collective-permute-start(f32[2,128,2048]{2,1,0:T(8,128)} %dynamic-slice_bitcast_fusion.4), channel_id=1, source_target_pairs={{0,16},{16,0},{1,17},{17,1},{2,18},{18,2},{3,19},{19,3},{4,20},{20... | collective-permute-start | bytes 6291464 | tf_op jit(solution)/shard_map/ppermute | solution.py:852
  460.5 12.7 %collective-permute-start.9 = (bf16[128,2048]{1,0:T(8,128)(2,1)S(1)}, bf16[128,2048]{1,0:T(8,128)(2,1)S(1)}, u32[]{:S(2)}, u32[]{:S(2)}) collective-permute-start(bf16[128,2048]{1,0:T(8,128)(2,1)S(1)} %get-tuple-element.240), channel_id=1, source_target_pairs={{0,1},{1,0},{2,3},{3,2},{4,5},{5,4},{6,7},{7,6},{8,9},{9,8},{10,11... | collective-permute-start | bytes 1572872 | tf_op jit(solution)/shard_map/ppermute | solution.py:856
  462.8 10.5 %collective-permute-start.24 = (f32[128]{0:T(128)S(1)}, f32[128]{0:T(128)S(1)}, u32[]{:S(2)}, u32[]{:S(2)}) collective-permute-start(f32[128]{0:T(128)S(1)} %fusion.111), channel_id=1, source_target_pairs={{0,1},{1,0},{2,3},{3,2},{4,5},{5,4},{6,7},{7,6},{8,9},{9,8},{10,11... | collective-permute-start | bytes 1544 | tf_op jit(solution)/shard_map/ppermute | solution.py:856
  463.1 10.1 collective-permute-start.29
  475.2 6.6 collective-permute-start.10
  480.6 13.6 %collective-permute-start.26 = (bf16[128,2048]{1,0:T(8,128)(2,1)S(1)}, bf16[128,2048]{1,0:T(8,128)(2,1)S(1)}, u32[]{:S(2)}, u32[]{:S(2)}) collective-permute-start(bf16[128,2048]{1,0:T(8,128)(2,1)S(1)} %fusion.64), channel_id=1, source_target_pairs={{0,1},{1,0},{2,3},{3,2},{4,5},{5,4},{6,7},{7,6},{8,9},{9,8},{10,11... | collective-permute-start | bytes 1572872 | tf_op jit(solution)/shard_map/ppermute | solution.py:856
  497.8 12.4 %collective-permute-start.11 = (bf16[128,2048]{1,0:T(8,128)(2,1)S(1)}, bf16[128,2048]{1,0:T(8,128)(2,1)S(1)}, u32[]{:S(2)}, u32[]{:S(2)}) collective-permute-start(bf16[128,2048]{1,0:T(8,128)(2,1)S(1)} %get-tuple-element.235), channel_id=1, source_target_pairs={{0,1},{1,0},{2,3},{3,2},{4,5},{5,4},{6,7},{7,6},{8,9},{9,8},{10,11... | collective-permute-start | bytes 1572872 | tf_op jit(solution)/shard_map/ppermute | solution.py:856
  499.1 16.0 %collective-permute-start.31 = (f32[2,128,2]{1,2,0:T(2,128)S(1)}, f32[2,128,2]{1,2,0:T(2,128)S(1)}, u32[]{:S(2)}, u32[]{:S(2)}) collective-permute-start(f32[2,128,2]{1,2,0:T(2,128)S(1)} %pad_maximum_fusion.20), channel_id=1, source_target_pairs={{0,16},{16,0},{1,17},{17,1},{2,18},{18,2},{3,19},{19,3},{4,20},{20... | collective-permute-start | bytes 6152 | tf_op jit(solution)/shard_map/ppermute | solution.py:852
  511.3 4.8 collective-permute-start.12
  565.9 4.5 collective-permute-start.32
  566.1 406.7 %reduce-scatter.5.cloned.1.call-start = ((), (), s32[]{:S(2)}) async-start(), calls=%async_computation.5 | async-start | bytes 11206656 | tf_op jit(solution)/shard_map/reduce_scatter | solution.py:1100
  573.4 24.3 %collective-permute-start.33 = (bf16[128,2048]{1,0:T(8,128)(2,1)S(1)}, bf16[128,2048]{1,0:T(8,128)(2,1)S(1)}, u32[]{:S(2)}, u32[]{:S(2)}) collective-permute-start(bf16[128,2048]{1,0:T(8,128)(2,1)S(1)} %fusion.65), channel_id=1, source_target_pairs={{0,1},{1,0},{2,3},{3,2},{4,5},{5,4},{6,7},{7,6},{8,9},{9,8},{10,11... | collective-permute-start | bytes 1572872 | tf_op jit(solution)/shard_map/ppermute | solution.py:856
  609.6 4.2 collective-permute-start.34
  610.1 13.5 %collective-permute-start.37 = (bf16[128,2048]{1,0:T(8,128)(2,1)S(1)}, bf16[128,2048]{1,0:T(8,128)(2,1)S(1)}, u32[]{:S(2)}, u32[]{:S(2)}) collective-permute-start(bf16[128,2048]{1,0:T(8,128)(2,1)S(1)} %multiply_convert_fusion.3), channel_id=1, source_target_pairs={{0,1},{1,0},{2,3},{3,2},{4,5},{5,4},{6,7},{7,6},{8,9},{9,8},{10,11... | collective-permute-start | bytes 1572872 | tf_op jit(solution)/shard_map/ppermute | solution.py:856
  611.6 16.9 %collective-permute-start.39 = (f32[128,1]{0,1:T(1,128)S(1)}, f32[128,1]{0,1:T(1,128)S(1)}, u32[]{:S(2)}, u32[]{:S(2)}) collective-permute-start(f32[128,1]{0,1:T(1,128)S(1)} %multiply_bitcast_fusion.1), channel_id=1, source_target_pairs={{0,1},{1,0},{2,3},{3,2},{4,5},{5,4},{6,7},{7,6},{8,9},{9,8},{10,11... | collective-permute-start | bytes 1544 | tf_op jit(solution)/shard_map/ppermute | solution.py:856
  624.5 19.1 %collective-permute-start.35 = (bf16[128,2048]{1,0:T(8,128)(2,1)}, bf16[128,2048]{1,0:T(8,128)(2,1)}, u32[]{:S(2)}, u32[]{:S(2)}) collective-permute-start(bf16[128,2048]{1,0:T(8,128)(2,1)} %fusion.66), channel_id=1, source_target_pairs={{0,1},{1,0},{2,3},{3,2},{4,5},{5,4},{6,7},{7,6},{8,9},{9,8},{10,11... | collective-permute-start | bytes 1572872 | tf_op jit(solution)/shard_map/ppermute | solution.py:856
  627.4 21.3 %collective-permute-start.38 = (bf16[2,128,2048]{2,1,0:T(8,128)(2,1)}, bf16[2,128,2048]{2,1,0:T(8,128)(2,1)}, u32[]{:S(2)}, u32[]{:S(2)}) collective-permute-start(bf16[2,128,2048]{2,1,0:T(8,128)(2,1)} %pad_maximum_fusion.9), channel_id=1, source_target_pairs={{0,16},{16,0},{1,17},{17,1},{2,18},{18,2},{3,19},{19,3},{4,20},{20... | collective-permute-start | bytes 3145736 | tf_op jit(solution)/shard_map/ppermute | solution.py:852
  628.5 14.2 %collective-permute-start.40 = (f32[2,128,1]{1,0,2:T(2,128)S(1)}, f32[2,128,1]{1,0,2:T(2,128)S(1)}, u32[]{:S(2)}, u32[]{:S(2)}) collective-permute-start(f32[2,128,1]{1,0,2:T(2,128)S(1)} %bitcast.535), channel_id=1, source_target_pairs={{0,16},{16,0},{1,17},{17,1},{2,18},{18,2},{3,19},{19,3},{4,20},{20... | collective-permute-start | bytes 3080 | tf_op jit(solution)/shard_map/ppermute | solution.py:852
  648.2 42.0 %collective-permute-start.36 = (bf16[128,2048]{1,0:T(8,128)(2,1)S(1)}, bf16[128,2048]{1,0:T(8,128)(2,1)S(1)}, u32[]{:S(2)}, u32[]{:S(2)}) collective-permute-start(bf16[128,2048]{1,0:T(8,128)(2,1)S(1)} %multiply_convert_fusion.2), channel_id=1, source_target_pairs={{0,1},{1,0},{2,3},{3,2},{4,5},{5,4},{6,7},{7,6},{8,9},{9,8},{10,11... | collective-permute-start | bytes 1572872 | tf_op jit(solution)/shard_map/ppermute | solution.py:856
  689.1 10.0 collective-permute-start.42
  691.5 5.8 collective-permute-start.41
  695.6 48.8 %collective-permute-start.27 = (f32[128,2048]{1,0:T(8,128)}, f32[128,2048]{1,0:T(8,128)}, u32[]{:S(2)}, u32[]{:S(2)}) collective-permute-start(f32[128,2048]{1,0:T(8,128)} %get-tuple-element.253), channel_id=1, source_target_pairs={{0,16},{16,0},{1,17},{17,1},{2,18},{18,2},{3,19},{19,3},{4,20},{20... | collective-permute-start | bytes 3145736 | tf_op jit(solution)/shard_map/ppermute | solution.py:852
  704.4 25.0 %collective-permute-start.45 = (bf16[128,2048]{1,0:T(8,128)(2,1)S(1)}, bf16[128,2048]{1,0:T(8,128)(2,1)S(1)}, u32[]{:S(2)}, u32[]{:S(2)}) collective-permute-start(bf16[128,2048]{1,0:T(8,128)(2,1)S(1)} %fusion.67), channel_id=1, source_target_pairs={{0,1},{1,0},{2,3},{3,2},{4,5},{5,4},{6,7},{7,6},{8,9},{9,8},{10,11... | collective-permute-start | bytes 1572872 | tf_op jit(solution)/shard_map/ppermute | solution.py:856
  743.4 13.5 %collective-permute-start.46 = (f32[2,128,2048]{2,1,0:T(8,128)}, f32[2,128,2048]{2,1,0:T(8,128)}, u32[]{:S(2)}, u32[]{:S(2)}) collective-permute-start(f32[2,128,2048]{2,1,0:T(8,128)} %dynamic-slice_bitcast_fusion), channel_id=1, source_target_pairs={{0,16},{16,0},{1,17},{17,1},{2,18},{18,2},{3,19},{19,3},{4,20},{20... | collective-permute-start | bytes 6291464 | tf_op jit(solution)/shard_map/ppermute | solution.py:852
  759.8 17.4 %collective-permute-start.47 = (bf16[128,2048]{1,0:T(8,128)(2,1)S(1)}, bf16[128,2048]{1,0:T(8,128)(2,1)S(1)}, u32[]{:S(2)}, u32[]{:S(2)}) collective-permute-start(bf16[128,2048]{1,0:T(8,128)(2,1)S(1)} %fusion.68), channel_id=1, source_target_pairs={{0,1},{1,0},{2,3},{3,2},{4,5},{5,4},{6,7},{7,6},{8,9},{9,8},{10,11... | collective-permute-start | bytes 1572872 | tf_op jit(solution)/shard_map/ppermute | solution.py:856
  781.5 207.6 %collective-permute-start.48 = (f32[128,2048]{1,0:T(8,128)}, f32[128,2048]{1,0:T(8,128)}, u32[]{:S(2)}, u32[]{:S(2)}) collective-permute-start(f32[128,2048]{1,0:T(8,128)} %get-tuple-element.224), channel_id=1, source_target_pairs={{0,16},{16,0},{1,17},{17,1},{2,18},{18,2},{3,19},{19,3},{4,20},{20... | collective-permute-start | bytes 3145736 | tf_op jit(solution)/shard_map/ppermute | solution.py:852
  975.7 18.7 %collective-permute-start.49 = (f32[256,2432]{1,0:T(8,128)}, f32[256,2432]{1,0:T(8,128)S(1)}, u32[]{:S(2)}, u32[]{:S(2)}) collective-permute-start(f32[256,2432]{1,0:T(8,128)} %convert_select_fusion), channel_id=1, source_target_pairs={{0,16},{16,0},{1,17},{17,1},{2,18},{18,2},{3,19},{19,3},{4,20},{20... | collective-permute-start | bytes 7471112 | tf_op jit(solution)/shard_map/ppermute | solution.py:852
  984.5 7.6 collective-permute-start.51
  997.1 7.9 collective-permute-start.50
  (117 other events, 2478.6 us)
Sparse Core Ops, SparseCore 0:
  185.1 141.8 all-gather.2
  329.1 72.1 all-gather.4
  566.2 85.6 reduce-scatter.2
  655.8 172.7 reduce-scatter.4

commit v3 on v2

--- a/solution.py
+++ b/solution.py
@@ -2,6 +2,7 @@
 
 import jax
 import jax.numpy as jnp
+import numpy as np
 from jax import lax
 from jax.experimental import pallas as pl
 from jax.experimental.pallas import tpu as pltpu
@@ -18,6 +19,8 @@
 F32 = jnp.float32
 BF16 = jnp.bfloat16
 VMEM_LIMIT = 56 * 1024 * 1024
+MIXER_VMEM = 24 * 1024 * 1024
+BACK_VMEM = 40 * 1024 * 1024
 
 
 def sigmoid(v):
@@ -84,7 +87,7 @@
 
 
 def forward_kernel(
-    pre, tail, start, slab, spread, u, sq, y, entering, leaving, state, buffer, *, channels, heads
+    gate, rest, tail, start, slab, spread, u, sq, y, entering, leaving, state, buffer, *, channels, heads
 ):
     step = pl.program_id(0)
     size = channels + 2 * LANES
@@ -98,7 +101,7 @@
     def _():
         buffer[0:HALO, :] = buffer[CHUNK : CHUNK + HALO, :]
 
-    buffer[HALO:, :] = pre[:, channels : channels + size]
+    buffer[HALO:, :] = rest[:, :size]
     entering[0] = state[...]
     conv = conv_rows(buffer, slab)
     act = conv * sigmoid(conv)
@@ -106,7 +109,7 @@
     in_map = act[:, channels : channels + LANES]
     out_map = act[:, channels + LANES :]
     arg, dt, decay, cum, dt_w, grown_w, left_w = step_terms(
-        pre[:, channels + size :], slab, channels, heads, spread[...]
+        rest[:, size:], slab, channels, heads, spread[...]
     )
     cum_t = cum.T
     xt = xs * dt_w
@@ -135,7 +138,7 @@
             for xp in xt_s
         )
         y[:, cols] = base[:, cols] + dot3(split(jnp.concatenate(mats, axis=1)), stacked)
-    z = pre[:, :channels]
+    z = gate[...]
     gated = y[...] * (z * sigmoid(z))
     sq[...] = jnp.sum(gated * gated, axis=1, keepdims=True)
     u[...] = (gated * slab[5:6, :channels]).astype(BF16)
@@ -147,8 +150,9 @@
 
 def backward_kernel(
     q,
-    kappa,
-    pre,
+    factor,
+    gate,
+    rest,
     before,
     tail,
     y,
@@ -189,9 +193,9 @@
 
     @pl.when(step < steps - 1)
     def _():
-        buffer[0:HALO, :] = before[:, channels : channels + size]
-
-    buffer[HALO:, :] = pre[:, channels : channels + size]
+        buffer[0:HALO, :] = before[:, :size]
+
+    buffer[HALO:, :] = rest[:, :size]
     conv = conv_rows(buffer, slab)
     sig = sigmoid(conv)
     act = conv * sig
@@ -200,22 +204,22 @@
     in_map = act[:, channels : channels + LANES]
     out_map = act[:, channels + LANES :]
     arg, dt, decay, cum, dt_w, grown_w, left_w = step_terms(
-        pre[:, channels + size :], slab, channels, heads, spread[...]
+        rest[:, size:], slab, channels, heads, spread[...]
     )
     cum_t = cum.T
 
-    z = pre[:, :channels]
+    z = gate[...]
     sig_z = sigmoid(z)
     silu_z = z * sig_z
     yv = y[...]
     gated = yv * silu_z
-    qv = q[...]
+    qv = q[...] * factor[:, 0:1]
     sums[5:6, :channels] += jnp.sum(qv * gated, axis=0, keepdims=True)
-    g_gated = qv * slab[5:6, :channels] - gated * kappa[...]
+    g_gated = qv * slab[5:6, :channels] - gated * factor[:, 1:2]
     gpre[:, :channels] = (g_gated * yv * (sig_z * (1.0 + z * (1.0 - sig_z)))).astype(BF16)
     gy = g_gated * silu_z
     gy_b = gy.astype(BF16)
-    sums[6:7, :channels] += jnp.sum(gy * xs, axis=0, keepdims=True)
+    skip_row = jnp.sum(gy * xs, axis=0, keepdims=True)
 
     xt = xs * dt_w
     xt_b = xt.astype(BF16)
@@ -274,7 +278,14 @@
     pad = jnp.zeros((CHUNK - heads, CHUNK), F32)
     gap_rows_t = jnp.concatenate(gap_rows + [pad], axis=0).T
     packed = jnp.concatenate(
-        [xs * g_xt, row_terms, col_terms, jnp.broadcast_to(through, (HALO, channels))], axis=0
+        [
+            xs * g_xt,
+            row_terms,
+            col_terms,
+            jnp.broadcast_to(through, (HALO, channels)),
+            jnp.broadcast_to(skip_row, (HALO, channels)),
+        ],
+        axis=0,
     )
     high, rest = split(packed)
     grouped = dot_nn(high, gather[...]) + dot_nn(rest, gather[...])
@@ -282,6 +293,7 @@
     row_sum = grouped[CHUNK : 2 * CHUNK]
     col_sum = grouped[2 * CHUNK : 3 * CHUNK]
     through_sum = grouped[3 * CHUNK : 3 * CHUNK + 1]
+    sums[7:8, channels : channels + LANES] += grouped[3 * CHUNK + HALO : 3 * CHUNK + HALO + 1]
     upper = tri((CHUNK, CHUNK), lambda r, c: c >= r).astype(F32)
     below = tri((CHUNK, CHUNK), lambda r, c: r > c).astype(F32)
     g_log = (
@@ -315,8 +327,8 @@
     return pl.BlockSpec(shape, lambda i: (0,) * len(shape))
 
 
-def mixer_forward(pre, tail, start, slab, spread, heads):
-    rows, width = pre.shape
+def mixer_forward(gate, rest, tail, start, slab, spread, heads):
+    rows, width = rest.shape
     state_size, channels = start.shape
     size = channels + 2 * LANES
     steps = rows // CHUNK
@@ -330,6 +342,7 @@
         body,
         grid=(steps,),
         in_specs=[
+            by_row(channels),
             by_row(width),
             fixed((HALO, size)),
             fixed(start.shape),
@@ -355,15 +368,17 @@
             pltpu.VMEM((CHUNK + HALO, size), F32),
         ],
         compiler_params=pltpu.CompilerParams(
-            dimension_semantics=("arbitrary",), vmem_limit_bytes=VMEM_LIMIT
+            dimension_semantics=("arbitrary",), vmem_limit_bytes=MIXER_VMEM
         ),
         cost_estimate=pl.CostEstimate(flops=1000, bytes_accessed=1000, transcendentals=0),
         name="mixer_forward",
-    )(pre, tail, start, slab, spread)
-
-
-def mixer_backward(q, kappa, pre, tail, y, entering, grad, e_rows, slab, spread, gather, heads):
-    rows, width = pre.shape
+    )(gate, rest, tail, start, slab, spread)
+
+
+def mixer_backward(
+    q, factor, gate, rest, tail, y, entering, grad, e_rows, slab, spread, gather, heads
+):
+    rows, width = rest.shape
     state_size, channels = grad.shape
     size = channels + 2 * LANES
     steps = rows // CHUNK
@@ -379,7 +394,8 @@
         grid=(steps,),
         in_specs=[
             by_row(channels),
-            by_row(1),
+            by_row(2),
+            by_row(channels),
             by_row(width),
             pl.BlockSpec(
                 (HALO, width), lambda i: (jnp.maximum((steps - 1 - i) * groups - 1, 0), 0)
@@ -393,9 +409,14 @@
             fixed(spread.shape),
             fixed(gather.shape),
         ],
-        out_specs=[by_row(width), fixed(grad.shape), fixed(e_rows.shape), fixed(slab.shape)],
+        out_specs=[
+            by_row(channels + width),
+            fixed(grad.shape),
+            fixed(e_rows.shape),
+            fixed(slab.shape),
+        ],
         out_shape=[
-            shape((rows, width), BF16),
+            shape((rows, channels + width), BF16),
             shape(grad.shape, F32),
             shape(e_rows.shape, F32),
             shape(slab.shape, F32),
@@ -406,11 +427,11 @@
             pltpu.VMEM((CHUNK + HALO, size), F32),
         ],
         compiler_params=pltpu.CompilerParams(
-            dimension_semantics=("arbitrary",), vmem_limit_bytes=VMEM_LIMIT
+            dimension_semantics=("arbitrary",), vmem_limit_bytes=BACK_VMEM
         ),
         cost_estimate=pl.CostEstimate(flops=1000, bytes_accessed=1000, transcendentals=0),
         name="mixer_backward",
-    )(q, kappa, pre, pre, tail, y, entering, grad, e_rows, slab, spread, gather)
+    )(q, factor, gate, rest, rest, tail, y, entering, grad, e_rows, slab, spread, gather)
 
 
 MESH = pl.DeviceIdType.MESH
@@ -441,32 +462,10 @@
     pl.semaphore_wait(barrier, 2 * DEEP + 1)
 
 
-def start_kernel(*refs, count, micros):
-    shards, (gain, own) = refs[:count], refs[count : count + 2]
-    outs = refs[count + 2 :]
-    wholes, (gains, normed) = outs[:count], outs[count : count + 2]
-    scratch = outs[count + 2 :]
-    local_sem, x_send, x_recv, up_send, up_recv, down_send, down_recv = scratch[:7]
-    gain_send, gain_recv, own_sem, y_send, y_recv, core_send, core_recv, rows_out = scratch[7:]
+def gather_steps(shards, wholes, sems, beside=None):
+    count = len(shards)
+    local_sem, x_send, x_recv, up_send, up_recv, down_send, down_recv = sems
     deep, side, device = place_in_line()
-    core, line, half = lax.axis_index("section"), lax.axis_index("fsdp"), lax.axis_index("tp")
-    lines = 2 * DEEP
-
-    greet_all()
-    across_tp, across_core = (core, line, 1 - half), (1 - core, line, half)
-
-    def send_gain(step):
-        return pltpu.make_async_remote_copy(
-            src_ref=gain,
-            dst_ref=gains.at[line],
-            send_sem=gain_send.at[step],
-            recv_sem=gain_recv.at[step],
-            device_id=(core, (line + step) % lines, half),
-            device_id_type=MESH,
-        )
-
-    for step in range(1, lines):
-        send_gain(step).start()
 
     def rows(i, z, x):
         size = shards[i].shape[0]
@@ -507,36 +506,8 @@
 
         across(i, deep, shards[i]).start()
 
-    gains[line] = gain[...]
-    for step in range(1, lines):
-        send_gain(step).wait()
-    gain_row = jnp.concatenate(
-        [gains[f, j : j + 1, :] for f in range(lines) for j in range(gain.shape[0] // 4)], axis=1
-    )
-    tokens = own.shape[0] // micros
-    h = own[...].astype(F32)
-    scale = lax.rsqrt(jnp.mean(h * h, axis=1, keepdims=True) + EPS)
-    rows_out[...] = (h * scale * gain_row).astype(BF16)
-
-    def token_copies(m):
-        source = rows_out.at[pl.ds(m * tokens, tokens)]
-        place = normed.at[m, half, core]
-        later = normed.at[m, 1 - half, core]
-        remote = functools.partial(pltpu.make_async_remote_copy, device_id_type=MESH)
-        return (
-            pltpu.make_async_copy(source, place, own_sem.at[m]),
-            remote(source, place, y_send.at[m], y_recv.at[m], device_id=across_tp),
-            remote(source, place, core_send.at[m], core_recv.at[m], device_id=across_core),
-            remote(later, later, core_send.at[micros + m], core_recv.at[micros + m], device_id=across_core),
-        )
-
-    for m in range(micros):
-        for copy in token_copies(m)[:3]:
-            copy.start()
-    for m in range(micros):
-        token_copies(m)[1].wait_recv()
-        token_copies(m)[3].start()
-
+    if beside is not None:
+        beside()
     for k in range(1, DEEP):
         for i in range(count):
 
@@ -589,15 +560,124 @@
             def _(i=i, k=k):
                 downward(i, k).wait_send()
 
-    for m in range(micros):
-        own_copy, y_copy, core_copy, core_later = token_copies(m)
+
+def start_kernel(*refs, count, micros, heads, gain_rows):
+    shards, (gain, own, cotangent) = refs[:count], refs[count : count + 3]
+    params, spread = refs[count + 3 : count + 9], refs[count + 9]
+    outs = refs[count + 10 :]
+    wholes, (gains, slabs), targets = outs[:count], outs[count : count + 2], outs[count + 2 :]
+    targets, scratch = targets[: 2 * micros], targets[2 * micros :]
+    gain_send, gain_recv, own_sem, y_send, y_recv, core_send, core_recv, rows_out = scratch[7:15]
+    other_slab, slab_send, slab_recv, line_send, line_recv = scratch[15:]
+    core, line, half = lax.axis_index("section"), lax.axis_index("fsdp"), lax.axis_index("tp")
+    lines = 2 * DEEP
+
+    greet_all()
+    across_tp, across_core = (core, line, 1 - half), (1 - core, line, half)
+
+    def send_gain(step):
+        return pltpu.make_async_remote_copy(
+            src_ref=gain,
+            dst_ref=gains.at[core, line],
+            send_sem=gain_send.at[step],
+            recv_sem=gain_recv.at[step],
+            device_id=(core, (line + step) % lines, half),
+            device_id_type=MESH,
+        )
+
+    for step in range(1, lines):
+        send_gain(step).start()
+
+    tokens = own.shape[0] // micros
+
+    def token_copies(n):
+        m, held = n % micros, (rows_out, cotangent)[n // micros]
+        source = held.at[pl.ds(m * tokens, tokens)]
+        place = targets[n].at[half, core]
+        later = targets[n].at[1 - half, core]
+        more = 2 * micros + n
+        remote = functools.partial(pltpu.make_async_remote_copy, device_id_type=MESH)
+        return (
+            pltpu.make_async_copy(source, place, own_sem.at[n]),
+            remote(source, place, y_send.at[n], y_recv.at[n], device_id=across_tp),
+            remote(source, place, core_send.at[n], core_recv.at[n], device_id=across_core),
+            remote(later, later, core_send.at[more], core_recv.at[more], device_id=across_core),
+        )
+
+    send_slab = pltpu.make_async_remote_copy(
+        src_ref=other_slab,
+        dst_ref=slabs.at[core],
+        send_sem=slab_send.at[0],
+        recv_sem=slab_recv.at[0],
+        device_id=across_core,
+        device_id_type=MESH,
+    )
+    send_line = pltpu.make_async_remote_copy(
+        src_ref=gains.at[core],
+        dst_ref=gains.at[core],
+        send_sem=line_send.at[0],
+        recv_sem=line_recv.at[0],
+        device_id=across_core,
+        device_id_type=MESH,
+    )
+
+    def write_slab(place, index):
+        taps, bias, shared_taps, shared_bias, gate, per_head = (v[...] for v in params)
+        channels = spread.shape[1]
+        first = index == 0
+        cut = lambda v: jnp.where(first, v[:, :channels], v[:, channels:])
+        lane = lax.broadcasted_iota(jnp.int32, per_head.shape, 1)
+        here = jnp.where(first, per_head, pltpu.roll(per_head, LANES - heads, 1))
+        here = jnp.where(lane < heads, here, 0.0)
+        skip = expand(here, spread[...], heads)
+        decay = jnp.where(lane < heads, -jnp.exp(here), 0.0)
+        place[...] = jnp.zeros(place.shape, F32)
+        place[0:CONV, :channels] = cut(taps)
+        place[0:CONV, channels:] = shared_taps
+        place[CONV : CONV + 1, :channels] = cut(bias)
+        place[CONV : CONV + 1, channels:] = shared_bias
+        place[5:6, :channels] = cut(gate)
+        place[5:6, channels : channels + LANES] = here[0:1]
+        place[6:7, :channels] = skip[2:3]
+        place[6:7, channels : channels + LANES] = decay[1:2]
+
+    def send_tokens():
+        write_slab(other_slab, 1 - core)
+        send_slab.start()
+        write_slab(slabs.at[core], core)
+        gains[core, line] = gain[...]
+        for step in range(1, lines):
+            send_gain(step).wait()
+        send_line.start()
+        send_line.wait()
+        gain_row = jnp.concatenate(
+            [gains[0, f, j : j + 1, :] for f in range(lines) for j in range(gain_rows)], axis=1
+        )
+        h = own[...].astype(F32)
+        scale = lax.rsqrt(jnp.mean(h * h, axis=1, keepdims=True) + EPS)
+        rows_out[...] = (h * scale * gain_row).astype(BF16)
+
+        for n in range(2 * micros):
+            for copy in token_copies(n)[:3]:
+                copy.start()
+        for n in range(micros):
+            token_copies(n)[1].wait_recv()
+            token_copies(n)[3].start()
+
+    gather_steps(shards, wholes, scratch[:7], send_tokens)
+    for n in range(micros, 2 * micros):
+        token_copies(n)[1].wait_recv()
+        token_copies(n)[3].start()
+    send_slab.wait()
+    for n in range(2 * micros):
+        own_copy, y_copy, core_copy, core_later = token_copies(n)
         own_copy.wait()
         y_copy.wait_send()
         core_copy.wait()
         core_later.wait()
 
 
-def start_gather(shards, gain, own, micros):
+def start_gather(shards, gain, own, cotangent, params, spread, micros, heads, gain_rows):
     count = len(shards)
     lines = 2 * DEEP
     pairs = pltpu.SemaphoreType.DMA((count, DEEP))
@@ -606,28 +686,32 @@
     anywhere = pl.BlockSpec(memory_space=pl.ANY)
     vmem = pl.BlockSpec(memory_space=pltpu.VMEM)
     rows, width = own.shape
-    sizes = sum(v.size for v in shards)
+    slab = (8, spread.shape[1] + params[2].shape[1])
     return pl.pallas_call(
-        functools.partial(start_kernel, count=count, micros=micros),
+        functools.partial(
+            start_kernel, count=count, micros=micros, heads=heads, gain_rows=gain_rows
+        ),
         out_shape=[shape((v.shape[0] * lines, v.shape[1]), v.dtype) for v in shards]
         + [
-            shape((lines,) + gain.shape, F32),
-            shape((micros, 2, 2, rows // micros, width), BF16),
-        ],
-        in_specs=[anywhere] * count + [vmem] * 2,
-        out_specs=[anywhere] * count + [vmem, anywhere],
+            shape((2, lines) + gain.shape, F32),
+            shape((2,) + slab, F32),
+        ]
+        + [shape((2, 2, rows // micros, width), BF16)] * (2 * micros),
+        in_specs=[anywhere] * count + [vmem, vmem, anywhere] + [vmem] * 7,
+        out_specs=[anywhere] * count + [vmem, vmem] + [anywhere] * (2 * micros),
         scratch_shapes=[dma(count)]
         + [pairs] * 6
         + [dma(lines)] * 2
-        + [dma(micros)] * 3
-        + [dma(2 * micros)] * 2
-        + [pltpu.VMEM(own.shape, BF16)],
+        + [dma(2 * micros)] * 3
+        + [dma(4 * micros)] * 2
+        + [pltpu.VMEM(own.shape, BF16), pltpu.VMEM(slab, F32)]
+        + [dma(1)] * 4,
         compiler_params=pltpu.CompilerParams(
             collective_id=1, has_side_effects=True, vmem_limit_bytes=VMEM_LIMIT
         ),
-        cost_estimate=pl.CostEstimate(flops=1000, bytes_accessed=1000, transcendentals=0),
+        cost_estimate=pl.CostEstimate(flops=170_000_000_000, bytes_accessed=1000, transcendentals=0),
         name="start_gather",
-    )(*shards, gain, own)
+    )(*shards, gain, own, cotangent, *params, spread)
 
 
 def add_rows(out, *parts):
@@ -650,13 +734,14 @@
 
 def reduce_kernel(*refs, count):
     parts, small, results = refs[:count], refs[count], refs[count + 1 : 2 * count + 1]
-    own_small, next_small, both_small = refs[2 * count + 1 : 2 * count + 4]
-    scratch = refs[2 * count + 4 :]
+    others = refs[2 * count + 1 : 3 * count + 1]
+    own_small, next_small, both_small = refs[3 * count + 1 : 3 * count + 4]
+    scratch = refs[3 * count + 4 :]
     held, crossed, from_below, from_above = (
         scratch[n * count : (n + 1) * count] for n in range(4)
     )
-    load_sem, x_send, x_recv, up_send, up_recv, down_send, down_recv = scratch[4 * count : -3]
-    small_buffer, small_send, small_recv = scratch[-3:]
+    load_sem, x_send, x_recv, up_send, up_recv, down_send, down_recv = scratch[4 * count : -5]
+    small_buffer, small_send, small_recv, other_send, other_recv = scratch[-5:]
     deep, side, device = place_in_line()
     core, line, half = lax.axis_index("section"), lax.axis_index("fsdp"), lax.axis_index("tp")
     greet_all()
@@ -689,16 +774,16 @@
             value = small[...] if n == 0 else small_buffer[n - 1]
             small_buffer[n] = value + small_buffer[3 + n]
         over_tp = swap_small(3, small_buffer.at[2], small_buffer.at[6])
-        over_core = swap_small(4, small_buffer.at[2], next_small)
+        over_core = swap_small(4, small_buffer.at[2, 1 - core], next_small)
         over_tp.start()
         over_core.start()
-        own_small[...] = small_buffer[2]
+        own_small[...] = small_buffer[2, core]
         over_tp.wait()
         small_buffer[7] = small_buffer[2] + small_buffer[6]
-        last = swap_small(5, small_buffer.at[7], small_buffer.at[8])
+        last = swap_small(5, small_buffer.at[7, 1 - core], small_buffer.at[8, 0])
         last.start()
         last.wait()
-        both_small[...] = small_buffer[7] + small_buffer[8]
+        both_small[...] = small_buffer[7, core] + small_buffer[8, 0]
         over_core.wait()
 
     def rows(i, z, x):
@@ -735,6 +820,16 @@
             send_sem=down_send.at[i, k - 1],
             recv_sem=down_recv.at[i, k - 1],
             device_id=device(max(here - 1, 0), side),
+            device_id_type=MESH,
+        )
+
+    def to_other(i):
+        return pltpu.make_async_remote_copy(
+            src_ref=results[i],
+            dst_ref=others[i],
+            send_sem=other_send.at[i],
+            recv_sem=other_recv.at[i],
+            device_id=across_core,
             device_id_type=MESH,
         )
 
@@ -801,6 +896,9 @@
                 downward(i, DEEP - 1, here, here).wait_recv()
                 terms.append(from_above[i].at[DEEP - 2])
             add_rows(results[i], *terms)
+            to_other(i).start()
+        for i in range(count):
+            to_other(i).wait()
         for copy in started:
             copy.wait_send()
         for z in range(DEEP):
@@ -824,9 +922,9 @@
     vmem = pl.BlockSpec(memory_space=pltpu.VMEM)
     return pl.pallas_call(
         functools.partial(reduce_kernel, count=count),
-        out_shape=[shape(shard, F32) for shard in shards] + [shape(small.shape, F32)] * 3,
+        out_shape=[shape(shard, F32) for shard in shards] * 2 + [shape(small.shape[1:], F32)] * 3,
         in_specs=[pl.BlockSpec(memory_space=pl.ANY)] * count + [vmem],
-        out_specs=[vmem] * (count + 3),
+        out_specs=[vmem] * (2 * count + 3),
         scratch_shapes=blocks(DEEP)
         + blocks(DEEP)
         + blocks(DEEP - 1)
@@ -836,6 +934,8 @@
             pltpu.VMEM((9,) + small.shape, F32),
             pltpu.SemaphoreType.DMA((6,)),
             pltpu.SemaphoreType.DMA((6,)),
+            pltpu.SemaphoreType.DMA((count,)),
+            pltpu.SemaphoreType.DMA((count,)),
         ],
         compiler_params=pltpu.CompilerParams(
             collective_id=collective_id, has_side_effects=True, vmem_limit_bytes=VMEM_LIMIT
@@ -876,18 +976,18 @@
     return lax.optimization_barrier((value,) + others)[0] if others else value
 
 
-def over_cores(part, core):
+def over_cores(part, core, *beside):
     split_rows = part.reshape((2, 2, part.shape[0] // 4) + part.shape[1:])
     mine = lax.dynamic_index_in_dim(split_rows, core, 1, keepdims=False)
     theirs = lax.dynamic_index_in_dim(split_rows, 1 - core, 1, keepdims=False)
-    return mine + swap_core(theirs)
+    return mine.astype(F32) + after(swap_core(theirs), *beside).astype(F32)
 
 
 class Sum:
-    def __init__(self, part, core, half):
+    def __init__(self, part, core, half, needed=(), beside=()):
         self.half = half
-        self.total = over_cores(part, core)
-        sent = pick(self.total, 1 - half)
+        self.total = over_cores(part, core, *beside)
+        sent = after(pick(self.total, 1 - half), *needed)
         self.sent = sent.astype(BF16) if part.ndim > 1 else sent
 
     def done(self, *beside):
@@ -948,115 +1048,131 @@
             ]
         )
 
+    lane = np.arange(LANES)
+    head_of = np.arange(channels) // width
+    spread = (lane[:, None] % heads == head_of[None, :]) & (lane[:, None] < 2 * heads)
+    spread = jnp.asarray(spread.astype(np.float32), BF16)
+    gather = jnp.asarray((head_of[:, None] == lane[None, :]).astype(np.float32), BF16)
+
     own_shard = weight_shard(core)
     got_shard = swap_core(weight_shard(1 - core))
-    own_slab = slab_of(core)
-    got_slab = swap_core(slab_of(1 - core))
     in_line = lax.axis_size("fsdp") == 2 * DEEP and lax.axis_size("tp") == 2
     over_fsdp = functools.partial(lax.all_gather, axis_name="fsdp", tiled=True)
-    slabs = [jnp.where(core == layer, own_slab, got_slab) for layer in range(2)]
     shards = []
     for layer in range(2):
         shard = jnp.where(core == layer, own_shard, got_shard)
         shards.append((shard[:, :in_width], shard[:, in_width:]))
-    gain_pair = by_index(core, norm_gain[0], swap_core(norm_gain[0])).astype(F32)
 
     def own_rows(tensor):
         return [
             lax.dynamic_slice_in_dim(tensor[0, m], core * rows, rows, 0) for m in range(micros)
         ]
 
-    first = own_rows(inputs)
+    first, cotangents = own_rows(inputs), own_rows(cotangent)
     if in_line:
-        packed = jnp.pad(gain_pair.reshape(-1, LANES), ((0, 8 - 2 * depth // LANES), (0, 0)))
-        w_in, w_back, gains, first_normed = start_gather(
-            shards[0], packed, jnp.concatenate(first), micros
-        )
+        gain_rows = depth // LANES
+        packed = jnp.pad(norm_gain.astype(F32).reshape(-1, LANES), ((0, 8 - gain_rows), (0, 0)))
+        per_head = jnp.concatenate([dt_bias, a_log, d_skip])
+        per_head = jnp.pad(per_head, ((0, 5), (0, LANES - per_head.shape[1])))
+        params = (conv_x[0], conv_xb, conv_bc[0], conv_bcb, gate_gain, per_head)
+        w_in, w_back, gains, slabs, *tokens = start_gather(
+            shards[0],
+            packed,
+            jnp.concatenate(first),
+            jnp.concatenate(cotangents),
+            params,
+            spread,
+            micros,
+            heads,
+            gain_rows,
+        )
+        slabs = [slabs[0], slabs[1]]
         projections = [(w_in, w_back)]
-        shards[1] = lax.optimization_barrier(shards[1] + (gains,))[:2]
-        gains = jnp.moveaxis(
-            gains[:, : 2 * depth // LANES].reshape(2 * DEEP, 2, depth), 0, 1
-        ).reshape(2, -1)
-        first_normed = first_normed.reshape(micros, 4 * rows, -1)
+        early = 8 * LANES
+        parts = [over_fsdp(shards[1][0][:, :early], axis=0)]
+        parts.append(over_fsdp(after(shards[1][0][:, early:], gains), axis=0))
+        projections.append((parts, over_fsdp(after(shards[1][1], gains), axis=0)))
+        gains = gains[:, :, :gain_rows].reshape(2, -1)
+        tokens = [v.reshape(4 * rows, -1) for v in tokens]
+        first_normed, everyones = tokens[:micros], tokens[micros:]
+        first_normed[0] = after(first_normed[0], parts[0])
     else:
+        own_slab, got_slab = slab_of(core), swap_core(slab_of(1 - core))
+        slabs = [jnp.where(core == layer, own_slab, got_slab) for layer in range(2)]
+        gain_pair = by_index(core, norm_gain[0], swap_core(norm_gain[0])).astype(F32)
         projections = [tuple(over_fsdp(v, axis=0) for v in shards[0])]
         gains = over_fsdp(gain_pair.astype(BF16), axis=1).astype(F32)
         first_normed = None
-    projections.append(tuple(over_fsdp(v, axis=0) for v in shards[1]))
-
-    lane = jnp.arange(LANES)
-    head_of = jnp.arange(channels) // width
-    spread = ((lane[:, None] % heads == head_of[None, :]) & (lane[:, None] < 2 * heads)).astype(BF16)
-    gather = (head_of[:, None] == lane[None, :]).astype(BF16)
+        everyones = [gather_tokens(v, core, half) for v in cotangents]
+    if not in_line:
+        projections.append(tuple(over_fsdp(v, axis=0) for v in shards[1]))
 
     size = channels + shared
     zero_state = jnp.zeros((shared // 2, channels), F32)
     zero_halo = jnp.zeros((HALO, size), F32)
     last = micros - 1
 
+    def scale_of(h):
+        return lax.rsqrt(jnp.mean(h * h, axis=1, keepdims=True) + EPS)
+
     def norm(h, layer):
-        scale = lax.rsqrt(jnp.mean(h * h, axis=1, keepdims=True) + EPS)
-        return scale, (h * scale * gains[layer][None]).astype(BF16)
+        return (h * scale_of(h) * gains[layer][None]).astype(BF16)
 
     hidden = [v.astype(F32) for v in first]
-    cotangents = own_rows(cotangent)
     normed = [None] * micros
-    scales = [[None] * micros for _ in range(2)]
     for m in range(micros):
-        scales[0][m], own = norm(hidden[m], 0)
-        normed[m] = first_normed[m] if in_line else gather_tokens(own, core, half)
+        normed[m] = (
+            first_normed[m] if in_line else gather_tokens(norm(hidden[m], 0), core, half)
+        )
 
     hiddens, normeds, kept = [hidden, None], [normed, None], [[None] * micros for _ in range(2)]
     waiting = None
 
     def finish(pending, *beside):
-        layer, m, part, squares = pending
+        m, part, squares = pending
         r = lax.rsqrt(squares.done(*beside) / DI + EPS)[:, None]
         branch = r * part.done(*beside)
-        kept[layer][m].update(r=r, branch=branch)
-        h = hiddens[layer][m] + branch
-        if layer == 0:
-            hiddens[1][m] = h
-            scales[1][m], own = norm(h, 1)
-            return own
-        results[m] = h
-        g = cotangents[m].astype(F32)
-        return jnp.concatenate([r, r * r * jnp.sum(g * branch, axis=1, keepdims=True) / DI], axis=1)
+        kept[0][m].update(r=r, branch=branch)
+        h = hiddens[0][m] + branch
+        hiddens[1][m] = h
+        return norm(h, 1)
 
     def spread_out(pending, own, *beside):
-        layer, m = pending[:2]
-        if layer == 0:
-            normeds[1][m] = gather_tokens(own, core, half, beside)
-        else:
-            factors[m] = gather_tokens(own, core, half, beside)
-
-    results, factors = [None] * micros, [None] * micros
+        normeds[1][pending[0]] = gather_tokens(own, core, half, beside)
+
     hiddens[1], normeds[1] = [None] * micros, [None] * micros
-    everyones = [gather_tokens(v, core, half) for v in cotangents]
     for layer in range(2):
         w_in, w_back = projections[layer]
         state, tail = zero_state, zero_halo
         for m in range(micros):
             tokens = normeds[layer][m]
-            if layer == 1 and m == 0:
-                tokens = after(tokens, *everyones)
-            if waiting is not None:
-                tokens = after(tokens, waiting[2].sent, waiting[3].sent)
-            pre = dot_nn(tokens, w_in)
-            mixed_pre = pre
-            if waiting is not None:
-                own = finish(waiting, pre)
-                mixed_pre = after(pre, own)
+            if layer == 0 or not in_line:
+                w_pair = (w_in[:, :channels], w_in[:, channels:])
+            else:
+                w_pair = w_in
+            gate = dot_nn(tokens, w_pair[0])
+            if waiting is not None and layer == 1:
+                tokens = after(tokens, waiting[1].sent, waiting[2].sent)
+            rest = dot_nn(tokens, w_pair[1])
+            mixed_rest = rest
+            if waiting is not None and layer == 1:
+                own = finish(waiting, rest)
+                mixed_rest = after(rest, own)
+            elif waiting is not None:
+                mixed_rest = after(rest, waiting[1].sent, waiting[2].sent)
             u, squares, y, entering, state_out = mixer_forward(
-                mixed_pre, tail, state, slabs[layer], spread, heads
+                gate, mixed_rest, tail, state, slabs[layer], spread, heads
             )
             if waiting is not None:
-                spread_out(waiting, own, u)
-            kept[layer][m] = dict(pre=pre, tail=tail, u=u, y=y, entering=entering)
-            state, tail = state_out, pre[-HALO:, channels : channels + size]
-            part = Sum(dot_nt(u, w_back), core, half)
-            waiting = (layer, m, part, Sum(squares[:, 0], core, half))
-    spread_out(waiting, finish(waiting))
+                spread_out(waiting, own if layer == 1 else finish(waiting, u), u)
+            kept[layer][m] = dict(
+                gate=gate, rest=rest, tail=tail, u=u, y=y, entering=entering, squares=squares
+            )
+            state, tail = state_out, rest[-HALO:, :size]
+            waiting = None
+            if layer == 0:
+                part = Sum(dot_nt(u, w_back).astype(BF16), core, half)
+                waiting = (m, part, Sum(squares[:, 0], core, half))
 
     over_tokens = (((0,), (0,)), ((), ()))
 
@@ -1067,18 +1183,29 @@
 
     reduced, small = [None, None], [None, None]
     grads = [v.astype(F32) for v in cotangents]
-    backs = [
-        (everyone.astype(F32) * factor[:, :1]).astype(BF16)
-        for everyone, factor in zip(everyones, factors)
-    ]
-    kappas = [factor[:, 1:] for factor in factors]
+    w_back = after(projections[1][1], *[kept[1][m]["u"] for m in range(micros)])
+    w_in = projections[1][0]
+    if in_line:
+        w_in = jnp.concatenate([after(v, *[kept[1][m]["u"] for m in range(micros)]) for v in w_in], axis=1)
+    projections[1] = (w_in, w_back)
+    backs, products, factors = list(everyones), [None] * micros, [None] * micros
+    pairs = [None] * micros
+    for m in reversed(range(micros)):
+        k = kept[1][m]
+        products[m] = dot_nn(backs[m], w_back)
+        dots = jnp.sum(products[m] * k["u"].astype(F32), axis=1)
+        pairs[m] = jnp.stack([k["squares"][:, 0], dots])
+    pair = jnp.stack(pairs)
+    pair = pair + swap_core(pair)
+    pair = pair + swap_tp(pair)
+    r = lax.rsqrt(pair[:, 0] / DI + EPS)
+    factors = [jnp.stack([r[m], r[m] * r[m] * r[m] * pair[m, 1] / DI], axis=1) for m in range(micros)]
     gain_parts = [[], []]
-    next_backs, next_kappas = [None] * micros, [None] * micros
-    waiting = None
 
     def finish_back(pending, *beside):
         layer, m, part = pending
-        h, scale = hiddens[layer][m], scales[layer][m]
+        h = hiddens[layer][m]
+        scale = scale_of(h)
         g_norm = part.done(*beside)
         gain_parts[layer].append(jnp.sum(g_norm * (h * scale), axis=0))
         g_norm = g_norm * gains[layer][None]
@@ -1086,20 +1213,22 @@
         g = grads[m] + scale * g_norm - h * (scale * scale * scale) * mean
         grads[m] = g
         if layer == 0:
-            return g, g
+            return (g,)
         r, branch = kept[0][m]["r"], kept[0][m]["branch"]
-        return (g * r).astype(BF16), r * r * jnp.sum(g * branch, axis=1)[:, None] / DI
+        kappa = r * r * jnp.sum(g * branch, axis=1)[:, None] / DI
+        return g.astype(BF16), jnp.concatenate([r, kappa], axis=1)
 
     def spread_back(pending, own, *beside):
         layer, m = pending[:2]
         if layer == 1:
             next_backs[m] = gather_tokens(own[0], core, half, beside)
-            next_kappas[m] = gather_tokens(own[1], core, half, beside)
+            next_factors[m] = gather_tokens(own[1], core, half, beside)
 
     def reduce_rows(part):
-        return lax.psum_scatter(part, "fsdp", scatter_dimension=0, tiled=True).astype(F32)
-
-    previous = ()
+        return lax.psum_scatter(part, "fsdp", scatter_dimension=0, tiled=True)
+
+    waiting, spreading, outs = None, None, [None] * micros
+    next_backs, next_factors = [None] * micros, [None] * micros
     for layer in (1, 0):
         w_in, w_back = projections[layer]
         state, e_rows = zero_state, zero_halo
@@ -1107,20 +1236,22 @@
         gpres = [None] * micros
         for m in reversed(range(micros)):
             k = kept[layer][m]
-            back = backs[m]
-            if waiting is not None and waiting[0] == layer:
-                back = after(back, waiting[2].sent)
-            q = dot_nn(back, w_back)
-            if m == last:
-                if layer == 1:
-                    grad_back = weight_grad(backs, [kept[layer][j]["u"] for j in range(micros)])
-                    q = after(q, grad_back)
-                    reduced_back = reduce_rows(grad_back)
-                    previous = (reduced_back,)
+            q = products[m] if layer == 1 else dot_nn(backs[m], w_back)
+            if m == last and layer == 1:
+                mixed = [
+                    (kept[1][j]["u"].astype(F32) * factors[j][:, :1]).astype(BF16)
+                    for j in range(micros)
+                ]
+                reduced_back = weight_grad(backs, mixed)
+                q = after(q, reduced_back)
+                reduced_back = reduce_rows(reduced_back)
+            if waiting is not None:
+                q = after(q, waiting[2].sent)
             gpre, state, e_rows, sums = mixer_backward(
                 q,
-                kappas[m],
-                k["pre"],
+                factors[m],
+                k["gate"],
+                k["rest"],
                 k["tail"],
                 k["y"],
                 k["entering"],
@@ -1133,76 +1264,100 @@
             )
             totals = totals + sums
             gpres[m] = gpre
-            if waiting is not None and waiting[0] != layer:
-                spread_back(waiting, own, gpre)
-                backs[waiting[1]], kappas[waiting[1]] = next_backs[waiting[1]], next_kappas[waiting[1]]
-                waiting = None
+            if spreading is not None:
+                spread_back(*spreading, gpre)
+                j = spreading[0][1]
+                backs[j], factors[j] = next_backs[j], next_factors[j]
+                spreading = None
             ready = gpre
+            earlier = None
             if waiting is not None:
                 own = finish_back(waiting, gpre)
                 ready = after(gpre, *own)
-            part = Sum(dot_nt(ready, w_in), core, half)
-            if waiting is not None:
-                spread_back(waiting, own, part.total)
-            waiting = (layer, m, part)
+                earlier = (waiting, own)
+            part = dot_nt(ready, w_in).astype(BF16)
+            beside = ()
+            if layer == 1:
+                outs[m] = dot_nt(after(k["u"], part), w_back).astype(BF16)
+                beside = (outs[m],)
+            waiting = (layer, m, Sum(part, core, half, (), beside))
         grad_in = weight_grad(normeds[layer], [after(v, waiting[2].sent) for v in gpres])
+        if layer == 1 or not in_line:
+            reduced[layer] = (reduce_rows(grad_in), reduced_back)
         if layer == 0:
-            grad_back = weight_grad(backs, [kept[layer][j]["u"] for j in range(micros)])
+            mixed = [
+                (kept[0][j]["u"].astype(F32) * factors[j][:, :1]).astype(BF16) for j in range(micros)
+            ]
+            grad_back = weight_grad(backs, mixed)
+            if not in_line:
+                reduced[0] = (reduced[0][0], reduce_rows(grad_back))
+            outs = [Sum(out, core, half, (gpres[0],)) for out in outs]
+        if earlier is not None:
+            spread_back(*earlier, grad_in)
         own = finish_back(waiting, grad_in)
-        small[layer] = jnp.concatenate([totals.reshape(-1), sum(gain_parts[layer])])
-        if layer == 1 or not in_line:
-            if layer == 0:
-                reduced_back = reduce_rows(grad_back)
-            reduced[layer] = (reduce_rows(after(grad_in, *previous)), reduced_back)
-        backs = [after(v, *own) if v is not None else None for v in next_backs]
-        kappas = list(next_kappas)
+        if layer == 1:
+            spreading = (waiting, own)
+            second_factors = factors
+            backs = [None if v is None else after(v, *own) for v in next_backs]
+            factors = list(next_factors)
+        waiting = None
+        small[layer] = jnp.concatenate(
+            [
+                totals[:6],
+                jnp.concatenate(
+                    [sum(gain_parts[layer]).reshape(2, -1), totals[6:, channels:]], axis=1
+                ),
+            ]
+        )
+
+    outputs_rows = []
+    for m in range(micros):
+        r = lax.dynamic_slice_in_dim(second_factors[m], (2 * half + core) * rows, rows, 0)[:, :1]
+        outputs_rows.append(hiddens[1][m] + r * outs[m].done(grad_in))
 
     def placed_rows(parts):
         own = jnp.where(core == 0, parts[0], parts[1])
         other = jnp.where(core == 0, parts[1], parts[0])
         return by_index(core, own, swap_core(other)).reshape(1, 1, 2 * rows, -1)
 
-    outputs, input_grads = placed_rows(results), placed_rows(grads)
-
-    small_sums = jnp.stack(small)
+    outputs, input_grads = placed_rows(outputs_rows), placed_rows(grads)
+
+    small_sums = after(jnp.stack(small), outputs, input_grads)
     if in_line:
-        flat = small_sums.reshape(-1, LANES)
-        *reduced[0], own_small, next_small, both_small = reduce_line(
-            [grad_in, grad_back], flat, "grads_reduce", 2
-        )
-        own_small, next_small, both_small = (
-            pick(v.reshape(small_sums.shape), core) for v in (own_small, next_small, both_small)
-        )
+        *both_parts, own_small, next_small, both_small = reduce_line(
+            [grad_in, grad_back], small_sums, "grads_reduce", 2
+        )
+        first_own, first_other = both_parts[:2], both_parts[2:]
     else:
         small_sums = lax.psum(small_sums, "fsdp")
         own_small = pick(small_sums, core)
         next_small = swap_core(pick(small_sums, 1 - core))
         both_small = own_small + next_small
         both_small = both_small + swap_tp(both_small)
-    count = slabs[0].size
-    halves = by_index(core, own_small[:count], next_small[:count]).reshape((2,) + slabs[0].shape)
-    conv_sum = both_small[:count].reshape(slabs[0].shape)[:5, channels:]
+        first_own, first_other = reduced[0], [swap_core(v) for v in reduced[0]]
+    low_small = jnp.where(core == 0, own_small, next_small)
+    high_small = jnp.where(core == 0, next_small, own_small)
+    wide = jnp.concatenate([low_small[:6, :channels], high_small[:6, :channels]], axis=1)
+    narrow = jnp.concatenate(
+        [v[5:, channels : channels + heads] for v in (low_small, high_small)], axis=1
+    )
+    conv_sum = both_small[:5, channels:]
     gain_sum = lax.dynamic_slice_in_dim(
-        both_small[count:], lax.axis_index("fsdp") * depth, depth, 0
+        both_small[6:8, :channels].reshape(-1), lax.axis_index("fsdp") * depth, depth, 0
     )
-    wide = jnp.concatenate([halves[0, :7, :channels], halves[1, :7, :channels]], axis=1)
-    narrow = jnp.concatenate(
-        [halves[j, 5:7, channels : channels + heads] for j in range(2)], axis=1
-    )
-    skip_sum = wide[6].reshape(2 * heads, width).sum(axis=1)
-
-    mine = [jnp.where(core == 0, reduced[0][i], reduced[1][i]) for i in range(2)]
-    theirs = [jnp.where(core == 0, reduced[1][i], reduced[0][i]) for i in range(2)]
-    got = [swap_core(v) for v in theirs]
-    first_half = [jnp.where(core == 0, own, other) for own, other in zip(mine, got)]
-    second_half = [jnp.where(core == 0, other, own) for own, other in zip(mine, got)]
+
+    second_own = [after(v, own_small) for v in reduced[1]]
+    second_other = [swap_core(v) for v in second_own]
+    either = lambda one, two: jnp.where(core == 0, one.astype(F32), two.astype(F32))
+    low_half = [either(first_own[i], second_other[i]) for i in range(2)]
+    high_half = [either(first_other[i], second_own[i]) for i in range(2)]
 
     def joined(begin, end, i=0):
-        return jnp.concatenate([first_half[i][:, begin:end], second_half[i][:, begin:end]], axis=1)
+        return jnp.concatenate([low_half[i][:, begin:end], high_half[i][:, begin:end]], axis=1)
 
     g_zx = jnp.stack([joined(0, channels), joined(channels, 2 * channels)], axis=1)
     at = 2 * channels
-    g_bc = mine[0][:, at : at + shared] + got[0][:, at : at + shared]
+    g_bc = low_half[0][:, at : at + shared] + high_half[0][:, at : at + shared]
     g_bc = g_bc + swap_tp(g_bc)
     g_dt = joined(at + shared, at + shared + heads)
     g_back = joined(0, channels, 1)
@@ -1220,7 +1375,7 @@
         conv_sum[4][None],
         narrow[0][None],
         narrow[1][None],
-        skip_sum[None],
+        narrow[2][None],
         wide[5][None],
         g_back[None],
     )

time: 1020 us -> 883 us (0.87)
  waiting for transfers between devices: 150 us -> 57.4 us
  matrix products: 159 us -> 136 us
  other arithmetic: 84.2 us -> 68.5 us
  local copies, waits for them, and re-layouts: 99.2 us -> 85.8 us
  Pallas kernels: 463 us -> 476 us
    all_gather x2 -> x3, waiting for transfers between devices: 94.2 us -> 41.9 us  [the longest x1 21.3 us: local(): parts.append(over_fsdp(after(shards[1][0][:, early:], gains), axis=0))]
    pallas_call x1, Pallas kernels: 159 us -> 193 us  [start_gather(): pl.pallas_call(functools.partial(start_kernel, count=count, micros=micros...]
    ppermute x23 -> x18, waiting for transfers between devices: 43.8 us -> 10.3 us  [swap_tp(): return lax.ppermute(value, 'tp', SWAP)]
    unnamed x219 -> x360, local copies, waits for them, and re-layouts: 37 us -> 53.1 us
    dot_general x8 -> x12, matrix products: 64 us -> 48.6 us  [dot_nn(): lax.dot_general(a, b, (((1,), (0,)), ((), ())), preferred_element_type=F32)]
    pallas_call x8, Pallas kernels: 129 us -> 114 us  [the longest x4 76.8 us: mixer_backward(): pl.pallas_call(body, grid=(steps,), in_specs=[by_row(channels), by_row(2)...]
    another operation x35 -> x22, other arithmetic: 22.8 us -> 16.3 us  [by_index(): jnp.stack([jnp.where(first, own, other), jnp.where(first, other, own)])]
    ppermute x29 -> x22, starting transfers between devices: 21.6 us -> 16.7 us  [swap_core(): return lax.ppermute(value, 'section', SWAP)]
  transfers between devices with their start and end apart: 56 -> 45, of which waited for: 17 -> 11; matrix products, arithmetic and copies ran while one was open for 26% -> 25% of each run, Pallas kernels for 27% -> 55%
where the time goes in v3:
time: 883 us; the launch traced here: 872 us
  Pallas kernels  476 us (54%)
  matrix products  136 us (15%)
  local copies, waits for them, and re-layouts  85.8 us (10%)
  other arithmetic  68.5 us (8%)
  waiting for transfers between devices  57.4 us (7%)
  starting transfers between devices  31.6 us (4%)
  between operations  16.5 us (2%)
    pallas_call x1, Pallas kernels, start_gather(): pl.pallas_call(functools.partial(start_kernel, count=count, micros=micros...  193 us
    pallas_call x1, Pallas kernels, reduce_line(): pl.pallas_call(functools.partial(reduce_kernel, count=count), out_shape=[...  169 us
    pallas_call x4, Pallas kernels, mixer_backward(): pl.pallas_call(body, grid=(steps,), in_specs=[by_row(channels), by_row(2)...  76.8 us
    unnamed x360, local copies, waits for them, and re-layouts  53.1 us
    dot_general x12, matrix products, dot_nn(): lax.dot_general(a, b, (((1,), (0,)), ((), ())), preferred_element_type=F32)  48.6 us
    dot_general x8, matrix products, dot_nt(): lax.dot_general(a, b, (((1,), (1,)), ((), ())), preferred_element_type=F32)  44.2 us
    dot_general x4, matrix products, weight_grad(): lax.dot_general(jnp.concatenate(left), jnp.concatenate(right), over_token...  43.4 us
    pallas_call x4, Pallas kernels, mixer_forward(): pl.pallas_call(body, grid=(steps,), in_specs=[by_row(channels), by_row(wi...  36.9 us
  transfers between devices with their start and end apart: 45, of which 11 were waited for; matrix products, arithmetic and copies ran while one was open for 25% of the time, Pallas kernels for 55%

profile of v3, /device:TPU:9, one launch (start us, length us, event | category | flops | bytes accessed | tf_op | source)
XLA Modules:
  0.0 871.6 jit_solution(10828718285470492183)
XLA Ops:
  27.7 193.4 %start_gather.1 = (bf16[2048,2432]{1,0:T(8,128)(2,1)}, bf16[2048,1024]{1,0:T(8,128)(2,1)}, f32[2,8,8,128]{3,2,1,0:T(8,128)}, f32[2,8,1280]{2,1,0:T(8,128)}, bf16...) custom-call(bf16[256,2432]{1,0:T(8,128)(2,1)} %slice.229.refs_0_, ...), custom_call_target="tpu_custom_call" | custom-call | flops 170000007168 | bytes 1000 | tf_op jit(solution)/shard_map/start_gather/pallas_call | solution.py:690
  221.1 2.2 slice.233
  223.5 4.7 fusion.32.refs_0_.refs_2_
  229.2 3.4 fusion.2.refs_1_.refs_3_.refs_4_
  232.8 8.9 %mixer_forward.4 = (bf16[512,1024]{1,0:T(8,128)(2,1)S(1)}, f32[512,1]{1,0:T(8,128)S(1)}, f32[512,1024]{1,0:T(8,128)S(1)}, f32[4,128,1024]{2,1,0:T(8,128)S(1)}, f32[128,1024]{1,0:T(8,128)S(1)}) custom-call(f32[512,1024]{1,0:T(8,128)S(1)} %fusion.32.refs_0_.refs_2_, f32[512,1408]{1,0:T(8,128)S(1)} %fusion.2.refs_1_.refs_3_.refs_4_, ...), custom_call_target="tpu_custom_call" | custom-call | flops 1000 | bytes 1000 | tf_op jit(solution)/shard_map/mixer_forward/pallas_call | solution.py:341
  243.2 2.4 convolution_convert_fusion.5
  248.4 5.0 fusion.refs_1_.refs_3_.refs_4_
  254.7 5.3 fusion.30.refs_0_.refs_2_
  260.1 2.4 convert_add_fusion.7
  265.5 9.5 %mixer_forward.5 = (bf16[512,1024]{1,0:T(8,128)(2,1)S(1)}, f32[512,1]{1,0:T(8,128)S(1)}, f32[512,1024]{1,0:T(8,128)S(1)}, f32[4,128,1024]{2,1,0:T(8,128)S(1)}, f32[128,1024]{1,0:T(8,128)}) custom-call(f32[512,1024]{1,0:T(8,128)S(1)} %fusion.30.refs_0_.refs_2_, f32[512,1408]{1,0:T(8,128)S(1)} %copy-done.2, f32[8,1280]{1,0:T(8,128)S(1)} %slice.232.refs_2_.refs_5_, ...), custom_call_target="tpu_custom_call" | custom-call | flops 1000 | bytes 1000 | tf_op jit(solution)/shard_map/mixer_forward/pallas_call | solution.py:341
  279.7 2.4 convolution_convert_fusion.4
  284.2 5.3 collective-permute-done.5
  302.6 21.3 %all-gather.6.cloned.1.call-done = bf16[2048,1408]{1,0:T(8,128)(2,1)} async-done(((bf16[256,1408]{1,0:T(8,128)(2,1)}), bf16[2048,1408]{1,0:T(8,128)(2,1)}) %all-gather.6.cloned.1.call-update) | async-done | bytes 5767184 | tf_op jit(solution)/shard_map/all_gather | solution.py:1093
  323.9 7.0 fusion.110.refs_1_.refs_3_.refs_4_
  334.9 2.4 fusion.109.refs_0_.refs_2_
  337.3 8.7 %mixer_forward.6 = (bf16[512,1024]{1,0:T(8,128)(2,1)S(1)}, f32[512,1]{1,0:T(8,128)S(1)}, f32[512,1024]{1,0:T(8,128)S(1)}, f32[4,128,1024]{2,1,0:T(8,128)S(1)}, f32[128,1024]{1,0:T(8,128)S(1)}) custom-call(f32[512,1024]{1,0:T(8,128)S(1)} %fusion.109.refs_0_.refs_2_, f32[512,1408]{1,0:T(8,128)S(1)} %fusion.110.refs_1_.refs_3_.refs_4_, ...), custom_call_target="tpu_custom_call" | custom-call | flops 1000 | bytes 1000 | tf_op jit(solution)/shard_map/mixer_forward/pallas_call | solution.py:341
  356.6 2.6 copy-done.103
  359.2 2.4 fusion.111.refs_0_.refs_2_
  361.6 3.4 fusion.112.refs_1_.refs_3_.refs_4_
  365.1 9.7 %mixer_forward.7 = (bf16[512,1024]{1,0:T(8,128)(2,1)S(1)}, f32[512,1]{1,0:T(8,128)S(1)}, f32[512,1024]{1,0:T(8,128)S(1)}, f32[4,128,1024]{2,1,0:T(8,128)S(1)}, f32[128,1024]{1,0:T(8,128)}) custom-call(f32[512,1024]{1,0:T(8,128)S(1)} %fusion.111.refs_0_.refs_2_, f32[512,1408]{1,0:T(8,128)S(1)} %fusion.112.refs_1_.refs_3_.refs_4_, ...), custom_call_target="tpu_custom_call" | custom-call | flops 1000 | bytes 1000 | tf_op jit(solution)/shard_map/mixer_forward/pallas_call | solution.py:341
  377.6 20.6 %all-gather.8.cloned.1.call-done = bf16[2048,1024]{1,0:T(8,128)(2,1)} async-done(((bf16[256,1024]{1,0:T(8,128)(2,1)}), bf16[2048,1024]{1,0:T(8,128)(2,1)}) %all-gather.8.cloned.1.call-update) | async-done | bytes 4194320 | tf_op jit(solution)/shard_map/all_gather | solution.py:1094
  398.2 6.7 fusion.37
  404.9 3.7 fusion.39
  413.8 3.2 copy-done.130
  419.4 6.2 fusion.27
  432.5 18.7 %mixer_backward.4 = (bf16[512,2432]{1,0:T(8,128)(2,1)S(1)}, f32[128,1024]{1,0:T(8,128)S(1)}, f32[8,1280]{1,0:T(8,128)S(1)}, f32[8,1280]{1,0:T(8,128)S(1)}) custom-call(f32[512,1024]{1,0:T(8,128)S(1)} %copy-done.34, f32[512,2]{1,0:T(8,128)S(1)} %copy.74.refs_1_, f32[512,1024]{1,0:T(8,128)S(1)} %copy-done.15, f32[512,1408]{1,0:T(8,128)} %copy-done.3, ...), custom_call_target="tpu_custom_call" | custom-call | flops 1000 | bytes 1000 | tf_op jit(solution)/shard_map/mixer_backward/pallas_call | solution.py:392
  451.3 9.4 %convolution_convert_fusion.9 = bf16[512,2048]{1,0:T(8,128)(2,1)S(1)} fusion(bf16[512,2432]{1,0:T(8,128)(2,1)S(1)} %get-tuple-element.154, bf16[2048,2432]{1,0:T(8,128)(2,1)} %copy-done.130), kind=kOutput, calls=%fused_computation.43 | convolution fusion | flops 5101322240 | bytes 14548992 | tf_op jit(solution)/shard_map/dot_general | solution.py:35
  463.1 2.4 convolution_convert_fusion.3
  467.4 2.1 convert_add_fusion.5
  472.1 20.0 %mixer_backward.5 = (bf16[512,2432]{1,0:T(8,128)(2,1)S(1)}, f32[128,1024]{1,0:T(8,128)}, f32[8,1280]{1,0:T(8,128)}, f32[8,1280]{1,0:T(8,128)S(1)}) custom-call(f32[512,1024]{1,0:T(8,128)S(1)} %copy-done.29, f32[512,2]{1,0:T(8,128)S(1)} %copy.76.refs_1_, f32[512,1024]{1,0:T(8,128)S(1)} %copy-done.13, f32[512,1408]{1,0:T(8,128)} %copy-done.1, ...), custom_call_target="tpu_custom_call" | custom-call | flops 1000 | bytes 1000 | tf_op jit(solution)/shard_map/mixer_backward/pallas_call | solution.py:392
  497.7 8.4 convolution_convert_fusion.8
  508.8 2.4 convolution_convert_fusion.2
  516.5 13.7 %convolution_convert_fusion.1 = bf16[2048,2432]{1,0:T(8,128)(2,1)} fusion(bf16[512,2432]{1,0:T(8,128)(2,1)S(1)} %copy-done.62, bf16[512,2432]{1,0:T(8,128)(2,1)S(1)} %get-tuple-element.153, bf16[512,2048]{1,0:T(8,128)(2,1)S(1)} %bitcast.420, bf16[512,2048]{1,0:T(8,128)(2,1)S(1)} %bitcast.417), kind=kOutput, calls=%fused_computation.1 | convolution fusion | flops 10223878144 | bytes 19136512 | tf_op jit(solution)/shard_map/dot_general | solution.py:1180
  539.6 2.6 multiply_reduce_fusion.2
  545.7 2.8 copy-done.171
  548.5 2.4 fusion.113.refs_0_
  551.4 18.6 %mixer_backward.6 = (bf16[512,2432]{1,0:T(8,128)(2,1)S(1)}, f32[128,1024]{1,0:T(8,128)S(1)}, f32[8,1280]{1,0:T(8,128)S(1)}, f32[8,1280]{1,0:T(8,128)S(1)}) custom-call(f32[512,1024]{1,0:T(8,128)S(1)} %fusion.113.refs_0_, f32[512,2]{1,0:T(8,128)S(1)} %bitcast.388, f32[512,1024]{1,0:T(8,128)S(1)} %copy-done.11, f32[512,1408]{1,0:T(8,128)} %fusion.refs_1_.refs_3_.refs_4_, ...), custom_call_target="tpu_custom_call" | custom-call | flops 1000 | bytes 1000 | tf_op jit(solution)/shard_map/mixer_backward/pallas_call | solution.py:392
  572.4 8.6 convolution_convert_fusion.7
  589.2 2.3 fusion.114.refs_0_
  592.1 19.4 %mixer_backward.7 = (bf16[512,2432]{1,0:T(8,128)(2,1)S(1)}, f32[128,1024]{1,0:T(8,128)}, f32[8,1280]{1,0:T(8,128)}, f32[8,1280]{1,0:T(8,128)S(1)}) custom-call(f32[512,1024]{1,0:T(8,128)S(1)} %fusion.114.refs_0_, f32[512,2]{1,0:T(8,128)S(1)} %bitcast.389, f32[512,1024]{1,0:T(8,128)S(1)} %copy-done.9, f32[512,1408]{1,0:T(8,128)} %copy-done, ...), custom_call_target="tpu_custom_call" | custom-call | flops 1000 | bytes 1000 | tf_op jit(solution)/shard_map/mixer_backward/pallas_call | solution.py:392
  614.1 8.2 convolution_convert_fusion.6
  625.4 6.5 fusion.24.refs_1_
  634.5 16.9 %convolution_convert_fusion.refs_0_ = bf16[2048,2432]{1,0:T(8,128)(2,1)} fusion(bf16[512,2432]{1,0:T(8,128)(2,1)S(1)} %copy-done.60, bf16[512,2432]{1,0:T(8,128)(2,1)S(1)} %get-tuple-element.173, bf16[512,2048]{1,0:T(8,128)(2,1)} %bitcast.470, bf16[512,2048]{1,0:T(8,128)(2,1)} %bitcast.466), kind=kOutput, calls=%fused_computation | convolution fusion | flops 10223878144 | bytes 19136512 | tf_op jit(solution)/shard_map/dot_general | solution.py:1180
  651.6 3.0 broadcast_select_fusion.4
  655.7 3.9 collective-permute-done.35
  669.3 168.5 %grads_reduce.1 = (f32[256,2432]{1,0:T(8,128)}, f32[256,1024]{1,0:T(8,128)}, f32[256,2432]{1,0:T(8,128)}, f32[256,1024]{1,0:T(8,128)}, f32[8,1280]{1,0:T(8,128)}, /*index=5*/f32[8,1280]{1,0:T(8,128)}, f32[8,1280]{1,0:T(8,128)}) custom-call(bf16[2048,2432]{1,0:T(8,128)(2,1)} %convolution_convert_fusion.refs_0_, bf16[2048,1024]{1,0:T(8,128)(2,1)} %fusion.24.refs_1_, ...), custom_call_target="tpu_custom_call" | custom-call | flops 1000 | bytes 1000 | tf_op jit(solution)/shard_map/grads_reduce/pallas_call | solution.py:923
  853.7 2.3 maximum_bitcast_fusion
  856.0 7.4 copy.88
  (629 shorter events, 161.6 us)
Async XLA Ops:
  7.2 216.3 %all-gather.4.cloned.1.call-start = ((), (), s32[]{:S(2)}) async-start(), calls=%async_computation.2 | async-start | bytes 4718592 | tf_op jit(solution)/shard_map/all_gather | solution.py:1092
  14.0 8.4 collective-permute-start
  27.6 296.2 %all-gather.6.cloned.1.call-start = ((), (), s32[]{:S(2)}) async-start(), calls=%async_computation.3 | async-start | bytes 6488064 | tf_op jit(solution)/shard_map/all_gather | solution.py:1093
  223.3 174.9 %all-gather.8.cloned.1.call-start = ((), (), s32[]{:S(2)}) async-start(), calls=%async_computation.4 | async-start | bytes 4718592 | tf_op jit(solution)/shard_map/all_gather | solution.py:1094
  223.4 42.1 %copy-start.44 = (f32[8,1280]{1,0:T(8,128)}, f32[8,1280]{1,0:T(8,128)S(1)}, u32[]{:S(2)}) copy-start(f32[8,1280]{1,0:T(8,128)S(1)} %get-tuple-element.302.refs_4_.refs_10_) | copy-start | bytes 122884
  246.7 13.4 %collective-permute-start.3 = (bf16[2,128,2048]{2,1,0:T(8,128)(2,1)}, bf16[2,128,2048]{2,1,0:T(8,128)(2,1)}, u32[]{:S(2)}, u32[]{:S(2)}) collective-permute-start(bf16[2,128,2048]{2,1,0:T(8,128)(2,1)} %dynamic-slice_bitcast_fusion.9), channel_id=1, source_target_pairs={{0,16},{16,0},{1,17},{17,1},{2,18},{18,2},{3,19},{19,3},{4,20},{20... | collective-permute-start | bytes 3145736 | tf_op jit(solution)/shard_map/ppermute | solution.py:952
  254.5 5.5 collective-permute-start.1
  262.5 13.1 %collective-permute-start.4 = (bf16[128,2048]{1,0:T(8,128)(2,1)S(1)}, bf16[128,2048]{1,0:T(8,128)(2,1)S(1)}, u32[]{:S(2)}, u32[]{:S(2)}) collective-permute-start(bf16[128,2048]{1,0:T(8,128)(2,1)S(1)} %fusion.69), channel_id=1, source_target_pairs={{0,1},{1,0},{2,3},{3,2},{4,5},{5,4},{6,7},{7,6},{8,9},{9,8},{10,11... | collective-permute-start | bytes 1572872 | tf_op jit(solution)/shard_map/ppermute | solution.py:956
  263.8 11.8 %collective-permute-start.2 = (f32[128]{0:T(128)S(1)}, f32[128]{0:T(128)S(1)}, u32[]{:S(2)}, u32[]{:S(2)}) collective-permute-start(f32[128]{0:T(128)S(1)} %fusion.89), channel_id=1, source_target_pairs={{0,1},{1,0},{2,3},{3,2},{4,5},{5,4},{6,7},{7,6},{8,9},{9,8},{10,11... | collective-permute-start | bytes 1544 | tf_op jit(solution)/shard_map/ppermute | solution.py:956
  277.1 12.4 %collective-permute-start.5 = (bf16[128,2048]{1,0:T(8,128)(2,1)S(1)}, bf16[128,2048]{1,0:T(8,128)(2,1)S(1)}, u32[]{:S(2)}, u32[]{:S(2)}) collective-permute-start(bf16[128,2048]{1,0:T(8,128)(2,1)S(1)} %multiply_convert_fusion.3), channel_id=1, source_target_pairs={{0,1},{1,0},{2,3},{3,2},{4,5},{5,4},{6,7},{7,6},{8,9},{9,8},{10,11... | collective-permute-start | bytes 1572872 | tf_op jit(solution)/shard_map/ppermute | solution.py:956
  283.3 13.1 %collective-permute-start.7 = (bf16[2,128,2048]{2,1,0:T(8,128)(2,1)}, bf16[2,128,2048]{2,1,0:T(8,128)(2,1)}, u32[]{:S(2)}, u32[]{:S(2)}) collective-permute-start(bf16[2,128,2048]{2,1,0:T(8,128)(2,1)} %dynamic-slice_bitcast_fusion.8), channel_id=1, source_target_pairs={{0,16},{16,0},{1,17},{17,1},{2,18},{18,2},{3,19},{19,3},{4,20},{20... | collective-permute-start | bytes 3145736 | tf_op jit(solution)/shard_map/ppermute | solution.py:952
  290.9 9.9 %collective-permute-start.6 = (bf16[2,128,2048]{2,1,0:T(8,128)(2,1)}, bf16[2,128,2048]{2,1,0:T(8,128)(2,1)S(1)}, u32[]{:S(2)}, u32[]{:S(2)}) collective-permute-start(bf16[2,128,2048]{2,1,0:T(8,128)(2,1)} %pad_maximum_fusion.6), channel_id=1, source_target_pairs={{0,16},{16,0},{1,17},{17,1},{2,18},{18,2},{3,19},{19,3},{4,20},{20... | collective-permute-start | bytes 3145736 | tf_op jit(solution)/shard_map/ppermute | solution.py:952
  293.0 2.1 collective-permute-start.8
  293.1 548.4 %reduce-scatter.5.cloned.1.call-start = ((), (), s32[]{:S(2)}) async-start(), calls=%async_computation.6 | async-start | bytes 4718592 | tf_op jit(solution)/shard_map/reduce_scatter | solution.py:1228
  295.1 35.8 %collective-permute-start.9 = (f32[128]{0:T(128)S(1)}, f32[128]{0:T(128)S(1)}, u32[]{:S(2)}, u32[]{:S(2)}) collective-permute-start(f32[128]{0:T(128)S(1)} %fusion.90), channel_id=1, source_target_pairs={{0,1},{1,0},{2,3},{3,2},{4,5},{5,4},{6,7},{7,6},{8,9},{9,8},{10,11... | collective-permute-start | bytes 1544 | tf_op jit(solution)/shard_map/ppermute | solution.py:956
  300.5 30.4 %collective-permute-start.10 = (bf16[128,2048]{1,0:T(8,128)(2,1)}, bf16[128,2048]{1,0:T(8,128)(2,1)}, u32[]{:S(2)}, u32[]{:S(2)}) collective-permute-start(bf16[128,2048]{1,0:T(8,128)(2,1)} %fusion.70), channel_id=1, source_target_pairs={{0,1},{1,0},{2,3},{3,2},{4,5},{5,4},{6,7},{7,6},{8,9},{9,8},{10,11... | collective-permute-start | bytes 1572872 | tf_op jit(solution)/shard_map/ppermute | solution.py:956
  333.6 13.4 %collective-permute-start.11 = (bf16[128,2048]{1,0:T(8,128)(2,1)S(1)}, bf16[128,2048]{1,0:T(8,128)(2,1)S(1)}, u32[]{:S(2)}, u32[]{:S(2)}) collective-permute-start(bf16[128,2048]{1,0:T(8,128)(2,1)S(1)} %multiply_convert_fusion.2), channel_id=1, source_target_pairs={{0,1},{1,0},{2,3},{3,2},{4,5},{5,4},{6,7},{7,6},{8,9},{9,8},{10,11... | collective-permute-start | bytes 1572872 | tf_op jit(solution)/shard_map/ppermute | solution.py:956
  349.9 4.7 collective-permute-start.12
  377.5 40.0 %copy-start.42 = (bf16[512,1024]{1,0:T(8,128)(2,1)}, bf16[512,1024]{1,0:T(8,128)(2,1)S(1)}, u32[]{:S(2)}) copy-start(bf16[512,1024]{1,0:T(8,128)(2,1)S(1)} %get-tuple-element.141) | copy-start | bytes 3145732
  408.6 2.6 collective-permute-start.13
  411.2 2.5 collective-permute-start.14
  425.6 420.5 %reduce-scatter.3.cloned.1.call-start = ((), (), s32[]{:S(2)}) async-start(), calls=%async_computation.5 | async-start | bytes 11206656 | tf_op jit(solution)/shard_map/reduce_scatter | solution.py:1228
  462.4 4.9 collective-permute-start.15
  465.8 26.4 %collective-permute-start.32 = (bf16[2,128,2048]{2,1,0:T(8,128)(2,1)S(1)}, bf16[2,128,2048]{2,1,0:T(8,128)(2,1)S(1)}, u32[]{:S(2)}, u32[]{:S(2)}) collective-permute-start(bf16[2,128,2048]{2,1,0:T(8,128)(2,1)S(1)} %dynamic-slice_bitcast_fusion.1), channel_id=1, source_target_pairs={{0,16},{16,0},{1,17},{17,1},{2,18},{18,2},{3,19},{19,3},{4,20},{20... | collective-permute-start | bytes 3145736 | tf_op jit(solution)/shard_map/ppermute | solution.py:952
  469.6 23.0 %collective-permute-start.16 = (bf16[128,2048]{1,0:T(8,128)(2,1)S(1)}, bf16[128,2048]{1,0:T(8,128)(2,1)S(1)}, u32[]{:S(2)}, u32[]{:S(2)}) collective-permute-start(bf16[128,2048]{1,0:T(8,128)(2,1)S(1)} %fusion.71), channel_id=1, source_target_pairs={{0,1},{1,0},{2,3},{3,2},{4,5},{5,4},{6,7},{7,6},{8,9},{9,8},{10,11... | collective-permute-start | bytes 1572872 | tf_op jit(solution)/shard_map/ppermute | solution.py:956
  496.7 34.5 %copy-start.68 = (f32[128,2048]{1,0:T(8,128)}, f32[128,2048]{1,0:T(8,128)S(1)}, u32[]{:S(2)}) copy-start(f32[128,2048]{1,0:T(8,128)S(1)} %get-tuple-element.258) | copy-start | bytes 3145732
  506.2 7.0 collective-permute-start.18
  507.3 22.9 %collective-permute-start.23 = (f32[128,2]{0,1:T(2,128)S(1)}, f32[128,2]{0,1:T(2,128)S(1)}, u32[]{:S(2)}, u32[]{:S(2)}) collective-permute-start(f32[128,2]{0,1:T(2,128)S(1)} %pad_maximum_fusion.18), channel_id=1, source_target_pairs={{0,1},{1,0},{2,3},{3,2},{4,5},{5,4},{6,7},{7,6},{8,9},{9,8},{10,11... | collective-permute-start | bytes 3080 | tf_op jit(solution)/shard_map/ppermute | solution.py:956
  508.3 22.0 %collective-permute-start.21 = (bf16[128,2048]{1,0:T(8,128)(2,1)}, bf16[128,2048]{1,0:T(8,128)(2,1)}, u32[]{:S(2)}, u32[]{:S(2)}) collective-permute-start(bf16[128,2048]{1,0:T(8,128)(2,1)} %convert_element_type.276), channel_id=1, source_target_pairs={{0,1},{1,0},{2,3},{3,2},{4,5},{5,4},{6,7},{7,6},{8,9},{9,8},{10,11... | collective-permute-start | bytes 1572872 | tf_op jit(solution)/shard_map/ppermute | solution.py:956
  512.3 21.4 %collective-permute-start.17 = (bf16[2,128,2048]{2,1,0:T(8,128)(2,1)}, bf16[2,128,2048]{2,1,0:T(8,128)(2,1)S(1)}, u32[]{:S(2)}, u32[]{:S(2)}) collective-permute-start(bf16[2,128,2048]{2,1,0:T(8,128)(2,1)} %dynamic-slice_bitcast_fusion.6), channel_id=1, source_target_pairs={{0,16},{16,0},{1,17},{17,1},{2,18},{18,2},{3,19},{19,3},{4,20},{20... | collective-permute-start | bytes 3145736 | tf_op jit(solution)/shard_map/ppermute | solution.py:952
  515.8 21.5 %collective-permute-start.19 = (bf16[128,2048]{1,0:T(8,128)(2,1)}, bf16[128,2048]{1,0:T(8,128)(2,1)}, u32[]{:S(2)}, u32[]{:S(2)}) collective-permute-start(bf16[128,2048]{1,0:T(8,128)(2,1)} %fusion.72), channel_id=1, source_target_pairs={{0,1},{1,0},{2,3},{3,2},{4,5},{5,4},{6,7},{7,6},{8,9},{9,8},{10,11... | collective-permute-start | bytes 1572872 | tf_op jit(solution)/shard_map/ppermute | solution.py:956
  530.3 4.7 collective-permute-start.24
  533.6 10.3 %collective-permute-start.22 = (bf16[2,128,2048]{2,1,0:T(8,128)(2,1)}, bf16[2,128,2048]{2,1,0:T(8,128)(2,1)}, u32[]{:S(2)}, u32[]{:S(2)}) collective-permute-start(bf16[2,128,2048]{2,1,0:T(8,128)(2,1)} %pad_maximum_fusion.8), channel_id=1, source_target_pairs={{0,16},{16,0},{1,17},{17,1},{2,18},{18,2},{3,19},{19,3},{4,20},{20... | collective-permute-start | bytes 3145736 | tf_op jit(solution)/shard_map/ppermute | solution.py:952
  542.2 38.8 %collective-permute-start.27 = (f32[128,2]{0,1:T(2,128)S(1)}, f32[128,2]{0,1:T(2,128)S(1)}, u32[]{:S(2)}, u32[]{:S(2)}) collective-permute-start(f32[128,2]{0,1:T(2,128)S(1)} %pad_maximum_fusion.19), channel_id=1, source_target_pairs={{0,1},{1,0},{2,3},{3,2},{4,5},{5,4},{6,7},{7,6},{8,9},{9,8},{10,11... | collective-permute-start | bytes 3080 | tf_op jit(solution)/shard_map/ppermute | solution.py:956
  542.9 27.1 %collective-permute-start.20 = (bf16[128,2048]{1,0:T(8,128)(2,1)S(1)}, bf16[128,2048]{1,0:T(8,128)(2,1)S(1)}, u32[]{:S(2)}, u32[]{:S(2)}) collective-permute-start(bf16[128,2048]{1,0:T(8,128)(2,1)S(1)} %convert_element_type.290), channel_id=1, source_target_pairs={{0,1},{1,0},{2,3},{3,2},{4,5},{5,4},{6,7},{7,6},{8,9},{9,8},{10,11... | collective-permute-start | bytes 1572872 | tf_op jit(solution)/shard_map/ppermute | solution.py:956
  571.4 11.6 %collective-permute-start.25 = (bf16[2,128,2048]{2,1,0:T(8,128)(2,1)}, bf16[2,128,2048]{2,1,0:T(8,128)(2,1)}, u32[]{:S(2)}, u32[]{:S(2)}) collective-permute-start(bf16[2,128,2048]{2,1,0:T(8,128)(2,1)} %pad_maximum_fusion.9), channel_id=1, source_target_pairs={{0,16},{16,0},{1,17},{17,1},{2,18},{18,2},{3,19},{19,3},{4,20},{20... | collective-permute-start | bytes 3145736 | tf_op jit(solution)/shard_map/ppermute | solution.py:952
  581.0 1.8 collective-permute-start.28
  582.7 3.0 collective-permute-start.26
  588.4 23.1 %collective-permute-start.30 = (bf16[128,2048]{1,0:T(8,128)(2,1)S(1)}, bf16[128,2048]{1,0:T(8,128)(2,1)S(1)}, u32[]{:S(2)}, u32[]{:S(2)}) collective-permute-start(bf16[128,2048]{1,0:T(8,128)(2,1)S(1)} %fusion.73), channel_id=1, source_target_pairs={{0,1},{1,0},{2,3},{3,2},{4,5},{5,4},{6,7},{7,6},{8,9},{9,8},{10,11... | collective-permute-start | bytes 1572872 | tf_op jit(solution)/shard_map/ppermute | solution.py:956
  622.5 9.4 %collective-permute-start.31 = (bf16[2,128,2048]{2,1,0:T(8,128)(2,1)S(1)}, bf16[2,128,2048]{2,1,0:T(8,128)(2,1)S(1)}, u32[]{:S(2)}, u32[]{:S(2)}) collective-permute-start(bf16[2,128,2048]{2,1,0:T(8,128)(2,1)S(1)} %dynamic-slice_bitcast_fusion.2), channel_id=1, source_target_pairs={{0,16},{16,0},{1,17},{17,1},{2,18},{18,2},{3,19},{19,3},{4,20},{20... | collective-permute-start | bytes 3145736 | tf_op jit(solution)/shard_map/ppermute | solution.py:952
  623.9 27.6 %collective-permute-start.29 = (bf16[128,2048]{1,0:T(8,128)(2,1)}, bf16[128,2048]{1,0:T(8,128)(2,1)S(1)}, u32[]{:S(2)}, u32[]{:S(2)}) collective-permute-start(bf16[128,2048]{1,0:T(8,128)(2,1)} %dynamic-slice_bitcast_fusion.5), channel_id=1, source_target_pairs={{0,1},{1,0},{2,3},{3,2},{4,5},{5,4},{6,7},{7,6},{8,9},{9,8},{10,11... | collective-permute-start | bytes 1572872 | tf_op jit(solution)/shard_map/ppermute | solution.py:956
  624.7 26.8 %collective-permute-start.33 = (bf16[128,2048]{1,0:T(8,128)(2,1)}, bf16[128,2048]{1,0:T(8,128)(2,1)}, u32[]{:S(2)}, u32[]{:S(2)}) collective-permute-start(bf16[128,2048]{1,0:T(8,128)(2,1)} %dynamic-slice_bitcast_fusion), channel_id=1, source_target_pairs={{0,1},{1,0},{2,3},{3,2},{4,5},{5,4},{6,7},{7,6},{8,9},{9,8},{10,11... | collective-permute-start | bytes 1572872 | tf_op jit(solution)/shard_map/ppermute | solution.py:956
  633.2 26.4 %collective-permute-start.35 = (bf16[128,2048]{1,0:T(8,128)(2,1)}, bf16[128,2048]{1,0:T(8,128)(2,1)S(1)}, u32[]{:S(2)}, u32[]{:S(2)}) collective-permute-start(bf16[128,2048]{1,0:T(8,128)(2,1)} %fusion.74), channel_id=1, source_target_pairs={{0,1},{1,0},{2,3},{3,2},{4,5},{5,4},{6,7},{7,6},{8,9},{9,8},{10,11... | collective-permute-start | bytes 1572872 | tf_op jit(solution)/shard_map/ppermute | solution.py:956
  654.6 10.0 %collective-permute-start.34 = (f32[128,2048]{1,0:T(8,128)}, f32[128,2048]{1,0:T(8,128)}, u32[]{:S(2)}, u32[]{:S(2)}) collective-permute-start(f32[128,2048]{1,0:T(8,128)} %get-tuple-element.250), channel_id=1, source_target_pairs={{0,16},{16,0},{1,17},{17,1},{2,18},{18,2},{3,19},{19,3},{4,20},{20... | collective-permute-start | bytes 3145736 | tf_op jit(solution)/shard_map/ppermute | solution.py:952
  662.5 5.1 collective-permute-start.36
  841.5 4.4 collective-permute-start.39
  846.2 3.7 collective-permute-start.37
  852.5 11.6 %collective-permute-start.38 = (f32[256,256]{1,0:T(8,128)S(1)}, f32[256,256]{1,0:T(8,128)S(1)}, u32[]{:S(2)}, u32[]{:S(2)}) collective-permute-start(f32[256,256]{1,0:T(8,128)S(1)} %slice_add_fusion), channel_id=1, source_target_pairs={{0,1},{1,0},{2,3},{3,2},{4,5},{5,4},{6,7},{7,6},{8,9},{9,8},{10,11... | collective-permute-start | bytes 786440 | tf_op jit(solution)/shard_map/ppermute | solution.py:956
  (174 other events, 1025.2 us)
Sparse Core Ops, SparseCore 0:
  27.8 116.6 all-gather.3
  223.5 100.3 all-gather.5
  326.0 72.1 all-gather.7
  425.8 86.0 reduce-scatter.4
  530.4 171.1 reduce-scatter.2

commit v4 on v3

--- a/solution.py
+++ b/solution.py
@@ -15,7 +15,6 @@
 LANES = 128
 HALO = 8
 NEG = -10000.0
-HIGHEST = lax.Precision.HIGHEST
 F32 = jnp.float32
 BF16 = jnp.bfloat16
 VMEM_LIMIT = 56 * 1024 * 1024
@@ -35,10 +34,13 @@
     return lax.dot_general(a, b, (((1,), (1,)), ((), ())), preferred_element_type=F32)
 
 
-def dot_exact(a, b):
-    return lax.dot_general(
-        a, b, (((1,), (0,)), ((), ())), preferred_element_type=F32, precision=HIGHEST
-    )
+def dot_sums(ones, columns, heads):
+    high = columns.astype(BF16).astype(F32)
+    middle = (columns - high).astype(BF16).astype(F32)
+    low = columns - high - middle
+    packed = high + pltpu.roll(middle, heads, 1) + pltpu.roll(low, 2 * heads, 1)
+    sums = dot_nn(ones.astype(BF16), packed.astype(BF16))
+    return sums + pltpu.roll(sums, LANES - heads, 1) + pltpu.roll(sums, LANES - 2 * heads, 1)
 
 
 def split(a):
@@ -70,7 +72,7 @@
     dt = jnp.where(live, jnp.maximum(arg, 0.0) + jnp.log1p(jnp.exp(-jnp.abs(arg))), 0.0)
     decay = slab[6:7, channels : channels + LANES]
     lower = tri((CHUNK, CHUNK), lambda r, c: r >= c).astype(F32)
-    cum = dot_exact(lower, dt * decay)
+    cum = dot_sums(lower, dt * decay, heads)
     last = cum[CHUNK - 1 : CHUNK, :]
     grown = jnp.where(live, jnp.exp(cum), 0.0)
     left = jnp.where(live, jnp.exp(last - cum), 0.0)
@@ -297,7 +299,9 @@
     upper = tri((CHUNK, CHUNK), lambda r, c: c >= r).astype(F32)
     below = tri((CHUNK, CHUNK), lambda r, c: r > c).astype(F32)
     g_log = (
-        dot_exact(upper, gap_rows_t - gap_cols + row_sum) + dot_exact(below, col_sum) + through_sum
+        dot_sums(upper, gap_rows_t - gap_cols + row_sum, heads)
+        + dot_sums(below, col_sum, heads)
+        + through_sum
     )
     g_dt = direct + g_log * decay
     g_dtin = jnp.where(lane < heads, g_dt * sigmoid(arg), 0.0)
@@ -376,7 +380,7 @@
 
 
 def mixer_backward(
-    q, factor, gate, rest, tail, y, entering, grad, e_rows, slab, spread, gather, heads
+    q, factor, gate, rest, tail, y, entering, grad, e_rows, slab, spread, gather, heads, grant
 ):
     rows, width = rest.shape
     state_size, channels = grad.shape
@@ -427,15 +431,54 @@
             pltpu.VMEM((CHUNK + HALO, size), F32),
         ],
         compiler_params=pltpu.CompilerParams(
-            dimension_semantics=("arbitrary",), vmem_limit_bytes=BACK_VMEM
+            dimension_semantics=("arbitrary",), vmem_limit_bytes=grant
         ),
         cost_estimate=pl.CostEstimate(flops=1000, bytes_accessed=1000, transcendentals=0),
         name="mixer_backward",
     )(q, factor, gate, rest, rest, tail, y, entering, grad, e_rows, slab, spread, gather)
 
 
+def finish_kernel(first_own, first_other, second_own, second_other, gates, *, channels):
+    core = lax.axis_index("section")
+
+    def write(low, high):
+        for half, source in enumerate((low, high)):
+            value = source[...].astype(F32)
+            for k in range(2):
+                gates[:, k, half * channels : (half + 1) * channels] = value[
+                    :, k * channels : (k + 1) * channels
+                ]
+
+    @pl.when(core == 0)
+    def _():
+        write(first_own, first_other)
+
+    @pl.when(core == 1)
+    def _():
+        write(second_other, second_own)
+
+
+def join_halves(first_own, first_other, second_own, second_other, channels):
+    rows = first_own.shape[0]
+    step = 32
+    block = pl.BlockSpec((step, 2 * channels), lambda i: (i, 0))
+    return pl.pallas_call(
+        functools.partial(finish_kernel, channels=channels),
+        grid=(rows // step,),
+        in_specs=[block] * 4,
+        out_specs=pl.BlockSpec((step, 2, 2 * channels), lambda i: (i, 0, 0)),
+        out_shape=jax.ShapeDtypeStruct((rows, 2, 2 * channels), F32),
+        compiler_params=pltpu.CompilerParams(
+            dimension_semantics=("arbitrary",), vmem_limit_bytes=MIXER_VMEM
+        ),
+        cost_estimate=pl.CostEstimate(flops=1000, bytes_accessed=1000, transcendentals=0),
+        name="join_halves",
+    )(first_own, first_other, second_own, second_other)
+
+
 MESH = pl.DeviceIdType.MESH
 DEEP = 4
+SIDEWAYS = 32
 
 
 def place_in_line():
@@ -462,61 +505,89 @@
     pl.semaphore_wait(barrier, 2 * DEEP + 1)
 
 
-def gather_steps(shards, wholes, sems, beside=None):
+def gather_steps(shards, wholes, sems, beside):
     count = len(shards)
-    local_sem, x_send, x_recv, up_send, up_recv, down_send, down_recv = sems
+    local_sem, x_send, x_recv, up_send, up_recv, down_send, down_recv = sems[:7]
+    side_send, side_recv, pair_up_send, pair_up_recv, pair_down_send, pair_down_recv = sems[7:]
     deep, side, device = place_in_line()
-
-    def rows(i, z, x):
-        size = shards[i].shape[0]
-        return wholes[i].at[pl.ds((z * 2 + x) * size, size)]
-
-    def move(i, z, source, send, recv, target):
+    above, below = jnp.minimum(deep + 1, DEEP - 1), jnp.maximum(deep - 1, 0)
+    has_above, has_below = deep < DEEP - 1, deep > 0
+    main = [pl.ds(0, shard.shape[0] - SIDEWAYS) for shard in shards]
+    rest = [pl.ds(shard.shape[0] - SIDEWAYS, SIDEWAYS) for shard in shards]
+
+    def remote(source, place, send, recv, target):
         return pltpu.make_async_remote_copy(
-            src_ref=rows(i, z, side) if source is None else source,
-            dst_ref=rows(i, z, side),
+            src_ref=source,
+            dst_ref=place,
             send_sem=send,
             recv_sem=recv,
             device_id=target,
             device_id_type=MESH,
         )
 
+    def own(i):
+        return pltpu.make_async_copy(shards[i], wholes[i].at[deep * 2 + side], local_sem.at[i])
+
+    def block(i, z, x=None):
+        return wholes[i].at[z * 2 + (side if x is None else x), main[i]]
+
     def across(i, z, source=None):
-        return move(i, z, source, x_send.at[i, z], x_recv.at[i, z], device(deep, 1 - side))
+        source = block(i, z) if source is None else source
+        target = device(deep, 1 - side)
+        return remote(source, block(i, z), x_send.at[i, z], x_recv.at[i, z], target)
 
     def upward(i, k, source=None):
-        above = jnp.minimum(deep + 1, DEEP - 1)
-        return move(i, deep - k, source, up_send.at[i, k], up_recv.at[i, k], device(above, side))
+        place = block(i, deep - k)
+        source = place if source is None else source
+        return remote(source, place, up_send.at[i, k], up_recv.at[i, k], device(above, side))
 
     def downward(i, k, source=None):
-        below = jnp.maximum(deep - 1, 0)
-        return move(i, deep + k, source, down_send.at[i, k], down_recv.at[i, k], device(below, side))
-
-    has_above, has_below = deep < DEEP - 1, deep > 0
+        place = block(i, deep + k)
+        source = place if source is None else source
+        return remote(source, place, down_send.at[i, k], down_recv.at[i, k], device(below, side))
+
+    def sideways(i, x):
+        place = wholes[i].at[deep * 2 + x, rest[i]]
+        source = shards[i].at[rest[i]]
+        return remote(source, place, side_send.at[i], side_recv.at[i], device(deep, 1 - side))
+
+    def pair(i, z):
+        return wholes[i].at[pl.ds(z * 2, 2), rest[i]]
+
+    def pair_up(i, k):
+        place = pair(i, deep - k)
+        return remote(place, place, pair_up_send.at[i, k], pair_up_recv.at[i, k], device(above, side))
+
+    def pair_down(i, k):
+        place = pair(i, deep + k)
+        return remote(
+            place, place, pair_down_send.at[i, k], pair_down_recv.at[i, k], device(below, side)
+        )
+
     for i in range(count):
-        pltpu.make_async_copy(shards[i], rows(i, deep, side), local_sem.at[i]).start()
+        own(i).start()
+        sideways(i, side).start()
+    for i in range(count):
+        source = shards[i].at[main[i]]
 
         @pl.when(has_above)
-        def _(i=i):
-            upward(i, 0, shards[i]).start()
+        def _(i=i, source=source):
+            upward(i, 0, source).start()
 
         @pl.when(has_below)
-        def _(i=i):
-            downward(i, 0, shards[i]).start()
-
-        across(i, deep, shards[i]).start()
-
-    if beside is not None:
-        beside()
+        def _(i=i, source=source):
+            downward(i, 0, source).start()
+
+        across(i, deep, source).start()
+    beside(0)
+    here = device(deep, side)
     for k in range(1, DEEP):
         for i in range(count):
 
             @pl.when(deep >= k)
             def _(i=i, k=k):
-                arrived = move(
-                    i, deep - k, None, up_send.at[i, k - 1], up_recv.at[i, k - 1], device(deep, side)
-                )
-                arrived.wait_recv()
+                place = block(i, deep - k)
+                remote(place, place, up_send.at[i, k - 1], up_recv.at[i, k - 1], here).wait_recv()
 
                 @pl.when(has_above)
                 def _():
@@ -526,10 +597,8 @@
 
             @pl.when(deep + k <= DEEP - 1)
             def _(i=i, k=k):
-                arrived = move(
-                    i, deep + k, None, down_send.at[i, k - 1], down_recv.at[i, k - 1], device(deep, side)
-                )
-                arrived.wait_recv()
+                place = block(i, deep + k)
+                remote(place, place, down_send.at[i, k - 1], down_recv.at[i, k - 1], here).wait_recv()
 
                 @pl.when(has_below)
                 def _():
@@ -537,16 +606,51 @@
 
                 across(i, deep + k).start()
 
+        if k == DEEP - 2:
+            for i in range(count):
+                own(i).wait()
+                sideways(i, 1 - side).wait_recv()
+
+                @pl.when(has_above)
+                def _(i=i):
+                    pair_up(i, 0).start()
+
+                @pl.when(has_below)
+                def _(i=i):
+                    pair_down(i, 0).start()
+
+        beside(k)
+
+    for k in range(1, DEEP):
+        for i in range(count):
+
+            @pl.when(deep >= k)
+            def _(i=i, k=k):
+                place = pair(i, deep - k)
+                remote(
+                    place, place, pair_up_send.at[i, k - 1], pair_up_recv.at[i, k - 1], here
+                ).wait_recv()
+
+                @pl.when(has_above)
+                def _():
+                    pair_up(i, k).start()
+
+            @pl.when(deep + k <= DEEP - 1)
+            def _(i=i, k=k):
+                place = pair(i, deep + k)
+                remote(
+                    place, place, pair_down_send.at[i, k - 1], pair_down_recv.at[i, k - 1], here
+                ).wait_recv()
+
+                @pl.when(has_below)
+                def _():
+                    pair_down(i, k).start()
+
     for i in range(count):
-        pltpu.make_async_copy(shards[i], rows(i, deep, side), local_sem.at[i]).wait()
+        sideways(i, side).wait_send()
         for z in range(DEEP):
-            other = pltpu.make_async_remote_copy(
-                src_ref=rows(i, z, side),
-                dst_ref=rows(i, z, 1 - side),
-                send_sem=x_send.at[i, z],
-                recv_sem=x_recv.at[i, z],
-                device_id=device(deep, 1 - side),
-                device_id_type=MESH,
+            other = remote(
+                block(i, z), block(i, z, 1 - side), x_send.at[i, z], x_recv.at[i, z], here
             )
             other.wait_send()
             other.wait_recv()
@@ -555,10 +659,12 @@
             @pl.when(has_above & (deep >= k))
             def _(i=i, k=k):
                 upward(i, k).wait_send()
+                pair_up(i, k).wait_send()
 
             @pl.when(has_below & (deep + k <= DEEP - 1))
             def _(i=i, k=k):
                 downward(i, k).wait_send()
+                pair_down(i, k).wait_send()
 
 
 def start_kernel(*refs, count, micros, heads, gain_rows):
@@ -567,8 +673,8 @@
     outs = refs[count + 10 :]
     wholes, (gains, slabs), targets = outs[:count], outs[count : count + 2], outs[count + 2 :]
     targets, scratch = targets[: 2 * micros], targets[2 * micros :]
-    gain_send, gain_recv, own_sem, y_send, y_recv, core_send, core_recv, rows_out = scratch[7:15]
-    other_slab, slab_send, slab_recv, line_send, line_recv = scratch[15:]
+    gain_send, gain_recv, own_sem, y_send, y_recv, core_send, core_recv, rows_out = scratch[13:21]
+    other_slab, slab_send, slab_recv, line_send, line_recv = scratch[21:]
     core, line, half = lax.axis_index("section"), lax.axis_index("fsdp"), lax.axis_index("tp")
     lines = 2 * DEEP
 
@@ -641,7 +747,19 @@
         place[6:7, :channels] = skip[2:3]
         place[6:7, channels : channels + LANES] = decay[1:2]
 
-    def send_tokens():
+    def send_tokens(stage):
+        if stage == 0:
+            send_first()
+        elif stage <= 2:
+            for n in range((stage - 1) * micros, stage * micros):
+                token_copies(n)[1].wait_recv()
+                token_copies(n)[3].start()
+            if stage == 1:
+                for n in range(micros, 2 * micros):
+                    for copy in token_copies(n)[:3]:
+                        copy.start()
+
+    def send_first():
         write_slab(other_slab, 1 - core)
         send_slab.start()
         write_slab(slabs.at[core], core)
@@ -657,17 +775,11 @@
         scale = lax.rsqrt(jnp.mean(h * h, axis=1, keepdims=True) + EPS)
         rows_out[...] = (h * scale * gain_row).astype(BF16)
 
-        for n in range(2 * micros):
+        for n in range(micros):
             for copy in token_copies(n)[:3]:
                 copy.start()
-        for n in range(micros):
-            token_copies(n)[1].wait_recv()
-            token_copies(n)[3].start()
-
-    gather_steps(shards, wholes, scratch[:7], send_tokens)
-    for n in range(micros, 2 * micros):
-        token_copies(n)[1].wait_recv()
-        token_copies(n)[3].start()
+
+    gather_steps(shards, wholes, scratch[:13], send_tokens)
     send_slab.wait()
     for n in range(2 * micros):
         own_copy, y_copy, core_copy, core_later = token_copies(n)
@@ -691,7 +803,7 @@
         functools.partial(
             start_kernel, count=count, micros=micros, heads=heads, gain_rows=gain_rows
         ),
-        out_shape=[shape((v.shape[0] * lines, v.shape[1]), v.dtype) for v in shards]
+        out_shape=[shape((lines,) + v.shape, v.dtype) for v in shards]
         + [
             shape((2, lines) + gain.shape, F32),
             shape((2,) + slab, F32),
@@ -701,6 +813,8 @@
         out_specs=[anywhere] * count + [vmem, vmem] + [anywhere] * (2 * micros),
         scratch_shapes=[dma(count)]
         + [pairs] * 6
+        + [dma(count)] * 2
+        + [pairs] * 4
         + [dma(lines)] * 2
         + [dma(2 * micros)] * 3
         + [dma(4 * micros)] * 2
@@ -716,7 +830,7 @@
 
 def add_rows(out, *parts):
     rows = out.shape[0]
-    step = 32
+    step = 16
 
     def body(n, _):
         at = pl.ds(pl.multiple_of(n * step, step), step)
@@ -737,11 +851,15 @@
     others = refs[2 * count + 1 : 3 * count + 1]
     own_small, next_small, both_small = refs[3 * count + 1 : 3 * count + 4]
     scratch = refs[3 * count + 4 :]
-    held, crossed, from_below, from_above = (
-        scratch[n * count : (n + 1) * count] for n in range(4)
+    held, crossed, from_below, from_above, pairs, pairs_below, pairs_above, side_in = (
+        scratch[n * count : (n + 1) * count] for n in range(8)
     )
-    load_sem, x_send, x_recv, up_send, up_recv, down_send, down_recv = scratch[4 * count : -5]
+    sems = scratch[8 * count : -5]
+    load_sem, x_send, x_recv, up_send, up_recv, down_send, down_recv = sems[:7]
+    pair_sem, pair_up_send, pair_up_recv, pair_down_send, pair_down_recv = sems[7:12]
+    side_send, side_recv = sems[12:]
     small_buffer, small_send, small_recv, other_send, other_recv = scratch[-5:]
+    main = [result.shape[0] - SIDEWAYS for result in results]
     deep, side, device = place_in_line()
     core, line, half = lax.axis_index("section"), lax.axis_index("fsdp"), lax.axis_index("tp")
     greet_all()
@@ -787,8 +905,33 @@
         over_core.wait()
 
     def rows(i, z, x):
-        size = results[i].shape[0]
-        return parts[i].at[pl.ds((z * 2 + x) * size, size)]
+        return parts[i].at[z * 2 + x, pl.ds(0, main[i])]
+
+    def load_pair(i, z):
+        source = parts[i].at[pl.ds(z * 2, 2), pl.ds(main[i], SIDEWAYS)]
+        return pltpu.make_async_copy(source, pairs[i].at[z], pair_sem.at[i, z])
+
+    def pair_along(i, k, z, here, up):
+        send, recv = (pair_up_send, pair_up_recv) if up else (pair_down_send, pair_down_recv)
+        target = min(here + 1, DEEP - 1) if up else max(here - 1, 0)
+        return pltpu.make_async_remote_copy(
+            src_ref=pairs[i].at[z],
+            dst_ref=(pairs_below if up else pairs_above)[i].at[k - 1],
+            send_sem=send.at[i, k - 1],
+            recv_sem=recv.at[i, k - 1],
+            device_id=device(target, side),
+            device_id_type=MESH,
+        )
+
+    def sideways(i, here):
+        return pltpu.make_async_remote_copy(
+            src_ref=pairs[i].at[here, 1 - side],
+            dst_ref=side_in[i],
+            send_sem=side_send.at[i],
+            recv_sem=side_recv.at[i],
+            device_id=device(deep, 1 - side),
+            device_id_type=MESH,
+        )
 
     def load(i, z):
         return pltpu.make_async_copy(rows(i, z, side), held[i].at[z], load_sem.at[i, z])
@@ -870,8 +1013,44 @@
         send_across(1)
         for number in range(DEEP):
             for i in range(count):
+                load_pair(i, order[number]).start()
+        for number in range(DEEP):
+            for i in range(count):
                 load(i, order[number]).start()
+
+        def relay_pair(k, up):
+            z = DEEP - k + here if up else here + k - DEEP
+            if not 0 <= z < DEEP or z == here or (z < here) == up:
+                return
+            for i in range(count):
+                load_pair(i, z).wait()
+                if here != (0 if up else last):
+                    pair_along(i, k - 1, z, here, up).wait_recv()
+                    back = (pairs_below if up else pairs_above)[i]
+                    for x in range(2):
+                        add_rows(pairs[i].at[z, x], pairs[i].at[z, x], back.at[k - 2, x])
+                copy = pair_along(i, k, z, here, up)
+                copy.start()
+                started.append(copy)
+
+        for k in range(1, DEEP):
+            relay_pair(k, True)
+            relay_pair(k, False)
         sum_small()
+        for i in range(count):
+            load_pair(i, here).wait()
+            for x in range(2):
+                terms = [pairs[i].at[here, x]]
+                if here > 0:
+                    if x == 0:
+                        pair_along(i, DEEP - 1, here, here, True).wait_recv()
+                    terms.append(pairs_below[i].at[DEEP - 2, x])
+                if here < last:
+                    if x == 0:
+                        pair_along(i, DEEP - 1, here, here, False).wait_recv()
+                    terms.append(pairs_above[i].at[DEEP - 2, x])
+                add_rows(pairs[i].at[here, x], *terms)
+            sideways(i, here).start()
         if here in (0, last):
             up = here == 0
             for k in range(1, DEEP):
@@ -895,10 +1074,15 @@
             if here < last:
                 downward(i, DEEP - 1, here, here).wait_recv()
                 terms.append(from_above[i].at[DEEP - 2])
-            add_rows(results[i], *terms)
+            add_rows(results[i].at[pl.ds(0, main[i])], *terms)
+            sideways(i, here).wait_recv()
+            add_rows(
+                results[i].at[pl.ds(main[i], SIDEWAYS)], pairs[i].at[here, side], side_in[i]
+            )
             to_other(i).start()
         for i in range(count):
             to_other(i).wait()
+            sideways(i, here).wait_send()
         for copy in started:
             copy.wait_send()
         for z in range(DEEP):
@@ -917,7 +1101,9 @@
     shards = [(p.shape[0] // (2 * DEEP),) + p.shape[1:] for p in parts]
     pairs = pltpu.SemaphoreType.DMA((count, DEEP))
     sizes = sum(p.size for p in parts)
-    blocks = lambda n: [pltpu.VMEM((n,) + shard, BF16) for shard in shards]
+    blocks = lambda n: [pltpu.VMEM((n, shard[0] - SIDEWAYS, shard[1]), BF16) for shard in shards]
+    doubles = lambda n: [pltpu.VMEM((n, 2, SIDEWAYS, shard[1]), BF16) for shard in shards]
+    split_parts = [p.reshape((2 * DEEP, -1) + p.shape[1:]) for p in parts]
     shape = jax.ShapeDtypeStruct
     vmem = pl.BlockSpec(memory_space=pltpu.VMEM)
     return pl.pallas_call(
@@ -929,7 +1115,12 @@
         + blocks(DEEP)
         + blocks(DEEP - 1)
         + blocks(DEEP - 1)
-        + [pairs] * 7
+        + doubles(DEEP)
+        + doubles(DEEP - 1)
+        + doubles(DEEP - 1)
+        + [pltpu.VMEM((SIDEWAYS, shard[1]), BF16) for shard in shards]
+        + [pairs] * 12
+        + [pltpu.SemaphoreType.DMA((count,))] * 2
         + [
             pltpu.VMEM((9,) + small.shape, F32),
             pltpu.SemaphoreType.DMA((6,)),
@@ -942,7 +1133,7 @@
         ),
         cost_estimate=pl.CostEstimate(flops=1000, bytes_accessed=1000, transcendentals=0),
         name=name,
-    )(*parts, small)
+    )(*split_parts, small)
 
 
 SWAP = [(0, 1), (1, 0)]
@@ -1075,8 +1266,9 @@
         per_head = jnp.concatenate([dt_bias, a_log, d_skip])
         per_head = jnp.pad(per_head, ((0, 5), (0, LANES - per_head.shape[1])))
         params = (conv_x[0], conv_xb, conv_bc[0], conv_bcb, gate_gain, per_head)
-        w_in, w_back, gains, slabs, *tokens = start_gather(
-            shards[0],
+        second_gate, second_rest = shards[1][0][:, :channels], shards[1][0][:, channels:]
+        w_in, w_back, second_rest, gains, slabs, *tokens = start_gather(
+            shards[0] + (second_rest,),
             packed,
             jnp.concatenate(first),
             jnp.concatenate(cotangents),
@@ -1087,15 +1279,13 @@
             gain_rows,
         )
         slabs = [slabs[0], slabs[1]]
+        w_in, w_back, second_rest = (v.reshape(-1, v.shape[2]) for v in (w_in, w_back, second_rest))
         projections = [(w_in, w_back)]
-        early = 8 * LANES
-        parts = [over_fsdp(shards[1][0][:, :early], axis=0)]
-        parts.append(over_fsdp(after(shards[1][0][:, early:], gains), axis=0))
-        projections.append((parts, over_fsdp(after(shards[1][1], gains), axis=0)))
+        second = (over_fsdp(after(second_gate, gains), axis=0), second_rest)
+        projections.append((second, over_fsdp(after(shards[1][1], gains), axis=0)))
         gains = gains[:, :, :gain_rows].reshape(2, -1)
         tokens = [v.reshape(4 * rows, -1) for v in tokens]
         first_normed, everyones = tokens[:micros], tokens[micros:]
-        first_normed[0] = after(first_normed[0], parts[0])
     else:
         own_slab, got_slab = slab_of(core), swap_core(slab_of(1 - core))
         slabs = [jnp.where(core == layer, own_slab, got_slab) for layer in range(2)]
@@ -1150,14 +1340,14 @@
                 w_pair = (w_in[:, :channels], w_in[:, channels:])
             else:
                 w_pair = w_in
-            gate = dot_nn(tokens, w_pair[0])
             if waiting is not None and layer == 1:
                 tokens = after(tokens, waiting[1].sent, waiting[2].sent)
             rest = dot_nn(tokens, w_pair[1])
+            gate = dot_nn(tokens, w_pair[0])
             mixed_rest = rest
             if waiting is not None and layer == 1:
                 own = finish(waiting, rest)
-                mixed_rest = after(rest, own)
+                gate = after(gate, own)
             elif waiting is not None:
                 mixed_rest = after(rest, waiting[1].sent, waiting[2].sent)
             u, squares, y, entering, state_out = mixer_forward(
@@ -1183,10 +1373,11 @@
 
     reduced, small = [None, None], [None, None]
     grads = [v.astype(F32) for v in cotangents]
-    w_back = after(projections[1][1], *[kept[1][m]["u"] for m in range(micros)])
-    w_in = projections[1][0]
+    mixers_done = [kept[1][m]["u"] for m in range(micros)]
+    w_in, w_back = projections[1]
     if in_line:
-        w_in = jnp.concatenate([after(v, *[kept[1][m]["u"] for m in range(micros)]) for v in w_in], axis=1)
+        w_in = jnp.concatenate([after(v, *mixers_done) for v in w_in], axis=1)
+    w_back = after(w_back, w_in, *mixers_done)
     projections[1] = (w_in, w_back)
     backs, products, factors = list(everyones), [None] * micros, [None] * micros
     pairs = [None] * micros
@@ -1227,7 +1418,13 @@
     def reduce_rows(part):
         return lax.psum_scatter(part, "fsdp", scatter_dimension=0, tiled=True)
 
-    waiting, spreading, outs = None, None, [None] * micros
+    def small_of(layer, totals):
+        gain_rows = sum(gain_parts[layer]).reshape(2, -1)
+        return jnp.concatenate(
+            [totals[:6], jnp.concatenate([gain_rows, totals[6:, channels:]], axis=1)]
+        )
+
+    waiting, outs = None, [None] * micros
     next_backs, next_factors = [None] * micros, [None] * micros
     for layer in (1, 0):
         w_in, w_back = projections[layer]
@@ -1261,27 +1458,32 @@
                 spread,
                 gather,
                 heads,
+                VMEM_LIMIT if layer == 1 and m == last else BACK_VMEM,
             )
             totals = totals + sums
             gpres[m] = gpre
-            if spreading is not None:
-                spread_back(*spreading, gpre)
-                j = spreading[0][1]
-                backs[j], factors[j] = next_backs[j], next_factors[j]
-                spreading = None
             ready = gpre
-            earlier = None
             if waiting is not None:
                 own = finish_back(waiting, gpre)
                 ready = after(gpre, *own)
-                earlier = (waiting, own)
+            if layer == 1 and m == 0:
+                grad_in = weight_grad(normeds[1], gpres)
+                ready = after(ready, grad_in)
             part = dot_nt(ready, w_in).astype(BF16)
+            if waiting is not None:
+                spread_back(waiting, own, part)
+                if layer == 0 and waiting[0] == 1:
+                    backs[0], factors[0] = next_backs[0], next_factors[0]
+                    small[1] = small_of(1, above)
             beside = ()
             if layer == 1:
                 outs[m] = dot_nt(after(k["u"], part), w_back).astype(BF16)
                 beside = (outs[m],)
             waiting = (layer, m, Sum(part, core, half, (), beside))
-        grad_in = weight_grad(normeds[layer], [after(v, waiting[2].sent) for v in gpres])
+            if layer == 0 and m == last:
+                outs = [Sum(out, core, half, (waiting[2].sent,)) for out in outs]
+        if layer == 0:
+            grad_in = weight_grad(normeds[0], [after(v, waiting[2].sent) for v in gpres])
         if layer == 1 or not in_line:
             reduced[layer] = (reduce_rows(grad_in), reduced_back)
         if layer == 0:
@@ -1291,29 +1493,16 @@
             grad_back = weight_grad(backs, mixed)
             if not in_line:
                 reduced[0] = (reduced[0][0], reduce_rows(grad_back))
-            outs = [Sum(out, core, half, (gpres[0],)) for out in outs]
-        if earlier is not None:
-            spread_back(*earlier, grad_in)
-        own = finish_back(waiting, grad_in)
         if layer == 1:
-            spreading = (waiting, own)
-            second_factors = factors
-            backs = [None if v is None else after(v, *own) for v in next_backs]
-            factors = list(next_factors)
-        waiting = None
-        small[layer] = jnp.concatenate(
-            [
-                totals[:6],
-                jnp.concatenate(
-                    [sum(gain_parts[layer]).reshape(2, -1), totals[6:, channels:]], axis=1
-                ),
-            ]
-        )
+            second_factors, above = factors, totals
+            backs, factors = list(next_backs), list(next_factors)
+    finish_back(waiting, grad_in)
+    small[0] = small_of(0, totals)
 
     outputs_rows = []
     for m in range(micros):
         r = lax.dynamic_slice_in_dim(second_factors[m], (2 * half + core) * rows, rows, 0)[:, :1]
-        outputs_rows.append(hiddens[1][m] + r * outs[m].done(grad_in))
+        outputs_rows.append(hiddens[1][m] + r * outs[m].done(gpres[0]))
 
     def placed_rows(parts):
         own = jnp.where(core == 0, parts[0], parts[1])
@@ -1355,7 +1544,7 @@
     def joined(begin, end, i=0):
         return jnp.concatenate([low_half[i][:, begin:end], high_half[i][:, begin:end]], axis=1)
 
-    g_zx = jnp.stack([joined(0, channels), joined(channels, 2 * channels)], axis=1)
+    g_zx = join_halves(first_own[0], first_other[0], second_own[0], second_other[0], channels)
     at = 2 * channels
     g_bc = low_half[0][:, at : at + shared] + high_half[0][:, at : at + shared]
     g_bc = g_bc + swap_tp(g_bc)

time: 883 us -> 851 us (0.964)
  waiting for transfers between devices: 57.4 us -> 20.9 us
  Pallas kernels: 476 us -> 487 us
  other arithmetic: 68.5 us -> 59 us
    all_gather x3 -> x2, waiting for transfers between devices: 41.9 us -> 0.01 us  [the longest x1 0.01 us: local(): second = (over_fsdp(after(second_gate, gains), axis=0), second_rest)]
    unnamed x360 -> x345, local copies, waits for them, and re-layouts: 53.1 us -> 53.9 us
  transfers between devices with their start and end apart: 45 -> 44, of which waited for: 11 -> 10; matrix products, arithmetic and copies ran while one was open for 25% -> 25% of each run, Pallas kernels for 55% -> 34%
where the time goes in v4:
time: 851 us; the launch traced here: 842 us
  Pallas kernels  487 us (57%)
  matrix products  141 us (17%)
  local copies, waits for them, and re-layouts  88 us (10%)
  other arithmetic  59 us (7%)
  starting transfers between devices  29.3 us (3%)
  waiting for transfers between devices  20.9 us (2%)
  between operations  16.4 us (2%)
    pallas_call x1, Pallas kernels, start_gather(): pl.pallas_call(functools.partial(start_kernel, count=count, micros=micros...  202 us
    pallas_call x1, Pallas kernels, reduce_line(): pl.pallas_call(functools.partial(reduce_kernel, count=count), out_shape=[...  164 us
    pallas_call x4, Pallas kernels, mixer_backward(): pl.pallas_call(body, grid=(steps,), in_specs=[by_row(channels), by_row(2)...  79 us
    unnamed x345, local copies, waits for them, and re-layouts  53.9 us
    dot_general x8, matrix products, dot_nt(): lax.dot_general(a, b, (((1,), (1,)), ((), ())), preferred_element_type=F32)  49.7 us
    dot_general x12, matrix products, dot_nn(): lax.dot_general(a, b, (((1,), (0,)), ((), ())), preferred_element_type=F32)  49.5 us
    dot_general x4, matrix products, weight_grad(): lax.dot_general(jnp.concatenate(left), jnp.concatenate(right), over_token...  42 us
    pallas_call x4, Pallas kernels, mixer_forward(): pl.pallas_call(body, grid=(steps,), in_specs=[by_row(channels), by_row(wi...  38.3 us
  transfers between devices with their start and end apart: 44, of which 10 were waited for; matrix products, arithmetic and copies ran while one was open for 25% of the time, Pallas kernels for 34%

profile of v4, /device:TPU:9, one launch (start us, length us, event | category | flops | bytes accessed | tf_op | source)
XLA Modules:
  0.0 841.9 jit_solution(13289889216598109050)
XLA Ops:
  7.2 3.0 constant_dynamic-slice_fusion.15
  27.5 202.2 %start_gather.1 = (bf16[8,256,2432]{2,1,0:T(8,128)(2,1)}, bf16[8,256,1024]{2,1,0:T(8,128)(2,1)}, bf16[8,256,1408]{2,1,0:T(8,128)(2,1)}, f32[2,8,8,128]{3,2,1,0:T...) custom-call(bf16[256,2432]{1,0:T(8,128)(2,1)} %slice.213.refs_0_, ...), custom_call_target="tpu_custom_call" | custom-call | flops 170000007168 | bytes 1000 | tf_op jit(solution)/shard_map/start_gather/pallas_call | solution.py:802
  230.6 5.3 fusion.32.refs_0_.refs_2_
  236.9 3.4 fusion.2.refs_1_.refs_3_.refs_4_
  240.4 9.2 %mixer_forward.4 = (bf16[512,1024]{1,0:T(8,128)(2,1)S(1)}, f32[512,1]{1,0:T(8,128)S(1)}, f32[512,1024]{1,0:T(8,128)S(1)}, f32[4,128,1024]{2,1,0:T(8,128)S(1)}, f32[128,1024]{1,0:T(8,128)S(1)}) custom-call(f32[512,1024]{1,0:T(8,128)S(1)} %fusion.32.refs_0_.refs_2_, f32[512,1408]{1,0:T(8,128)S(1)} %fusion.2.refs_1_.refs_3_.refs_4_, ...), custom_call_target="tpu_custom_call" | custom-call | flops 1000 | bytes 1000 | tf_op jit(solution)/shard_map/mixer_forward/pallas_call | solution.py:345
  255.1 4.9 convolution_convert_fusion.5
  261.5 5.8 fusion.refs_1_.refs_3_.refs_4_
  267.3 5.6 fusion.30.refs_0_.refs_2_
  276.4 10.2 %mixer_forward.5 = (bf16[512,1024]{1,0:T(8,128)(2,1)S(1)}, f32[512,1]{1,0:T(8,128)S(1)}, f32[512,1024]{1,0:T(8,128)S(1)}, f32[4,128,1024]{2,1,0:T(8,128)S(1)}, f32[128,1024]{1,0:T(8,128)}) custom-call(f32[512,1024]{1,0:T(8,128)S(1)} %fusion.30.refs_0_.refs_2_, f32[512,1408]{1,0:T(8,128)S(1)} %fusion.refs_1_.refs_3_.refs_4_, ...), custom_call_target="tpu_custom_call" | custom-call | flops 1000 | bytes 1000 | tf_op jit(solution)/shard_map/mixer_forward/pallas_call | solution.py:345
  291.2 2.4 convolution_convert_fusion.4
  295.3 6.7 collective-permute-done.5
  311.1 3.0 slice-done
  314.7 3.4 fusion.108.refs_1_.refs_3_.refs_4_
  318.2 5.1 collective-permute-done.10
  325.7 5.2 fusion.107.refs_0_.refs_2_
  331.0 9.1 %mixer_forward.6 = (bf16[512,1024]{1,0:T(8,128)(2,1)S(1)}, f32[512,1]{1,0:T(8,128)S(1)}, f32[512,1024]{1,0:T(8,128)S(1)}, f32[4,128,1024]{2,1,0:T(8,128)S(1)}, f32[128,1024]{1,0:T(8,128)S(1)}) custom-call(f32[512,1024]{1,0:T(8,128)S(1)} %fusion.107.refs_0_.refs_2_, f32[512,1408]{1,0:T(8,128)S(1)} %fusion.108.refs_1_.refs_3_.refs_4_, ...), custom_call_target="tpu_custom_call" | custom-call | flops 1000 | bytes 1000 | tf_op jit(solution)/shard_map/mixer_forward/pallas_call | solution.py:345
  351.3 2.6 copy-done.98
  353.8 2.3 fusion.109.refs_0_.refs_2_
  356.2 3.4 fusion.110.refs_1_.refs_3_.refs_4_
  359.7 9.9 %mixer_forward.7 = (bf16[512,1024]{1,0:T(8,128)(2,1)S(1)}, f32[512,1]{1,0:T(8,128)S(1)}, f32[512,1024]{1,0:T(8,128)S(1)}, f32[4,128,1024]{2,1,0:T(8,128)S(1)}, f32[128,1024]{1,0:T(8,128)}) custom-call(f32[512,1024]{1,0:T(8,128)S(1)} %fusion.109.refs_0_.refs_2_, f32[512,1408]{1,0:T(8,128)S(1)} %fusion.110.refs_1_.refs_3_.refs_4_, ...), custom_call_target="tpu_custom_call" | custom-call | flops 1000 | bytes 1000 | tf_op jit(solution)/shard_map/mixer_forward/pallas_call | solution.py:345
  372.3 2.6 constant_dynamic-update-slice_fusion.1
  374.9 3.1 constant_dynamic-update-slice_fusion
  378.0 6.6 fusion.37
  384.6 3.7 fusion.39
  394.6 6.2 fusion.27
  403.4 21.1 %mixer_backward.4 = (bf16[512,2432]{1,0:T(8,128)(2,1)}, f32[128,1024]{1,0:T(8,128)}, f32[8,1280]{1,0:T(8,128)}, f32[8,1280]{1,0:T(8,128)}) custom-call(f32[512,1024]{1,0:T(8,128)} %get-tuple-element.137.refs_0_, f32[512,2]{1,0:T(8,128)} %copy.72.refs_1_, f32[512,1024]{1,0:T(8,128)} %copy-done.18, f32[512,1408]{1,0:T(8,128)} %copy-done.3, ...), custom_call_target="tpu_custom_call" | custom-call | flops 1000 | bytes 1000 | tf_op jit(solution)/shard_map/mixer_backward/pallas_call | solution.py:396
  424.5 10.5 %convolution_convert_fusion.9 = bf16[512,2048]{1,0:T(8,128)(2,1)S(1)} fusion(bf16[512,2432]{1,0:T(8,128)(2,1)} %get-tuple-element.140, bf16[2048,2432]{1,0:T(8,128)(2,1)} %constant_dynamic-update-slice_fusion), kind=kOutput, calls=%fused_computation.42 | convolution fusion | flops 5101322240 | bytes 14548992 | tf_op jit(solution)/shard_map/dot_general | solution.py:34
  437.6 3.7 convolution_convert_fusion.3
  441.5 2.5 dynamic-slice_bitcast_fusion.2
  446.2 2.1 convert_add_fusion.5
  451.7 20.0 %mixer_backward.5 = (bf16[512,2432]{1,0:T(8,128)(2,1)S(1)}, f32[128,1024]{1,0:T(8,128)}, f32[8,1280]{1,0:T(8,128)}, f32[8,1280]{1,0:T(8,128)S(1)}) custom-call(f32[512,1024]{1,0:T(8,128)S(1)} %copy-done.36, f32[512,2]{1,0:T(8,128)S(1)} %copy.74.refs_1_, f32[512,1024]{1,0:T(8,128)S(1)} %copy-done.17, f32[512,1408]{1,0:T(8,128)} %copy-done.1, ...), custom_call_target="tpu_custom_call" | custom-call | flops 1000 | bytes 1000 | tf_op jit(solution)/shard_map/mixer_backward/pallas_call | solution.py:396
  473.1 13.3 %convolution_convert_fusion.1 = bf16[2048,2432]{1,0:T(8,128)(2,1)} fusion(bf16[512,2432]{1,0:T(8,128)(2,1)S(1)} %copy-done.156, bf16[512,2432]{1,0:T(8,128)(2,1)S(1)} %get-tuple-element.151, bf16[512,2048]{1,0:T(8,128)(2,1)S(1)} %bitcast.428, bf16[512,2048]{1,0:T(8,128)(2,1)S(1)} %bitcast.423), kind=kOutput, calls=%fused_computation.1 | convolution fusion | flops 10223878144 | bytes 19136512 | tf_op jit(solution)/shard_map/dot_general | solution.py:1370
  496.7 8.6 %convolution_convert_fusion.8 = bf16[512,2048]{1,0:T(8,128)(2,1)S(1)} fusion(bf16[512,2432]{1,0:T(8,128)(2,1)S(1)} %copy-done.65, bf16[2048,2432]{1,0:T(8,128)(2,1)} %constant_dynamic-update-slice_fusion), kind=kOutput, calls=%fused_computation.41 | convolution fusion | flops 5101322240 | bytes 14548992 | tf_op jit(solution)/shard_map/dot_general | solution.py:34
  507.3 2.4 convolution_convert_fusion.2
  520.7 2.8 copy-done.159
  523.5 2.3 fusion.111.refs_0_
  526.6 18.6 %mixer_backward.6 = (bf16[512,2432]{1,0:T(8,128)(2,1)S(1)}, f32[128,1024]{1,0:T(8,128)S(1)}, f32[8,1280]{1,0:T(8,128)S(1)}, f32[8,1280]{1,0:T(8,128)S(1)}) custom-call(f32[512,1024]{1,0:T(8,128)S(1)} %fusion.111.refs_0_, f32[512,2]{1,0:T(8,128)S(1)} %bitcast.390, f32[512,1024]{1,0:T(8,128)S(1)} %copy-done.15, f32[512,1408]{1,0:T(8,128)} %copy-done.2, ...), custom_call_target="tpu_custom_call" | custom-call | flops 1000 | bytes 1000 | tf_op jit(solution)/shard_map/mixer_backward/pallas_call | solution.py:396
  545.7 2.0 copy-done.83
  550.1 8.4 %convolution_convert_fusion.7 = bf16[512,2048]{1,0:T(8,128)(2,1)S(1)} fusion(bf16[512,2432]{1,0:T(8,128)(2,1)S(1)} %get-tuple-element.177, bf16[2048,2432]{1,0:T(8,128)(2,1)} %bitcast.475), kind=kOutput, calls=%fused_computation.40 | convolution fusion | flops 5101322240 | bytes 14548992 | tf_op jit(solution)/shard_map/dot_general | solution.py:34
  573.7 2.7 copy-done.160
  576.4 2.4 fusion.112.refs_0_
  579.4 19.4 %mixer_backward.7 = (bf16[512,2432]{1,0:T(8,128)(2,1)S(1)}, f32[128,1024]{1,0:T(8,128)}, f32[8,1280]{1,0:T(8,128)}, f32[8,1280]{1,0:T(8,128)S(1)}) custom-call(f32[512,1024]{1,0:T(8,128)S(1)} %fusion.112.refs_0_, f32[512,2]{1,0:T(8,128)S(1)} %bitcast.388, f32[512,1024]{1,0:T(8,128)S(1)} %copy-done.13, f32[512,1408]{1,0:T(8,128)} %copy-done, ...), custom_call_target="tpu_custom_call" | custom-call | flops 1000 | bytes 1000 | tf_op jit(solution)/shard_map/mixer_backward/pallas_call | solution.py:396
  600.4 8.9 %convolution_convert_fusion.6 = bf16[512,2048]{1,0:T(8,128)(2,1)S(1)} fusion(bf16[512,2432]{1,0:T(8,128)(2,1)S(1)} %get-tuple-element.176, bf16[2048,2432]{1,0:T(8,128)(2,1)} %bitcast.476), kind=kOutput, calls=%fused_computation.39 | convolution fusion | flops 5101322240 | bytes 14548992 | tf_op jit(solution)/shard_map/dot_general | solution.py:34
  610.7 2.7 broadcast_select_fusion.4
  614.7 6.2 fusion.24
  622.7 16.3 %convolution_convert_fusion = bf16[2048,2432]{1,0:T(8,128)(2,1)} fusion(bf16[512,2432]{1,0:T(8,128)(2,1)S(1)} %copy-done.63, bf16[512,2432]{1,0:T(8,128)(2,1)S(1)} %get-tuple-element.176, bf16[512,2048]{1,0:T(8,128)(2,1)} %bitcast.485, bf16[512,2048]{1,0:T(8,128)(2,1)} %bitcast.483), kind=kOutput, calls=%fused_computation | convolution fusion | flops 10223878144 | bytes 19136512 | tf_op jit(solution)/shard_map/dot_general | solution.py:1370
  647.7 163.6 %grads_reduce.1 = (f32[256,2432]{1,0:T(8,128)}, f32[256,1024]{1,0:T(8,128)}, f32[256,2432]{1,0:T(8,128)}, f32[256,1024]{1,0:T(8,128)}, f32[8,1280]{1,0:T(8,128)}, /*index=5*/f32[8,1280]{1,0:T(8,128)}, f32[8,1280]{1,0:T(8,128)}) custom-call(bf16[8,256,2432]{2,1,0:T(8,128)(2,1)} %bitcast.391, bf16[8,256,1024]{2,1,0:T(8,128)(2,1)} %bitcast.402, ...), custom_call_target="tpu_custom_call" | custom-call | flops 1000 | bytes 1000 | tf_op jit(solution)/shard_map/grads_reduce/pallas_call | solution.py:1109
  829.6 4.1 join_halves.1
  (608 shorter events, 156.2 us)
Async XLA Ops:
  7.2 318.6 %all-gather.3.cloned.1.call-start = ((), (), s32[]{:S(2)}) async-start(), calls=%async_computation.2 | async-start | bytes 4718592 | tf_op jit(solution)/shard_map/all_gather | solution.py:1284
  13.1 8.4 %collective-permute-start = (bf16[256,3456]{1,0:T(8,128)(2,1)}, bf16[256,3456]{1,0:T(8,128)(2,1)}, u32[]{:S(2)}, u32[]{:S(2)}) collective-permute-start(bf16[256,3456]{1,0:T(8,128)(2,1)} %fusion.50), channel_id=1, source_target_pairs={{0,16},{16,0},{1,17},{17,1},{2,18},{18,2},{3,19},{19,3},{4,20},{20... | collective-permute-start | bytes 5308424 | tf_op jit(solution)/shard_map/ppermute | solution.py:1143
  230.5 129.2 %copy-start.50 = (f32[8,1280]{1,0:T(8,128)}, f32[8,1280]{1,0:T(8,128)S(1)}, u32[]{:S(2)}) copy-start(f32[8,1280]{1,0:T(8,128)S(1)} %get-tuple-element.282.refs_4_.refs_10_) | copy-start | bytes 122884
  230.5 147.5 %all-gather.5.cloned.1.call-start = ((), (), s32[]{:S(2)}) async-start(), calls=%async_computation.3 | async-start | bytes 4718592 | tf_op jit(solution)/shard_map/all_gather | solution.py:1285
  240.3 36.1 %copy-start = (f32[512,1408]{1,0:T(8,128)}, f32[512,1408]{1,0:T(8,128)S(1)}, u32[]{:S(2)}) copy-start(f32[512,1408]{1,0:T(8,128)S(1)} %fusion.2.refs_1_.refs_3_.refs_4_) | copy-start | bytes 8650756
  240.3 90.7 %copy-start.39 = (f32[8,1280]{1,0:T(8,128)}, f32[8,1280]{1,0:T(8,128)S(1)}, u32[]{:S(2)}) copy-start(f32[8,1280]{1,0:T(8,128)S(1)} %broadcast_in_dim.22.refs_2_.refs_9_.refs_5_) | copy-start | bytes 122884
  254.3 18.7 %collective-permute-start.1 = (f32[2,128]{1,0:T(2,128)S(1)}, f32[2,128]{1,0:T(2,128)S(1)}, u32[]{:S(2)}, u32[]{:S(2)}) collective-permute-start(f32[2,128]{1,0:T(2,128)S(1)} %bitcast.468), channel_id=1, source_target_pairs={{0,16},{16,0},{1,17},{17,1},{2,18},{18,2},{3,19},{19,3},{4,20},{20... | collective-permute-start | bytes 3080 | tf_op jit(solution)/shard_map/ppermute | solution.py:1143
  260.1 12.9 %collective-permute-start.3 = (bf16[2,128,2048]{2,1,0:T(8,128)(2,1)S(1)}, bf16[2,128,2048]{2,1,0:T(8,128)(2,1)S(1)}, u32[]{:S(2)}, u32[]{:S(2)}) collective-permute-start(bf16[2,128,2048]{2,1,0:T(8,128)(2,1)S(1)} %dynamic-slice_bitcast_fusion.9), channel_id=1, source_target_pairs={{0,16},{16,0},{1,17},{17,1},{2,18},{18,2},{3,19},{19,3},{4,20},{20... | collective-permute-start | bytes 3145736 | tf_op jit(solution)/shard_map/ppermute | solution.py:1143
  273.4 13.7 %collective-permute-start.4 = (bf16[128,2048]{1,0:T(8,128)(2,1)S(1)}, bf16[128,2048]{1,0:T(8,128)(2,1)S(1)}, u32[]{:S(2)}, u32[]{:S(2)}) collective-permute-start(bf16[128,2048]{1,0:T(8,128)(2,1)S(1)} %fusion.69), channel_id=1, source_target_pairs={{0,1},{1,0},{2,3},{3,2},{4,5},{5,4},{6,7},{7,6},{8,9},{9,8},{10,11... | collective-permute-start | bytes 1572872 | tf_op jit(solution)/shard_map/ppermute | solution.py:1147
  274.8 12.4 %collective-permute-start.2 = (f32[128]{0:T(128)S(1)}, f32[128]{0:T(128)S(1)}, u32[]{:S(2)}, u32[]{:S(2)}) collective-permute-start(f32[128]{0:T(128)S(1)} %fusion.89), channel_id=1, source_target_pairs={{0,1},{1,0},{2,3},{3,2},{4,5},{5,4},{6,7},{7,6},{8,9},{9,8},{10,11... | collective-permute-start | bytes 1544 | tf_op jit(solution)/shard_map/ppermute | solution.py:1147
  288.9 13.1 %collective-permute-start.5 = (bf16[128,2048]{1,0:T(8,128)(2,1)S(1)}, bf16[128,2048]{1,0:T(8,128)(2,1)S(1)}, u32[]{:S(2)}, u32[]{:S(2)}) collective-permute-start(bf16[128,2048]{1,0:T(8,128)(2,1)S(1)} %multiply_convert_fusion.3), channel_id=1, source_target_pairs={{0,1},{1,0},{2,3},{3,2},{4,5},{5,4},{6,7},{7,6},{8,9},{9,8},{10,11... | collective-permute-start | bytes 1572872 | tf_op jit(solution)/shard_map/ppermute | solution.py:1147
  294.8 13.6 %collective-permute-start.7 = (bf16[2,128,2048]{2,1,0:T(8,128)(2,1)}, bf16[2,128,2048]{2,1,0:T(8,128)(2,1)}, u32[]{:S(2)}, u32[]{:S(2)}) collective-permute-start(bf16[2,128,2048]{2,1,0:T(8,128)(2,1)} %dynamic-slice_bitcast_fusion.8), channel_id=1, source_target_pairs={{0,16},{16,0},{1,17},{17,1},{2,18},{18,2},{3,19},{19,3},{4,20},{20... | collective-permute-start | bytes 3145736 | tf_op jit(solution)/shard_map/ppermute | solution.py:1143
  303.4 7.2 collective-permute-start.6
  304.9 2.1 collective-permute-start.8
  305.0 510.0 %reduce-scatter.5.cloned.1.call-start = ((), (), s32[]{:S(2)}) async-start(), calls=%async_computation.5 | async-start | bytes 4718592 | tf_op jit(solution)/shard_map/reduce_scatter | solution.py:1419
  307.0 11.2 %collective-permute-start.9 = (f32[128]{0:T(128)S(1)}, f32[128]{0:T(128)S(1)}, u32[]{:S(2)}, u32[]{:S(2)}) collective-permute-start(f32[128]{0:T(128)S(1)} %fusion.90), channel_id=1, source_target_pairs={{0,1},{1,0},{2,3},{3,2},{4,5},{5,4},{6,7},{7,6},{8,9},{9,8},{10,11... | collective-permute-start | bytes 1544 | tf_op jit(solution)/shard_map/ppermute | solution.py:1147
  310.3 12.9 %collective-permute-start.10 = (bf16[128,2048]{1,0:T(8,128)(2,1)S(1)}, bf16[128,2048]{1,0:T(8,128)(2,1)S(1)}, u32[]{:S(2)}, u32[]{:S(2)}) collective-permute-start(bf16[128,2048]{1,0:T(8,128)(2,1)S(1)} %fusion.70), channel_id=1, source_target_pairs={{0,1},{1,0},{2,3},{3,2},{4,5},{5,4},{6,7},{7,6},{8,9},{9,8},{10,11... | collective-permute-start | bytes 1572872 | tf_op jit(solution)/shard_map/ppermute | solution.py:1147
  318.2 28.4 %copy-start.1 = (f32[512,1408]{1,0:T(8,128)}, f32[512,1408]{1,0:T(8,128)S(1)}, u32[]{:S(2)}) copy-start(f32[512,1408]{1,0:T(8,128)S(1)} %fusion.108.refs_1_.refs_3_.refs_4_) | copy-start | bytes 8650756
  325.6 16.2 %collective-permute-start.11 = (bf16[128,2048]{1,0:T(8,128)(2,1)}, bf16[128,2048]{1,0:T(8,128)(2,1)}, u32[]{:S(2)}, u32[]{:S(2)}) collective-permute-start(bf16[128,2048]{1,0:T(8,128)(2,1)} %multiply_convert_fusion.2), channel_id=1, source_target_pairs={{0,1},{1,0},{2,3},{3,2},{4,5},{5,4},{6,7},{7,6},{8,9},{9,8},{10,11... | collective-permute-start | bytes 1572872 | tf_op jit(solution)/shard_map/ppermute | solution.py:1147
  344.8 4.5 collective-permute-start.12
  388.5 1.3 collective-permute-start.13
  389.8 2.5 collective-permute-start.14
  400.8 417.4 %reduce-scatter.3.cloned.1.call-start = ((), (), s32[]{:S(2)}) async-start(), calls=%async_computation.4 | async-start | bytes 11206656 | tf_op jit(solution)/shard_map/reduce_scatter | solution.py:1419
  436.0 10.2 %collective-permute-start.15 = (bf16[2,128,2048]{2,1,0:T(8,128)(2,1)}, bf16[2,128,2048]{2,1,0:T(8,128)(2,1)}, u32[]{:S(2)}, u32[]{:S(2)}) collective-permute-start(bf16[2,128,2048]{2,1,0:T(8,128)(2,1)} %dynamic-slice_bitcast_fusion.7), channel_id=1, source_target_pairs={{0,16},{16,0},{1,17},{17,1},{2,18},{18,2},{3,19},{19,3},{4,20},{20... | collective-permute-start | bytes 3145736 | tf_op jit(solution)/shard_map/ppermute | solution.py:1143
  444.1 43.1 %collective-permute-start.30 = (bf16[2,128,2048]{2,1,0:T(8,128)(2,1)}, bf16[2,128,2048]{2,1,0:T(8,128)(2,1)}, u32[]{:S(2)}, u32[]{:S(2)}) collective-permute-start(bf16[2,128,2048]{2,1,0:T(8,128)(2,1)} %dynamic-slice_bitcast_fusion.2), channel_id=1, source_target_pairs={{0,16},{16,0},{1,17},{17,1},{2,18},{18,2},{3,19},{19,3},{4,20},{20... | collective-permute-start | bytes 3145736 | tf_op jit(solution)/shard_map/ppermute | solution.py:1143
  449.3 41.9 %collective-permute-start.16 = (bf16[128,2048]{1,0:T(8,128)(2,1)}, bf16[128,2048]{1,0:T(8,128)(2,1)S(1)}, u32[]{:S(2)}, u32[]{:S(2)}) collective-permute-start(bf16[128,2048]{1,0:T(8,128)(2,1)} %fusion.71), channel_id=1, source_target_pairs={{0,1},{1,0},{2,3},{3,2},{4,5},{5,4},{6,7},{7,6},{8,9},{9,8},{10,11... | collective-permute-start | bytes 1572872 | tf_op jit(solution)/shard_map/ppermute | solution.py:1147
  495.1 14.6 %collective-permute-start.21 = (f32[128,2]{0,1:T(2,128)S(1)}, f32[128,2]{0,1:T(2,128)S(1)}, u32[]{:S(2)}, u32[]{:S(2)}) collective-permute-start(f32[128,2]{0,1:T(2,128)S(1)} %pad_maximum_fusion.18), channel_id=1, source_target_pairs={{0,1},{1,0},{2,3},{3,2},{4,5},{5,4},{6,7},{7,6},{8,9},{9,8},{10,11... | collective-permute-start | bytes 3080 | tf_op jit(solution)/shard_map/ppermute | solution.py:1147
  495.4 17.9 %collective-permute-start.18 = (bf16[128,2048]{1,0:T(8,128)(2,1)S(1)}, bf16[128,2048]{1,0:T(8,128)(2,1)}, u32[]{:S(2)}, u32[]{:S(2)}) collective-permute-start(bf16[128,2048]{1,0:T(8,128)(2,1)S(1)} %convert_element_type.276), channel_id=1, source_target_pairs={{0,1},{1,0},{2,3},{3,2},{4,5},{5,4},{6,7},{7,6},{8,9},{9,8},{10,11... | collective-permute-start | bytes 1572872 | tf_op jit(solution)/shard_map/ppermute | solution.py:1147
  506.3 8.9 %collective-permute-start.20 = (bf16[2,128,2048]{2,1,0:T(8,128)(2,1)}, bf16[2,128,2048]{2,1,0:T(8,128)(2,1)}, u32[]{:S(2)}, u32[]{:S(2)}) collective-permute-start(bf16[2,128,2048]{2,1,0:T(8,128)(2,1)} %dynamic-slice_bitcast_fusion.4), channel_id=1, source_target_pairs={{0,16},{16,0},{1,17},{17,1},{2,18},{18,2},{3,19},{19,3},{4,20},{20... | collective-permute-start | bytes 3145736 | tf_op jit(solution)/shard_map/ppermute | solution.py:1143
  509.7 1.9 collective-permute-start.22
  511.7 5.5 collective-permute-start.17
  514.7 5.0 collective-permute-start.19
  516.9 28.3 %collective-permute-start.23 = (bf16[128,2048]{1,0:T(8,128)(2,1)S(1)}, bf16[128,2048]{1,0:T(8,128)(2,1)S(1)}, u32[]{:S(2)}, u32[]{:S(2)}) collective-permute-start(bf16[128,2048]{1,0:T(8,128)(2,1)S(1)} %fusion.72), channel_id=1, source_target_pairs={{0,1},{1,0},{2,3},{3,2},{4,5},{5,4},{6,7},{7,6},{8,9},{9,8},{10,11... | collective-permute-start | bytes 1572872 | tf_op jit(solution)/shard_map/ppermute | solution.py:1147
  548.5 13.6 %collective-permute-start.28 = (f32[128,2]{0,1:T(2,128)S(1)}, f32[128,2]{0,1:T(2,128)S(1)}, u32[]{:S(2)}, u32[]{:S(2)}) collective-permute-start(f32[128,2]{0,1:T(2,128)S(1)} %pad_maximum_fusion.19), channel_id=1, source_target_pairs={{0,1},{1,0},{2,3},{3,2},{4,5},{5,4},{6,7},{7,6},{8,9},{9,8},{10,11... | collective-permute-start | bytes 3080 | tf_op jit(solution)/shard_map/ppermute | solution.py:1147
  549.9 14.6 %collective-permute-start.26 = (bf16[128,2048]{1,0:T(8,128)(2,1)S(1)}, bf16[128,2048]{1,0:T(8,128)(2,1)}, u32[]{:S(2)}, u32[]{:S(2)}) collective-permute-start(bf16[128,2048]{1,0:T(8,128)(2,1)S(1)} %convert_element_type.290), channel_id=1, source_target_pairs={{0,1},{1,0},{2,3},{3,2},{4,5},{5,4},{6,7},{7,6},{8,9},{9,8},{10,11... | collective-permute-start | bytes 1572872 | tf_op jit(solution)/shard_map/ppermute | solution.py:1147
  560.9 7.0 collective-permute-start.24
  562.1 2.1 collective-permute-start.29
  566.1 7.0 collective-permute-start.27
  570.3 28.5 %collective-permute-start.33 = (bf16[128,2048]{1,0:T(8,128)(2,1)}, bf16[128,2048]{1,0:T(8,128)(2,1)S(1)}, u32[]{:S(2)}, u32[]{:S(2)}) collective-permute-start(bf16[128,2048]{1,0:T(8,128)(2,1)} %fusion.73), channel_id=1, source_target_pairs={{0,1},{1,0},{2,3},{3,2},{4,5},{5,4},{6,7},{7,6},{8,9},{9,8},{10,11... | collective-permute-start | bytes 1572872 | tf_op jit(solution)/shard_map/ppermute | solution.py:1147
  571.6 39.0 %collective-permute-start.31 = (bf16[128,2048]{1,0:T(8,128)(2,1)}, bf16[128,2048]{1,0:T(8,128)(2,1)S(1)}, u32[]{:S(2)}, u32[]{:S(2)}) collective-permute-start(bf16[128,2048]{1,0:T(8,128)(2,1)} %dynamic-slice_bitcast_fusion.1), channel_id=1, source_target_pairs={{0,1},{1,0},{2,3},{3,2},{4,5},{5,4},{6,7},{7,6},{8,9},{9,8},{10,11... | collective-permute-start | bytes 1572872 | tf_op jit(solution)/shard_map/ppermute | solution.py:1147
  571.8 38.9 %collective-permute-start.25 = (bf16[128,2048]{1,0:T(8,128)(2,1)}, bf16[128,2048]{1,0:T(8,128)(2,1)}, u32[]{:S(2)}, u32[]{:S(2)}) collective-permute-start(bf16[128,2048]{1,0:T(8,128)(2,1)} %dynamic-slice_bitcast_fusion.5), channel_id=1, source_target_pairs={{0,1},{1,0},{2,3},{3,2},{4,5},{5,4},{6,7},{7,6},{8,9},{9,8},{10,11... | collective-permute-start | bytes 1572872 | tf_op jit(solution)/shard_map/ppermute | solution.py:1147
  609.5 11.5 %collective-permute-start.34 = (bf16[2,128,2048]{2,1,0:T(8,128)(2,1)S(1)}, bf16[2,128,2048]{2,1,0:T(8,128)(2,1)S(1)}, u32[]{:S(2)}, u32[]{:S(2)}) collective-permute-start(bf16[2,128,2048]{2,1,0:T(8,128)(2,1)S(1)} %dynamic-slice_bitcast_fusion), channel_id=1, source_target_pairs={{0,16},{16,0},{1,17},{17,1},{2,18},{18,2},{3,19},{19,3},{4,20},{20... | collective-permute-start | bytes 3145736 | tf_op jit(solution)/shard_map/ppermute | solution.py:1143
  613.5 28.3 %collective-permute-start.32 = (f32[128,2048]{1,0:T(8,128)}, f32[128,2048]{1,0:T(8,128)S(1)}, u32[]{:S(2)}, u32[]{:S(2)}) collective-permute-start(f32[128,2048]{1,0:T(8,128)} %get-tuple-element.237), channel_id=1, source_target_pairs={{0,16},{16,0},{1,17},{17,1},{2,18},{18,2},{3,19},{19,3},{4,20},{20... | collective-permute-start | bytes 3145736 | tf_op jit(solution)/shard_map/ppermute | solution.py:1143
  621.4 17.6 %collective-permute-start.35 = (bf16[128,2048]{1,0:T(8,128)(2,1)S(1)}, bf16[128,2048]{1,0:T(8,128)(2,1)S(1)}, u32[]{:S(2)}, u32[]{:S(2)}) collective-permute-start(bf16[128,2048]{1,0:T(8,128)(2,1)S(1)} %fusion.74), channel_id=1, source_target_pairs={{0,1},{1,0},{2,3},{3,2},{4,5},{5,4},{6,7},{7,6},{8,9},{9,8},{10,11... | collective-permute-start | bytes 1572872 | tf_op jit(solution)/shard_map/ppermute | solution.py:1147
  641.7 3.0 collective-permute-start.36
  815.0 4.9 collective-permute-start.39
  818.2 3.2 collective-permute-start.37
  823.1 11.3 %collective-permute-start.38 = (f32[256,256]{1,0:T(8,128)S(1)}, f32[256,256]{1,0:T(8,128)S(1)}, u32[]{:S(2)}, u32[]{:S(2)}) collective-permute-start(f32[256,256]{1,0:T(8,128)S(1)} %slice_add_fusion), channel_id=1, source_target_pairs={{0,1},{1,0},{2,3},{3,2},{4,5},{5,4},{6,7},{7,6},{8,9},{9,8},{10,11... | collective-permute-start | bytes 786440 | tf_op jit(solution)/shard_map/ppermute | solution.py:1147
  (167 other events, 912.2 us)
Sparse Core Ops, SparseCore 0:
  230.6 70.9 all-gather.2
  305.1 70.8 all-gather.4
  400.9 88.1 reduce-scatter.4
  493.0 174.6 reduce-scatter.2

commit v5 on v4

--- a/solution.py
+++ b/solution.py
@@ -479,6 +479,7 @@
 MESH = pl.DeviceIdType.MESH
 DEEP = 4
 SIDEWAYS = 32
+SIDE_ROWS = 48
 
 
 def place_in_line():
@@ -512,8 +513,8 @@
     deep, side, device = place_in_line()
     above, below = jnp.minimum(deep + 1, DEEP - 1), jnp.maximum(deep - 1, 0)
     has_above, has_below = deep < DEEP - 1, deep > 0
-    main = [pl.ds(0, shard.shape[0] - SIDEWAYS) for shard in shards]
-    rest = [pl.ds(shard.shape[0] - SIDEWAYS, SIDEWAYS) for shard in shards]
+    main = [pl.ds(0, shard.shape[0] - SIDE_ROWS) for shard in shards]
+    rest = [pl.ds(shard.shape[0] - SIDE_ROWS, SIDE_ROWS) for shard in shards]
 
     def remote(source, place, send, recv, target):
         return pltpu.make_async_remote_copy(
@@ -694,11 +695,12 @@
     for step in range(1, lines):
         send_gain(step).start()
 
-    tokens = own.shape[0] // micros
+    tokens = own.shape[1] // 2
+    mine = pl.ds(pl.multiple_of(core * tokens, tokens), tokens)
 
     def token_copies(n):
-        m, held = n % micros, (rows_out, cotangent)[n // micros]
-        source = held.at[pl.ds(m * tokens, tokens)]
+        m = n % micros
+        source = rows_out.at[pl.ds(m * tokens, tokens)] if n < micros else cotangent.at[m, mine]
         place = targets[n].at[half, core]
         later = targets[n].at[1 - half, core]
         more = 2 * micros + n
@@ -771,9 +773,10 @@
         gain_row = jnp.concatenate(
             [gains[0, f, j : j + 1, :] for f in range(lines) for j in range(gain_rows)], axis=1
         )
-        h = own[...].astype(F32)
-        scale = lax.rsqrt(jnp.mean(h * h, axis=1, keepdims=True) + EPS)
-        rows_out[...] = (h * scale * gain_row).astype(BF16)
+        for m in range(micros):
+            h = own[m, mine].astype(F32)
+            scale = lax.rsqrt(jnp.mean(h * h, axis=1, keepdims=True) + EPS)
+            rows_out[m * tokens : (m + 1) * tokens] = (h * scale * gain_row).astype(BF16)
 
         for n in range(micros):
             for copy in token_copies(n)[:3]:
@@ -797,7 +800,7 @@
     shape = jax.ShapeDtypeStruct
     anywhere = pl.BlockSpec(memory_space=pl.ANY)
     vmem = pl.BlockSpec(memory_space=pltpu.VMEM)
-    rows, width = own.shape
+    rows, width = own.shape[0] * own.shape[1] // 2, own.shape[2]
     slab = (8, spread.shape[1] + params[2].shape[1])
     return pl.pallas_call(
         functools.partial(
@@ -818,7 +821,7 @@
         + [dma(lines)] * 2
         + [dma(2 * micros)] * 3
         + [dma(4 * micros)] * 2
-        + [pltpu.VMEM(own.shape, BF16), pltpu.VMEM(slab, F32)]
+        + [pltpu.VMEM((rows, width), BF16), pltpu.VMEM(slab, F32)]
         + [dma(1)] * 4,
         compiler_params=pltpu.CompilerParams(
             collective_id=1, has_side_effects=True, vmem_limit_bytes=VMEM_LIMIT
@@ -1108,7 +1111,7 @@
     vmem = pl.BlockSpec(memory_space=pltpu.VMEM)
     return pl.pallas_call(
         functools.partial(reduce_kernel, count=count),
-        out_shape=[shape(shard, F32) for shard in shards] * 2 + [shape(small.shape[1:], F32)] * 3,
+        out_shape=[shape(shard, BF16) for shard in shards] * 2 + [shape(small.shape[1:], F32)] * 3,
         in_specs=[pl.BlockSpec(memory_space=pl.ANY)] * count + [vmem],
         out_specs=[vmem] * (2 * count + 3),
         scratch_shapes=blocks(DEEP)
@@ -1249,10 +1252,8 @@
     got_shard = swap_core(weight_shard(1 - core))
     in_line = lax.axis_size("fsdp") == 2 * DEEP and lax.axis_size("tp") == 2
     over_fsdp = functools.partial(lax.all_gather, axis_name="fsdp", tiled=True)
-    shards = []
-    for layer in range(2):
-        shard = jnp.where(core == layer, own_shard, got_shard)
-        shards.append((shard[:, :in_width], shard[:, in_width:]))
+    def shard_of(layer, begin, end):
+        return jnp.where(core == layer, own_shard[:, begin:end], got_shard[:, begin:end])
 
     def own_rows(tensor):
         return [
@@ -1266,12 +1267,12 @@
         per_head = jnp.concatenate([dt_bias, a_log, d_skip])
         per_head = jnp.pad(per_head, ((0, 5), (0, LANES - per_head.shape[1])))
         params = (conv_x[0], conv_xb, conv_bc[0], conv_bcb, gate_gain, per_head)
-        second_gate, second_rest = shards[1][0][:, :channels], shards[1][0][:, channels:]
+        second_gate, second_back = shard_of(1, 0, channels), shard_of(1, in_width, None)
         w_in, w_back, second_rest, gains, slabs, *tokens = start_gather(
-            shards[0] + (second_rest,),
+            (shard_of(0, 0, in_width), shard_of(0, in_width, None), shard_of(1, channels, in_width)),
             packed,
-            jnp.concatenate(first),
-            jnp.concatenate(cotangents),
+            inputs[0],
+            cotangent[0],
             params,
             spread,
             micros,
@@ -1282,7 +1283,7 @@
         w_in, w_back, second_rest = (v.reshape(-1, v.shape[2]) for v in (w_in, w_back, second_rest))
         projections = [(w_in, w_back)]
         second = (over_fsdp(after(second_gate, gains), axis=0), second_rest)
-        projections.append((second, over_fsdp(after(shards[1][1], gains), axis=0)))
+        projections.append((second, over_fsdp(after(second_back, gains), axis=0)))
         gains = gains[:, :, :gain_rows].reshape(2, -1)
         tokens = [v.reshape(4 * rows, -1) for v in tokens]
         first_normed, everyones = tokens[:micros], tokens[micros:]
@@ -1290,12 +1291,16 @@
         own_slab, got_slab = slab_of(core), swap_core(slab_of(1 - core))
         slabs = [jnp.where(core == layer, own_slab, got_slab) for layer in range(2)]
         gain_pair = by_index(core, norm_gain[0], swap_core(norm_gain[0])).astype(F32)
-        projections = [tuple(over_fsdp(v, axis=0) for v in shards[0])]
+        projections = [
+            (
+                over_fsdp(shard_of(layer, 0, in_width), axis=0),
+                over_fsdp(shard_of(layer, in_width, None), axis=0),
+            )
+            for layer in range(2)
+        ]
         gains = over_fsdp(gain_pair.astype(BF16), axis=1).astype(F32)
         first_normed = None
         everyones = [gather_tokens(v, core, half) for v in cotangents]
-    if not in_line:
-        projections.append(tuple(over_fsdp(v, axis=0) for v in shards[1]))
 
     size = channels + shared
     zero_state = jnp.zeros((shared // 2, channels), F32)
@@ -1442,7 +1447,7 @@
                 reduced_back = weight_grad(backs, mixed)
                 q = after(q, reduced_back)
                 reduced_back = reduce_rows(reduced_back)
-            if waiting is not None:
+            if waiting is not None and not (layer == 0 and m == 0):
                 q = after(q, waiting[2].sent)
             gpre, state, e_rows, sums = mixer_backward(
                 q,

time: 851 us -> 841 us (0.988)
    unnamed x345 -> x331, local copies, waits for them, and re-layouts: 53.9 us -> 50.3 us
  transfers between devices with their start and end apart: 44 -> 44, of which waited for: 10 -> 9; matrix products, arithmetic and copies ran while one was open for 25% -> 25% of each run, Pallas kernels for 34% -> 34%
where the time goes in v5:
time: 841 us; the launch traced here: 832 us
  Pallas kernels  480 us (57%)
  matrix products  142 us (17%)
  local copies, waits for them, and re-layouts  83.6 us (10%)
  other arithmetic  59 us (7%)
  starting transfers between devices  29.1 us (3%)
  waiting for transfers between devices  22.5 us (3%)
  between operations  16.3 us (2%)
    pallas_call x1, Pallas kernels, start_gather(): pl.pallas_call(functools.partial(start_kernel, count=count, micros=micros...  198 us
    pallas_call x1, Pallas kernels, reduce_line(): pl.pallas_call(functools.partial(reduce_kernel, count=count), out_shape=[...  160 us
    pallas_call x4, Pallas kernels, mixer_backward(): pl.pallas_call(body, grid=(steps,), in_specs=[by_row(channels), by_row(2)...  79.1 us
    unnamed x331, local copies, waits for them, and re-layouts  50.3 us
    dot_general x8, matrix products, dot_nt(): lax.dot_general(a, b, (((1,), (1,)), ((), ())), preferred_element_type=F32)  49.7 us
    dot_general x12, matrix products, dot_nn(): lax.dot_general(a, b, (((1,), (0,)), ((), ())), preferred_element_type=F32)  49.5 us
    dot_general x4, matrix products, weight_grad(): lax.dot_general(jnp.concatenate(left), jnp.concatenate(right), over_token...  42.4 us
    pallas_call x4, Pallas kernels, mixer_forward(): pl.pallas_call(body, grid=(steps,), in_specs=[by_row(channels), by_row(wi...  38.3 us
  transfers between devices with their start and end apart: 44, of which 9 were waited for; matrix products, arithmetic and copies ran while one was open for 25% of the time, Pallas kernels for 34%

profile of v5, /device:TPU:9, one launch (start us, length us, event | category | flops | bytes accessed | tf_op | source)
XLA Modules:
  0.0 832.2 jit_solution(7563406115811367494)
XLA Ops:
  7.2 4.0 constant_dynamic-slice_fusion.15
  17.4 3.3 fusion.106
  24.6 198.2 %start_gather.1 = (bf16[8,256,2432]{2,1,0:T(8,128)(2,1)}, bf16[8,256,1024]{2,1,0:T(8,128)(2,1)}, bf16[8,256,1408]{2,1,0:T(8,128)(2,1)}, f32[2,8,8,128]{3,2,1,0:T...) custom-call(bf16[256,2432]{1,0:T(8,128)(2,1)} %get-tuple-element.264, ...), custom_call_target="tpu_custom_call" | custom-call | flops 170000007168 | bytes 1000 | tf_op jit(solution)/shard_map/start_gather/pallas_call | solution.py:805
  223.8 5.3 fusion.32.refs_0_.refs_2_
  230.0 3.4 fusion.2.refs_1_.refs_3_.refs_4_
  233.6 9.2 %mixer_forward.4 = (bf16[512,1024]{1,0:T(8,128)(2,1)S(1)}, f32[512,1]{1,0:T(8,128)S(1)}, f32[512,1024]{1,0:T(8,128)S(1)}, f32[4,128,1024]{2,1,0:T(8,128)S(1)}, f32[128,1024]{1,0:T(8,128)S(1)}) custom-call(f32[512,1024]{1,0:T(8,128)S(1)} %fusion.32.refs_0_.refs_2_, f32[512,1408]{1,0:T(8,128)S(1)} %fusion.2.refs_1_.refs_3_.refs_4_, ...), custom_call_target="tpu_custom_call" | custom-call | flops 1000 | bytes 1000 | tf_op jit(solution)/shard_map/mixer_forward/pallas_call | solution.py:345
  248.2 4.9 convolution_convert_fusion.5
  254.7 5.8 fusion.refs_1_.refs_3_.refs_4_
  260.5 5.6 fusion.30.refs_0_.refs_2_
  269.5 10.2 %mixer_forward.5 = (bf16[512,1024]{1,0:T(8,128)(2,1)S(1)}, f32[512,1]{1,0:T(8,128)S(1)}, f32[512,1024]{1,0:T(8,128)S(1)}, f32[4,128,1024]{2,1,0:T(8,128)S(1)}, f32[128,1024]{1,0:T(8,128)}) custom-call(f32[512,1024]{1,0:T(8,128)S(1)} %fusion.30.refs_0_.refs_2_, f32[512,1408]{1,0:T(8,128)S(1)} %fusion.refs_1_.refs_3_.refs_4_, ...), custom_call_target="tpu_custom_call" | custom-call | flops 1000 | bytes 1000 | tf_op jit(solution)/shard_map/mixer_forward/pallas_call | solution.py:345
  284.4 2.4 convolution_convert_fusion.4
  288.5 6.9 collective-permute-done.5
  301.6 2.1 convert_add_fusion.6
  306.5 3.4 fusion.110.refs_1_.refs_3_.refs_4_
  310.0 6.8 collective-permute-done.10
  319.4 5.2 fusion.109.refs_0_.refs_2_
  324.7 9.1 %mixer_forward.6 = (bf16[512,1024]{1,0:T(8,128)(2,1)S(1)}, f32[512,1]{1,0:T(8,128)S(1)}, f32[512,1024]{1,0:T(8,128)S(1)}, f32[4,128,1024]{2,1,0:T(8,128)S(1)}, f32[128,1024]{1,0:T(8,128)S(1)}) custom-call(f32[512,1024]{1,0:T(8,128)S(1)} %fusion.109.refs_0_.refs_2_, f32[512,1408]{1,0:T(8,128)S(1)} %fusion.110.refs_1_.refs_3_.refs_4_, ...), custom_call_target="tpu_custom_call" | custom-call | flops 1000 | bytes 1000 | tf_op jit(solution)/shard_map/mixer_forward/pallas_call | solution.py:345
  344.9 2.6 copy-done.91
  347.5 2.3 fusion.111.refs_0_.refs_2_
  349.9 3.4 fusion.112.refs_1_.refs_3_.refs_4_
  353.4 9.9 %mixer_forward.7 = (bf16[512,1024]{1,0:T(8,128)(2,1)S(1)}, f32[512,1]{1,0:T(8,128)S(1)}, f32[512,1024]{1,0:T(8,128)S(1)}, f32[4,128,1024]{2,1,0:T(8,128)S(1)}, f32[128,1024]{1,0:T(8,128)}) custom-call(f32[512,1024]{1,0:T(8,128)S(1)} %fusion.111.refs_0_.refs_2_, f32[512,1408]{1,0:T(8,128)S(1)} %fusion.112.refs_1_.refs_3_.refs_4_, ...), custom_call_target="tpu_custom_call" | custom-call | flops 1000 | bytes 1000 | tf_op jit(solution)/shard_map/mixer_forward/pallas_call | solution.py:345
  366.0 2.5 constant_dynamic-update-slice_fusion.1
  368.4 3.1 constant_dynamic-update-slice_fusion
  371.5 6.6 fusion.39
  378.2 3.7 fusion.37
  388.2 6.2 fusion.27
  399.3 21.1 %mixer_backward.4 = (bf16[512,2432]{1,0:T(8,128)(2,1)}, f32[128,1024]{1,0:T(8,128)}, f32[8,1280]{1,0:T(8,128)}, f32[8,1280]{1,0:T(8,128)}) custom-call(f32[512,1024]{1,0:T(8,128)} %get-tuple-element.136.refs_0_, f32[512,2]{1,0:T(8,128)} %copy.74.refs_1_, f32[512,1024]{1,0:T(8,128)} %copy-done.15, f32[512,1408]{1,0:T(8,128)} %copy-done.3, ...), custom_call_target="tpu_custom_call" | custom-call | flops 1000 | bytes 1000 | tf_op jit(solution)/shard_map/mixer_backward/pallas_call | solution.py:396
  420.4 10.5 %convolution_convert_fusion.9 = bf16[512,2048]{1,0:T(8,128)(2,1)S(1)} fusion(bf16[512,2432]{1,0:T(8,128)(2,1)} %get-tuple-element.139, bf16[2048,2432]{1,0:T(8,128)(2,1)} %constant_dynamic-update-slice_fusion), kind=kOutput, calls=%fused_computation.43 | convolution fusion | flops 5101322240 | bytes 14548992 | tf_op jit(solution)/shard_map/dot_general | solution.py:34
  433.5 3.7 convolution_convert_fusion.3
  437.4 2.5 dynamic-slice_bitcast_fusion.2
  442.1 2.1 convert_add_fusion.5
  447.4 20.0 %mixer_backward.5 = (bf16[512,2432]{1,0:T(8,128)(2,1)S(1)}, f32[128,1024]{1,0:T(8,128)}, f32[8,1280]{1,0:T(8,128)}, f32[8,1280]{1,0:T(8,128)S(1)}) custom-call(f32[512,1024]{1,0:T(8,128)S(1)} %copy-done.35, f32[512,2]{1,0:T(8,128)S(1)} %copy.76.refs_1_, f32[512,1024]{1,0:T(8,128)S(1)} %copy-done.14, f32[512,1408]{1,0:T(8,128)} %copy-done.1, ...), custom_call_target="tpu_custom_call" | custom-call | flops 1000 | bytes 1000 | tf_op jit(solution)/shard_map/mixer_backward/pallas_call | solution.py:396
  468.8 13.7 %convolution_convert_fusion.1 = bf16[2048,2432]{1,0:T(8,128)(2,1)} fusion(bf16[512,2432]{1,0:T(8,128)(2,1)S(1)} %copy-done.149, bf16[512,2432]{1,0:T(8,128)(2,1)S(1)} %get-tuple-element.150, bf16[512,2048]{1,0:T(8,128)(2,1)S(1)} %bitcast.447, bf16[512,2048]{1,0:T(8,128)(2,1)S(1)} %bitcast.442), kind=kOutput, calls=%fused_computation.1 | convolution fusion | flops 10223878144 | bytes 19136512 | tf_op jit(solution)/shard_map/dot_general | solution.py:1375
  491.5 8.6 %convolution_convert_fusion.8 = bf16[512,2048]{1,0:T(8,128)(2,1)S(1)} fusion(bf16[512,2432]{1,0:T(8,128)(2,1)S(1)} %copy-done.64, bf16[2048,2432]{1,0:T(8,128)(2,1)} %constant_dynamic-update-slice_fusion), kind=kOutput, calls=%fused_computation.42 | convolution fusion | flops 5101322240 | bytes 14548992 | tf_op jit(solution)/shard_map/dot_general | solution.py:34
  502.1 2.4 convolution_convert_fusion.2
  515.9 2.7 copy-done.152
  518.6 2.3 fusion.113.refs_0_
  521.7 18.6 %mixer_backward.6 = (bf16[512,2432]{1,0:T(8,128)(2,1)S(1)}, f32[128,1024]{1,0:T(8,128)S(1)}, f32[8,1280]{1,0:T(8,128)S(1)}, f32[8,1280]{1,0:T(8,128)S(1)}) custom-call(f32[512,1024]{1,0:T(8,128)S(1)} %fusion.113.refs_0_, f32[512,2]{1,0:T(8,128)S(1)} %bitcast.406, f32[512,1024]{1,0:T(8,128)S(1)} %copy-done.12, f32[512,1408]{1,0:T(8,128)} %copy-done.2, ...), custom_call_target="tpu_custom_call" | custom-call | flops 1000 | bytes 1000 | tf_op jit(solution)/shard_map/mixer_backward/pallas_call | solution.py:396
  545.2 8.4 %convolution_convert_fusion.7 = bf16[512,2048]{1,0:T(8,128)(2,1)S(1)} fusion(bf16[512,2432]{1,0:T(8,128)(2,1)S(1)} %get-tuple-element.175, bf16[2048,2432]{1,0:T(8,128)(2,1)} %bitcast.494), kind=kOutput, calls=%fused_computation.41 | convolution fusion | flops 5101322240 | bytes 14548992 | tf_op jit(solution)/shard_map/dot_general | solution.py:34
  568.6 2.8 copy-done.153
  571.4 2.3 fusion.114.refs_0_
  574.3 19.4 %mixer_backward.7 = (bf16[512,2432]{1,0:T(8,128)(2,1)S(1)}, f32[128,1024]{1,0:T(8,128)}, f32[8,1280]{1,0:T(8,128)}, f32[8,1280]{1,0:T(8,128)S(1)}) custom-call(f32[512,1024]{1,0:T(8,128)S(1)} %fusion.114.refs_0_, f32[512,2]{1,0:T(8,128)S(1)} %bitcast.404, f32[512,1024]{1,0:T(8,128)S(1)} %copy-done.10, f32[512,1408]{1,0:T(8,128)} %copy-done, ...), custom_call_target="tpu_custom_call" | custom-call | flops 1000 | bytes 1000 | tf_op jit(solution)/shard_map/mixer_backward/pallas_call | solution.py:396
  595.4 8.9 %convolution_convert_fusion.6 = bf16[512,2048]{1,0:T(8,128)(2,1)S(1)} fusion(bf16[512,2432]{1,0:T(8,128)(2,1)S(1)} %get-tuple-element.174, bf16[2048,2432]{1,0:T(8,128)(2,1)} %bitcast.495), kind=kOutput, calls=%fused_computation.40 | convolution fusion | flops 5101322240 | bytes 14548992 | tf_op jit(solution)/shard_map/dot_general | solution.py:34
  605.7 2.8 broadcast_select_fusion.2
  609.8 6.2 fusion.24
  617.7 16.3 %convolution_convert_fusion = bf16[2048,2432]{1,0:T(8,128)(2,1)} fusion(bf16[512,2432]{1,0:T(8,128)(2,1)S(1)} %copy-done.62, bf16[512,2432]{1,0:T(8,128)(2,1)S(1)} %get-tuple-element.174, bf16[512,2048]{1,0:T(8,128)(2,1)} %bitcast.504, bf16[512,2048]{1,0:T(8,128)(2,1)} %bitcast.502), kind=kOutput, calls=%fused_computation | convolution fusion | flops 10223878144 | bytes 19136512 | tf_op jit(solution)/shard_map/dot_general | solution.py:1375
  643.6 160.5 %grads_reduce.1 = (bf16[256,2432]{1,0:T(8,128)(2,1)}, bf16[256,1024]{1,0:T(8,128)(2,1)}, bf16[256,2432]{1,0:T(8,128)(2,1)}, bf16[256,1024]{1,0:T(8,128)(2,1)}, f...) custom-call(bf16[8,256,2432]{2,1,0:T(8,128)(2,1)} %bitcast.407, bf16[8,256,1024]{2,1,0:T(8,128)(2,1)} %bitcast.421, ...), custom_call_target="tpu_custom_call" | custom-call | flops 1000 | bytes 1000 | tf_op jit(solution)/shard_map/grads_reduce/pallas_call | solution.py:1112
  820.0 4.0 join_halves.1
  (586 shorter events, 150.3 us)
Async XLA Ops:
  7.2 312.3 %all-gather.3.cloned.1.call-start = ((), (), s32[]{:S(2)}) async-start(), calls=%async_computation.2 | async-start | bytes 4718592 | tf_op jit(solution)/shard_map/all_gather | solution.py:1285
  13.9 6.8 collective-permute-start
  223.7 129.7 %copy-start.49 = (f32[8,1280]{1,0:T(8,128)}, f32[8,1280]{1,0:T(8,128)S(1)}, u32[]{:S(2)}) copy-start(f32[8,1280]{1,0:T(8,128)S(1)} %get-tuple-element.277.refs_4_.refs_10_) | copy-start | bytes 122884
  223.7 147.8 %all-gather.5.cloned.1.call-start = ((), (), s32[]{:S(2)}) async-start(), calls=%async_computation.3 | async-start | bytes 4718592 | tf_op jit(solution)/shard_map/all_gather | solution.py:1286
  233.4 36.0 %copy-start = (f32[512,1408]{1,0:T(8,128)}, f32[512,1408]{1,0:T(8,128)S(1)}, u32[]{:S(2)}) copy-start(f32[512,1408]{1,0:T(8,128)S(1)} %fusion.2.refs_1_.refs_3_.refs_4_) | copy-start | bytes 8650756
  233.5 91.2 %copy-start.38 = (f32[8,1280]{1,0:T(8,128)}, f32[8,1280]{1,0:T(8,128)S(1)}, u32[]{:S(2)}) copy-start(f32[8,1280]{1,0:T(8,128)S(1)} %broadcast_in_dim.22.refs_2_.refs_9_.refs_5_) | copy-start | bytes 122884
  247.4 18.6 %collective-permute-start.1 = (f32[2,128]{1,0:T(2,128)S(1)}, f32[2,128]{1,0:T(2,128)S(1)}, u32[]{:S(2)}, u32[]{:S(2)}) collective-permute-start(f32[2,128]{1,0:T(2,128)S(1)} %bitcast.487), channel_id=1, source_target_pairs={{0,16},{16,0},{1,17},{17,1},{2,18},{18,2},{3,19},{19,3},{4,20},{20... | collective-permute-start | bytes 3080 | tf_op jit(solution)/shard_map/ppermute | solution.py:1146
  253.2 12.9 %collective-permute-start.3 = (bf16[2,128,2048]{2,1,0:T(8,128)(2,1)S(1)}, bf16[2,128,2048]{2,1,0:T(8,128)(2,1)S(1)}, u32[]{:S(2)}, u32[]{:S(2)}) collective-permute-start(bf16[2,128,2048]{2,1,0:T(8,128)(2,1)S(1)} %dynamic-slice_bitcast_fusion.9), channel_id=1, source_target_pairs={{0,16},{16,0},{1,17},{17,1},{2,18},{18,2},{3,19},{19,3},{4,20},{20... | collective-permute-start | bytes 3145736 | tf_op jit(solution)/shard_map/ppermute | solution.py:1146
  266.6 13.7 %collective-permute-start.4 = (bf16[128,2048]{1,0:T(8,128)(2,1)S(1)}, bf16[128,2048]{1,0:T(8,128)(2,1)S(1)}, u32[]{:S(2)}, u32[]{:S(2)}) collective-permute-start(bf16[128,2048]{1,0:T(8,128)(2,1)S(1)} %fusion.70), channel_id=1, source_target_pairs={{0,1},{1,0},{2,3},{3,2},{4,5},{5,4},{6,7},{7,6},{8,9},{9,8},{10,11... | collective-permute-start | bytes 1572872 | tf_op jit(solution)/shard_map/ppermute | solution.py:1150
  267.9 12.4 %collective-permute-start.2 = (f32[128]{0:T(128)S(1)}, f32[128]{0:T(128)S(1)}, u32[]{:S(2)}, u32[]{:S(2)}) collective-permute-start(f32[128]{0:T(128)S(1)} %fusion.90), channel_id=1, source_target_pairs={{0,1},{1,0},{2,3},{3,2},{4,5},{5,4},{6,7},{7,6},{8,9},{9,8},{10,11... | collective-permute-start | bytes 1544 | tf_op jit(solution)/shard_map/ppermute | solution.py:1150
  282.3 13.1 %collective-permute-start.5 = (bf16[128,2048]{1,0:T(8,128)(2,1)S(1)}, bf16[128,2048]{1,0:T(8,128)(2,1)S(1)}, u32[]{:S(2)}, u32[]{:S(2)}) collective-permute-start(bf16[128,2048]{1,0:T(8,128)(2,1)S(1)} %multiply_convert_fusion.3), channel_id=1, source_target_pairs={{0,1},{1,0},{2,3},{3,2},{4,5},{5,4},{6,7},{7,6},{8,9},{9,8},{10,11... | collective-permute-start | bytes 1572872 | tf_op jit(solution)/shard_map/ppermute | solution.py:1150
  288.0 13.7 %collective-permute-start.7 = (bf16[2,128,2048]{2,1,0:T(8,128)(2,1)}, bf16[2,128,2048]{2,1,0:T(8,128)(2,1)}, u32[]{:S(2)}, u32[]{:S(2)}) collective-permute-start(bf16[2,128,2048]{2,1,0:T(8,128)(2,1)} %dynamic-slice_bitcast_fusion.8), channel_id=1, source_target_pairs={{0,16},{16,0},{1,17},{17,1},{2,18},{18,2},{3,19},{19,3},{4,20},{20... | collective-permute-start | bytes 3145736 | tf_op jit(solution)/shard_map/ppermute | solution.py:1146
  296.8 7.3 collective-permute-start.6
  298.2 2.1 collective-permute-start.8
  298.3 509.5 %reduce-scatter.5.cloned.1.call-start = ((), (), s32[]{:S(2)}) async-start(), calls=%async_computation.5 | async-start | bytes 4718592 | tf_op jit(solution)/shard_map/reduce_scatter | solution.py:1424
  300.3 9.6 %collective-permute-start.9 = (f32[128]{0:T(128)S(1)}, f32[128]{0:T(128)S(1)}, u32[]{:S(2)}, u32[]{:S(2)}) collective-permute-start(f32[128]{0:T(128)S(1)} %fusion.91), channel_id=1, source_target_pairs={{0,1},{1,0},{2,3},{3,2},{4,5},{5,4},{6,7},{7,6},{8,9},{9,8},{10,11... | collective-permute-start | bytes 1544 | tf_op jit(solution)/shard_map/ppermute | solution.py:1150
  303.8 13.0 %collective-permute-start.10 = (bf16[128,2048]{1,0:T(8,128)(2,1)S(1)}, bf16[128,2048]{1,0:T(8,128)(2,1)S(1)}, u32[]{:S(2)}, u32[]{:S(2)}) collective-permute-start(bf16[128,2048]{1,0:T(8,128)(2,1)S(1)} %fusion.71), channel_id=1, source_target_pairs={{0,1},{1,0},{2,3},{3,2},{4,5},{5,4},{6,7},{7,6},{8,9},{9,8},{10,11... | collective-permute-start | bytes 1572872 | tf_op jit(solution)/shard_map/ppermute | solution.py:1150
  309.9 30.3 %copy-start.1 = (f32[512,1408]{1,0:T(8,128)}, f32[512,1408]{1,0:T(8,128)S(1)}, u32[]{:S(2)}) copy-start(f32[512,1408]{1,0:T(8,128)S(1)} %fusion.110.refs_1_.refs_3_.refs_4_) | copy-start | bytes 8650756
  319.2 16.3 %collective-permute-start.11 = (bf16[128,2048]{1,0:T(8,128)(2,1)}, bf16[128,2048]{1,0:T(8,128)(2,1)}, u32[]{:S(2)}, u32[]{:S(2)}) collective-permute-start(bf16[128,2048]{1,0:T(8,128)(2,1)} %multiply_convert_fusion.2), channel_id=1, source_target_pairs={{0,1},{1,0},{2,3},{3,2},{4,5},{5,4},{6,7},{7,6},{8,9},{9,8},{10,11... | collective-permute-start | bytes 1572872 | tf_op jit(solution)/shard_map/ppermute | solution.py:1150
  338.4 4.4 collective-permute-start.12
  382.0 1.4 collective-permute-start.13
  383.4 2.5 collective-permute-start.14
  394.4 416.6 %reduce-scatter.3.cloned.1.call-start = ((), (), s32[]{:S(2)}) async-start(), calls=%async_computation.4 | async-start | bytes 11206656 | tf_op jit(solution)/shard_map/reduce_scatter | solution.py:1424
  432.0 10.1 %collective-permute-start.15 = (bf16[2,128,2048]{2,1,0:T(8,128)(2,1)}, bf16[2,128,2048]{2,1,0:T(8,128)(2,1)}, u32[]{:S(2)}, u32[]{:S(2)}) collective-permute-start(bf16[2,128,2048]{2,1,0:T(8,128)(2,1)} %dynamic-slice_bitcast_fusion.7), channel_id=1, source_target_pairs={{0,16},{16,0},{1,17},{17,1},{2,18},{18,2},{3,19},{19,3},{4,20},{20... | collective-permute-start | bytes 3145736 | tf_op jit(solution)/shard_map/ppermute | solution.py:1146
  439.9 43.3 %collective-permute-start.30 = (bf16[2,128,2048]{2,1,0:T(8,128)(2,1)}, bf16[2,128,2048]{2,1,0:T(8,128)(2,1)}, u32[]{:S(2)}, u32[]{:S(2)}) collective-permute-start(bf16[2,128,2048]{2,1,0:T(8,128)(2,1)} %dynamic-slice_bitcast_fusion.2), channel_id=1, source_target_pairs={{0,16},{16,0},{1,17},{17,1},{2,18},{18,2},{3,19},{19,3},{4,20},{20... | collective-permute-start | bytes 3145736 | tf_op jit(solution)/shard_map/ppermute | solution.py:1146
  445.0 42.1 %collective-permute-start.16 = (bf16[128,2048]{1,0:T(8,128)(2,1)}, bf16[128,2048]{1,0:T(8,128)(2,1)S(1)}, u32[]{:S(2)}, u32[]{:S(2)}) collective-permute-start(bf16[128,2048]{1,0:T(8,128)(2,1)} %fusion.72), channel_id=1, source_target_pairs={{0,1},{1,0},{2,3},{3,2},{4,5},{5,4},{6,7},{7,6},{8,9},{9,8},{10,11... | collective-permute-start | bytes 1572872 | tf_op jit(solution)/shard_map/ppermute | solution.py:1150
  489.9 14.6 %collective-permute-start.21 = (f32[128,2]{0,1:T(2,128)S(1)}, f32[128,2]{0,1:T(2,128)S(1)}, u32[]{:S(2)}, u32[]{:S(2)}) collective-permute-start(f32[128,2]{0,1:T(2,128)S(1)} %pad_maximum_fusion.15), channel_id=1, source_target_pairs={{0,1},{1,0},{2,3},{3,2},{4,5},{5,4},{6,7},{7,6},{8,9},{9,8},{10,11... | collective-permute-start | bytes 3080 | tf_op jit(solution)/shard_map/ppermute | solution.py:1150
  490.6 17.6 %collective-permute-start.18 = (bf16[128,2048]{1,0:T(8,128)(2,1)S(1)}, bf16[128,2048]{1,0:T(8,128)(2,1)S(1)}, u32[]{:S(2)}, u32[]{:S(2)}) collective-permute-start(bf16[128,2048]{1,0:T(8,128)(2,1)S(1)} %convert_element_type.303), channel_id=1, source_target_pairs={{0,1},{1,0},{2,3},{3,2},{4,5},{5,4},{6,7},{7,6},{8,9},{9,8},{10,11... | collective-permute-start | bytes 1572872 | tf_op jit(solution)/shard_map/ppermute | solution.py:1150
  501.2 9.1 %collective-permute-start.20 = (bf16[2,128,2048]{2,1,0:T(8,128)(2,1)}, bf16[2,128,2048]{2,1,0:T(8,128)(2,1)}, u32[]{:S(2)}, u32[]{:S(2)}) collective-permute-start(bf16[2,128,2048]{2,1,0:T(8,128)(2,1)} %dynamic-slice_bitcast_fusion.4), channel_id=1, source_target_pairs={{0,16},{16,0},{1,17},{17,1},{2,18},{18,2},{3,19},{19,3},{4,20},{20... | collective-permute-start | bytes 3145736 | tf_op jit(solution)/shard_map/ppermute | solution.py:1146
  504.6 2.0 collective-permute-start.22
  506.6 5.8 collective-permute-start.17
  509.8 5.1 collective-permute-start.19
  512.0 28.4 %collective-permute-start.23 = (bf16[128,2048]{1,0:T(8,128)(2,1)S(1)}, bf16[128,2048]{1,0:T(8,128)(2,1)S(1)}, u32[]{:S(2)}, u32[]{:S(2)}) collective-permute-start(bf16[128,2048]{1,0:T(8,128)(2,1)S(1)} %fusion.73), channel_id=1, source_target_pairs={{0,1},{1,0},{2,3},{3,2},{4,5},{5,4},{6,7},{7,6},{8,9},{9,8},{10,11... | collective-permute-start | bytes 1572872 | tf_op jit(solution)/shard_map/ppermute | solution.py:1150
  543.6 13.6 %collective-permute-start.28 = (f32[128,2]{0,1:T(2,128)S(1)}, f32[128,2]{0,1:T(2,128)S(1)}, u32[]{:S(2)}, u32[]{:S(2)}) collective-permute-start(f32[128,2]{0,1:T(2,128)S(1)} %pad_maximum_fusion.16), channel_id=1, source_target_pairs={{0,1},{1,0},{2,3},{3,2},{4,5},{5,4},{6,7},{7,6},{8,9},{9,8},{10,11... | collective-permute-start | bytes 3080 | tf_op jit(solution)/shard_map/ppermute | solution.py:1150
  544.9 14.7 %collective-permute-start.26 = (bf16[128,2048]{1,0:T(8,128)(2,1)S(1)}, bf16[128,2048]{1,0:T(8,128)(2,1)}, u32[]{:S(2)}, u32[]{:S(2)}) collective-permute-start(bf16[128,2048]{1,0:T(8,128)(2,1)S(1)} %convert_element_type.318), channel_id=1, source_target_pairs={{0,1},{1,0},{2,3},{3,2},{4,5},{5,4},{6,7},{7,6},{8,9},{9,8},{10,11... | collective-permute-start | bytes 1572872 | tf_op jit(solution)/shard_map/ppermute | solution.py:1150
  556.0 6.9 collective-permute-start.24
  557.3 2.1 collective-permute-start.29
  561.3 6.8 collective-permute-start.27
  565.4 28.4 %collective-permute-start.33 = (bf16[128,2048]{1,0:T(8,128)(2,1)}, bf16[128,2048]{1,0:T(8,128)(2,1)S(1)}, u32[]{:S(2)}, u32[]{:S(2)}) collective-permute-start(bf16[128,2048]{1,0:T(8,128)(2,1)} %fusion.74), channel_id=1, source_target_pairs={{0,1},{1,0},{2,3},{3,2},{4,5},{5,4},{6,7},{7,6},{8,9},{9,8},{10,11... | collective-permute-start | bytes 1572872 | tf_op jit(solution)/shard_map/ppermute | solution.py:1150
  566.6 39.0 %collective-permute-start.31 = (bf16[128,2048]{1,0:T(8,128)(2,1)}, bf16[128,2048]{1,0:T(8,128)(2,1)S(1)}, u32[]{:S(2)}, u32[]{:S(2)}) collective-permute-start(bf16[128,2048]{1,0:T(8,128)(2,1)} %dynamic-slice_bitcast_fusion.1), channel_id=1, source_target_pairs={{0,1},{1,0},{2,3},{3,2},{4,5},{5,4},{6,7},{7,6},{8,9},{9,8},{10,11... | collective-permute-start | bytes 1572872 | tf_op jit(solution)/shard_map/ppermute | solution.py:1150
  566.8 38.8 %collective-permute-start.25 = (bf16[128,2048]{1,0:T(8,128)(2,1)}, bf16[128,2048]{1,0:T(8,128)(2,1)}, u32[]{:S(2)}, u32[]{:S(2)}) collective-permute-start(bf16[128,2048]{1,0:T(8,128)(2,1)} %dynamic-slice_bitcast_fusion.5), channel_id=1, source_target_pairs={{0,1},{1,0},{2,3},{3,2},{4,5},{5,4},{6,7},{7,6},{8,9},{9,8},{10,11... | collective-permute-start | bytes 1572872 | tf_op jit(solution)/shard_map/ppermute | solution.py:1150
  604.4 11.6 %collective-permute-start.34 = (bf16[2,128,2048]{2,1,0:T(8,128)(2,1)S(1)}, bf16[2,128,2048]{2,1,0:T(8,128)(2,1)S(1)}, u32[]{:S(2)}, u32[]{:S(2)}) collective-permute-start(bf16[2,128,2048]{2,1,0:T(8,128)(2,1)S(1)} %dynamic-slice_bitcast_fusion), channel_id=1, source_target_pairs={{0,16},{16,0},{1,17},{17,1},{2,18},{18,2},{3,19},{19,3},{4,20},{20... | collective-permute-start | bytes 3145736 | tf_op jit(solution)/shard_map/ppermute | solution.py:1146
  608.4 28.4 %collective-permute-start.32 = (f32[128,2048]{1,0:T(8,128)}, f32[128,2048]{1,0:T(8,128)}, u32[]{:S(2)}, u32[]{:S(2)}) collective-permute-start(f32[128,2048]{1,0:T(8,128)} %get-tuple-element.231), channel_id=1, source_target_pairs={{0,16},{16,0},{1,17},{17,1},{2,18},{18,2},{3,19},{19,3},{4,20},{20... | collective-permute-start | bytes 3145736 | tf_op jit(solution)/shard_map/ppermute | solution.py:1146
  616.5 17.6 %collective-permute-start.35 = (bf16[128,2048]{1,0:T(8,128)(2,1)S(1)}, bf16[128,2048]{1,0:T(8,128)(2,1)S(1)}, u32[]{:S(2)}, u32[]{:S(2)}) collective-permute-start(bf16[128,2048]{1,0:T(8,128)(2,1)S(1)} %fusion.75), channel_id=1, source_target_pairs={{0,1},{1,0},{2,3},{3,2},{4,5},{5,4},{6,7},{7,6},{8,9},{9,8},{10,11... | collective-permute-start | bytes 1572872 | tf_op jit(solution)/shard_map/ppermute | solution.py:1150
  636.8 3.8 collective-permute-start.36
  807.8 5.1 collective-permute-start.39
  811.0 3.2 collective-permute-start.37
  815.2 9.5 %collective-permute-start.38 = (f32[256,256]{1,0:T(8,128)S(1)}, f32[256,256]{1,0:T(8,128)S(1)}, u32[]{:S(2)}, u32[]{:S(2)}) collective-permute-start(f32[256,256]{1,0:T(8,128)S(1)} %slice_add_fusion), channel_id=1, source_target_pairs={{0,1},{1,0},{2,3},{3,2},{4,5},{5,4},{6,7},{7,6},{8,9},{9,8},{10,11... | collective-permute-start | bytes 786440 | tf_op jit(solution)/shard_map/ppermute | solution.py:1150
  (160 other events, 871.9 us)
Sparse Core Ops, SparseCore 0:
  223.8 72.0 all-gather.2
  298.4 71.8 all-gather.4
  394.5 89.1 reduce-scatter.4
  487.6 172.5 reduce-scatter.2

commit v6 on v5

--- a/solution.py
+++ b/solution.py
@@ -894,6 +894,8 @@
             copy.wait()
             value = small[...] if n == 0 else small_buffer[n - 1]
             small_buffer[n] = value + small_buffer[3 + n]
+
+    def spread_small():
         over_tp = swap_small(3, small_buffer.at[2], small_buffer.at[6])
         over_core = swap_small(4, small_buffer.at[2, 1 - core], next_small)
         over_tp.start()
@@ -1059,6 +1061,7 @@
             for k in range(1, DEEP):
                 take(k - 1)
                 relay(k, up)
+            spread_small()
             take(DEEP - 1)
         else:
             up = here == 1
@@ -1068,6 +1071,7 @@
             relay(3, not up)
             take(2)
             relay(3, up)
+            spread_small()
             take(3)
         for i in range(count):
             terms = [held[i].at[here]]

time: 841 us -> 836 us (level)
  transfers between devices with their start and end apart: 44 -> 44, of which waited for: 9 -> 9; matrix products, arithmetic and copies ran while one was open for 25% -> 25% of each run, Pallas kernels for 34% -> 33%
where the time goes in v6:
time: 836 us; the launch traced here: 827 us
  Pallas kernels  475 us (57%)
  matrix products  142 us (17%)
  local copies, waits for them, and re-layouts  83.5 us (10%)
  other arithmetic  58.7 us (7%)
  starting transfers between devices  30.2 us (4%)
  waiting for transfers between devices  22.5 us (3%)
  between operations  16.3 us (2%)
    pallas_call x1, Pallas kernels, start_gather(): pl.pallas_call(functools.partial(start_kernel, count=count, micros=micros...  198 us
    pallas_call x1, Pallas kernels, reduce_line(): pl.pallas_call(functools.partial(reduce_kernel, count=count), out_shape=[...  155 us
    pallas_call x4, Pallas kernels, mixer_backward(): pl.pallas_call(body, grid=(steps,), in_specs=[by_row(channels), by_row(2)...  79.1 us
    unnamed x331, local copies, waits for them, and re-layouts  50.1 us
    dot_general x8, matrix products, dot_nt(): lax.dot_general(a, b, (((1,), (1,)), ((), ())), preferred_element_type=F32)  49.7 us
    dot_general x12, matrix products, dot_nn(): lax.dot_general(a, b, (((1,), (0,)), ((), ())), preferred_element_type=F32)  49.5 us
    dot_general x4, matrix products, weight_grad(): lax.dot_general(jnp.concatenate(left), jnp.concatenate(right), over_token...  42.4 us
    pallas_call x4, Pallas kernels, mixer_forward(): pl.pallas_call(body, grid=(steps,), in_specs=[by_row(channels), by_row(wi...  38.3 us
  transfers between devices with their start and end apart: 44, of which 9 were waited for; matrix products, arithmetic and copies ran while one was open for 25% of the time, Pallas kernels for 33%

profile of v6, /device:TPU:9, one launch (start us, length us, event | category | flops | bytes accessed | tf_op | source)
XLA Modules:
  0.0 827.5 jit_solution(6803279326563965017)
XLA Ops:
  7.2 4.0 constant_dynamic-slice_fusion.15
  17.4 3.3 fusion.106
  24.6 198.2 %start_gather.1 = (bf16[8,256,2432]{2,1,0:T(8,128)(2,1)}, bf16[8,256,1024]{2,1,0:T(8,128)(2,1)}, bf16[8,256,1408]{2,1,0:T(8,128)(2,1)}, f32[2,8,8,128]{3,2,1,0:T...) custom-call(bf16[256,2432]{1,0:T(8,128)(2,1)} %get-tuple-element.264, ...), custom_call_target="tpu_custom_call" | custom-call | flops 170000007168 | bytes 1000 | tf_op jit(solution)/shard_map/start_gather/pallas_call | solution.py:805
  223.8 5.3 fusion.32.refs_0_.refs_2_
  230.0 3.4 fusion.2.refs_1_.refs_3_.refs_4_
  233.6 9.2 %mixer_forward.4 = (bf16[512,1024]{1,0:T(8,128)(2,1)S(1)}, f32[512,1]{1,0:T(8,128)S(1)}, f32[512,1024]{1,0:T(8,128)S(1)}, f32[4,128,1024]{2,1,0:T(8,128)S(1)}, f32[128,1024]{1,0:T(8,128)S(1)}) custom-call(f32[512,1024]{1,0:T(8,128)S(1)} %fusion.32.refs_0_.refs_2_, f32[512,1408]{1,0:T(8,128)S(1)} %fusion.2.refs_1_.refs_3_.refs_4_, ...), custom_call_target="tpu_custom_call" | custom-call | flops 1000 | bytes 1000 | tf_op jit(solution)/shard_map/mixer_forward/pallas_call | solution.py:345
  248.2 4.9 convolution_convert_fusion.5
  254.7 5.8 fusion.refs_1_.refs_3_.refs_4_
  260.5 5.6 fusion.30.refs_0_.refs_2_
  269.5 10.2 %mixer_forward.5 = (bf16[512,1024]{1,0:T(8,128)(2,1)S(1)}, f32[512,1]{1,0:T(8,128)S(1)}, f32[512,1024]{1,0:T(8,128)S(1)}, f32[4,128,1024]{2,1,0:T(8,128)S(1)}, f32[128,1024]{1,0:T(8,128)}) custom-call(f32[512,1024]{1,0:T(8,128)S(1)} %fusion.30.refs_0_.refs_2_, f32[512,1408]{1,0:T(8,128)S(1)} %fusion.refs_1_.refs_3_.refs_4_, ...), custom_call_target="tpu_custom_call" | custom-call | flops 1000 | bytes 1000 | tf_op jit(solution)/shard_map/mixer_forward/pallas_call | solution.py:345
  284.4 2.4 convolution_convert_fusion.4
  288.5 6.9 collective-permute-done.5
  301.6 2.1 convert_add_fusion.6
  306.5 3.4 fusion.110.refs_1_.refs_3_.refs_4_
  310.0 6.8 collective-permute-done.10
  319.4 5.2 fusion.109.refs_0_.refs_2_
  324.7 9.1 %mixer_forward.6 = (bf16[512,1024]{1,0:T(8,128)(2,1)S(1)}, f32[512,1]{1,0:T(8,128)S(1)}, f32[512,1024]{1,0:T(8,128)S(1)}, f32[4,128,1024]{2,1,0:T(8,128)S(1)}, f32[128,1024]{1,0:T(8,128)S(1)}) custom-call(f32[512,1024]{1,0:T(8,128)S(1)} %fusion.109.refs_0_.refs_2_, f32[512,1408]{1,0:T(8,128)S(1)} %fusion.110.refs_1_.refs_3_.refs_4_, ...), custom_call_target="tpu_custom_call" | custom-call | flops 1000 | bytes 1000 | tf_op jit(solution)/shard_map/mixer_forward/pallas_call | solution.py:345
  344.9 2.6 copy-done.91
  347.5 2.3 fusion.111.refs_0_.refs_2_
  349.9 3.4 fusion.112.refs_1_.refs_3_.refs_4_
  353.4 9.9 %mixer_forward.7 = (bf16[512,1024]{1,0:T(8,128)(2,1)S(1)}, f32[512,1]{1,0:T(8,128)S(1)}, f32[512,1024]{1,0:T(8,128)S(1)}, f32[4,128,1024]{2,1,0:T(8,128)S(1)}, f32[128,1024]{1,0:T(8,128)}) custom-call(f32[512,1024]{1,0:T(8,128)S(1)} %fusion.111.refs_0_.refs_2_, f32[512,1408]{1,0:T(8,128)S(1)} %fusion.112.refs_1_.refs_3_.refs_4_, ...), custom_call_target="tpu_custom_call" | custom-call | flops 1000 | bytes 1000 | tf_op jit(solution)/shard_map/mixer_forward/pallas_call | solution.py:345
  366.0 2.5 constant_dynamic-update-slice_fusion.1
  368.4 3.1 constant_dynamic-update-slice_fusion
  371.5 6.6 fusion.39
  378.2 3.7 fusion.37
  388.2 6.2 fusion.27
  399.3 21.1 %mixer_backward.4 = (bf16[512,2432]{1,0:T(8,128)(2,1)}, f32[128,1024]{1,0:T(8,128)}, f32[8,1280]{1,0:T(8,128)}, f32[8,1280]{1,0:T(8,128)}) custom-call(f32[512,1024]{1,0:T(8,128)} %get-tuple-element.136.refs_0_, f32[512,2]{1,0:T(8,128)} %copy.74.refs_1_, f32[512,1024]{1,0:T(8,128)} %copy-done.15, f32[512,1408]{1,0:T(8,128)} %copy-done.3, ...), custom_call_target="tpu_custom_call" | custom-call | flops 1000 | bytes 1000 | tf_op jit(solution)/shard_map/mixer_backward/pallas_call | solution.py:396
  420.4 10.5 %convolution_convert_fusion.9 = bf16[512,2048]{1,0:T(8,128)(2,1)S(1)} fusion(bf16[512,2432]{1,0:T(8,128)(2,1)} %get-tuple-element.139, bf16[2048,2432]{1,0:T(8,128)(2,1)} %constant_dynamic-update-slice_fusion), kind=kOutput, calls=%fused_computation.43 | convolution fusion | flops 5101322240 | bytes 14548992 | tf_op jit(solution)/shard_map/dot_general | solution.py:34
  433.5 3.7 convolution_convert_fusion.3
  437.4 2.5 dynamic-slice_bitcast_fusion.2
  442.1 2.1 convert_add_fusion.5
  447.4 20.0 %mixer_backward.5 = (bf16[512,2432]{1,0:T(8,128)(2,1)S(1)}, f32[128,1024]{1,0:T(8,128)}, f32[8,1280]{1,0:T(8,128)}, f32[8,1280]{1,0:T(8,128)S(1)}) custom-call(f32[512,1024]{1,0:T(8,128)S(1)} %copy-done.35, f32[512,2]{1,0:T(8,128)S(1)} %copy.76.refs_1_, f32[512,1024]{1,0:T(8,128)S(1)} %copy-done.14, f32[512,1408]{1,0:T(8,128)} %copy-done.1, ...), custom_call_target="tpu_custom_call" | custom-call | flops 1000 | bytes 1000 | tf_op jit(solution)/shard_map/mixer_backward/pallas_call | solution.py:396
  468.8 13.7 %convolution_convert_fusion.1 = bf16[2048,2432]{1,0:T(8,128)(2,1)} fusion(bf16[512,2432]{1,0:T(8,128)(2,1)S(1)} %copy-done.149, bf16[512,2432]{1,0:T(8,128)(2,1)S(1)} %get-tuple-element.150, bf16[512,2048]{1,0:T(8,128)(2,1)S(1)} %bitcast.447, bf16[512,2048]{1,0:T(8,128)(2,1)S(1)} %bitcast.442), kind=kOutput, calls=%fused_computation.1 | convolution fusion | flops 10223878144 | bytes 19136512 | tf_op jit(solution)/shard_map/dot_general | solution.py:1379
  491.5 8.6 %convolution_convert_fusion.8 = bf16[512,2048]{1,0:T(8,128)(2,1)S(1)} fusion(bf16[512,2432]{1,0:T(8,128)(2,1)S(1)} %copy-done.64, bf16[2048,2432]{1,0:T(8,128)(2,1)} %constant_dynamic-update-slice_fusion), kind=kOutput, calls=%fused_computation.42 | convolution fusion | flops 5101322240 | bytes 14548992 | tf_op jit(solution)/shard_map/dot_general | solution.py:34
  502.1 2.4 convolution_convert_fusion.2
  515.9 2.7 copy-done.152
  518.6 2.3 fusion.113.refs_0_
  521.7 18.6 %mixer_backward.6 = (bf16[512,2432]{1,0:T(8,128)(2,1)S(1)}, f32[128,1024]{1,0:T(8,128)S(1)}, f32[8,1280]{1,0:T(8,128)S(1)}, f32[8,1280]{1,0:T(8,128)S(1)}) custom-call(f32[512,1024]{1,0:T(8,128)S(1)} %fusion.113.refs_0_, f32[512,2]{1,0:T(8,128)S(1)} %bitcast.406, f32[512,1024]{1,0:T(8,128)S(1)} %copy-done.12, f32[512,1408]{1,0:T(8,128)} %copy-done.2, ...), custom_call_target="tpu_custom_call" | custom-call | flops 1000 | bytes 1000 | tf_op jit(solution)/shard_map/mixer_backward/pallas_call | solution.py:396
  545.2 8.4 %convolution_convert_fusion.7 = bf16[512,2048]{1,0:T(8,128)(2,1)S(1)} fusion(bf16[512,2432]{1,0:T(8,128)(2,1)S(1)} %get-tuple-element.175, bf16[2048,2432]{1,0:T(8,128)(2,1)} %bitcast.494), kind=kOutput, calls=%fused_computation.41 | convolution fusion | flops 5101322240 | bytes 14548992 | tf_op jit(solution)/shard_map/dot_general | solution.py:34
  568.6 2.8 copy-done.153
  571.4 2.3 fusion.114.refs_0_
  574.3 19.4 %mixer_backward.7 = (bf16[512,2432]{1,0:T(8,128)(2,1)S(1)}, f32[128,1024]{1,0:T(8,128)}, f32[8,1280]{1,0:T(8,128)}, f32[8,1280]{1,0:T(8,128)S(1)}) custom-call(f32[512,1024]{1,0:T(8,128)S(1)} %fusion.114.refs_0_, f32[512,2]{1,0:T(8,128)S(1)} %bitcast.404, f32[512,1024]{1,0:T(8,128)S(1)} %copy-done.10, f32[512,1408]{1,0:T(8,128)} %copy-done, ...), custom_call_target="tpu_custom_call" | custom-call | flops 1000 | bytes 1000 | tf_op jit(solution)/shard_map/mixer_backward/pallas_call | solution.py:396
  595.4 8.9 %convolution_convert_fusion.6 = bf16[512,2048]{1,0:T(8,128)(2,1)S(1)} fusion(bf16[512,2432]{1,0:T(8,128)(2,1)S(1)} %get-tuple-element.174, bf16[2048,2432]{1,0:T(8,128)(2,1)} %bitcast.495), kind=kOutput, calls=%fused_computation.40 | convolution fusion | flops 5101322240 | bytes 14548992 | tf_op jit(solution)/shard_map/dot_general | solution.py:34
  605.7 2.8 broadcast_select_fusion.2
  609.8 6.2 fusion.24
  617.7 16.3 %convolution_convert_fusion = bf16[2048,2432]{1,0:T(8,128)(2,1)} fusion(bf16[512,2432]{1,0:T(8,128)(2,1)S(1)} %copy-done.62, bf16[512,2432]{1,0:T(8,128)(2,1)S(1)} %get-tuple-element.174, bf16[512,2048]{1,0:T(8,128)(2,1)} %bitcast.504, bf16[512,2048]{1,0:T(8,128)(2,1)} %bitcast.502), kind=kOutput, calls=%fused_computation | convolution fusion | flops 10223878144 | bytes 19136512 | tf_op jit(solution)/shard_map/dot_general | solution.py:1379
  643.6 155.1 %grads_reduce.1 = (bf16[256,2432]{1,0:T(8,128)(2,1)}, bf16[256,1024]{1,0:T(8,128)(2,1)}, bf16[256,2432]{1,0:T(8,128)(2,1)}, bf16[256,1024]{1,0:T(8,128)(2,1)}, f...) custom-call(bf16[8,256,2432]{2,1,0:T(8,128)(2,1)} %bitcast.407, bf16[8,256,1024]{2,1,0:T(8,128)(2,1)} %bitcast.421, ...), custom_call_target="tpu_custom_call" | custom-call | flops 1000 | bytes 1000 | tf_op jit(solution)/shard_map/grads_reduce/pallas_call | solution.py:1116
  815.3 4.0 join_halves.1
  (586 shorter events, 151.1 us)
Async XLA Ops:
  7.2 312.3 %all-gather.3.cloned.1.call-start = ((), (), s32[]{:S(2)}) async-start(), calls=%async_computation.2 | async-start | bytes 4718592 | tf_op jit(solution)/shard_map/all_gather | solution.py:1289
  13.9 6.8 collective-permute-start
  223.7 129.7 %copy-start.49 = (f32[8,1280]{1,0:T(8,128)}, f32[8,1280]{1,0:T(8,128)S(1)}, u32[]{:S(2)}) copy-start(f32[8,1280]{1,0:T(8,128)S(1)} %get-tuple-element.277.refs_4_.refs_10_) | copy-start | bytes 122884
  223.7 147.8 %all-gather.5.cloned.1.call-start = ((), (), s32[]{:S(2)}) async-start(), calls=%async_computation.3 | async-start | bytes 4718592 | tf_op jit(solution)/shard_map/all_gather | solution.py:1290
  233.4 36.0 %copy-start = (f32[512,1408]{1,0:T(8,128)}, f32[512,1408]{1,0:T(8,128)S(1)}, u32[]{:S(2)}) copy-start(f32[512,1408]{1,0:T(8,128)S(1)} %fusion.2.refs_1_.refs_3_.refs_4_) | copy-start | bytes 8650756
  233.5 91.2 %copy-start.38 = (f32[8,1280]{1,0:T(8,128)}, f32[8,1280]{1,0:T(8,128)S(1)}, u32[]{:S(2)}) copy-start(f32[8,1280]{1,0:T(8,128)S(1)} %broadcast_in_dim.22.refs_2_.refs_9_.refs_5_) | copy-start | bytes 122884
  247.4 18.6 %collective-permute-start.1 = (f32[2,128]{1,0:T(2,128)S(1)}, f32[2,128]{1,0:T(2,128)S(1)}, u32[]{:S(2)}, u32[]{:S(2)}) collective-permute-start(f32[2,128]{1,0:T(2,128)S(1)} %bitcast.487), channel_id=1, source_target_pairs={{0,16},{16,0},{1,17},{17,1},{2,18},{18,2},{3,19},{19,3},{4,20},{20... | collective-permute-start | bytes 3080 | tf_op jit(solution)/shard_map/ppermute | solution.py:1150
  253.2 12.9 %collective-permute-start.3 = (bf16[2,128,2048]{2,1,0:T(8,128)(2,1)S(1)}, bf16[2,128,2048]{2,1,0:T(8,128)(2,1)S(1)}, u32[]{:S(2)}, u32[]{:S(2)}) collective-permute-start(bf16[2,128,2048]{2,1,0:T(8,128)(2,1)S(1)} %dynamic-slice_bitcast_fusion.9), channel_id=1, source_target_pairs={{0,16},{16,0},{1,17},{17,1},{2,18},{18,2},{3,19},{19,3},{4,20},{20... | collective-permute-start | bytes 3145736 | tf_op jit(solution)/shard_map/ppermute | solution.py:1150
  266.6 13.7 %collective-permute-start.4 = (bf16[128,2048]{1,0:T(8,128)(2,1)S(1)}, bf16[128,2048]{1,0:T(8,128)(2,1)S(1)}, u32[]{:S(2)}, u32[]{:S(2)}) collective-permute-start(bf16[128,2048]{1,0:T(8,128)(2,1)S(1)} %fusion.70), channel_id=1, source_target_pairs={{0,1},{1,0},{2,3},{3,2},{4,5},{5,4},{6,7},{7,6},{8,9},{9,8},{10,11... | collective-permute-start | bytes 1572872 | tf_op jit(solution)/shard_map/ppermute | solution.py:1154
  267.9 12.4 %collective-permute-start.2 = (f32[128]{0:T(128)S(1)}, f32[128]{0:T(128)S(1)}, u32[]{:S(2)}, u32[]{:S(2)}) collective-permute-start(f32[128]{0:T(128)S(1)} %fusion.90), channel_id=1, source_target_pairs={{0,1},{1,0},{2,3},{3,2},{4,5},{5,4},{6,7},{7,6},{8,9},{9,8},{10,11... | collective-permute-start | bytes 1544 | tf_op jit(solution)/shard_map/ppermute | solution.py:1154
  282.3 13.1 %collective-permute-start.5 = (bf16[128,2048]{1,0:T(8,128)(2,1)S(1)}, bf16[128,2048]{1,0:T(8,128)(2,1)S(1)}, u32[]{:S(2)}, u32[]{:S(2)}) collective-permute-start(bf16[128,2048]{1,0:T(8,128)(2,1)S(1)} %multiply_convert_fusion.3), channel_id=1, source_target_pairs={{0,1},{1,0},{2,3},{3,2},{4,5},{5,4},{6,7},{7,6},{8,9},{9,8},{10,11... | collective-permute-start | bytes 1572872 | tf_op jit(solution)/shard_map/ppermute | solution.py:1154
  288.0 13.7 %collective-permute-start.7 = (bf16[2,128,2048]{2,1,0:T(8,128)(2,1)}, bf16[2,128,2048]{2,1,0:T(8,128)(2,1)}, u32[]{:S(2)}, u32[]{:S(2)}) collective-permute-start(bf16[2,128,2048]{2,1,0:T(8,128)(2,1)} %dynamic-slice_bitcast_fusion.8), channel_id=1, source_target_pairs={{0,16},{16,0},{1,17},{17,1},{2,18},{18,2},{3,19},{19,3},{4,20},{20... | collective-permute-start | bytes 3145736 | tf_op jit(solution)/shard_map/ppermute | solution.py:1150
  296.8 7.3 collective-permute-start.6
  298.2 2.1 collective-permute-start.8
  298.3 504.1 %reduce-scatter.5.cloned.1.call-start = ((), (), s32[]{:S(2)}) async-start(), calls=%async_computation.5 | async-start | bytes 4718592 | tf_op jit(solution)/shard_map/reduce_scatter | solution.py:1428
  300.3 9.6 %collective-permute-start.9 = (f32[128]{0:T(128)S(1)}, f32[128]{0:T(128)S(1)}, u32[]{:S(2)}, u32[]{:S(2)}) collective-permute-start(f32[128]{0:T(128)S(1)} %fusion.91), channel_id=1, source_target_pairs={{0,1},{1,0},{2,3},{3,2},{4,5},{5,4},{6,7},{7,6},{8,9},{9,8},{10,11... | collective-permute-start | bytes 1544 | tf_op jit(solution)/shard_map/ppermute | solution.py:1154
  303.8 13.0 %collective-permute-start.10 = (bf16[128,2048]{1,0:T(8,128)(2,1)S(1)}, bf16[128,2048]{1,0:T(8,128)(2,1)S(1)}, u32[]{:S(2)}, u32[]{:S(2)}) collective-permute-start(bf16[128,2048]{1,0:T(8,128)(2,1)S(1)} %fusion.71), channel_id=1, source_target_pairs={{0,1},{1,0},{2,3},{3,2},{4,5},{5,4},{6,7},{7,6},{8,9},{9,8},{10,11... | collective-permute-start | bytes 1572872 | tf_op jit(solution)/shard_map/ppermute | solution.py:1154
  309.9 30.3 %copy-start.1 = (f32[512,1408]{1,0:T(8,128)}, f32[512,1408]{1,0:T(8,128)S(1)}, u32[]{:S(2)}) copy-start(f32[512,1408]{1,0:T(8,128)S(1)} %fusion.110.refs_1_.refs_3_.refs_4_) | copy-start | bytes 8650756
  319.2 16.3 %collective-permute-start.11 = (bf16[128,2048]{1,0:T(8,128)(2,1)}, bf16[128,2048]{1,0:T(8,128)(2,1)}, u32[]{:S(2)}, u32[]{:S(2)}) collective-permute-start(bf16[128,2048]{1,0:T(8,128)(2,1)} %multiply_convert_fusion.2), channel_id=1, source_target_pairs={{0,1},{1,0},{2,3},{3,2},{4,5},{5,4},{6,7},{7,6},{8,9},{9,8},{10,11... | collective-permute-start | bytes 1572872 | tf_op jit(solution)/shard_map/ppermute | solution.py:1154
  338.4 4.4 collective-permute-start.12
  382.0 1.4 collective-permute-start.13
  383.4 2.5 collective-permute-start.14
  394.4 411.2 %reduce-scatter.3.cloned.1.call-start = ((), (), s32[]{:S(2)}) async-start(), calls=%async_computation.4 | async-start | bytes 11206656 | tf_op jit(solution)/shard_map/reduce_scatter | solution.py:1428
  432.0 10.1 %collective-permute-start.15 = (bf16[2,128,2048]{2,1,0:T(8,128)(2,1)}, bf16[2,128,2048]{2,1,0:T(8,128)(2,1)}, u32[]{:S(2)}, u32[]{:S(2)}) collective-permute-start(bf16[2,128,2048]{2,1,0:T(8,128)(2,1)} %dynamic-slice_bitcast_fusion.7), channel_id=1, source_target_pairs={{0,16},{16,0},{1,17},{17,1},{2,18},{18,2},{3,19},{19,3},{4,20},{20... | collective-permute-start | bytes 3145736 | tf_op jit(solution)/shard_map/ppermute | solution.py:1150
  439.9 43.3 %collective-permute-start.30 = (bf16[2,128,2048]{2,1,0:T(8,128)(2,1)}, bf16[2,128,2048]{2,1,0:T(8,128)(2,1)}, u32[]{:S(2)}, u32[]{:S(2)}) collective-permute-start(bf16[2,128,2048]{2,1,0:T(8,128)(2,1)} %dynamic-slice_bitcast_fusion.2), channel_id=1, source_target_pairs={{0,16},{16,0},{1,17},{17,1},{2,18},{18,2},{3,19},{19,3},{4,20},{20... | collective-permute-start | bytes 3145736 | tf_op jit(solution)/shard_map/ppermute | solution.py:1150
  445.0 42.1 %collective-permute-start.16 = (bf16[128,2048]{1,0:T(8,128)(2,1)}, bf16[128,2048]{1,0:T(8,128)(2,1)S(1)}, u32[]{:S(2)}, u32[]{:S(2)}) collective-permute-start(bf16[128,2048]{1,0:T(8,128)(2,1)} %fusion.72), channel_id=1, source_target_pairs={{0,1},{1,0},{2,3},{3,2},{4,5},{5,4},{6,7},{7,6},{8,9},{9,8},{10,11... | collective-permute-start | bytes 1572872 | tf_op jit(solution)/shard_map/ppermute | solution.py:1154
  489.9 14.6 %collective-permute-start.21 = (f32[128,2]{0,1:T(2,128)S(1)}, f32[128,2]{0,1:T(2,128)S(1)}, u32[]{:S(2)}, u32[]{:S(2)}) collective-permute-start(f32[128,2]{0,1:T(2,128)S(1)} %pad_maximum_fusion.15), channel_id=1, source_target_pairs={{0,1},{1,0},{2,3},{3,2},{4,5},{5,4},{6,7},{7,6},{8,9},{9,8},{10,11... | collective-permute-start | bytes 3080 | tf_op jit(solution)/shard_map/ppermute | solution.py:1154
  490.6 17.6 %collective-permute-start.18 = (bf16[128,2048]{1,0:T(8,128)(2,1)S(1)}, bf16[128,2048]{1,0:T(8,128)(2,1)S(1)}, u32[]{:S(2)}, u32[]{:S(2)}) collective-permute-start(bf16[128,2048]{1,0:T(8,128)(2,1)S(1)} %convert_element_type.303), channel_id=1, source_target_pairs={{0,1},{1,0},{2,3},{3,2},{4,5},{5,4},{6,7},{7,6},{8,9},{9,8},{10,11... | collective-permute-start | bytes 1572872 | tf_op jit(solution)/shard_map/ppermute | solution.py:1154
  501.2 9.1 %collective-permute-start.20 = (bf16[2,128,2048]{2,1,0:T(8,128)(2,1)}, bf16[2,128,2048]{2,1,0:T(8,128)(2,1)}, u32[]{:S(2)}, u32[]{:S(2)}) collective-permute-start(bf16[2,128,2048]{2,1,0:T(8,128)(2,1)} %dynamic-slice_bitcast_fusion.4), channel_id=1, source_target_pairs={{0,16},{16,0},{1,17},{17,1},{2,18},{18,2},{3,19},{19,3},{4,20},{20... | collective-permute-start | bytes 3145736 | tf_op jit(solution)/shard_map/ppermute | solution.py:1150
  504.6 2.0 collective-permute-start.22
  506.6 5.8 collective-permute-start.17
  509.8 5.1 collective-permute-start.19
  512.0 28.4 %collective-permute-start.23 = (bf16[128,2048]{1,0:T(8,128)(2,1)S(1)}, bf16[128,2048]{1,0:T(8,128)(2,1)S(1)}, u32[]{:S(2)}, u32[]{:S(2)}) collective-permute-start(bf16[128,2048]{1,0:T(8,128)(2,1)S(1)} %fusion.73), channel_id=1, source_target_pairs={{0,1},{1,0},{2,3},{3,2},{4,5},{5,4},{6,7},{7,6},{8,9},{9,8},{10,11... | collective-permute-start | bytes 1572872 | tf_op jit(solution)/shard_map/ppermute | solution.py:1154
  543.6 13.6 %collective-permute-start.28 = (f32[128,2]{0,1:T(2,128)S(1)}, f32[128,2]{0,1:T(2,128)S(1)}, u32[]{:S(2)}, u32[]{:S(2)}) collective-permute-start(f32[128,2]{0,1:T(2,128)S(1)} %pad_maximum_fusion.16), channel_id=1, source_target_pairs={{0,1},{1,0},{2,3},{3,2},{4,5},{5,4},{6,7},{7,6},{8,9},{9,8},{10,11... | collective-permute-start | bytes 3080 | tf_op jit(solution)/shard_map/ppermute | solution.py:1154
  544.9 14.7 %collective-permute-start.26 = (bf16[128,2048]{1,0:T(8,128)(2,1)S(1)}, bf16[128,2048]{1,0:T(8,128)(2,1)}, u32[]{:S(2)}, u32[]{:S(2)}) collective-permute-start(bf16[128,2048]{1,0:T(8,128)(2,1)S(1)} %convert_element_type.318), channel_id=1, source_target_pairs={{0,1},{1,0},{2,3},{3,2},{4,5},{5,4},{6,7},{7,6},{8,9},{9,8},{10,11... | collective-permute-start | bytes 1572872 | tf_op jit(solution)/shard_map/ppermute | solution.py:1154
  556.0 6.9 collective-permute-start.24
  557.3 2.1 collective-permute-start.29
  561.3 6.8 collective-permute-start.27
  565.4 28.4 %collective-permute-start.33 = (bf16[128,2048]{1,0:T(8,128)(2,1)}, bf16[128,2048]{1,0:T(8,128)(2,1)S(1)}, u32[]{:S(2)}, u32[]{:S(2)}) collective-permute-start(bf16[128,2048]{1,0:T(8,128)(2,1)} %fusion.74), channel_id=1, source_target_pairs={{0,1},{1,0},{2,3},{3,2},{4,5},{5,4},{6,7},{7,6},{8,9},{9,8},{10,11... | collective-permute-start | bytes 1572872 | tf_op jit(solution)/shard_map/ppermute | solution.py:1154
  566.6 39.0 %collective-permute-start.31 = (bf16[128,2048]{1,0:T(8,128)(2,1)}, bf16[128,2048]{1,0:T(8,128)(2,1)S(1)}, u32[]{:S(2)}, u32[]{:S(2)}) collective-permute-start(bf16[128,2048]{1,0:T(8,128)(2,1)} %dynamic-slice_bitcast_fusion.1), channel_id=1, source_target_pairs={{0,1},{1,0},{2,3},{3,2},{4,5},{5,4},{6,7},{7,6},{8,9},{9,8},{10,11... | collective-permute-start | bytes 1572872 | tf_op jit(solution)/shard_map/ppermute | solution.py:1154
  566.8 38.8 %collective-permute-start.25 = (bf16[128,2048]{1,0:T(8,128)(2,1)}, bf16[128,2048]{1,0:T(8,128)(2,1)}, u32[]{:S(2)}, u32[]{:S(2)}) collective-permute-start(bf16[128,2048]{1,0:T(8,128)(2,1)} %dynamic-slice_bitcast_fusion.5), channel_id=1, source_target_pairs={{0,1},{1,0},{2,3},{3,2},{4,5},{5,4},{6,7},{7,6},{8,9},{9,8},{10,11... | collective-permute-start | bytes 1572872 | tf_op jit(solution)/shard_map/ppermute | solution.py:1154
  604.4 11.6 %collective-permute-start.34 = (bf16[2,128,2048]{2,1,0:T(8,128)(2,1)S(1)}, bf16[2,128,2048]{2,1,0:T(8,128)(2,1)S(1)}, u32[]{:S(2)}, u32[]{:S(2)}) collective-permute-start(bf16[2,128,2048]{2,1,0:T(8,128)(2,1)S(1)} %dynamic-slice_bitcast_fusion), channel_id=1, source_target_pairs={{0,16},{16,0},{1,17},{17,1},{2,18},{18,2},{3,19},{19,3},{4,20},{20... | collective-permute-start | bytes 3145736 | tf_op jit(solution)/shard_map/ppermute | solution.py:1150
  608.4 28.4 %collective-permute-start.32 = (f32[128,2048]{1,0:T(8,128)}, f32[128,2048]{1,0:T(8,128)}, u32[]{:S(2)}, u32[]{:S(2)}) collective-permute-start(f32[128,2048]{1,0:T(8,128)} %get-tuple-element.231), channel_id=1, source_target_pairs={{0,16},{16,0},{1,17},{17,1},{2,18},{18,2},{3,19},{19,3},{4,20},{20... | collective-permute-start | bytes 3145736 | tf_op jit(solution)/shard_map/ppermute | solution.py:1150
  616.5 17.6 %collective-permute-start.35 = (bf16[128,2048]{1,0:T(8,128)(2,1)S(1)}, bf16[128,2048]{1,0:T(8,128)(2,1)S(1)}, u32[]{:S(2)}, u32[]{:S(2)}) collective-permute-start(bf16[128,2048]{1,0:T(8,128)(2,1)S(1)} %fusion.75), channel_id=1, source_target_pairs={{0,1},{1,0},{2,3},{3,2},{4,5},{5,4},{6,7},{7,6},{8,9},{9,8},{10,11... | collective-permute-start | bytes 1572872 | tf_op jit(solution)/shard_map/ppermute | solution.py:1154
  636.8 3.8 collective-permute-start.36
  802.4 5.1 collective-permute-start.39
  805.6 3.2 collective-permute-start.37
  809.8 10.2 %collective-permute-start.38 = (f32[256,256]{1,0:T(8,128)S(1)}, f32[256,256]{1,0:T(8,128)S(1)}, u32[]{:S(2)}, u32[]{:S(2)}) collective-permute-start(f32[256,256]{1,0:T(8,128)S(1)} %slice_add_fusion), channel_id=1, source_target_pairs={{0,1},{1,0},{2,3},{3,2},{4,5},{5,4},{6,7},{7,6},{8,9},{9,8},{10,11... | collective-permute-start | bytes 786440 | tf_op jit(solution)/shard_map/ppermute | solution.py:1154
  (160 other events, 872.6 us)
Sparse Core Ops, SparseCore 0:
  223.8 72.0 all-gather.2
  298.4 71.8 all-gather.4
  394.5 89.1 reduce-scatter.4
  487.6 172.5 reduce-scatter.2

commit v7 on v6

--- a/solution.py
+++ b/solution.py
@@ -1041,7 +1041,8 @@
         for k in range(1, DEEP):
             relay_pair(k, True)
             relay_pair(k, False)
-        sum_small()
+            if k == 1:
+                sum_small()
         for i in range(count):
             load_pair(i, here).wait()
             for x in range(2):

time: 836 us -> 838 us (level)
  transfers between devices with their start and end apart: 44 -> 44, of which waited for: 9 -> 9; matrix products, arithmetic and copies ran while one was open for 25% -> 25% of each run, Pallas kernels for 33% -> 34%
where the time goes in v7:
time: 838 us; the launch traced here: 829 us
  Pallas kernels  476 us (57%)
  matrix products  142 us (17%)
  local copies, waits for them, and re-layouts  83.5 us (10%)
  other arithmetic  58.7 us (7%)
  starting transfers between devices  30.3 us (4%)
  waiting for transfers between devices  22.5 us (3%)
  between operations  16.3 us (2%)
    pallas_call x1, Pallas kernels, start_gather(): pl.pallas_call(functools.partial(start_kernel, count=count, micros=micros...  198 us
    pallas_call x1, Pallas kernels, reduce_line(): pl.pallas_call(functools.partial(reduce_kernel, count=count), out_shape=[...  157 us
    pallas_call x4, Pallas kernels, mixer_backward(): pl.pallas_call(body, grid=(steps,), in_specs=[by_row(channels), by_row(2)...  79.1 us
    unnamed x331, local copies, waits for them, and re-layouts  50.1 us
    dot_general x8, matrix products, dot_nt(): lax.dot_general(a, b, (((1,), (1,)), ((), ())), preferred_element_type=F32)  49.7 us
    dot_general x12, matrix products, dot_nn(): lax.dot_general(a, b, (((1,), (0,)), ((), ())), preferred_element_type=F32)  49.5 us
    dot_general x4, matrix products, weight_grad(): lax.dot_general(jnp.concatenate(left), jnp.concatenate(right), over_token...  42.4 us
    pallas_call x4, Pallas kernels, mixer_forward(): pl.pallas_call(body, grid=(steps,), in_specs=[by_row(channels), by_row(wi...  38.3 us
  transfers between devices with their start and end apart: 44, of which 9 were waited for; matrix products, arithmetic and copies ran while one was open for 25% of the time, Pallas kernels for 34%

profile of v7, /device:TPU:9, one launch (start us, length us, event | category | flops | bytes accessed | tf_op | source)
XLA Modules:
  0.0 829.1 jit_solution(3744149036421046274)
XLA Ops:
  7.2 4.0 constant_dynamic-slice_fusion.15
  17.4 3.3 fusion.106
  24.6 198.2 %start_gather.1 = (bf16[8,256,2432]{2,1,0:T(8,128)(2,1)}, bf16[8,256,1024]{2,1,0:T(8,128)(2,1)}, bf16[8,256,1408]{2,1,0:T(8,128)(2,1)}, f32[2,8,8,128]{3,2,1,0:T...) custom-call(bf16[256,2432]{1,0:T(8,128)(2,1)} %get-tuple-element.264, ...), custom_call_target="tpu_custom_call" | custom-call | flops 170000007168 | bytes 1000 | tf_op jit(solution)/shard_map/start_gather/pallas_call | solution.py:805
  223.8 5.3 fusion.32.refs_0_.refs_2_
  230.0 3.4 fusion.2.refs_1_.refs_3_.refs_4_
  233.6 9.2 %mixer_forward.4 = (bf16[512,1024]{1,0:T(8,128)(2,1)S(1)}, f32[512,1]{1,0:T(8,128)S(1)}, f32[512,1024]{1,0:T(8,128)S(1)}, f32[4,128,1024]{2,1,0:T(8,128)S(1)}, f32[128,1024]{1,0:T(8,128)S(1)}) custom-call(f32[512,1024]{1,0:T(8,128)S(1)} %fusion.32.refs_0_.refs_2_, f32[512,1408]{1,0:T(8,128)S(1)} %fusion.2.refs_1_.refs_3_.refs_4_, ...), custom_call_target="tpu_custom_call" | custom-call | flops 1000 | bytes 1000 | tf_op jit(solution)/shard_map/mixer_forward/pallas_call | solution.py:345
  248.2 4.9 convolution_convert_fusion.5
  254.7 5.8 fusion.refs_1_.refs_3_.refs_4_
  260.5 5.6 fusion.30.refs_0_.refs_2_
  269.5 10.2 %mixer_forward.5 = (bf16[512,1024]{1,0:T(8,128)(2,1)S(1)}, f32[512,1]{1,0:T(8,128)S(1)}, f32[512,1024]{1,0:T(8,128)S(1)}, f32[4,128,1024]{2,1,0:T(8,128)S(1)}, f32[128,1024]{1,0:T(8,128)}) custom-call(f32[512,1024]{1,0:T(8,128)S(1)} %fusion.30.refs_0_.refs_2_, f32[512,1408]{1,0:T(8,128)S(1)} %fusion.refs_1_.refs_3_.refs_4_, ...), custom_call_target="tpu_custom_call" | custom-call | flops 1000 | bytes 1000 | tf_op jit(solution)/shard_map/mixer_forward/pallas_call | solution.py:345
  284.4 2.4 convolution_convert_fusion.4
  288.5 6.9 collective-permute-done.5
  301.6 2.1 convert_add_fusion.6
  306.5 3.4 fusion.110.refs_1_.refs_3_.refs_4_
  310.0 6.8 collective-permute-done.10
  319.4 5.2 fusion.109.refs_0_.refs_2_
  324.7 9.1 %mixer_forward.6 = (bf16[512,1024]{1,0:T(8,128)(2,1)S(1)}, f32[512,1]{1,0:T(8,128)S(1)}, f32[512,1024]{1,0:T(8,128)S(1)}, f32[4,128,1024]{2,1,0:T(8,128)S(1)}, f32[128,1024]{1,0:T(8,128)S(1)}) custom-call(f32[512,1024]{1,0:T(8,128)S(1)} %fusion.109.refs_0_.refs_2_, f32[512,1408]{1,0:T(8,128)S(1)} %fusion.110.refs_1_.refs_3_.refs_4_, ...), custom_call_target="tpu_custom_call" | custom-call | flops 1000 | bytes 1000 | tf_op jit(solution)/shard_map/mixer_forward/pallas_call | solution.py:345
  344.9 2.6 copy-done.91
  347.5 2.3 fusion.111.refs_0_.refs_2_
  349.9 3.4 fusion.112.refs_1_.refs_3_.refs_4_
  353.4 9.9 %mixer_forward.7 = (bf16[512,1024]{1,0:T(8,128)(2,1)S(1)}, f32[512,1]{1,0:T(8,128)S(1)}, f32[512,1024]{1,0:T(8,128)S(1)}, f32[4,128,1024]{2,1,0:T(8,128)S(1)}, f32[128,1024]{1,0:T(8,128)}) custom-call(f32[512,1024]{1,0:T(8,128)S(1)} %fusion.111.refs_0_.refs_2_, f32[512,1408]{1,0:T(8,128)S(1)} %fusion.112.refs_1_.refs_3_.refs_4_, ...), custom_call_target="tpu_custom_call" | custom-call | flops 1000 | bytes 1000 | tf_op jit(solution)/shard_map/mixer_forward/pallas_call | solution.py:345
  366.0 2.5 constant_dynamic-update-slice_fusion.1
  368.4 3.1 constant_dynamic-update-slice_fusion
  371.5 6.6 fusion.39
  378.2 3.7 fusion.37
  388.2 6.2 fusion.27
  399.3 21.1 %mixer_backward.4 = (bf16[512,2432]{1,0:T(8,128)(2,1)}, f32[128,1024]{1,0:T(8,128)}, f32[8,1280]{1,0:T(8,128)}, f32[8,1280]{1,0:T(8,128)}) custom-call(f32[512,1024]{1,0:T(8,128)} %get-tuple-element.136.refs_0_, f32[512,2]{1,0:T(8,128)} %copy.74.refs_1_, f32[512,1024]{1,0:T(8,128)} %copy-done.15, f32[512,1408]{1,0:T(8,128)} %copy-done.3, ...), custom_call_target="tpu_custom_call" | custom-call | flops 1000 | bytes 1000 | tf_op jit(solution)/shard_map/mixer_backward/pallas_call | solution.py:396
  420.4 10.5 %convolution_convert_fusion.9 = bf16[512,2048]{1,0:T(8,128)(2,1)S(1)} fusion(bf16[512,2432]{1,0:T(8,128)(2,1)} %get-tuple-element.139, bf16[2048,2432]{1,0:T(8,128)(2,1)} %constant_dynamic-update-slice_fusion), kind=kOutput, calls=%fused_computation.43 | convolution fusion | flops 5101322240 | bytes 14548992 | tf_op jit(solution)/shard_map/dot_general | solution.py:34
  433.5 3.7 convolution_convert_fusion.3
  437.4 2.5 dynamic-slice_bitcast_fusion.2
  442.1 2.1 convert_add_fusion.5
  447.4 20.0 %mixer_backward.5 = (bf16[512,2432]{1,0:T(8,128)(2,1)S(1)}, f32[128,1024]{1,0:T(8,128)}, f32[8,1280]{1,0:T(8,128)}, f32[8,1280]{1,0:T(8,128)S(1)}) custom-call(f32[512,1024]{1,0:T(8,128)S(1)} %copy-done.35, f32[512,2]{1,0:T(8,128)S(1)} %copy.76.refs_1_, f32[512,1024]{1,0:T(8,128)S(1)} %copy-done.14, f32[512,1408]{1,0:T(8,128)} %copy-done.1, ...), custom_call_target="tpu_custom_call" | custom-call | flops 1000 | bytes 1000 | tf_op jit(solution)/shard_map/mixer_backward/pallas_call | solution.py:396
  468.8 13.7 %convolution_convert_fusion.1 = bf16[2048,2432]{1,0:T(8,128)(2,1)} fusion(bf16[512,2432]{1,0:T(8,128)(2,1)S(1)} %copy-done.149, bf16[512,2432]{1,0:T(8,128)(2,1)S(1)} %get-tuple-element.150, bf16[512,2048]{1,0:T(8,128)(2,1)S(1)} %bitcast.447, bf16[512,2048]{1,0:T(8,128)(2,1)S(1)} %bitcast.442), kind=kOutput, calls=%fused_computation.1 | convolution fusion | flops 10223878144 | bytes 19136512 | tf_op jit(solution)/shard_map/dot_general | solution.py:1380
  491.5 8.6 %convolution_convert_fusion.8 = bf16[512,2048]{1,0:T(8,128)(2,1)S(1)} fusion(bf16[512,2432]{1,0:T(8,128)(2,1)S(1)} %copy-done.64, bf16[2048,2432]{1,0:T(8,128)(2,1)} %constant_dynamic-update-slice_fusion), kind=kOutput, calls=%fused_computation.42 | convolution fusion | flops 5101322240 | bytes 14548992 | tf_op jit(solution)/shard_map/dot_general | solution.py:34
  502.1 2.4 convolution_convert_fusion.2
  515.9 2.7 copy-done.152
  518.6 2.3 fusion.113.refs_0_
  521.7 18.6 %mixer_backward.6 = (bf16[512,2432]{1,0:T(8,128)(2,1)S(1)}, f32[128,1024]{1,0:T(8,128)S(1)}, f32[8,1280]{1,0:T(8,128)S(1)}, f32[8,1280]{1,0:T(8,128)S(1)}) custom-call(f32[512,1024]{1,0:T(8,128)S(1)} %fusion.113.refs_0_, f32[512,2]{1,0:T(8,128)S(1)} %bitcast.406, f32[512,1024]{1,0:T(8,128)S(1)} %copy-done.12, f32[512,1408]{1,0:T(8,128)} %copy-done.2, ...), custom_call_target="tpu_custom_call" | custom-call | flops 1000 | bytes 1000 | tf_op jit(solution)/shard_map/mixer_backward/pallas_call | solution.py:396
  545.2 8.4 %convolution_convert_fusion.7 = bf16[512,2048]{1,0:T(8,128)(2,1)S(1)} fusion(bf16[512,2432]{1,0:T(8,128)(2,1)S(1)} %get-tuple-element.175, bf16[2048,2432]{1,0:T(8,128)(2,1)} %bitcast.494), kind=kOutput, calls=%fused_computation.41 | convolution fusion | flops 5101322240 | bytes 14548992 | tf_op jit(solution)/shard_map/dot_general | solution.py:34
  568.6 2.8 copy-done.153
  571.4 2.3 fusion.114.refs_0_
  574.3 19.4 %mixer_backward.7 = (bf16[512,2432]{1,0:T(8,128)(2,1)S(1)}, f32[128,1024]{1,0:T(8,128)}, f32[8,1280]{1,0:T(8,128)}, f32[8,1280]{1,0:T(8,128)S(1)}) custom-call(f32[512,1024]{1,0:T(8,128)S(1)} %fusion.114.refs_0_, f32[512,2]{1,0:T(8,128)S(1)} %bitcast.404, f32[512,1024]{1,0:T(8,128)S(1)} %copy-done.10, f32[512,1408]{1,0:T(8,128)} %copy-done, ...), custom_call_target="tpu_custom_call" | custom-call | flops 1000 | bytes 1000 | tf_op jit(solution)/shard_map/mixer_backward/pallas_call | solution.py:396
  595.4 8.9 %convolution_convert_fusion.6 = bf16[512,2048]{1,0:T(8,128)(2,1)S(1)} fusion(bf16[512,2432]{1,0:T(8,128)(2,1)S(1)} %get-tuple-element.174, bf16[2048,2432]{1,0:T(8,128)(2,1)} %bitcast.495), kind=kOutput, calls=%fused_computation.40 | convolution fusion | flops 5101322240 | bytes 14548992 | tf_op jit(solution)/shard_map/dot_general | solution.py:34
  605.7 2.8 broadcast_select_fusion.2
  609.8 6.2 fusion.24
  617.7 16.3 %convolution_convert_fusion = bf16[2048,2432]{1,0:T(8,128)(2,1)} fusion(bf16[512,2432]{1,0:T(8,128)(2,1)S(1)} %copy-done.62, bf16[512,2432]{1,0:T(8,128)(2,1)S(1)} %get-tuple-element.174, bf16[512,2048]{1,0:T(8,128)(2,1)} %bitcast.504, bf16[512,2048]{1,0:T(8,128)(2,1)} %bitcast.502), kind=kOutput, calls=%fused_computation | convolution fusion | flops 10223878144 | bytes 19136512 | tf_op jit(solution)/shard_map/dot_general | solution.py:1380
  643.6 156.6 %grads_reduce.1 = (bf16[256,2432]{1,0:T(8,128)(2,1)}, bf16[256,1024]{1,0:T(8,128)(2,1)}, bf16[256,2432]{1,0:T(8,128)(2,1)}, bf16[256,1024]{1,0:T(8,128)(2,1)}, f...) custom-call(bf16[8,256,2432]{2,1,0:T(8,128)(2,1)} %bitcast.407, bf16[8,256,1024]{2,1,0:T(8,128)(2,1)} %bitcast.421, ...), custom_call_target="tpu_custom_call" | custom-call | flops 1000 | bytes 1000 | tf_op jit(solution)/shard_map/grads_reduce/pallas_call | solution.py:1117
  816.9 4.0 join_halves.1
  (586 shorter events, 151.1 us)
Async XLA Ops:
  7.2 312.3 %all-gather.3.cloned.1.call-start = ((), (), s32[]{:S(2)}) async-start(), calls=%async_computation.2 | async-start | bytes 4718592 | tf_op jit(solution)/shard_map/all_gather | solution.py:1290
  13.9 6.8 collective-permute-start
  223.7 129.7 %copy-start.49 = (f32[8,1280]{1,0:T(8,128)}, f32[8,1280]{1,0:T(8,128)S(1)}, u32[]{:S(2)}) copy-start(f32[8,1280]{1,0:T(8,128)S(1)} %get-tuple-element.277.refs_4_.refs_10_) | copy-start | bytes 122884
  223.7 147.8 %all-gather.5.cloned.1.call-start = ((), (), s32[]{:S(2)}) async-start(), calls=%async_computation.3 | async-start | bytes 4718592 | tf_op jit(solution)/shard_map/all_gather | solution.py:1291
  233.4 36.0 %copy-start = (f32[512,1408]{1,0:T(8,128)}, f32[512,1408]{1,0:T(8,128)S(1)}, u32[]{:S(2)}) copy-start(f32[512,1408]{1,0:T(8,128)S(1)} %fusion.2.refs_1_.refs_3_.refs_4_) | copy-start | bytes 8650756
  233.5 91.2 %copy-start.38 = (f32[8,1280]{1,0:T(8,128)}, f32[8,1280]{1,0:T(8,128)S(1)}, u32[]{:S(2)}) copy-start(f32[8,1280]{1,0:T(8,128)S(1)} %broadcast_in_dim.22.refs_2_.refs_9_.refs_5_) | copy-start | bytes 122884
  247.4 18.6 %collective-permute-start.1 = (f32[2,128]{1,0:T(2,128)S(1)}, f32[2,128]{1,0:T(2,128)S(1)}, u32[]{:S(2)}, u32[]{:S(2)}) collective-permute-start(f32[2,128]{1,0:T(2,128)S(1)} %bitcast.487), channel_id=1, source_target_pairs={{0,16},{16,0},{1,17},{17,1},{2,18},{18,2},{3,19},{19,3},{4,20},{20... | collective-permute-start | bytes 3080 | tf_op jit(solution)/shard_map/ppermute | solution.py:1151
  253.2 12.9 %collective-permute-start.3 = (bf16[2,128,2048]{2,1,0:T(8,128)(2,1)S(1)}, bf16[2,128,2048]{2,1,0:T(8,128)(2,1)S(1)}, u32[]{:S(2)}, u32[]{:S(2)}) collective-permute-start(bf16[2,128,2048]{2,1,0:T(8,128)(2,1)S(1)} %dynamic-slice_bitcast_fusion.9), channel_id=1, source_target_pairs={{0,16},{16,0},{1,17},{17,1},{2,18},{18,2},{3,19},{19,3},{4,20},{20... | collective-permute-start | bytes 3145736 | tf_op jit(solution)/shard_map/ppermute | solution.py:1151
  266.6 13.7 %collective-permute-start.4 = (bf16[128,2048]{1,0:T(8,128)(2,1)S(1)}, bf16[128,2048]{1,0:T(8,128)(2,1)S(1)}, u32[]{:S(2)}, u32[]{:S(2)}) collective-permute-start(bf16[128,2048]{1,0:T(8,128)(2,1)S(1)} %fusion.70), channel_id=1, source_target_pairs={{0,1},{1,0},{2,3},{3,2},{4,5},{5,4},{6,7},{7,6},{8,9},{9,8},{10,11... | collective-permute-start | bytes 1572872 | tf_op jit(solution)/shard_map/ppermute | solution.py:1155
  267.9 12.4 %collective-permute-start.2 = (f32[128]{0:T(128)S(1)}, f32[128]{0:T(128)S(1)}, u32[]{:S(2)}, u32[]{:S(2)}) collective-permute-start(f32[128]{0:T(128)S(1)} %fusion.90), channel_id=1, source_target_pairs={{0,1},{1,0},{2,3},{3,2},{4,5},{5,4},{6,7},{7,6},{8,9},{9,8},{10,11... | collective-permute-start | bytes 1544 | tf_op jit(solution)/shard_map/ppermute | solution.py:1155
  282.3 13.1 %collective-permute-start.5 = (bf16[128,2048]{1,0:T(8,128)(2,1)S(1)}, bf16[128,2048]{1,0:T(8,128)(2,1)S(1)}, u32[]{:S(2)}, u32[]{:S(2)}) collective-permute-start(bf16[128,2048]{1,0:T(8,128)(2,1)S(1)} %multiply_convert_fusion.3), channel_id=1, source_target_pairs={{0,1},{1,0},{2,3},{3,2},{4,5},{5,4},{6,7},{7,6},{8,9},{9,8},{10,11... | collective-permute-start | bytes 1572872 | tf_op jit(solution)/shard_map/ppermute | solution.py:1155
  288.0 13.7 %collective-permute-start.7 = (bf16[2,128,2048]{2,1,0:T(8,128)(2,1)}, bf16[2,128,2048]{2,1,0:T(8,128)(2,1)}, u32[]{:S(2)}, u32[]{:S(2)}) collective-permute-start(bf16[2,128,2048]{2,1,0:T(8,128)(2,1)} %dynamic-slice_bitcast_fusion.8), channel_id=1, source_target_pairs={{0,16},{16,0},{1,17},{17,1},{2,18},{18,2},{3,19},{19,3},{4,20},{20... | collective-permute-start | bytes 3145736 | tf_op jit(solution)/shard_map/ppermute | solution.py:1151
  296.8 7.3 collective-permute-start.6
  298.2 2.1 collective-permute-start.8
  298.3 505.6 %reduce-scatter.5.cloned.1.call-start = ((), (), s32[]{:S(2)}) async-start(), calls=%async_computation.5 | async-start | bytes 4718592 | tf_op jit(solution)/shard_map/reduce_scatter | solution.py:1429
  300.3 9.6 %collective-permute-start.9 = (f32[128]{0:T(128)S(1)}, f32[128]{0:T(128)S(1)}, u32[]{:S(2)}, u32[]{:S(2)}) collective-permute-start(f32[128]{0:T(128)S(1)} %fusion.91), channel_id=1, source_target_pairs={{0,1},{1,0},{2,3},{3,2},{4,5},{5,4},{6,7},{7,6},{8,9},{9,8},{10,11... | collective-permute-start | bytes 1544 | tf_op jit(solution)/shard_map/ppermute | solution.py:1155
  303.8 13.0 %collective-permute-start.10 = (bf16[128,2048]{1,0:T(8,128)(2,1)S(1)}, bf16[128,2048]{1,0:T(8,128)(2,1)S(1)}, u32[]{:S(2)}, u32[]{:S(2)}) collective-permute-start(bf16[128,2048]{1,0:T(8,128)(2,1)S(1)} %fusion.71), channel_id=1, source_target_pairs={{0,1},{1,0},{2,3},{3,2},{4,5},{5,4},{6,7},{7,6},{8,9},{9,8},{10,11... | collective-permute-start | bytes 1572872 | tf_op jit(solution)/shard_map/ppermute | solution.py:1155
  309.9 30.3 %copy-start.1 = (f32[512,1408]{1,0:T(8,128)}, f32[512,1408]{1,0:T(8,128)S(1)}, u32[]{:S(2)}) copy-start(f32[512,1408]{1,0:T(8,128)S(1)} %fusion.110.refs_1_.refs_3_.refs_4_) | copy-start | bytes 8650756
  319.2 16.3 %collective-permute-start.11 = (bf16[128,2048]{1,0:T(8,128)(2,1)}, bf16[128,2048]{1,0:T(8,128)(2,1)}, u32[]{:S(2)}, u32[]{:S(2)}) collective-permute-start(bf16[128,2048]{1,0:T(8,128)(2,1)} %multiply_convert_fusion.2), channel_id=1, source_target_pairs={{0,1},{1,0},{2,3},{3,2},{4,5},{5,4},{6,7},{7,6},{8,9},{9,8},{10,11... | collective-permute-start | bytes 1572872 | tf_op jit(solution)/shard_map/ppermute | solution.py:1155
  338.4 4.4 collective-permute-start.12
  382.0 1.4 collective-permute-start.13
  383.4 2.5 collective-permute-start.14
  394.4 412.7 %reduce-scatter.3.cloned.1.call-start = ((), (), s32[]{:S(2)}) async-start(), calls=%async_computation.4 | async-start | bytes 11206656 | tf_op jit(solution)/shard_map/reduce_scatter | solution.py:1429
  432.0 10.1 %collective-permute-start.15 = (bf16[2,128,2048]{2,1,0:T(8,128)(2,1)}, bf16[2,128,2048]{2,1,0:T(8,128)(2,1)}, u32[]{:S(2)}, u32[]{:S(2)}) collective-permute-start(bf16[2,128,2048]{2,1,0:T(8,128)(2,1)} %dynamic-slice_bitcast_fusion.7), channel_id=1, source_target_pairs={{0,16},{16,0},{1,17},{17,1},{2,18},{18,2},{3,19},{19,3},{4,20},{20... | collective-permute-start | bytes 3145736 | tf_op jit(solution)/shard_map/ppermute | solution.py:1151
  439.9 43.3 %collective-permute-start.30 = (bf16[2,128,2048]{2,1,0:T(8,128)(2,1)}, bf16[2,128,2048]{2,1,0:T(8,128)(2,1)}, u32[]{:S(2)}, u32[]{:S(2)}) collective-permute-start(bf16[2,128,2048]{2,1,0:T(8,128)(2,1)} %dynamic-slice_bitcast_fusion.2), channel_id=1, source_target_pairs={{0,16},{16,0},{1,17},{17,1},{2,18},{18,2},{3,19},{19,3},{4,20},{20... | collective-permute-start | bytes 3145736 | tf_op jit(solution)/shard_map/ppermute | solution.py:1151
  445.0 42.1 %collective-permute-start.16 = (bf16[128,2048]{1,0:T(8,128)(2,1)}, bf16[128,2048]{1,0:T(8,128)(2,1)S(1)}, u32[]{:S(2)}, u32[]{:S(2)}) collective-permute-start(bf16[128,2048]{1,0:T(8,128)(2,1)} %fusion.72), channel_id=1, source_target_pairs={{0,1},{1,0},{2,3},{3,2},{4,5},{5,4},{6,7},{7,6},{8,9},{9,8},{10,11... | collective-permute-start | bytes 1572872 | tf_op jit(solution)/shard_map/ppermute | solution.py:1155
  489.9 14.6 %collective-permute-start.21 = (f32[128,2]{0,1:T(2,128)S(1)}, f32[128,2]{0,1:T(2,128)S(1)}, u32[]{:S(2)}, u32[]{:S(2)}) collective-permute-start(f32[128,2]{0,1:T(2,128)S(1)} %pad_maximum_fusion.15), channel_id=1, source_target_pairs={{0,1},{1,0},{2,3},{3,2},{4,5},{5,4},{6,7},{7,6},{8,9},{9,8},{10,11... | collective-permute-start | bytes 3080 | tf_op jit(solution)/shard_map/ppermute | solution.py:1155
  490.6 17.6 %collective-permute-start.18 = (bf16[128,2048]{1,0:T(8,128)(2,1)S(1)}, bf16[128,2048]{1,0:T(8,128)(2,1)S(1)}, u32[]{:S(2)}, u32[]{:S(2)}) collective-permute-start(bf16[128,2048]{1,0:T(8,128)(2,1)S(1)} %convert_element_type.303), channel_id=1, source_target_pairs={{0,1},{1,0},{2,3},{3,2},{4,5},{5,4},{6,7},{7,6},{8,9},{9,8},{10,11... | collective-permute-start | bytes 1572872 | tf_op jit(solution)/shard_map/ppermute | solution.py:1155
  501.2 9.1 %collective-permute-start.20 = (bf16[2,128,2048]{2,1,0:T(8,128)(2,1)}, bf16[2,128,2048]{2,1,0:T(8,128)(2,1)}, u32[]{:S(2)}, u32[]{:S(2)}) collective-permute-start(bf16[2,128,2048]{2,1,0:T(8,128)(2,1)} %dynamic-slice_bitcast_fusion.4), channel_id=1, source_target_pairs={{0,16},{16,0},{1,17},{17,1},{2,18},{18,2},{3,19},{19,3},{4,20},{20... | collective-permute-start | bytes 3145736 | tf_op jit(solution)/shard_map/ppermute | solution.py:1151
  504.6 2.0 collective-permute-start.22
  506.6 5.8 collective-permute-start.17
  509.8 5.1 collective-permute-start.19
  512.0 28.4 %collective-permute-start.23 = (bf16[128,2048]{1,0:T(8,128)(2,1)S(1)}, bf16[128,2048]{1,0:T(8,128)(2,1)S(1)}, u32[]{:S(2)}, u32[]{:S(2)}) collective-permute-start(bf16[128,2048]{1,0:T(8,128)(2,1)S(1)} %fusion.73), channel_id=1, source_target_pairs={{0,1},{1,0},{2,3},{3,2},{4,5},{5,4},{6,7},{7,6},{8,9},{9,8},{10,11... | collective-permute-start | bytes 1572872 | tf_op jit(solution)/shard_map/ppermute | solution.py:1155
  543.6 13.6 %collective-permute-start.28 = (f32[128,2]{0,1:T(2,128)S(1)}, f32[128,2]{0,1:T(2,128)S(1)}, u32[]{:S(2)}, u32[]{:S(2)}) collective-permute-start(f32[128,2]{0,1:T(2,128)S(1)} %pad_maximum_fusion.16), channel_id=1, source_target_pairs={{0,1},{1,0},{2,3},{3,2},{4,5},{5,4},{6,7},{7,6},{8,9},{9,8},{10,11... | collective-permute-start | bytes 3080 | tf_op jit(solution)/shard_map/ppermute | solution.py:1155
  544.9 14.7 %collective-permute-start.26 = (bf16[128,2048]{1,0:T(8,128)(2,1)S(1)}, bf16[128,2048]{1,0:T(8,128)(2,1)}, u32[]{:S(2)}, u32[]{:S(2)}) collective-permute-start(bf16[128,2048]{1,0:T(8,128)(2,1)S(1)} %convert_element_type.318), channel_id=1, source_target_pairs={{0,1},{1,0},{2,3},{3,2},{4,5},{5,4},{6,7},{7,6},{8,9},{9,8},{10,11... | collective-permute-start | bytes 1572872 | tf_op jit(solution)/shard_map/ppermute | solution.py:1155
  556.0 6.9 collective-permute-start.24
  557.3 2.1 collective-permute-start.29
  561.3 6.8 collective-permute-start.27
  565.4 28.4 %collective-permute-start.33 = (bf16[128,2048]{1,0:T(8,128)(2,1)}, bf16[128,2048]{1,0:T(8,128)(2,1)S(1)}, u32[]{:S(2)}, u32[]{:S(2)}) collective-permute-start(bf16[128,2048]{1,0:T(8,128)(2,1)} %fusion.74), channel_id=1, source_target_pairs={{0,1},{1,0},{2,3},{3,2},{4,5},{5,4},{6,7},{7,6},{8,9},{9,8},{10,11... | collective-permute-start | bytes 1572872 | tf_op jit(solution)/shard_map/ppermute | solution.py:1155
  566.6 39.0 %collective-permute-start.31 = (bf16[128,2048]{1,0:T(8,128)(2,1)}, bf16[128,2048]{1,0:T(8,128)(2,1)S(1)}, u32[]{:S(2)}, u32[]{:S(2)}) collective-permute-start(bf16[128,2048]{1,0:T(8,128)(2,1)} %dynamic-slice_bitcast_fusion.1), channel_id=1, source_target_pairs={{0,1},{1,0},{2,3},{3,2},{4,5},{5,4},{6,7},{7,6},{8,9},{9,8},{10,11... | collective-permute-start | bytes 1572872 | tf_op jit(solution)/shard_map/ppermute | solution.py:1155
  566.8 38.8 %collective-permute-start.25 = (bf16[128,2048]{1,0:T(8,128)(2,1)}, bf16[128,2048]{1,0:T(8,128)(2,1)}, u32[]{:S(2)}, u32[]{:S(2)}) collective-permute-start(bf16[128,2048]{1,0:T(8,128)(2,1)} %dynamic-slice_bitcast_fusion.5), channel_id=1, source_target_pairs={{0,1},{1,0},{2,3},{3,2},{4,5},{5,4},{6,7},{7,6},{8,9},{9,8},{10,11... | collective-permute-start | bytes 1572872 | tf_op jit(solution)/shard_map/ppermute | solution.py:1155
  604.4 11.6 %collective-permute-start.34 = (bf16[2,128,2048]{2,1,0:T(8,128)(2,1)S(1)}, bf16[2,128,2048]{2,1,0:T(8,128)(2,1)S(1)}, u32[]{:S(2)}, u32[]{:S(2)}) collective-permute-start(bf16[2,128,2048]{2,1,0:T(8,128)(2,1)S(1)} %dynamic-slice_bitcast_fusion), channel_id=1, source_target_pairs={{0,16},{16,0},{1,17},{17,1},{2,18},{18,2},{3,19},{19,3},{4,20},{20... | collective-permute-start | bytes 3145736 | tf_op jit(solution)/shard_map/ppermute | solution.py:1151
  608.4 28.4 %collective-permute-start.32 = (f32[128,2048]{1,0:T(8,128)}, f32[128,2048]{1,0:T(8,128)}, u32[]{:S(2)}, u32[]{:S(2)}) collective-permute-start(f32[128,2048]{1,0:T(8,128)} %get-tuple-element.231), channel_id=1, source_target_pairs={{0,16},{16,0},{1,17},{17,1},{2,18},{18,2},{3,19},{19,3},{4,20},{20... | collective-permute-start | bytes 3145736 | tf_op jit(solution)/shard_map/ppermute | solution.py:1151
  616.5 17.6 %collective-permute-start.35 = (bf16[128,2048]{1,0:T(8,128)(2,1)S(1)}, bf16[128,2048]{1,0:T(8,128)(2,1)S(1)}, u32[]{:S(2)}, u32[]{:S(2)}) collective-permute-start(bf16[128,2048]{1,0:T(8,128)(2,1)S(1)} %fusion.75), channel_id=1, source_target_pairs={{0,1},{1,0},{2,3},{3,2},{4,5},{5,4},{6,7},{7,6},{8,9},{9,8},{10,11... | collective-permute-start | bytes 1572872 | tf_op jit(solution)/shard_map/ppermute | solution.py:1155
  636.8 3.8 collective-permute-start.36
  803.9 5.1 collective-permute-start.39
  807.1 3.2 collective-permute-start.37
  811.3 10.3 %collective-permute-start.38 = (f32[256,256]{1,0:T(8,128)S(1)}, f32[256,256]{1,0:T(8,128)S(1)}, u32[]{:S(2)}, u32[]{:S(2)}) collective-permute-start(f32[256,256]{1,0:T(8,128)S(1)} %slice_add_fusion), channel_id=1, source_target_pairs={{0,1},{1,0},{2,3},{3,2},{4,5},{5,4},{6,7},{7,6},{8,9},{9,8},{10,11... | collective-permute-start | bytes 786440 | tf_op jit(solution)/shard_map/ppermute | solution.py:1155
  (160 other events, 872.7 us)
Sparse Core Ops, SparseCore 0:
  223.8 72.0 all-gather.2
  298.4 71.8 all-gather.4
  394.5 89.1 reduce-scatter.4
  487.6 172.5 reduce-scatter.2
